TPU v7x, 32 devices: a whole 2x2x4 slice. The times are simulated.
32 devices in a mesh: gx: 8 (over z, x), gy: 4 (over y, core).
Axes of the slice: x: 2, y: 2, z: 4, core: 2. Of those that a mesh axis runs over, the one named last changes fastest.
Arguments:
- trial_stress: float32 [16, 1024, 512], P(None, 'gx', 'gy'), may hold values from 1.5 to 3.5
- old_strain: float32 [16, 1024, 512], P(None, 'gx', 'gy'), may hold values from 0 to 0.5
- yield_mask: int32 [16, 1024, 512], P(None, 'gx', 'gy'), may hold values from 0 to 1
- newton_count: int32 [16, 1024, 512], P(None, 'gx', 'gy'), may hold values from 3 to 6
- damage_threshold: float32 [16, 1024, 512], P(None, 'gx', 'gy'), may hold values from 0.1 to 0.5
Outputs:
- plastic_strain: float32 [16, 1024, 512], P(None, 'gx', 'gy')
- damage: float32 [16, 1024, 512], P(None, 'gx', 'gy')
- nodal_force: float32 [2, 16, 1024, 512], P(None, None, 'gx', 'gy')
All inputs are finite; a program needn't handle non-finite values.
Results may differ from a plain program's by a relative error of at most 0.00002.
Values sent between devices are 32-bit elements; how exact they have to be, the bound alone decides.
No kernel may reach another device: no remote copies, remote signals or barrier semaphores. Data moves between devices by JAX's collectives and lax.ppermute only.
A program may use at most 64 MiB of HBM per device.

v0:
```python
import math

import jax
import jax.numpy as jnp
from jax import lax
from jax.sharding import PartitionSpec as P

NEWTON_MAX = 6
OUTER = 3


gauss_taps = [math.exp(-((offset - 8) ** 2) / 32.0) for offset in range(17)]


def extended_2(block, sides, width):
    for axis, dim in sides:
        count = lax.axis_size(axis)
        forward = [(i, i + 1) for i in range(count - 1)]
        backward = [(target, source) for source, target in forward]
        low = lax.ppermute(
            lax.slice_in_dim(block, block.shape[dim] - width, None, axis=dim), axis, forward
        )
        high = lax.ppermute(lax.slice_in_dim(block, 0, width, axis=dim), axis, backward)
        block = jnp.concatenate([low, block, high], axis=dim)
    return block


def from_behind(value, axis, steps):
    count = lax.axis_size(axis)
    first, last = (max(0, -steps), min(count, count - steps))
    return lax.ppermute(value, axis, [(source, source + steps) for source in range(first, last)])


def masked_sweeps(stress_in, strain_in, count_in, damage_in):
    increment = jnp.zeros_like(stress_in)
    soften = 1.0 - 0.5 * damage_in
    for sweep_no in range(1, NEWTON_MAX + 1):
        decay_term = jnp.exp(-4.0 * (strain_in + increment))
        residual = stress_in - increment - (1.0 + 0.5 * (1.0 - decay_term)) * soften
        update = increment + 0.4 * residual / (1.0 + 2.0 * decay_term)
        increment = jnp.where(count_in >= sweep_no, update, increment)
    return increment


def smooth_axis(source, axis_index, length):
    summed = lax.slice_in_dim(source, 0, length, axis=axis_index) * gauss_taps[0]
    for offset in range(1, 17):
        summed = summed + gauss_taps[offset] * lax.slice_in_dim(
            source, offset, offset + length, axis=axis_index
        )
    return summed


def edge_weights(global_start, length, extent):
    positions = global_start + jnp.arange(length, dtype=jnp.int32)
    summed = jnp.zeros((length,), jnp.float32)
    for offset in range(17):
        target = positions + (offset - 8)
        inside = (target >= 0) & (target < extent)
        summed = summed + jnp.where(inside, gauss_taps[offset], 0.0)
    return summed


def local(trial_stress, old_strain, yield_mask, newton_count, damage_threshold):
    layers, row_count, col_count = trial_stress.shape
    counts = yield_mask * newton_count
    weight_z = edge_weights(jnp.int32(0), layers, layers)
    weight_x = edge_weights(
        lax.axis_index("gx") * row_count, row_count, row_count * lax.axis_size("gx")
    )
    weight_y = edge_weights(
        lax.axis_index("gy") * col_count, col_count, col_count * lax.axis_size("gy")
    )
    normal = weight_z[:, None, None] * weight_x[None, :, None] * weight_y[None, None, :]
    damage = jnp.zeros_like(trial_stress)
    for outer_no in range(OUTER):
        increment = masked_sweeps(trial_stress, old_strain, counts, damage)
        plastic_strain = old_strain + increment
        widened = extended_2(plastic_strain, (("gx", 1), ("gy", 2)), 8)
        along_rows = smooth_axis(widened, 1, row_count)
        along_both = smooth_axis(along_rows, 2, col_count)
        depth_padded = jnp.pad(along_both, ((8, 8), (0, 0), (0, 0)))
        averaged = smooth_axis(depth_padded, 0, layers)
        nonlocal_strain = averaged / normal
        damage = 1.0 - jnp.exp(-jnp.maximum(nonlocal_strain - damage_threshold, 0.0) / 0.3)
    stress = (1.0 - damage) * (trial_stress - increment)
    upper_row = from_behind(stress[:, row_count - 1, :], "gx", 1)
    with_upper = jnp.concatenate([upper_row[:, None, :], stress], axis=1)
    left_column = from_behind(with_upper[:, :, col_count - 1], "gy", 1)
    extended = jnp.concatenate([left_column[:, :, None], with_upper], axis=2)
    own_cell = extended[:, 1:, 1:]
    upper_cell = extended[:, :-1, 1:]
    left_cell = extended[:, 1:, :-1]
    corner_cell = extended[:, :-1, :-1]
    force_x = 0.5 * (upper_cell + corner_cell - own_cell - left_cell)
    force_y = 0.5 * (left_cell + corner_cell - own_cell - upper_cell)
    return (plastic_strain, damage, jnp.stack([force_x, force_y]))


def solution(mesh):
    placed = (
        P(None, "gx", "gy"),
        P(None, "gx", "gy"),
        P(None, "gx", "gy"),
        P(None, "gx", "gy"),
        P(None, "gx", "gy"),
    )
    return jax.shard_map(
        local,
        mesh=mesh,
        in_specs=placed,
        out_specs=(P(None, "gx", "gy"), P(None, "gx", "gy"), P(None, None, "gx", "gy")),
        check_vma=False,
    )
```

profile of v0, /device:TPU:0, one launch (start us, length us, event | category | flops | bytes accessed | tf_op | source)
XLA Modules:
  0.0 158.9 jit_solution(2026945582172999797)
XLA Ops:
  0.6 8.8 %fusion.46 = (f32[16,128,128]{2,0,1:T(8,128)S(1)}, pred[16,128,128]{2,0,1:T(8,128)(4,1)}, pred[16,128,128]{2,0,1:T(8,128)(4,1)}, pred[16,128,128]{2,0,1:T(8,128)...) fusion(f32[16,128,128]{2,1,0:T(8,128)} %param.6, ...), kind=kLoop, calls=%fused_computation.173 | loop fusion | flops 21757952 | bytes 6815744 | tf_op jit(solution)/shard_map/add | solution.py:78
  9.5 4.8 %collective-permute-start = (f32[16,8,128]{2,0,1:T(8,128)S(1)}, f32[16,8,128]{2,0,1:T(8,128)S(1)}, u32[]{:S(2)}, u32[]{:S(2)}) collective-permute-start(f32[16,8,128]{2,0,1:T(8,128)S(1)} %get-tuple-element.38), channel_id=1, source_target_pairs={{0,4},{4,8},{8,12},{12,16},{16,20},{20,24},{24,28},{1,5},{5,9},{9,... | collective-permute-start | bytes 196616 | tf_op jit(solution)/shard_map/ppermute | solution.py:20
  14.3 1.3 collective-permute-start.1
  15.7 0.1 broadcast_multiply_fusion
  15.8 0.4 collective-permute-done
  16.2 4.3 %collective-permute-done.1 = f32[16,8,128]{2,0,1:T(8,128)S(1)} collective-permute-done((f32[16,8,128]{2,0,1:T(8,128)S(1)}, f32[16,8,128]{2,0,1:T(8,128)S(1)}, u32[]{:S(2)}, u32[]{:S(2)}) %collective-permute-start.1) | collective-permute-done | bytes 65568 | tf_op jit(solution)/shard_map/ppermute | solution.py:23
  20.5 0.6 copy-done.18
  21.1 0.1 pad_maximum_fusion.4
  21.2 0.4 fusion.259
  21.6 1.3 copy.168
  22.8 1.3 collective-permute-start.2
  24.1 0.6 copy.169
  24.7 1.5 collective-permute-start.3
  26.3 0.5 copy.170
  26.8 3.0 %collective-permute-done.3 = f32[16,144,8]{1,2,0:T(8,128)} collective-permute-done((f32[16,144,8]{1,2,0:T(8,128)S(1)}, f32[16,144,8]{1,2,0:T(8,128)}, u32[]{:S(2)}, u32[]{:S(2)}) %collective-permute-start.3) | collective-permute-done | bytes 73760 | tf_op jit(solution)/shard_map/ppermute | solution.py:23
  29.9 1.5 copy.171
  31.3 1.8 %pad_maximum_fusion = f32[16,144,144]{2,0,1:T(8,128)S(1)} fusion(f32[16,144,8]{2,0,1:T(8,128)S(1)} %copy.171, f32[16,8,128]{2,0,1:T(8,128)} %copy-done.18, f32[16,128,128]{2,0,1:T(8,128)S(1)} %get-tuple-element.19, f32[16,8,128]{2,0,1:T(8,128)S(1)} %collective-permute-done, f32[16,144,8]{2,0,1:T(8,128)S(1)} %copy.170), kind=kLoop, calls=%fused_computation.48 | loop fusion | flops 1327104 | bytes 2654208 | tf_op jit(solution)/shard_map/concatenate | solution.py:24
  33.2 4.6 %fusion.30 = f32[16,128,144]{2,0,1:T(8,128)S(1)} fusion(f32[16,144,144]{2,0,1:T(8,128)S(1)} %pad_maximum_fusion), kind=kLoop, calls=%fused_computation.116 | loop fusion | flops 9437184 | bytes 21233664 | tf_op jit(solution)/shard_map/add | solution.py:48
  37.8 4.5 %fusion.192 = f32[16,128,128]{2,0,1:T(8,128)S(1)} fusion(f32[16,128,144]{2,0,1:T(8,128)S(1)} %fusion.30), kind=kLoop, calls=%fused_computation.357 | loop fusion | flops 8388608 | bytes 18874368 | tf_op jit(solution)/shard_map/add | solution.py:48
  42.4 7.3 %fusion.47 = f32[16,128,128]{2,0,1:T(8,128)S(1)} fusion(pred[16,128,128]{2,0,1:T(8,128)(4,1)S(1)} %copy-done.16, pred[16,128,128]{2,0,1:T(8,128)(4,1)S(1)} %copy-done.14, pred[16,128,128]{2,0,1:T(8,128)(4,1)S(1)} %copy-done.12, pred[16,128,128]{2,0,1:T(8,128)(4,1)S(1)} %copy-done.10, pred[16,128,128]{2,0,1:T(8,128)(4,1)S(1)} %copy-done.8, ...), kind=kLoop, calls=%fused_computation.174 | loop fusion | flops 32243712 | bytes 6824448 | tf_op jit(solution)/shard_map/add | solution.py:78
  49.8 4.4 %collective-permute-start.4 = (f32[16,8,128]{2,0,1:T(8,128)S(1)}, f32[16,8,128]{2,0,1:T(8,128)S(1)}, u32[]{:S(2)}, u32[]{:S(2)}) collective-permute-start(f32[16,8,128]{2,0,1:T(8,128)S(1)} %get-tuple-element.36), channel_id=1, source_target_pairs={{0,4},{4,8},{8,12},{12,16},{16,20},{20,24},{24,28},{1,5},{5,9},{9,... | collective-permute-start | bytes 196616 | tf_op jit(solution)/shard_map/ppermute | solution.py:20
  54.2 1.3 collective-permute-start.5
  55.5 0.6 collective-permute-done.4
  56.0 4.3 %collective-permute-done.5 = f32[16,8,128]{2,0,1:T(8,128)S(1)} collective-permute-done((f32[16,8,128]{2,0,1:T(8,128)S(1)}, f32[16,8,128]{2,0,1:T(8,128)S(1)}, u32[]{:S(2)}, u32[]{:S(2)}) %collective-permute-start.5) | collective-permute-done | bytes 65568 | tf_op jit(solution)/shard_map/ppermute | solution.py:23
  60.3 0.6 copy-done.19
  60.9 0.1 pad_maximum_fusion.5
  61.0 1.8 %fusion.258 = (f32[16,144,8]{2,0,1:T(8,128)}, f32[16,144,8]{2,0,1:T(8,128)}) fusion(f32[16,144,128]{2,0,1:T(8,128)S(1)} %pad_maximum_fusion.5), kind=kLoop, calls=%fused_computation.521 | loop fusion | bytes 294912 | tf_op jit(solution)/shard_map/slice | solution.py:21
  62.8 2.5 %copy.185 = f32[16,144,8]{1,2,0:T(8,128)} copy(f32[16,144,8]{2,0,1:T(8,128)} %get-tuple-element.30) | data formatting | bytes 147456 | tf_op jit(solution)/shard_map/slice | solution.py:21
  65.3 4.6 %collective-permute-start.6 = (f32[16,144,8]{1,2,0:T(8,128)}, f32[16,144,8]{1,2,0:T(8,128)}, u32[]{:S(2)}, u32[]{:S(2)}) collective-permute-start(f32[16,144,8]{1,2,0:T(8,128)} %copy.185), channel_id=1, source_target_pairs={{0,1},{1,2},{2,3},{4,5},{5,6},{6,7},{8,9},{9,10},{10,11},{12,13},{... | collective-permute-start | bytes 221192 | tf_op jit(solution)/shard_map/ppermute | solution.py:20
  69.9 2.5 %copy.186 = f32[16,144,8]{1,2,0:T(8,128)} copy(f32[16,144,8]{2,0,1:T(8,128)} %get-tuple-element.31) | data formatting | bytes 147456 | tf_op jit(solution)/shard_map/slice | solution.py:23
  72.4 1.5 collective-permute-start.7
  74.0 2.4 %copy.187 = f32[16,144,8]{2,0,1:T(8,128)} copy(f32[16,144,8]{1,2,0:T(8,128)} %collective-permute-done.6) | data formatting | bytes 147456 | tf_op jit(solution)/shard_map/ppermute | solution.py:20
  76.4 2.4 %copy.188 = f32[16,144,8]{2,0,1:T(8,128)} copy(f32[16,144,8]{1,2,0:T(8,128)} %collective-permute-done.7) | data formatting | bytes 147456 | tf_op jit(solution)/shard_map/ppermute | solution.py:23
  78.8 2.6 %pad_maximum_fusion.1 = f32[16,144,144]{2,0,1:T(8,128)S(1)} fusion(f32[16,144,8]{2,0,1:T(8,128)} %copy.188, f32[16,8,128]{2,0,1:T(8,128)} %copy-done.19, f32[16,128,128]{2,0,1:T(8,128)S(1)} %fusion.47, f32[16,8,128]{2,0,1:T(8,128)S(1)} %collective-permute-done.4, f32[16,144,8]{2,0,1:T(8,128)} %copy.187), kind=kLoop, calls=%fused_computation.49 | loop fusion | flops 1327104 | bytes 2654208 | tf_op jit(solution)/shard_map/concatenate | solution.py:24
  81.4 4.6 %fusion.15 = f32[16,128,144]{2,0,1:T(8,128)S(1)} fusion(f32[16,144,144]{2,0,1:T(8,128)S(1)} %pad_maximum_fusion.1), kind=kLoop, calls=%fused_computation.84 | loop fusion | flops 9437184 | bytes 21233664 | tf_op jit(solution)/shard_map/add | solution.py:48
  86.0 4.5 %fusion.177 = f32[16,128,128]{2,0,1:T(8,128)S(1)} fusion(f32[16,128,144]{2,0,1:T(8,128)S(1)} %fusion.15), kind=kLoop, calls=%fused_computation.325 | loop fusion | flops 8388608 | bytes 18874368 | tf_op jit(solution)/shard_map/add | solution.py:48
  90.6 8.1 %copy_add_fusion = (f32[16,128,128]{2,0,1:T(8,128)S(1)}, f32[16,128,128]{2,0,1:T(8,128)}) fusion(f32[16,128,128]{2,1,0:T(8,128)S(1)} %copy-done.4, pred[16,128,128]{2,0,1:T(8,128)(4,1)S(1)} %copy-done.17, pred[16,128,128]{2,0,1:T(8,128)(4,1)S(1)} %copy-done.15, pred[16,128,128]{2,0,1:T(8,128)(4,1)S(1)} %copy-done.13, ...), kind=kLoop, calls=%fused_computation.395 | loop fusion | flops 32243712 | bytes 7873024 | tf_op jit(solution)/shard_map/add | solution.py:78
  98.7 3.4 %collective-permute-start.8 = (f32[16,8,128]{2,0,1:T(8,128)S(1)}, f32[16,8,128]{2,0,1:T(8,128)S(1)}, u32[]{:S(2)}, u32[]{:S(2)}) collective-permute-start(f32[16,8,128]{2,0,1:T(8,128)S(1)} %get-tuple-element.34), channel_id=1, source_target_pairs={{0,4},{4,8},{8,12},{12,16},{16,20},{20,24},{24,28},{1,5},{5,9},{9,... | collective-permute-start | bytes 196616 | tf_op jit(solution)/shard_map/ppermute | solution.py:20
  102.1 1.3 collective-permute-start.9
  103.4 0.6 collective-permute-done.8
  104.0 4.3 %collective-permute-done.9 = f32[16,8,128]{2,0,1:T(8,128)S(1)} collective-permute-done((f32[16,8,128]{2,0,1:T(8,128)S(1)}, f32[16,8,128]{2,0,1:T(8,128)S(1)}, u32[]{:S(2)}, u32[]{:S(2)}) %collective-permute-start.9) | collective-permute-done | bytes 65568 | tf_op jit(solution)/shard_map/ppermute | solution.py:23
  108.3 1.4 fusion.257
  109.7 2.5 %copy.202 = f32[16,144,8]{1,2,0:T(8,128)} copy(f32[16,144,8]{2,0,1:T(8,128)} %get-tuple-element.28) | data formatting | bytes 147456 | tf_op jit(solution)/shard_map/slice | solution.py:21
  112.2 4.4 %collective-permute-start.10 = (f32[16,144,8]{1,2,0:T(8,128)}, f32[16,144,8]{1,2,0:T(8,128)}, u32[]{:S(2)}, u32[]{:S(2)}) collective-permute-start(f32[16,144,8]{1,2,0:T(8,128)} %copy.202), channel_id=1, source_target_pairs={{0,1},{1,2},{2,3},{4,5},{5,6},{6,7},{8,9},{9,10},{10,11},{12,13},{... | collective-permute-start | bytes 221192 | tf_op jit(solution)/shard_map/ppermute | solution.py:20
  116.6 1.3 copy.203
  117.8 1.5 collective-permute-start.11
  119.4 1.5 copy.204
  120.9 0.7 collective-permute-done.11
  121.6 2.4 %copy.205 = f32[16,144,8]{2,0,1:T(8,128)} copy(f32[16,144,8]{1,2,0:T(8,128)} %collective-permute-done.11) | data formatting | bytes 147456 | tf_op jit(solution)/shard_map/ppermute | solution.py:23
  124.0 2.2 %pad_maximum_fusion.2 = f32[16,144,144]{2,0,1:T(8,128)S(1)} fusion(f32[16,144,8]{2,0,1:T(8,128)} %copy.205, f32[16,8,128]{2,0,1:T(8,128)S(1)} %collective-permute-done.9, f32[16,128,128]{2,0,1:T(8,128)S(1)} %get-tuple-element.17, f32[16,8,128]{2,0,1:T(8,128)S(1)} %collective-permute-done.8, f32[16,144,8]{2,0,1:T(8,128)S(1)} %copy.204), kind=kLoop, calls=%fused_computation.50 | loop fusion | flops 1327104 | bytes 2654208 | tf_op jit(solution)/shard_map/concatenate | solution.py:24
  126.2 4.6 %fusion = f32[16,128,144]{2,0,1:T(8,128)S(1)} fusion(f32[16,144,144]{2,0,1:T(8,128)S(1)} %pad_maximum_fusion.2), kind=kLoop, calls=%fused_computation.52 | loop fusion | flops 9437184 | bytes 21233664 | tf_op jit(solution)/shard_map/add | solution.py:48
  130.8 4.5 %fusion.162 = f32[16,128,128]{2,0,1:T(8,128)S(1)} fusion(f32[16,128,144]{2,0,1:T(8,128)S(1)} %fusion), kind=kLoop, calls=%fused_computation.293 | loop fusion | flops 8388608 | bytes 18874368 | tf_op jit(solution)/shard_map/add | solution.py:48
  135.4 3.9 %subtract_multiply_fusion = (f32[16,128,128]{2,0,1:T(8,128)S(1)}, f32[16,128,128]{2,0,1:T(8,128)}) fusion(f32[16,128,128]{2,0,1:T(8,128)S(1)} %copy-done.5, f32[16,128,128]{2,1,0:T(8,128)S(1)} %copy-done, f32[16,128,128]{2,1,0:T(8,128)S(1)} %copy-done.2, f32[128]{0:T(128)S(1)} %fusion.254, f32[16,128]{0,1:T(8,128)S(1)} %broadcast_multiply_fusion, ...), kind=kLoop, calls=%fused_computation.391 | loop fusion | flops 11010048 | bytes 6300160 | tf_op jit(solution)/shard_map/mul | solution.py:86
  139.3 4.3 %collective-permute-start.12 = (f32[16,128]{1,0:T(8,128)S(1)}, f32[16,128]{1,0:T(8,128)S(1)}, u32[]{:S(2)}, u32[]{:S(2)}) collective-permute-start(f32[16,128]{1,0:T(8,128)S(1)} %slice_bitcast_fusion), channel_id=1, source_target_pairs={{0,4},{4,8},{8,12},{12,16},{16,20},{20,24},{24,28},{1,5},{5,9},{9,... | collective-permute-start | bytes 24584 | tf_op jit(solution)/shard_map/ppermute | solution.py:31
  143.6 1.3 collective-permute-done.12
  145.0 1.3 pad_maximum_fusion.7
  146.3 1.9 %copy.208 = f32[16,129,1]{1,0,2:T(8,128)S(1)} copy(f32[16,129,1]{2,0,1:T(8,128)} %pad_maximum_fusion.7) | data formatting | bytes 16512 | tf_op jit(solution)/shard_map/slice | solution.py:89
  148.3 4.6 %collective-permute-start.13 = (f32[16,129]{1,0:T(8,128)S(1)}, f32[16,129]{1,0:T(8,128)S(1)}, u32[]{:S(2)}, u32[]{:S(2)}) collective-permute-start(f32[16,129]{1,0:T(8,128)S(1)} %bitcast.11), channel_id=1, source_target_pairs={{0,1},{1,2},{2,3},{4,5},{5,6},{6,7},{8,9},{9,10},{10,11},{12,13},{... | collective-permute-start | bytes 24776 | tf_op jit(solution)/shard_map/ppermute | solution.py:31
  152.8 1.3 copy.210
  154.1 1.3 copy.211
  155.4 0.8 copy.209
  156.2 0.6 multiply_bitcast_fusion.1
  156.8 0.1 pad_maximum_fusion.3
  157.0 1.9 %copy.212 = f32[2,16,128,128]{3,2,1,0:T(8,128)} copy(f32[2,16,128,128]{3,1,2,0:T(8,128)S(1)} %pad_maximum_fusion.3) | data formatting | bytes 4194304
  (51 shorter events, 0.3 us)
Async XLA Ops:
  9.5 6.7 %collective-permute-start = (f32[16,8,128]{2,0,1:T(8,128)S(1)}, f32[16,8,128]{2,0,1:T(8,128)S(1)}, u32[]{:S(2)}, u32[]{:S(2)}) collective-permute-start(f32[16,8,128]{2,0,1:T(8,128)S(1)} %get-tuple-element.38), channel_id=1, source_target_pairs={{0,4},{4,8},{8,12},{12,16},{16,20},{20,24},{24,28},{1,5},{5,9},{9,... | collective-permute-start | bytes 196616 | tf_op jit(solution)/shard_map/ppermute | solution.py:20
  14.3 6.2 %collective-permute-start.1 = (f32[16,8,128]{2,0,1:T(8,128)S(1)}, f32[16,8,128]{2,0,1:T(8,128)S(1)}, u32[]{:S(2)}, u32[]{:S(2)}) collective-permute-start(f32[16,8,128]{2,0,1:T(8,128)S(1)} %get-tuple-element.39), channel_id=1, source_target_pairs={{4,0},{8,4},{12,8},{16,12},{20,16},{24,20},{28,24},{5,1},{9,5},{13... | collective-permute-start | bytes 196616 | tf_op jit(solution)/shard_map/ppermute | solution.py:23
  20.5 0.6 copy-start.18
  22.8 3.4 %collective-permute-start.2 = (f32[16,144,8]{1,2,0:T(8,128)}, f32[16,144,8]{1,2,0:T(8,128)S(1)}, u32[]{:S(2)}, u32[]{:S(2)}) collective-permute-start(f32[16,144,8]{1,2,0:T(8,128)} %copy.168), channel_id=1, source_target_pairs={{0,1},{1,2},{2,3},{4,5},{5,6},{6,7},{8,9},{9,10},{10,11},{12,13},{... | collective-permute-start | bytes 221192 | tf_op jit(solution)/shard_map/ppermute | solution.py:20
  24.7 5.1 %collective-permute-start.3 = (f32[16,144,8]{1,2,0:T(8,128)S(1)}, f32[16,144,8]{1,2,0:T(8,128)}, u32[]{:S(2)}, u32[]{:S(2)}) collective-permute-start(f32[16,144,8]{1,2,0:T(8,128)S(1)} %copy.169), channel_id=1, source_target_pairs={{1,0},{2,1},{3,2},{5,4},{6,5},{7,6},{9,8},{10,9},{11,10},{13,12},{... | collective-permute-start | bytes 221192 | tf_op jit(solution)/shard_map/ppermute | solution.py:23
  37.7 4.6 %copy-start = (f32[16,128,128]{2,1,0:T(8,128)S(1)}, f32[16,128,128]{2,1,0:T(8,128)}, u32[]{:S(2)}) copy-start(f32[16,128,128]{2,1,0:T(8,128)} %param.5) | copy-start | bytes 3145732
  37.8 4.6 %copy-start.1 = (f32[16,128,128]{2,1,0:T(8,128)S(1)}, f32[16,128,128]{2,1,0:T(8,128)}, u32[]{:S(2)}) copy-start(f32[16,128,128]{2,1,0:T(8,128)} %param.9) | copy-start | bytes 3145732
  37.8 4.6 %copy-start.3 = (f32[16,128,128]{2,1,0:T(8,128)S(1)}, f32[16,128,128]{2,1,0:T(8,128)}, u32[]{:S(2)}) copy-start(f32[16,128,128]{2,1,0:T(8,128)} %param.6) | copy-start | bytes 3145732
  37.8 4.6 %copy-start.7 = (pred[16,128,128]{2,0,1:T(8,128)(4,1)S(1)}, pred[16,128,128]{2,0,1:T(8,128)(4,1)}, u32[]{:S(2)}) copy-start(pred[16,128,128]{2,0,1:T(8,128)(4,1)} %get-tuple-element.20) | copy-start | bytes 786436
  37.8 4.6 %copy-start.8 = (pred[16,128,128]{2,0,1:T(8,128)(4,1)S(1)}, pred[16,128,128]{2,0,1:T(8,128)(4,1)}, u32[]{:S(2)}) copy-start(pred[16,128,128]{2,0,1:T(8,128)(4,1)} %get-tuple-element.21) | copy-start | bytes 786436
  37.8 4.6 %copy-start.10 = (pred[16,128,128]{2,0,1:T(8,128)(4,1)S(1)}, pred[16,128,128]{2,0,1:T(8,128)(4,1)}, u32[]{:S(2)}) copy-start(pred[16,128,128]{2,0,1:T(8,128)(4,1)} %get-tuple-element.22) | copy-start | bytes 786436
  37.8 4.6 %copy-start.12 = (pred[16,128,128]{2,0,1:T(8,128)(4,1)S(1)}, pred[16,128,128]{2,0,1:T(8,128)(4,1)}, u32[]{:S(2)}) copy-start(pred[16,128,128]{2,0,1:T(8,128)(4,1)} %get-tuple-element.23) | copy-start | bytes 786436
  37.8 4.6 %copy-start.14 = (pred[16,128,128]{2,0,1:T(8,128)(4,1)S(1)}, pred[16,128,128]{2,0,1:T(8,128)(4,1)}, u32[]{:S(2)}) copy-start(pred[16,128,128]{2,0,1:T(8,128)(4,1)} %get-tuple-element.24) | copy-start | bytes 786436
  37.8 4.6 %copy-start.16 = (pred[16,128,128]{2,0,1:T(8,128)(4,1)S(1)}, pred[16,128,128]{2,0,1:T(8,128)(4,1)}, u32[]{:S(2)}) copy-start(pred[16,128,128]{2,0,1:T(8,128)(4,1)} %get-tuple-element.25) | copy-start | bytes 786436
  49.8 6.2 %collective-permute-start.4 = (f32[16,8,128]{2,0,1:T(8,128)S(1)}, f32[16,8,128]{2,0,1:T(8,128)S(1)}, u32[]{:S(2)}, u32[]{:S(2)}) collective-permute-start(f32[16,8,128]{2,0,1:T(8,128)S(1)} %get-tuple-element.36), channel_id=1, source_target_pairs={{0,4},{4,8},{8,12},{12,16},{16,20},{20,24},{24,28},{1,5},{5,9},{9,... | collective-permute-start | bytes 196616 | tf_op jit(solution)/shard_map/ppermute | solution.py:20
  54.2 6.2 %collective-permute-start.5 = (f32[16,8,128]{2,0,1:T(8,128)S(1)}, f32[16,8,128]{2,0,1:T(8,128)S(1)}, u32[]{:S(2)}, u32[]{:S(2)}) collective-permute-start(f32[16,8,128]{2,0,1:T(8,128)S(1)} %get-tuple-element.37), channel_id=1, source_target_pairs={{4,0},{8,4},{12,8},{16,12},{20,16},{24,20},{28,24},{5,1},{9,5},{13... | collective-permute-start | bytes 196616 | tf_op jit(solution)/shard_map/ppermute | solution.py:23
  60.3 0.6 copy-start.19
  65.3 8.6 %collective-permute-start.6 = (f32[16,144,8]{1,2,0:T(8,128)}, f32[16,144,8]{1,2,0:T(8,128)}, u32[]{:S(2)}, u32[]{:S(2)}) collective-permute-start(f32[16,144,8]{1,2,0:T(8,128)} %copy.185), channel_id=1, source_target_pairs={{0,1},{1,2},{2,3},{4,5},{5,6},{6,7},{8,9},{9,10},{10,11},{12,13},{... | collective-permute-start | bytes 221192 | tf_op jit(solution)/shard_map/ppermute | solution.py:20
  72.4 3.9 %collective-permute-start.7 = (f32[16,144,8]{1,2,0:T(8,128)}, f32[16,144,8]{1,2,0:T(8,128)}, u32[]{:S(2)}, u32[]{:S(2)}) collective-permute-start(f32[16,144,8]{1,2,0:T(8,128)} %copy.186), channel_id=1, source_target_pairs={{1,0},{2,1},{3,2},{5,4},{6,5},{7,6},{9,8},{10,9},{11,10},{13,12},{... | collective-permute-start | bytes 221192 | tf_op jit(solution)/shard_map/ppermute | solution.py:23
  86.0 4.6 %copy-start.4 = (f32[16,128,128]{2,1,0:T(8,128)S(1)}, f32[16,128,128]{2,1,0:T(8,128)}, u32[]{:S(2)}) copy-start(f32[16,128,128]{2,1,0:T(8,128)} %param.6) | copy-start | bytes 3145732
  86.0 4.6 %copy-start.9 = (pred[16,128,128]{2,0,1:T(8,128)(4,1)S(1)}, pred[16,128,128]{2,0,1:T(8,128)(4,1)}, u32[]{:S(2)}) copy-start(pred[16,128,128]{2,0,1:T(8,128)(4,1)} %get-tuple-element.21) | copy-start | bytes 786436
  86.0 4.6 %copy-start.11 = (pred[16,128,128]{2,0,1:T(8,128)(4,1)S(1)}, pred[16,128,128]{2,0,1:T(8,128)(4,1)}, u32[]{:S(2)}) copy-start(pred[16,128,128]{2,0,1:T(8,128)(4,1)} %get-tuple-element.22) | copy-start | bytes 786436
  86.0 4.6 %copy-start.13 = (pred[16,128,128]{2,0,1:T(8,128)(4,1)S(1)}, pred[16,128,128]{2,0,1:T(8,128)(4,1)}, u32[]{:S(2)}) copy-start(pred[16,128,128]{2,0,1:T(8,128)(4,1)} %get-tuple-element.23) | copy-start | bytes 786436
  86.0 4.6 %copy-start.15 = (pred[16,128,128]{2,0,1:T(8,128)(4,1)S(1)}, pred[16,128,128]{2,0,1:T(8,128)(4,1)}, u32[]{:S(2)}) copy-start(pred[16,128,128]{2,0,1:T(8,128)(4,1)} %get-tuple-element.24) | copy-start | bytes 786436
  86.0 4.6 %copy-start.17 = (pred[16,128,128]{2,0,1:T(8,128)(4,1)S(1)}, pred[16,128,128]{2,0,1:T(8,128)(4,1)}, u32[]{:S(2)}) copy-start(pred[16,128,128]{2,0,1:T(8,128)(4,1)} %get-tuple-element.25) | copy-start | bytes 786436
  98.7 5.3 %collective-permute-start.8 = (f32[16,8,128]{2,0,1:T(8,128)S(1)}, f32[16,8,128]{2,0,1:T(8,128)S(1)}, u32[]{:S(2)}, u32[]{:S(2)}) collective-permute-start(f32[16,8,128]{2,0,1:T(8,128)S(1)} %get-tuple-element.34), channel_id=1, source_target_pairs={{0,4},{4,8},{8,12},{12,16},{16,20},{20,24},{24,28},{1,5},{5,9},{9,... | collective-permute-start | bytes 196616 | tf_op jit(solution)/shard_map/ppermute | solution.py:20
  102.1 6.2 %collective-permute-start.9 = (f32[16,8,128]{2,0,1:T(8,128)S(1)}, f32[16,8,128]{2,0,1:T(8,128)S(1)}, u32[]{:S(2)}, u32[]{:S(2)}) collective-permute-start(f32[16,8,128]{2,0,1:T(8,128)S(1)} %get-tuple-element.35), channel_id=1, source_target_pairs={{4,0},{8,4},{12,8},{16,12},{20,16},{24,20},{28,24},{5,1},{9,5},{13... | collective-permute-start | bytes 196616 | tf_op jit(solution)/shard_map/ppermute | solution.py:23
  112.2 7.2 %collective-permute-start.10 = (f32[16,144,8]{1,2,0:T(8,128)}, f32[16,144,8]{1,2,0:T(8,128)}, u32[]{:S(2)}, u32[]{:S(2)}) collective-permute-start(f32[16,144,8]{1,2,0:T(8,128)} %copy.202), channel_id=1, source_target_pairs={{0,1},{1,2},{2,3},{4,5},{5,6},{6,7},{8,9},{9,10},{10,11},{12,13},{... | collective-permute-start | bytes 221192 | tf_op jit(solution)/shard_map/ppermute | solution.py:20
  117.8 3.7 %collective-permute-start.11 = (f32[16,144,8]{1,2,0:T(8,128)}, f32[16,144,8]{1,2,0:T(8,128)}, u32[]{:S(2)}, u32[]{:S(2)}) collective-permute-start(f32[16,144,8]{1,2,0:T(8,128)} %copy.203), channel_id=1, source_target_pairs={{1,0},{2,1},{3,2},{5,4},{6,5},{7,6},{9,8},{10,9},{11,10},{13,12},{... | collective-permute-start | bytes 221192 | tf_op jit(solution)/shard_map/ppermute | solution.py:23
  130.8 4.5 %copy-start.2 = (f32[16,128,128]{2,1,0:T(8,128)S(1)}, f32[16,128,128]{2,1,0:T(8,128)}, u32[]{:S(2)}) copy-start(f32[16,128,128]{2,1,0:T(8,128)} %param.9) | copy-start | bytes 3145732
  130.8 4.5 %copy-start.5 = (f32[16,128,128]{2,0,1:T(8,128)S(1)}, f32[16,128,128]{2,0,1:T(8,128)}, u32[]{:S(2)}) copy-start(f32[16,128,128]{2,0,1:T(8,128)} %get-tuple-element.18) | copy-start | bytes 3145732
  139.3 5.7 %collective-permute-start.12 = (f32[16,128]{1,0:T(8,128)S(1)}, f32[16,128]{1,0:T(8,128)S(1)}, u32[]{:S(2)}, u32[]{:S(2)}) collective-permute-start(f32[16,128]{1,0:T(8,128)S(1)} %slice_bitcast_fusion), channel_id=1, source_target_pairs={{0,4},{4,8},{8,12},{12,16},{16,20},{20,24},{24,28},{1,5},{5,9},{9,... | collective-permute-start | bytes 24584 | tf_op jit(solution)/shard_map/ppermute | solution.py:31
  146.3 7.8 %copy-start.6 = (f32[16,128,128]{2,0,1:T(8,128)S(1)}, f32[16,128,128]{2,0,1:T(8,128)}, u32[]{:S(2)}) copy-start(f32[16,128,128]{2,0,1:T(8,128)} %get-tuple-element.16) | copy-start | bytes 3145732
  148.3 7.2 %collective-permute-start.13 = (f32[16,129]{1,0:T(8,128)S(1)}, f32[16,129]{1,0:T(8,128)S(1)}, u32[]{:S(2)}, u32[]{:S(2)}) collective-permute-start(f32[16,129]{1,0:T(8,128)S(1)} %bitcast.11), channel_id=1, source_target_pairs={{0,1},{1,2},{2,3},{4,5},{5,6},{6,7},{8,9},{9,10},{10,11},{12,13},{... | collective-permute-start | bytes 24776 | tf_op jit(solution)/shard_map/ppermute | solution.py:31
where the time goes:
time: 160 us; the launch traced here: 159 us
  other arithmetic  64.5 us (40%)
  starting transfers between devices  40.2 us (25%)
  local copies, waits for them, and re-layouts  33.5 us (21%)
  waiting for transfers between devices  19.5 us (12%)
    add x6, other arithmetic, smooth_axis(): summed + gauss_taps[offset] * lax.slice_in_dim(source, offset, offset + l...  27.2 us
    add x3, other arithmetic, local(): plastic_strain = old_strain + increment  24.2 us
    ppermute x6, starting transfers between devices, extended_2(): lax.ppermute(lax.slice_in_dim(block, block.shape[dim] - width, None, axis...  22.9 us
    ppermute x6, waiting for transfers between devices, extended_2(): lax.ppermute(lax.slice_in_dim(block, 0, width, axis=dim), axis, backward)  16.6 us
    slice x9, local copies, waits for them, and re-layouts, extended_2(): lax.slice_in_dim(block, block.shape[dim] - width, None, axis=dim)  9.84 us
    ppermute x2, starting transfers between devices, from_behind(): lax.ppermute(value, axis, [(source, source + steps) for source in range(f...  8.91 us
    ppermute x6, starting transfers between devices, extended_2(): lax.ppermute(lax.slice_in_dim(block, 0, width, axis=dim), axis, backward)  8.4 us
    concatenate x6, other arithmetic, extended_2(): block = jnp.concatenate([low, block, high], axis=dim)  6.91 us
  transfers between devices with their start and end apart: 14, of which 9 were waited for; matrix products, arithmetic and copies ran while one was open for 7% of the time, Pallas kernels for 0%

commit v1 on v0

v1 whole, which is shorter than its diff:
```python
import functools
import math

import jax
import jax.numpy as jnp
import ml_dtypes
import numpy as np
from jax import lax
from jax.experimental import pallas as pl
from jax.experimental.pallas import tpu as pltpu
from jax.sharding import PartitionSpec as P

OUTER = 3
REACH = 8
LOG2E = math.log2(math.e)
HALF_LN2 = 0.5 * math.log(2.0)
VMEM_BYTES = 24 * 1024 * 1024


def tap(offset):
    return math.exp(-(offset**2) / 32.0) if abs(offset) <= REACH else 0.0


def band(length):
    return np.array([[tap(c - r) for c in range(length)] for r in range(length)])


def depth_matrix(layers):
    weights = band(layers)
    return weights / weights.sum(axis=1, keepdims=True)


def down_block():
    return np.array([[tap(REACH + i - r) for r in range(REACH)] for i in range(REACH)])


def up_block():
    return np.array([[tap(REACH + r - i) for r in range(REACH)] for i in range(REACH)])


def halves(matrix):
    exact = np.asarray(matrix, np.float64)
    high = exact.astype(ml_dtypes.bfloat16)
    low = (exact - high.astype(np.float64)).astype(ml_dtypes.bfloat16)
    return high, low


def left_constant(matrix):
    high, low = halves(matrix)
    return np.block([[high, high], [low, low]])


def right_constant(matrix):
    high, low = halves(matrix)
    return np.block([[high, low], [high, low]])


def split(value):
    high = value.astype(jnp.bfloat16)
    low = (value - high.astype(jnp.float32)).astype(jnp.bfloat16)
    return high, low


def left_product(constant, value):
    rows = constant.shape[0] // 2
    both = jnp.dot(constant, jnp.concatenate(split(value), axis=0), preferred_element_type=jnp.float32)
    return both[:rows] + both[rows:]


def right_product(value, constant):
    cols = constant.shape[1] // 2
    both = jnp.dot(jnp.concatenate(split(value), axis=1), constant, preferred_element_type=jnp.float32)
    return both[:, :cols] + both[:, cols:]


def newton_state(stress, strain, yields, count, soften):
    start = 2.0 * stress - 3.5 * soften
    shift = start + (2.0 * strain - HALF_LN2)
    drop = 0.2 * soften
    state = start
    for sweep_no in range(1, 7):
        update = state * (0.8 - 0.2 * jnp.tanh(shift - state)) - drop
        state = update if sweep_no <= 3 else jnp.where(count >= sweep_no, update, state)
    return jnp.where(yields > 0, state, start)


def plastic(stress, strain, soften, state):
    return (strain + (stress - 1.75 * soften)) - 0.5 * state


def depth_smooth(layers, matrix):
    count = len(layers)
    half = count // 2
    sums = [layers[k] + layers[count - 1 - k] for k in range(half)]
    diffs = [layers[k] - layers[count - 1 - k] for k in range(half)]
    out = [None] * count
    for row in range(half):
        even = odd = None
        for k in range(half):
            near, far = matrix[row, k], matrix[row, count - 1 - k]
            plus, minus = float(0.5 * (near + far)), float(0.5 * (near - far))
            if plus == 0.0 and minus == 0.0:
                continue
            even = sums[k] * plus if even is None else even + sums[k] * plus
            odd = diffs[k] * minus if odd is None else odd + diffs[k] * minus
        out[row] = even + odd
        out[count - 1 - row] = even - odd
    return out


def slot_ids(shape):
    return lax.broadcasted_iota(jnp.int32, shape, 1) // REACH


def sides(axis, even, odd):
    first = lax.axis_index(axis) % 2 == 0
    return jnp.where(first, odd, even), jnp.where(first, even, odd)


def partners(axis, low, high):
    first = lax.axis_index(axis) % 2 == 0
    return jnp.where(first, high, low), jnp.where(first, low, high)


def add_columns(value, layer, low, high):
    cols = value.shape[1]
    slots = slot_ids(value.shape)
    packed = jnp.where(slots == layer, low, high)
    moved = pltpu.roll(packed, (cols - layer * REACH) % cols, 1) if layer else packed
    return value + jnp.where((slots == 0) | (slots == cols // REACH - 1), moved, 0.0)


def retained(smooth, norm, threshold):
    return jnp.exp2(jnp.minimum(threshold - smooth * norm, 0.0) * (LOG2E / 0.3))


def edge_kernel(fresh, *refs):
    if fresh:
        (stress, strain, yields, count, up_ref, down_ref, even_ref, odd_ref, block) = refs
    else:
        (stress, strain, yields, count, threshold, smooth, col_even, col_odd, norm,
         up_ref, down_ref, even_ref, odd_ref, block) = refs
    layers, rows = stress.shape[0], stress.shape[1]
    sent = []
    for first_row, constant in ((0, up_ref), (rows - REACH, down_ref)):
        part = pl.ds(first_row, REACH)
        if not fresh:
            low, high = sides("gy", col_even[part, :], col_odd[part, :])
        for layer in range(layers):
            if fresh:
                soften = jnp.ones_like(stress[layer, part, :])
            else:
                full = add_columns(smooth[layer, part, :], layer, low, high)
                soften = 0.5 + 0.5 * retained(full, norm[part, :], threshold[layer, part, :])
            at = (layer, part, slice(None))
            state = newton_state(stress[at], strain[at], yields[at], count[at], soften)
            block[pl.ds(layer * REACH, REACH), :] = plastic(stress[at], strain[at], soften, state)
        sent.append(left_product(constant[...], block[...]))
    even, odd = partners("gx", *sent)
    even_ref[...] = even
    odd_ref[...] = odd


def main_kernel(depth, fresh, last, *refs):
    if fresh:
        (stress, strain, yields, count, band_ref, toward_low, toward_high, *outs) = refs
    else:
        (stress, strain, yields, count, threshold, smooth, col_even, col_odd, norm,
         band_ref, toward_low, toward_high, *outs) = refs
    if last:
        across, low_cols, high_cols, plastic_out, effective, deep, pack_low, pack_high = outs
    else:
        across, low_cols, high_cols, deep, pack_low, pack_high = outs
    layers, rows, cols = stress.shape

    def sweep(index, carry):
        part = pl.ds(pl.multiple_of(index * REACH, REACH), REACH)
        if not fresh:
            low, high = sides("gy", col_even[part, :], col_odd[part, :])
        values = []
        for layer in range(layers):
            at = (layer, part, slice(None))
            if fresh:
                soften = jnp.ones_like(stress[at])
            else:
                full = add_columns(smooth[at], layer, low, high)
                soften = 0.5 + 0.5 * retained(full, norm[part, :], threshold[at])
            state = newton_state(stress[at], strain[at], yields[at], count[at], soften)
            value = plastic(stress[at], strain[at], soften, state)
            values.append(value)
            if last:
                plastic_out[at] = value
                effective[at] = 1.75 * soften + 0.5 * state
        for layer, value in enumerate(depth_smooth(values, depth)):
            deep[layer, part, :] = value
        return carry

    lax.fori_loop(0, rows // REACH, sweep, 0)

    constant = band_ref[...]
    for layer in range(0, layers, 2):
        pair = jnp.concatenate([deep[layer], deep[layer + 1]], axis=1)
        result = left_product(constant, pair)
        across[layer] = result[:, :cols]
        across[layer + 1] = result[:, cols:]

    def pack(index, carry):
        part = pl.ds(pl.multiple_of(index * REACH, REACH), REACH)
        low, high = pack_edges([across[layer, part, :] for layer in range(layers)])
        pack_low[part, :] = low
        pack_high[part, :] = high
        return carry

    lax.fori_loop(0, rows // REACH, pack, 0)
    low_cols[...] = right_product(pack_low[...], toward_low[...])
    high_cols[...] = right_product(pack_high[...], toward_high[...])


def pack_edges(values):
    cols = values[0].shape[1]
    slots = slot_ids(values[0].shape)
    low = high = jnp.zeros_like(values[0])
    for layer, value in enumerate(values):
        moved = pltpu.roll(value, layer * REACH, 1) if layer else value
        low = jnp.where(slots == layer, moved, low)
        high = jnp.where(slots == (layer - 1) % (cols // REACH), moved, high)
    return low, high


def corner_kernel(row_even, row_odd, low_cols, high_cols, toward_low, toward_high, even_ref, odd_ref):
    rows, cols = low_cols.shape
    layers = row_even.shape[0] // REACH
    low_rows, high_rows = sides("gx", row_even[...], row_odd[...])
    packs = [
        pack_edges([block[layer * REACH : (layer + 1) * REACH] for layer in range(layers)])
        for block in (low_rows, high_rows)
    ]
    low_add = right_product(jnp.concatenate([packs[0][0], packs[1][0]], axis=0), toward_low[...])
    high_add = right_product(jnp.concatenate([packs[0][1], packs[1][1]], axis=0), toward_high[...])
    even, odd = partners("gy", low_cols[...], high_cols[...])
    even_add, odd_add = partners("gy", low_add, high_add)
    for ref, base, add in ((even_ref, even, even_add), (odd_ref, odd, odd_add)):
        ref[...] = base
        ref[pl.ds(0, REACH), :] = base[:REACH] + add[:REACH]
        ref[pl.ds(rows - REACH, REACH), :] = base[rows - REACH :] + add[REACH:]


def column_kernel(across, row_even, row_odd, band_ref, smooth):
    layers, rows, cols = across.shape
    constant = band_ref[...]
    low_rows, high_rows = sides("gx", row_even[...], row_odd[...])
    for layer in range(layers):
        block = slice(layer * REACH, (layer + 1) * REACH)
        value = across[layer]
        value = jnp.concatenate(
            [
                value[:REACH] + low_rows[block],
                value[REACH : rows - REACH],
                value[rows - REACH :] + high_rows[block],
            ],
            axis=0,
        )
        smooth[layer] = right_product(value, constant)


def final_kernel(effective, threshold, smooth, col_even, col_odd, norm, damage, stress):
    layers, rows, cols = effective.shape

    def finish(index, carry):
        part = pl.ds(pl.multiple_of(index * REACH, REACH), REACH)
        low, high = sides("gy", col_even[part, :], col_odd[part, :])
        for layer in range(layers):
            at = (layer, part, slice(None))
            full = add_columns(smooth[at], layer, low, high)
            kept = retained(full, norm[part, :], threshold[at])
            damage[at] = 1.0 - kept
            stress[at] = kept * effective[at]
        return carry

    lax.fori_loop(0, rows // REACH, finish, 0)


def call(kernel, outs, scratch, cost, *operands):
    space = pl.BlockSpec(memory_space=pltpu.VMEM)
    return pl.pallas_call(
        kernel,
        out_shape=[jax.ShapeDtypeStruct(shape, jnp.float32) for shape in outs],
        in_specs=[space] * len(operands),
        out_specs=[space] * len(outs),
        scratch_shapes=[pltpu.VMEM(shape, jnp.float32) for shape in scratch],
        compiler_params=pltpu.CompilerParams(vmem_limit_bytes=VMEM_BYTES),
        cost_estimate=pl.CostEstimate(flops=cost, bytes_accessed=cost // 16, transcendentals=0),
    )(*operands)


def exchange(axis, even, odd):
    count = lax.axis_size(axis)
    results = []
    for start, value in ((0, even), (1, odd)):
        pairs = []
        for low in range(start, count - 1, 2):
            pairs += [(low, low + 1), (low + 1, low)]
        results.append(lax.ppermute(value, axis, pairs))
    return results


def edge_weights(axis, length):
    extent = length * lax.axis_size(axis)
    positions = lax.axis_index(axis) * length + jnp.arange(length, dtype=jnp.int32)
    total = jnp.zeros((length,), jnp.float32)
    for offset in range(-REACH, REACH + 1):
        inside = (positions + offset >= 0) & (positions + offset < extent)
        total = total + jnp.where(inside, tap(offset), 0.0)
    return total


def from_behind(value, axis):
    count = lax.axis_size(axis)
    return lax.ppermute(value, axis, [(source, source + 1) for source in range(count - 1)])


def local(trial_stress, old_strain, yield_mask, newton_count, damage_threshold):
    layers, rows, cols = trial_stress.shape
    slots = cols // REACH
    assert layers == slots and layers % 2 == 0
    depth = depth_matrix(layers)
    to_above = left_constant(np.kron(depth, down_block()))
    to_below = left_constant(np.kron(depth, up_block()))
    row_band = left_constant(band(rows))
    col_band = right_constant(band(cols))
    low_matrix = np.zeros((cols, cols))
    high_matrix = np.zeros((cols, cols))
    for layer in range(layers):
        own = slice(layer * REACH, (layer + 1) * REACH)
        before = (layer - 1) % slots
        other = slice(before * REACH, (before + 1) * REACH)
        low_matrix[own, other] = up_block().T
        high_matrix[other, own] = down_block().T
    toward_low = right_constant(low_matrix)
    toward_high = right_constant(high_matrix)

    norm = 1.0 / (edge_weights("gx", rows)[:, None] * edge_weights("gy", cols)[None, :])
    inputs = (trial_stress, old_strain, yield_mask, newton_count)
    whole = (layers, rows, cols)
    strip = (layers * REACH, cols)
    packed = (rows, layers * REACH)
    work = layers * rows * cols

    state = ()
    for outer_no in range(OUTER):
        fresh, last = outer_no == 0, outer_no == OUTER - 1
        row_even, row_odd = call(
            functools.partial(edge_kernel, fresh),
            [strip, strip], [strip], work * 16,
            *inputs, *state, to_below, to_above,
        )
        row_even, row_odd = exchange("gx", row_even, row_odd)
        across, low_cols, high_cols, *results = call(
            functools.partial(main_kernel, depth, fresh, last),
            [whole, packed, packed] + ([whole, whole] if last else []),
            [whole, packed, packed], work * 400,
            *inputs, *state, row_band, toward_low, toward_high,
        )
        col_even, col_odd = call(
            corner_kernel, [packed, packed], [], work * 16,
            row_even, row_odd, low_cols, high_cols, toward_low, toward_high,
        )
        col_even, col_odd = exchange("gy", col_even, col_odd)
        (smooth,) = call(
            column_kernel, [whole], [], work * 100, across, row_even, row_odd, col_band
        )
        state = (damage_threshold, smooth, col_even, col_odd, norm)
    plastic_strain, effective = results
    damage, stress = call(final_kernel, [whole, whole], [], work * 100, effective, *state)

    upper_row = from_behind(stress[:, rows - 1, :], "gx")
    with_upper = jnp.concatenate([upper_row[:, None, :], stress], axis=1)
    left_column = from_behind(with_upper[:, :, cols - 1], "gy")
    extended = jnp.concatenate([left_column[:, :, None], with_upper], axis=2)
    own_cell = extended[:, 1:, 1:]
    upper_cell = extended[:, :-1, 1:]
    left_cell = extended[:, 1:, :-1]
    corner_cell = extended[:, :-1, :-1]
    force_x = 0.5 * (upper_cell + corner_cell - own_cell - left_cell)
    force_y = 0.5 * (left_cell + corner_cell - own_cell - upper_cell)
    return plastic_strain, damage, jnp.stack([force_x, force_y])


def solution(mesh):
    split_in = P(None, "gx", "gy")
    return jax.shard_map(
        local,
        mesh=mesh,
        in_specs=(split_in,) * 5,
        out_specs=(split_in, split_in, P(None, None, "gx", "gy")),
        check_vma=False,
    )
```

time: 160 us -> 82.7 us (0.52)
  the two profiles are of different devices: /device:TPU:0 before, /device:TPU:6 now
where the time goes in v1:
time: 82.7 us; the launch traced here: 82.1 us
  Pallas kernels  29.1 us (35%)
  starting transfers between devices  25.2 us (30%)
  waiting for transfers between devices  14.5 us (18%)
  local copies, waits for them, and re-layouts  9.02 us (11%)
  other arithmetic  3.37 us (4%)
  between operations  1 us (1%)
    pallas_call x13, Pallas kernels, call(): pl.pallas_call(kernel, out_shape=[jax.ShapeDtypeStruct(shape, jnp.float32...  29.1 us
    ppermute x12, starting transfers between devices, exchange(): results.append(lax.ppermute(value, axis, pairs))  21.3 us
    unnamed x36, local copies, waits for them, and re-layouts  7.98 us
    ppermute x12, waiting for transfers between devices, exchange(): results.append(lax.ppermute(value, axis, pairs))  7.76 us
    ppermute x2, waiting for transfers between devices, from_behind(): lax.ppermute(value, axis, [(source, source + 1) for source in range(count...  6.74 us
    ppermute x2, starting transfers between devices, from_behind(): lax.ppermute(value, axis, [(source, source + 1) for source in range(count...  3.84 us
    another operation x2, other arithmetic, local(): return (plastic_strain, damage, jnp.stack([force_x, force_y]))  2.28 us
  transfers between devices with their start and end apart: 14, of which 5 were waited for; matrix products, arithmetic and copies ran while one was open for 0% of the time, Pallas kernels for 27%

profile of v1, /device:TPU:6, one launch (start us, length us, event | category | flops | bytes accessed | tf_op | source)
XLA Modules:
  0.0 82.1 jit_solution(7483361893448146360)
XLA Ops:
  0.6 0.0 copy-start
  0.6 1.2 %copy-done = f32[16,128,128]{2,1,0:T(8,128)S(1)} copy-done((f32[16,128,128]{2,1,0:T(8,128)S(1)}, f32[16,128,128]{2,1,0:T(8,128)}, u32[]{:S(2)}) %copy-start) | copy-done | bytes 1048600
  1.9 1.2 %copy-done.2 = f32[16,128,128]{2,1,0:T(8,128)S(1)} copy-done((f32[16,128,128]{2,1,0:T(8,128)S(1)}, f32[16,128,128]{2,1,0:T(8,128)}, u32[]{:S(2)}) %copy-start.2) | copy-done | bytes 1048600
  3.1 1.2 %copy-done.4 = s32[16,128,128]{2,1,0:T(8,128)S(1)} copy-done((s32[16,128,128]{2,1,0:T(8,128)S(1)}, s32[16,128,128]{2,1,0:T(8,128)}, u32[]{:S(2)}) %copy-start.4) | copy-done | bytes 1048600
  4.3 1.2 %copy-done.6 = s32[16,128,128]{2,1,0:T(8,128)S(1)} copy-done((s32[16,128,128]{2,1,0:T(8,128)S(1)}, s32[16,128,128]{2,1,0:T(8,128)}, u32[]{:S(2)}) %copy-start.6) | copy-done | bytes 1048600
  5.5 0.9 %copy-done.13 = bf16[256,256]{1,0:T(8,128)(2,1)S(1)} copy-done((bf16[256,256]{1,0:T(8,128)(2,1)S(1)}, bf16[256,256]{1,0:T(8,128)(2,1)}, u32[]{:S(2)}) %copy-start.13) | copy-done | bytes 131096
  6.4 0.9 %copy-done.15 = bf16[256,256]{1,0:T(8,128)(2,1)S(1)} copy-done((bf16[256,256]{1,0:T(8,128)(2,1)S(1)}, bf16[256,256]{1,0:T(8,128)(2,1)}, u32[]{:S(2)}) %copy-start.15) | copy-done | bytes 131096
  7.4 0.0 copy-start.11
  7.4 0.0 copy-start.17
  7.4 1.1 %shard_map.131 = (f32[128,128]{1,0:T(8,128)}, f32[128,128]{1,0:T(8,128)}) custom-call(f32[16,128,128]{2,1,0:T(8,128)S(1)} %copy-done, f32[16,128,128]{2,1,0:T(8,128)S(1)} %copy-done.2, s32[16,128,128]{2,1,0:T(8,128)S(1)} %copy-done.4, s32[16,128,128]{2,1,0:T(8,128)S(1)} %copy-done.6, bf16[256,256]{1,0:T(8,128)(2,1)S(1)} %copy-done.15, ...), custom_call_target="tpu_custom_call" | custom-call | flops 4194304 | bytes 262144 | tf_op jit(solution)/shard_map/pallas_call | solution.py:285
  8.5 0.5 collective-permute-start
  9.1 4.4 %collective-permute-start.1 = (f32[128,128]{1,0:T(8,128)}, f32[128,128]{1,0:T(8,128)}, u32[]{:S(2)}, u32[]{:S(2)}) collective-permute-start(f32[128,128]{1,0:T(8,128)} %get-tuple-element.30), channel_id=1, source_target_pairs={{4,8},{8,4},{12,16},{16,12},{20,24},{24,20},{5,9},{9,5},{13,17},{1... | collective-permute-start | bytes 196616 | tf_op jit(solution)/shard_map/ppermute | solution.py:303
  13.5 0.0 copy-start.7
  13.5 1.2 %copy-done.7 = s32[16,128,128]{2,1,0:T(8,128)S(1)} copy-done((s32[16,128,128]{2,1,0:T(8,128)S(1)}, s32[16,128,128]{2,1,0:T(8,128)}, u32[]{:S(2)}) %copy-start.7) | copy-done | bytes 1048600
  14.8 5.1 %shard_map.130 = (f32[16,128,128]{2,1,0:T(8,128)S(1)}, f32[128,128]{1,0:T(8,128)S(1)}, f32[128,128]{1,0:T(8,128)S(1)}) custom-call(f32[16,128,128]{2,1,0:T(8,128)S(1)} %copy-done.1, f32[16,128,128]{2,1,0:T(8,128)S(1)} %copy-done.3, s32[16,128,128]{2,1,0:T(8,128)S(1)} %copy-done.5, s32[16,128,128]{2,1,0:T(8,128)S(1)} %copy-done.7, ...), custom_call_target="tpu_custom_call" | custom-call | flops 104857600 | bytes 6553600 | tf_op jit(solution)/shard_map/pallas_call | solution.py:285
  19.9 0.0 collective-permute-done.row_even
  19.9 0.0 collective-permute-done.1.row_odd
  19.9 1.1 %shard_map.133 = (f32[128,128]{1,0:T(8,128)S(1)}, f32[128,128]{1,0:T(8,128)S(1)}) custom-call(f32[128,128]{1,0:T(8,128)} %collective-permute-done.row_even, f32[128,128]{1,0:T(8,128)} %collective-permute-done.1.row_odd, f32[128,128]{1,0:T(8,128)S(1)} %get-tuple-element.31.low_cols, f32[128,128]{1,0:T(8,128)S(1)} %get-tuple-element.32.high_cols, ...), custom_call_target="tpu_custom_call" | custom-call | flops 4194304 | bytes 262144 | tf_op jit(solution)/shard_map/pallas_call | solution.py:285
  21.1 0.0 collective-permute-start.2
  21.1 2.5 %collective-permute-start.3 = (f32[128,128]{1,0:T(8,128)S(1)}, f32[128,128]{1,0:T(8,128)S(1)}, u32[]{:S(2)}, u32[]{:S(2)}) collective-permute-start(f32[128,128]{1,0:T(8,128)S(1)} %get-tuple-element.34), channel_id=1, source_target_pairs={{1,2},{2,1},{5,6},{6,5},{9,10},{10,9},{13,14},{14,13},{17,18},{18,... | collective-permute-start | bytes 196616 | tf_op jit(solution)/shard_map/ppermute | solution.py:303
  23.6 0.1 multiply_divide_fusion.refs_8_.norm
  23.7 0.0 copy-start.8
  23.7 0.0 copy-start.9
  23.7 0.0 copy-start.14
  23.7 0.0 copy-start.16
  23.7 1.5 %shard_map.132.refs_5_ = f32[16,128,128]{2,1,0:T(8,128)S(1)} custom-call(f32[16,128,128]{2,1,0:T(8,128)S(1)} %get-tuple-element.28.across, f32[128,128]{1,0:T(8,128)} %collective-permute-done.row_even, f32[128,128]{1,0:T(8,128)} %collective-permute-done.1.row_odd, bf16[256,256]{1,0:T(8,128)(2,1)S(1)} %copy-done.12), custom_call_target="tpu_custom_call" | custom-call | flops 26214400 | bytes 1638400 | tf_op jit(solution)/shard_map/pallas_call | solution.py:285
  25.2 0.0 collective-permute-done.2.refs_6_
  25.2 1.4 %collective-permute-done.3.refs_7_ = f32[128,128]{1,0:T(8,128)S(1)} collective-permute-done((f32[128,128]{1,0:T(8,128)S(1)}, f32[128,128]{1,0:T(8,128)S(1)}, u32[]{:S(2)}, u32[]{:S(2)}) %collective-permute-start.3) | collective-permute-done | bytes 65568 | tf_op jit(solution)/shard_map/ppermute | solution.py:303
  26.6 0.0 copy-done.14
  26.6 0.0 copy-done.16
  26.7 0.6 shard_map.135
  27.3 0.1 collective-permute-start.4
  27.3 4.9 %collective-permute-start.5 = (f32[128,128]{1,0:T(8,128)S(1)}, f32[128,128]{1,0:T(8,128)S(1)}, u32[]{:S(2)}, u32[]{:S(2)}) collective-permute-start(f32[128,128]{1,0:T(8,128)S(1)} %get-tuple-element.37), channel_id=1, source_target_pairs={{4,8},{8,4},{12,16},{16,12},{20,24},{24,20},{5,9},{9,5},{13,17},{1... | collective-permute-start | bytes 196616 | tf_op jit(solution)/shard_map/ppermute | solution.py:303
  32.3 7.0 %shard_map.134 = (f32[16,128,128]{2,1,0:T(8,128)S(1)}, f32[128,128]{1,0:T(8,128)S(1)}, f32[128,128]{1,0:T(8,128)S(1)}) custom-call(f32[16,128,128]{2,1,0:T(8,128)S(1)} %copy-done.1, f32[16,128,128]{2,1,0:T(8,128)S(1)} %copy-done.3, s32[16,128,128]{2,1,0:T(8,128)S(1)} %copy-done.5, s32[16,128,128]{2,1,0:T(8,128)S(1)} %copy-done.8, ...), custom_call_target="tpu_custom_call" | custom-call | flops 104857600 | bytes 6553600 | tf_op jit(solution)/shard_map/pallas_call | solution.py:285
  39.3 0.0 collective-permute-done.4.row_even
  39.3 0.0 collective-permute-done.5.row_odd
  39.3 0.2 shard_map.137
  39.5 0.0 collective-permute-start.6
  39.5 2.0 %collective-permute-start.7 = (f32[128,128]{1,0:T(8,128)S(1)}, f32[128,128]{1,0:T(8,128)S(1)}, u32[]{:S(2)}, u32[]{:S(2)}) collective-permute-start(f32[128,128]{1,0:T(8,128)S(1)} %get-tuple-element.41), channel_id=1, source_target_pairs={{1,2},{2,1},{5,6},{6,5},{9,10},{10,9},{13,14},{14,13},{17,18},{18,... | collective-permute-start | bytes 196616 | tf_op jit(solution)/shard_map/ppermute | solution.py:303
  41.5 0.5 shard_map.136.refs_5_
  42.0 0.0 collective-permute-done.6.refs_6_
  42.0 3.1 %collective-permute-done.7.refs_7_ = f32[128,128]{1,0:T(8,128)S(1)} collective-permute-done((f32[128,128]{1,0:T(8,128)S(1)}, f32[128,128]{1,0:T(8,128)S(1)}, u32[]{:S(2)}, u32[]{:S(2)}) %collective-permute-start.7) | collective-permute-done | bytes 65568 | tf_op jit(solution)/shard_map/ppermute | solution.py:303
  45.1 0.6 shard_map.139
  45.7 0.1 collective-permute-start.8
  45.8 4.9 %collective-permute-start.9 = (f32[128,128]{1,0:T(8,128)S(1)}, f32[128,128]{1,0:T(8,128)S(1)}, u32[]{:S(2)}, u32[]{:S(2)}) collective-permute-start(f32[128,128]{1,0:T(8,128)S(1)} %get-tuple-element.46), channel_id=1, source_target_pairs={{4,8},{8,4},{12,16},{16,12},{20,24},{24,20},{5,9},{9,5},{13,17},{1... | collective-permute-start | bytes 196616 | tf_op jit(solution)/shard_map/ppermute | solution.py:303
  50.7 7.9 %shard_map.138 = (f32[16,128,128]{2,1,0:T(8,128)S(1)}, f32[128,128]{1,0:T(8,128)S(1)}, f32[128,128]{1,0:T(8,128)S(1)}, f32[16,128,128]{2,1,0:T(8,128)}, f32[16,128,128]{2,1,0:T(8,128)S(1)}) custom-call(f32[16,128,128]{2,1,0:T(8,128)S(1)} %copy-done.1, f32[16,128,128]{2,1,0:T(8,128)S(1)} %copy-done.3, s32[16,128,128]{2,1,0:T(8,128)S(1)} %copy-done.5, ...), custom_call_target="tpu_custom_call" | custom-call | flops 104857600 | bytes 6553600 | tf_op jit(solution)/shard_map/pallas_call | solution.py:285
  58.7 0.0 collective-permute-done.8.row_even
  58.7 0.0 collective-permute-done.9.row_odd
  58.7 0.2 shard_map.141
  58.9 0.0 collective-permute-start.10
  58.9 1.9 %collective-permute-start.11 = (f32[128,128]{1,0:T(8,128)S(1)}, f32[128,128]{1,0:T(8,128)S(1)}, u32[]{:S(2)}, u32[]{:S(2)}) collective-permute-start(f32[128,128]{1,0:T(8,128)S(1)} %get-tuple-element.50), channel_id=1, source_target_pairs={{1,2},{2,1},{5,6},{6,5},{9,10},{10,9},{13,14},{14,13},{17,18},{18,... | collective-permute-start | bytes 196616 | tf_op jit(solution)/shard_map/ppermute | solution.py:303
  60.8 0.5 shard_map.140.smooth
  61.3 0.0 collective-permute-done.10.col_even
  61.3 3.2 %collective-permute-done.11.col_odd = f32[128,128]{1,0:T(8,128)S(1)} collective-permute-done((f32[128,128]{1,0:T(8,128)S(1)}, f32[128,128]{1,0:T(8,128)S(1)}, u32[]{:S(2)}, u32[]{:S(2)}) %collective-permute-start.11) | collective-permute-done | bytes 65568 | tf_op jit(solution)/shard_map/ppermute | solution.py:303
  64.5 2.7 %shard_map.142 = (f32[16,128,128]{2,1,0:T(8,128)}, f32[16,128,128]{2,1,0:T(8,128)S(1)}) custom-call(f32[16,128,128]{2,1,0:T(8,128)S(1)} %get-tuple-element.43.effective, f32[16,128,128]{2,1,0:T(8,128)S(1)} %copy-done.9, f32[16,128,128]{2,1,0:T(8,128)S(1)} %shard_map.140.smooth, f32[128,128]{1,0:T(8,128)S(1)} %collective-permute-done.10.col_even, ...), custom_call_target="tpu_custom_call" | custom-call | flops 26214400 | bytes 1638400 | tf_op jit(solution)/shard_map/pallas_call | solution.py:285
  67.2 0.6 copy.18
  67.9 1.9 %collective-permute-start.12 = (f32[16,128]{1,0:T(8,128)S(1)}, f32[16,128]{1,0:T(8,128)S(1)}, u32[]{:S(2)}, u32[]{:S(2)}) collective-permute-start(f32[16,128]{1,0:T(8,128)S(1)} %slice_bitcast_fusion), channel_id=1, source_target_pairs={{0,4},{4,8},{8,12},{12,16},{16,20},{20,24},{24,28},{1,5},{5,9},{9,... | collective-permute-start | bytes 24584 | tf_op jit(solution)/shard_map/ppermute | solution.py:319
  69.8 3.6 %collective-permute-done.12 = f32[16,128]{1,0:T(8,128)S(1)} collective-permute-done((f32[16,128]{1,0:T(8,128)S(1)}, f32[16,128]{1,0:T(8,128)S(1)}, u32[]{:S(2)}, u32[]{:S(2)}) %collective-permute-start.12) | collective-permute-done | bytes 8224 | tf_op jit(solution)/shard_map/ppermute | solution.py:319
  73.4 1.0 %fusion = f32[16,129]{1,0:T(8,128)S(1)} fusion(f32[16,128,128]{2,1,0:T(8,128)S(1)} %get-tuple-element.52, f32[16,1,128]{2,1,0:T(1,128)S(1)} %bitcast.8), kind=kLoop, calls=%fused_computation.2 | loop fusion | flops 2064 | bytes 1065024 | tf_op jit(solution)/shard_map/slice | solution.py:378
  74.4 1.9 %collective-permute-start.13 = (f32[16,129]{1,0:T(8,128)S(1)}, f32[16,129]{1,0:T(8,128)S(1)}, u32[]{:S(2)}, u32[]{:S(2)}) collective-permute-start(f32[16,129]{1,0:T(8,128)S(1)} %fusion), channel_id=1, source_target_pairs={{0,1},{1,2},{2,3},{4,5},{5,6},{6,7},{8,9},{9,10},{10,11},{12,13},{... | collective-permute-start | bytes 24776 | tf_op jit(solution)/shard_map/ppermute | solution.py:319
  76.3 3.1 %collective-permute-done.13 = f32[16,129]{1,0:T(8,128)S(1)} collective-permute-done((f32[16,129]{1,0:T(8,128)S(1)}, f32[16,129]{1,0:T(8,128)S(1)}, u32[]{:S(2)}, u32[]{:S(2)}) %collective-permute-start.13) | collective-permute-done | bytes 8288 | tf_op jit(solution)/shard_map/ppermute | solution.py:319
  79.4 0.4 copy.19
  79.9 0.8 multiply_bitcast_fusion.1
  80.7 1.5 %pad_maximum_fusion = f32[2,16,128,128]{3,2,1,0:T(8,128)} fusion(f32[1,16,128,128]{3,2,1,0:T(8,128)S(1)} %get-tuple-element.54, f32[1,16,128,128]{3,2,1,0:T(8,128)S(1)} %get-tuple-element.53), kind=kLoop, calls=%fused_computation | loop fusion | flops 524288 | bytes 4194304 | tf_op jit(solution)/shard_map/stack | solution.py:386
  (21 shorter events, 0.1 us)
Async XLA Ops:
  0.6 1.2 %copy-start = (f32[16,128,128]{2,1,0:T(8,128)S(1)}, f32[16,128,128]{2,1,0:T(8,128)}, u32[]{:S(2)}) copy-start(f32[16,128,128]{2,1,0:T(8,128)} %refs_0_.11) | copy-start | bytes 3145732
  1.9 1.2 %copy-start.2 = (f32[16,128,128]{2,1,0:T(8,128)S(1)}, f32[16,128,128]{2,1,0:T(8,128)}, u32[]{:S(2)}) copy-start(f32[16,128,128]{2,1,0:T(8,128)} %refs_1_.11) | copy-start | bytes 3145732
  3.1 1.2 %copy-start.4 = (s32[16,128,128]{2,1,0:T(8,128)S(1)}, s32[16,128,128]{2,1,0:T(8,128)}, u32[]{:S(2)}) copy-start(s32[16,128,128]{2,1,0:T(8,128)} %refs_2_.11) | copy-start | bytes 3145732
  4.3 1.2 %copy-start.6 = (s32[16,128,128]{2,1,0:T(8,128)S(1)}, s32[16,128,128]{2,1,0:T(8,128)}, u32[]{:S(2)}) copy-start(s32[16,128,128]{2,1,0:T(8,128)} %refs_3_.11) | copy-start | bytes 3145732
  5.5 0.9 %copy-start.13 = (bf16[256,256]{1,0:T(8,128)(2,1)S(1)}, bf16[256,256]{1,0:T(8,128)(2,1)}, u32[]{:S(2)}) copy-start(bf16[256,256]{1,0:T(8,128)(2,1)} %constant.85.clone.refs_5_.refs_10_) | copy-start | bytes 393220
  6.4 0.9 %copy-start.15 = (bf16[256,256]{1,0:T(8,128)(2,1)S(1)}, bf16[256,256]{1,0:T(8,128)(2,1)}, u32[]{:S(2)}) copy-start(bf16[256,256]{1,0:T(8,128)(2,1)} %constant.84.clone.refs_4_.refs_9_) | copy-start | bytes 393220
  7.3 6.1 %copy-start.1 = (f32[16,128,128]{2,1,0:T(8,128)S(1)}, f32[16,128,128]{2,1,0:T(8,128)}, u32[]{:S(2)}) copy-start(f32[16,128,128]{2,1,0:T(8,128)} %refs_0_.11) | copy-start | bytes 3145732
  7.3 6.1 %copy-start.3 = (f32[16,128,128]{2,1,0:T(8,128)S(1)}, f32[16,128,128]{2,1,0:T(8,128)}, u32[]{:S(2)}) copy-start(f32[16,128,128]{2,1,0:T(8,128)} %refs_1_.11) | copy-start | bytes 3145732
  7.3 6.1 %copy-start.5 = (s32[16,128,128]{2,1,0:T(8,128)S(1)}, s32[16,128,128]{2,1,0:T(8,128)}, u32[]{:S(2)}) copy-start(s32[16,128,128]{2,1,0:T(8,128)} %refs_2_.11) | copy-start | bytes 3145732
  7.3 6.2 %copy-start.10 = (bf16[256,256]{1,0:T(8,128)(2,1)S(1)}, bf16[256,256]{1,0:T(8,128)(2,1)}, u32[]{:S(2)}) copy-start(bf16[256,256]{1,0:T(8,128)(2,1)} %constant.88.clone.refs_6_.toward_high.refs_11_) | copy-start | bytes 393220
  7.4 6.2 %copy-start.11 = (bf16[256,256]{1,0:T(8,128)(2,1)S(1)}, bf16[256,256]{1,0:T(8,128)(2,1)}, u32[]{:S(2)}) copy-start(bf16[256,256]{1,0:T(8,128)(2,1)} %constant.87.clone.refs_5_.toward_low.refs_10_) | copy-start | bytes 393220
  7.4 6.2 %copy-start.17 = (bf16[256,256]{1,0:T(8,128)(2,1)S(1)}, bf16[256,256]{1,0:T(8,128)(2,1)}, u32[]{:S(2)}) copy-start(bf16[256,256]{1,0:T(8,128)(2,1)} %constant.86.clone.refs_4_.refs_9_) | copy-start | bytes 393220
  8.5 11.4 %collective-permute-start = (f32[128,128]{1,0:T(8,128)}, f32[128,128]{1,0:T(8,128)}, u32[]{:S(2)}, u32[]{:S(2)}) collective-permute-start(f32[128,128]{1,0:T(8,128)} %get-tuple-element.29), channel_id=1, source_target_pairs={{0,4},{4,0},{8,12},{12,8},{16,20},{20,16},{24,28},{28,24},{1,5},{5... | collective-permute-start | bytes 196616 | tf_op jit(solution)/shard_map/ppermute | solution.py:303
  9.1 10.9 %collective-permute-start.1 = (f32[128,128]{1,0:T(8,128)}, f32[128,128]{1,0:T(8,128)}, u32[]{:S(2)}, u32[]{:S(2)}) collective-permute-start(f32[128,128]{1,0:T(8,128)} %get-tuple-element.30), channel_id=1, source_target_pairs={{4,8},{8,4},{12,16},{16,12},{20,24},{24,20},{5,9},{9,5},{13,17},{1... | collective-permute-start | bytes 196616 | tf_op jit(solution)/shard_map/ppermute | solution.py:303
  13.5 1.2 %copy-start.7 = (s32[16,128,128]{2,1,0:T(8,128)S(1)}, s32[16,128,128]{2,1,0:T(8,128)}, u32[]{:S(2)}) copy-start(s32[16,128,128]{2,1,0:T(8,128)} %refs_3_.11) | copy-start | bytes 3145732
  14.8 8.9 %copy-start.12 = (bf16[256,256]{1,0:T(8,128)(2,1)S(1)}, bf16[256,256]{1,0:T(8,128)(2,1)}, u32[]{:S(2)}) copy-start(bf16[256,256]{1,0:T(8,128)(2,1)} %constant.89.clone.band_ref) | copy-start | bytes 393220
  21.1 4.2 %collective-permute-start.2 = (f32[128,128]{1,0:T(8,128)S(1)}, f32[128,128]{1,0:T(8,128)S(1)}, u32[]{:S(2)}, u32[]{:S(2)}) collective-permute-start(f32[128,128]{1,0:T(8,128)S(1)} %get-tuple-element.33), channel_id=1, source_target_pairs={{0,1},{1,0},{2,3},{3,2},{4,5},{5,4},{6,7},{7,6},{8,9},{9,8},{10,11... | collective-permute-start | bytes 196616 | tf_op jit(solution)/shard_map/ppermute | solution.py:303
  21.1 5.6 %collective-permute-start.3 = (f32[128,128]{1,0:T(8,128)S(1)}, f32[128,128]{1,0:T(8,128)S(1)}, u32[]{:S(2)}, u32[]{:S(2)}) collective-permute-start(f32[128,128]{1,0:T(8,128)S(1)} %get-tuple-element.34), channel_id=1, source_target_pairs={{1,2},{2,1},{5,6},{6,5},{9,10},{10,9},{13,14},{14,13},{17,18},{18,... | collective-permute-start | bytes 196616 | tf_op jit(solution)/shard_map/ppermute | solution.py:303
  23.7 2.9 %copy-start.8 = (s32[16,128,128]{2,1,0:T(8,128)S(1)}, s32[16,128,128]{2,1,0:T(8,128)}, u32[]{:S(2)}) copy-start(s32[16,128,128]{2,1,0:T(8,128)} %refs_3_.11) | copy-start | bytes 3145732
  23.7 2.9 %copy-start.9 = (f32[16,128,128]{2,1,0:T(8,128)S(1)}, f32[16,128,128]{2,1,0:T(8,128)}, u32[]{:S(2)}) copy-start(f32[16,128,128]{2,1,0:T(8,128)} %threshold.1) | copy-start | bytes 3145732
  23.7 2.9 %copy-start.14 = (bf16[256,256]{1,0:T(8,128)(2,1)S(1)}, bf16[256,256]{1,0:T(8,128)(2,1)}, u32[]{:S(2)}) copy-start(bf16[256,256]{1,0:T(8,128)(2,1)} %constant.85.clone.refs_5_.refs_10_) | copy-start | bytes 393220
  23.7 2.9 %copy-start.16 = (bf16[256,256]{1,0:T(8,128)(2,1)S(1)}, bf16[256,256]{1,0:T(8,128)(2,1)}, u32[]{:S(2)}) copy-start(bf16[256,256]{1,0:T(8,128)(2,1)} %constant.84.clone.refs_4_.refs_9_) | copy-start | bytes 393220
  27.3 12.0 %collective-permute-start.4 = (f32[128,128]{1,0:T(8,128)S(1)}, f32[128,128]{1,0:T(8,128)S(1)}, u32[]{:S(2)}, u32[]{:S(2)}) collective-permute-start(f32[128,128]{1,0:T(8,128)S(1)} %get-tuple-element.36), channel_id=1, source_target_pairs={{0,4},{4,0},{8,12},{12,8},{16,20},{20,16},{24,28},{28,24},{1,5},{5... | collective-permute-start | bytes 196616 | tf_op jit(solution)/shard_map/ppermute | solution.py:303
  27.3 12.0 %collective-permute-start.5 = (f32[128,128]{1,0:T(8,128)S(1)}, f32[128,128]{1,0:T(8,128)S(1)}, u32[]{:S(2)}, u32[]{:S(2)}) collective-permute-start(f32[128,128]{1,0:T(8,128)S(1)} %get-tuple-element.37), channel_id=1, source_target_pairs={{4,8},{8,4},{12,16},{16,12},{20,24},{24,20},{5,9},{9,5},{13,17},{1... | collective-permute-start | bytes 196616 | tf_op jit(solution)/shard_map/ppermute | solution.py:303
  39.5 2.4 %collective-permute-start.6 = (f32[128,128]{1,0:T(8,128)S(1)}, f32[128,128]{1,0:T(8,128)S(1)}, u32[]{:S(2)}, u32[]{:S(2)}) collective-permute-start(f32[128,128]{1,0:T(8,128)S(1)} %get-tuple-element.40), channel_id=1, source_target_pairs={{0,1},{1,0},{2,3},{3,2},{4,5},{5,4},{6,7},{7,6},{8,9},{9,8},{10,11... | collective-permute-start | bytes 196616 | tf_op jit(solution)/shard_map/ppermute | solution.py:303
  39.5 5.6 %collective-permute-start.7 = (f32[128,128]{1,0:T(8,128)S(1)}, f32[128,128]{1,0:T(8,128)S(1)}, u32[]{:S(2)}, u32[]{:S(2)}) collective-permute-start(f32[128,128]{1,0:T(8,128)S(1)} %get-tuple-element.41), channel_id=1, source_target_pairs={{1,2},{2,1},{5,6},{6,5},{9,10},{10,9},{13,14},{14,13},{17,18},{18,... | collective-permute-start | bytes 196616 | tf_op jit(solution)/shard_map/ppermute | solution.py:303
  45.7 12.9 %collective-permute-start.8 = (f32[128,128]{1,0:T(8,128)S(1)}, f32[128,128]{1,0:T(8,128)S(1)}, u32[]{:S(2)}, u32[]{:S(2)}) collective-permute-start(f32[128,128]{1,0:T(8,128)S(1)} %get-tuple-element.45), channel_id=1, source_target_pairs={{0,4},{4,0},{8,12},{12,8},{16,20},{20,16},{24,28},{28,24},{1,5},{5... | collective-permute-start | bytes 196616 | tf_op jit(solution)/shard_map/ppermute | solution.py:303
  45.8 12.9 %collective-permute-start.9 = (f32[128,128]{1,0:T(8,128)S(1)}, f32[128,128]{1,0:T(8,128)S(1)}, u32[]{:S(2)}, u32[]{:S(2)}) collective-permute-start(f32[128,128]{1,0:T(8,128)S(1)} %get-tuple-element.46), channel_id=1, source_target_pairs={{4,8},{8,4},{12,16},{16,12},{20,24},{24,20},{5,9},{9,5},{13,17},{1... | collective-permute-start | bytes 196616 | tf_op jit(solution)/shard_map/ppermute | solution.py:303
  58.9 2.4 %collective-permute-start.10 = (f32[128,128]{1,0:T(8,128)S(1)}, f32[128,128]{1,0:T(8,128)S(1)}, u32[]{:S(2)}, u32[]{:S(2)}) collective-permute-start(f32[128,128]{1,0:T(8,128)S(1)} %get-tuple-element.49), channel_id=1, source_target_pairs={{0,1},{1,0},{2,3},{3,2},{4,5},{5,4},{6,7},{7,6},{8,9},{9,8},{10,11... | collective-permute-start | bytes 196616 | tf_op jit(solution)/shard_map/ppermute | solution.py:303
  58.9 5.6 %collective-permute-start.11 = (f32[128,128]{1,0:T(8,128)S(1)}, f32[128,128]{1,0:T(8,128)S(1)}, u32[]{:S(2)}, u32[]{:S(2)}) collective-permute-start(f32[128,128]{1,0:T(8,128)S(1)} %get-tuple-element.50), channel_id=1, source_target_pairs={{1,2},{2,1},{5,6},{6,5},{9,10},{10,9},{13,14},{14,13},{17,18},{18,... | collective-permute-start | bytes 196616 | tf_op jit(solution)/shard_map/ppermute | solution.py:303
  67.9 5.5 %collective-permute-start.12 = (f32[16,128]{1,0:T(8,128)S(1)}, f32[16,128]{1,0:T(8,128)S(1)}, u32[]{:S(2)}, u32[]{:S(2)}) collective-permute-start(f32[16,128]{1,0:T(8,128)S(1)} %slice_bitcast_fusion), channel_id=1, source_target_pairs={{0,4},{4,8},{8,12},{12,16},{16,20},{20,24},{24,28},{1,5},{5,9},{9,... | collective-permute-start | bytes 24584 | tf_op jit(solution)/shard_map/ppermute | solution.py:319
  74.4 5.1 %collective-permute-start.13 = (f32[16,129]{1,0:T(8,128)S(1)}, f32[16,129]{1,0:T(8,128)S(1)}, u32[]{:S(2)}, u32[]{:S(2)}) collective-permute-start(f32[16,129]{1,0:T(8,128)S(1)} %fusion), channel_id=1, source_target_pairs={{0,1},{1,2},{2,3},{4,5},{5,6},{6,7},{8,9},{9,10},{10,11},{12,13},{... | collective-permute-start | bytes 24776 | tf_op jit(solution)/shard_map/ppermute | solution.py:319

commit v2 on v0

v2 whole, which is shorter than its diff:
```python
import functools
import math

import jax
import jax.numpy as jnp
import numpy as np
from jax import lax
from jax.experimental import pallas as pl
from jax.experimental.pallas import tpu as pltpu
from jax.sharding import PartitionSpec as P

OUTER = 3
REACH = 8
RATE = math.log2(math.e) / 0.3
HALF_LN2 = 0.5 * math.log(2.0)
VMEM_BYTES = 24 * 1024 * 1024


def tap(offset):
    return math.exp(-(offset**2) / 32.0) if abs(offset) <= REACH else 0.0


def band(rows, cols, shift=0):
    return np.array([[tap(c - r + shift) for c in range(cols)] for r in range(rows)])


def depth_matrix(layers):
    weights = band(layers, layers)
    return weights / weights.sum(axis=1, keepdims=True)


def split(value):
    high = value.astype(jnp.bfloat16)
    low = (value - high.astype(jnp.float32)).astype(jnp.bfloat16)
    return high, low


def left_constant(matrix):
    high, low = split(matrix)
    return jnp.concatenate(
        [jnp.concatenate([high, high], axis=1), jnp.concatenate([low, low], axis=1)], axis=0
    )


def right_constant(matrix):
    both = jnp.concatenate(split(matrix), axis=1)
    return jnp.concatenate([both, both], axis=0)


def left_product(constant, value):
    rows = constant.shape[0] // 2
    halves = jnp.concatenate(split(value), axis=0)
    both = jnp.dot(constant, halves, preferred_element_type=jnp.float32)
    return both[:rows] + both[rows:]


def right_product(value, constant):
    cols = constant.shape[1] // 2
    halves = jnp.concatenate(split(value), axis=1)
    both = jnp.dot(halves, constant, preferred_element_type=jnp.float32)
    return both[:, :cols] + both[:, cols:]


def newton(stress, strain, yields, count, soften):
    start = 2.0 * stress - 3.5 * soften
    shift = start + (2.0 * strain - HALF_LN2)
    drop = 0.2 * soften
    state = start
    for sweep_no in range(1, 7):
        update = state * (0.8 - 0.2 * jnp.tanh(shift - state)) - drop
        state = update if sweep_no <= 3 else jnp.where(count >= sweep_no, update, state)
    moved = (strain + (stress - 1.75 * soften)) - 0.5 * state
    return jnp.where(yields > 0, moved, strain)


def depth_smooth(layers, matrix):
    count = len(layers)
    half = count // 2
    sums = [layers[k] + layers[count - 1 - k] for k in range(half)]
    diffs = [layers[k] - layers[count - 1 - k] for k in range(half)]
    out = [None] * count
    for row in range(half):
        even = odd = None
        for k in range(half):
            near, far = matrix[row, k], matrix[row, count - 1 - k]
            plus, minus = float(0.5 * (near + far)), float(0.5 * (near - far))
            if plus == 0.0 and minus == 0.0:
                continue
            even = sums[k] * plus if even is None else even + sums[k] * plus
            odd = diffs[k] * minus if odd is None else odd + diffs[k] * minus
        out[row] = even + odd
        out[count - 1 - row] = even - odd
    return out


def lane_ids(shape):
    return lax.broadcasted_iota(jnp.int32, shape, len(shape) - 1)


def on_even(axis):
    return lax.axis_index(axis) % 2 == 0


def sides(axis, even, odd):
    return jnp.where(on_even(axis), odd, even), jnp.where(on_even(axis), even, odd)


def send(axis, low, high, even_ref, odd_ref):
    even_ref[...] = jnp.where(on_even(axis), high, low)
    odd_ref[...] = jnp.where(on_even(axis), low, high)


def add_columns(value, layer, low, high):
    cols = value.shape[1]
    slots = lane_ids(value.shape) // REACH
    packed = jnp.where(slots == layer, low, high)
    shift = (cols - layer * REACH) % cols
    moved = packed if isinstance(layer, int) and layer == 0 else pltpu.roll(packed, shift, 1)
    return value + jnp.where((slots == 0) | (slots == cols // REACH - 1), moved, 0.0)


def retained(full, norm, threshold):
    return jnp.exp2(jnp.minimum(threshold - full * norm, 0.0) * RATE)


def first_edge_kernel(stress, strain, yields, count, below, above, even_ref, odd_ref,
                      stress_s, strain_s, yields_s, count_s, block, sems):
    layers, rows, cols = stress.shape
    pairs = ((stress, stress_s), (strain, strain_s), (yields, yields_s), (count, count_s))
    starts = (0, rows - REACH)
    copies = []
    for side, first_row in enumerate(starts):
        for index, (source, target) in enumerate(pairs):
            copies.append(
                pltpu.make_async_copy(
                    source.at[:, pl.ds(first_row, REACH), :], target.at[side], sems.at[side, index]
                )
            )
            copies[-1].start()
    sent = []
    extra = jnp.zeros((even_ref.shape[0] - layers * REACH, cols), jnp.float32)
    for side, matrix in enumerate((below, above)):
        for copy in copies[side * len(pairs) : (side + 1) * len(pairs)]:
            copy.wait()
        for layer in range(layers):
            at = (side, layer)
            block[pl.ds(layer * REACH, REACH), :] = newton(
                stress_s[at], strain_s[at], yields_s[at], count_s[at], jnp.ones((REACH, cols), jnp.float32)
            )
        product = left_product(left_constant(matrix[...]), block[...])
        sent.append(jnp.concatenate([product, extra], axis=0))
    send("gx", *sent, even_ref, odd_ref)


def edge_kernel(group, stress, strain, yields, count, threshold, smooth, col_even, col_odd, norm,
                below, above, even_ref, odd_ref, low_block, high_block, rest):
    layers, rows, cols = stress.shape
    starts = (0, rows - 2 * REACH, rows - REACH)
    received = []
    for first_row in starts:
        part = pl.ds(first_row + REACH, REACH)
        received.append(sides("gy", col_even[part, :], col_odd[part, :]))

    def layer_step(layer):
        for index, first_row in enumerate(starts):
            at = (layer, pl.ds(first_row, REACH), slice(None))
            extended = pl.ds(first_row + REACH, REACH)
            full = add_columns(smooth[layer, extended, :], layer, *received[index])
            soften = 0.5 + 0.5 * retained(full, norm[extended, :], threshold[at])
            value = newton(stress[at], strain[at], yields[at], count[at], soften)
            if index == 0:
                low_block[pl.ds(pl.multiple_of(layer * REACH, REACH), REACH), :] = value
            else:
                row = pl.multiple_of((2 * layer + index - 1) * REACH, REACH)
                high_block[pl.ds(row, REACH), :] = value
            if index == 2:
                kept = (stress[at] + strain[at]) - value
                rest[pl.ds(layer, 1), :] = kept[REACH - 1 :]
                rest[pl.ds(layers + layer, 1), :] = threshold[at][REACH - 1 :]

    def step(index, carry):
        for inner in range(group):
            layer_step(index * group + inner)
        return carry

    lax.fori_loop(0, layers // group, step, 0)
    low = left_product(left_constant(below[...]), low_block[...])
    high = left_product(left_constant(above[...]), high_block[...])
    extra = jnp.zeros((even_ref.shape[0] - low.shape[0], cols), jnp.float32)
    send(
        "gx", jnp.concatenate([low, extra], axis=0), jnp.concatenate([high, rest[...]], axis=0),
        even_ref, odd_ref,
    )


def main_kernel(depth, fresh, *refs):
    if fresh:
        (stress, strain, yields, count, band_ref, low_ref, high_ref, next_ref,
         across, low_cols, high_cols, deep, pack_low, pack_high, pack_next) = refs
    else:
        (stress, strain, yields, count, threshold, smooth, col_even, col_odd, norm, norm_last,
         band_ref, low_ref, high_ref, next_ref,
         across, low_cols, high_cols, plastic,
         deep, pack_low, pack_high, pack_next, pack_threshold, pack_kept) = refs
    layers, rows, cols = stress.shape
    blocks = rows // REACH
    constant = left_constant(band_ref[...])

    def layer_pair(index, carry):
        pair = []
        for inner in range(2):
            layer = 2 * index + inner
            values = []
            for block in range(blocks):
                at = (layer, pl.ds(block * REACH, REACH), slice(None))
                if fresh:
                    soften = jnp.ones((REACH, cols), jnp.float32)
                else:
                    extended = pl.ds((block + 1) * REACH, REACH)
                    low, high = sides("gy", col_even[extended, :], col_odd[extended, :])
                    full = add_columns(smooth[layer, extended, :], layer, low, high)
                    soften = 0.5 + 0.5 * retained(full, norm[extended, :], threshold[at])
                value = newton(stress[at], strain[at], yields[at], count[at], soften)
                values.append(value)
                if not fresh:
                    plastic[at] = value
            pair.append(jnp.concatenate(values, axis=0))
        result = left_product(constant, jnp.concatenate(pair, axis=1))
        deep[2 * index] = result[:, :cols]
        deep[2 * index + 1] = result[:, cols:]
        return carry

    lax.fori_loop(0, layers // 2, layer_pair, 0)

    def row_block(index, carry):
        part = pl.ds(pl.multiple_of(index * REACH, REACH), REACH)
        values = depth_smooth([deep[layer, part, :] for layer in range(layers)], depth)
        for layer, value in enumerate(values):
            across[layer, part, :] = value
        for ref, packed in zip((pack_low, pack_high, pack_next), pack_edges(values)):
            ref[part, :] = packed
        return carry

    lax.fori_loop(0, blocks + 1, row_block, 0)
    low_cols[...] = right_product(pack_low[...], right_constant(low_ref[...]))
    high = right_product(pack_high[...], right_constant(high_ref[...]))
    behind = right_product(pack_next[...], right_constant(next_ref[...]))
    if fresh:
        high_cols[...] = high
        return

    def last_column(index, carry):
        part = pl.ds(pl.multiple_of(index * REACH, REACH), REACH)
        lanes = lane_ids((REACH, cols))
        limit = kept = jnp.zeros((REACH, cols), jnp.float32)
        for layer in range(layers):
            at = (layer, part, slice(None))
            limit = jnp.where(lanes == layer, pltpu.roll(threshold[at], layer + 1, 1), limit)
            rest = (stress[at] + strain[at]) - plastic[at]
            kept = jnp.where(lanes == layers + layer, pltpu.roll(rest, layers + layer + 1, 1), kept)
        extended = pl.ds(pl.multiple_of((index + 1) * REACH, REACH), REACH)
        pack_threshold[extended, :] = limit
        pack_kept[extended, :] = kept
        return carry

    pack_threshold[pl.ds(0, REACH), :] = jnp.zeros((REACH, cols), jnp.float32)
    pack_kept[pl.ds(0, REACH), :] = jnp.zeros((REACH, cols), jnp.float32)
    lax.fori_loop(0, blocks, last_column, 0)
    lanes = lane_ids(pack_kept.shape)
    column = pack_threshold[...] - (high[:, cols:] + behind) * norm_last[...]
    high_cols[:, :cols] = high[:, :cols]
    high_cols[:, cols:] = jnp.where(lanes < layers, column, pack_kept[...])


def pack_edges(values):
    cols = values[0].shape[1]
    count = cols // REACH
    slots = lane_ids(values[0].shape) // REACH
    low = high = ahead = jnp.zeros_like(values[0])
    for layer, value in enumerate(values):
        moved = pltpu.roll(value, layer * REACH, 1) if layer else value
        low = jnp.where(slots == layer, moved, low)
        high = jnp.where(slots == (layer - 1) % count, moved, high)
        ahead = jnp.where(slots == (layer - 2) % count, moved, ahead)
    return low, high, ahead


def corner_kernel(row_even, row_odd, low_cols, high_cols, norm_last, low_ref, high_ref, next_ref,
                  even_ref, odd_ref, own_ref):
    cols = low_ref.shape[0]
    total = low_cols.shape[0]
    layers = (total - REACH) // REACH
    strip = layers * REACH
    from_low, from_high = sides("gx", row_even[...], row_odd[...])
    partial = from_low[strip : strip + layers]
    kept = from_low[strip + layers : strip + 2 * layers]
    limit = from_low[strip + 2 * layers : strip + 3 * layers]
    before = [jnp.broadcast_to(partial[layer : layer + 1], (REACH, cols)) for layer in range(layers)]
    packs = [pack_edges(before)] + [
        pack_edges([block[layer * REACH : (layer + 1) * REACH] for layer in range(layers)])
        for block in (from_low, from_high)
    ]
    low, high, ahead = (jnp.concatenate(group, axis=0) for group in zip(*packs))
    low_add = right_product(low, right_constant(low_ref[...]))
    high_add = right_product(high, right_constant(high_ref[...]))
    behind_add = right_product(ahead, right_constant(next_ref[...]))

    lanes = lane_ids((layers, cols))
    level = lax.broadcasted_iota(jnp.int32, (layers, cols), 0)
    corner_limit = jnp.where(lanes == level, limit[:, cols - 1 :], 0.0)
    corner_kept = jnp.where(lanes == layers + level, kept[:, cols - 1 :], 0.0)
    corner = jnp.sum(corner_limit + corner_kept, axis=0, keepdims=True)

    def place(base, add):
        return jnp.concatenate(
            [base[: 2 * REACH] + add[: 2 * REACH], base[2 * REACH : total - REACH],
             base[total - REACH :] + add[2 * REACH :]],
            axis=0,
        )

    low_all = place(low_cols[...], low_add)
    high_all = place(high_cols[:, :cols], high_add[:, :cols])
    last = norm_last[...]
    behind = high_add[:, cols:] + behind_add
    edges = jnp.concatenate([last[: 2 * REACH], last[total - REACH :]], axis=0)
    lanes = lane_ids(behind.shape)
    drop = jnp.where(lanes < layers, behind * edges, 0.0)
    column = place(high_cols[:, cols:], -drop)
    first = column[:REACH] + corner
    main = column[REACH:]
    quarter = strip // 4
    lanes = lane_ids((quarter, cols))
    folded = main[:quarter]
    for part in range(1, 4):
        moved = pltpu.roll(main[part * quarter : (part + 1) * quarter], part * 2 * layers, 1)
        folded = jnp.where(lanes // (2 * layers) == part, moved, folded)
    extra = jnp.zeros((quarter + REACH, cols), jnp.float32)
    send(
        "gy", jnp.concatenate([low_all[:, :cols], extra], axis=0),
        jnp.concatenate([high_all, folded, first], axis=0), even_ref, odd_ref,
    )
    own_ref[...] = low_all[:, cols:]


def column_kernel(across, row_even, row_odd, band_ref, smooth):
    layers, total, cols = across.shape
    strip = layers * REACH
    constant = right_constant(band_ref[...])

    def step(index, carry):
        for inner in range(2):
            layer = 2 * index + inner
            part = pl.ds(pl.multiple_of(layer * REACH, REACH), REACH)
            low, high = sides("gx", row_even[part, :], row_odd[part, :])
            line = pl.ds(strip + layer, 1)
            before, _ = sides("gx", row_even[line, :], row_odd[line, :])
            value = across[layer]
            value = jnp.concatenate(
                [value[:REACH] + before, value[REACH : 2 * REACH] + low,
                 value[2 * REACH : total - REACH], value[total - REACH :] + high],
                axis=0,
            )
            smooth[layer] = right_product(value, constant)
        return carry

    lax.fori_loop(0, layers // 2, step, 0)


def final_kernel(stress, strain, plastic, threshold, smooth, col_even, col_odd, row_even, row_odd,
                 norm, norm_before, own_cols, plastic_out, damage_out, force_out,
                 columns, damage_s, force_s, copy_sem, sems):
    layers, rows, cols = stress.shape
    total = rows + REACH
    strip = layers * REACH
    whole = pltpu.make_async_copy(plastic, plastic_out, copy_sem)
    whole.start()

    from_low, _ = sides("gy", col_even[...], col_odd[...])
    quarter = rows // 4
    folded = from_low[total : total + quarter]
    pieces = [from_low[total + quarter :], folded]
    for part in range(1, 4):
        pieces.append(pltpu.roll(folded, cols - part * 2 * layers, 1))
    column = jnp.concatenate(pieces, axis=0)
    limit = column - own_cols[...] * norm_before[...]
    kept = jnp.exp2(jnp.minimum(limit, 0.0) * RATE)
    columns[...] = kept * pltpu.roll(column, cols - layers, 1)

    def copies(layer):
        return (
            pltpu.make_async_copy(damage_s.at[layer], damage_out.at[layer], sems.at[0, layer]),
            pltpu.make_async_copy(force_s.at[0, layer], force_out.at[0, layer], sems.at[1, layer]),
            pltpu.make_async_copy(force_s.at[1, layer], force_out.at[1, layer], sems.at[2, layer]),
        )

    def step(layer, carry):
        lanes = lane_ids((REACH, cols))
        top = lax.broadcasted_iota(jnp.int32, (REACH, cols), 0) == 0
        above_sum = above_diff = None
        for block in range(rows // REACH + 1):
            extended = pl.ds(block * REACH, REACH)
            low, high = sides("gy", col_even[extended, :], col_odd[extended, :])
            full = add_columns(smooth[layer, extended, :], layer, low, high)
            if block == 0:
                line = pl.ds(strip + layers + layer, 1)
                rest, _ = sides("gx", row_even[line, :], row_odd[line, :])
                line = pl.ds(strip + 2 * layers + layer, 1)
                limit, _ = sides("gx", row_even[line, :], row_odd[line, :])
            else:
                at = (layer, pl.ds((block - 1) * REACH, REACH), slice(None))
                rest = (stress[at] + strain[at]) - plastic[at]
                limit = threshold[at]
            ratio = retained(full, norm[extended, :], limit)
            value = ratio * rest
            left = jnp.where(
                lanes == 0,
                pltpu.roll(columns[extended, :], (cols - layer) % cols, 1),
                pltpu.roll(value, 1, 1),
            )
            both = pltpu.roll(left + value, 1, 0)
            diff = pltpu.roll(left - value, 1, 0)
            if block:
                damage_s[at] = 1.0 - ratio
                force_s[(0, *at)] = 0.5 * (jnp.where(top, above_sum, both) - (left + value))
                force_s[(1, *at)] = 0.5 * (jnp.where(top, above_diff, diff) + (left - value))
            above_sum, above_diff = both, diff
        for copy in copies(layer):
            copy.start()
        return carry

    lax.fori_loop(0, layers, step, 0)

    def drain(layer, carry):
        for copy in copies(layer):
            copy.wait()
        return carry

    lax.fori_loop(0, layers, drain, 0)
    whole.wait()


def call(kernel, outs, scratch, cost, operands, anywhere=False, outs_anywhere=False):
    inside, outside = pl.BlockSpec(memory_space=pltpu.VMEM), pl.BlockSpec(memory_space=pl.ANY)
    far = 4 if anywhere else 0
    return pl.pallas_call(
        kernel,
        out_shape=[jax.ShapeDtypeStruct(shape, jnp.float32) for shape in outs],
        in_specs=[outside] * far + [inside] * (len(operands) - far),
        out_specs=[outside if outs_anywhere else inside] * len(outs),
        scratch_shapes=[pltpu.VMEM(s, jnp.float32) if isinstance(s, tuple) else s for s in scratch],
        compiler_params=pltpu.CompilerParams(vmem_limit_bytes=VMEM_BYTES),
        cost_estimate=pl.CostEstimate(flops=cost, bytes_accessed=cost // 16, transcendentals=0),
    )(*operands)


def exchange(axis, even, odd):
    count = lax.axis_size(axis)
    results = []
    for start, value in ((0, even), (1, odd)):
        pairs = []
        for low in range(start, count - 1, 2):
            pairs += [(low, low + 1), (low + 1, low)]
        results.append(lax.ppermute(value, axis, pairs))
    return results


def inverse_weights(axis, first, positions, length):
    extent = length * lax.axis_size(axis)
    places = lax.axis_index(axis) * length + first + jnp.arange(positions, dtype=jnp.int32)
    total = jnp.zeros((positions,), jnp.float32)
    for offset in range(-REACH, REACH + 1):
        inside = (places + offset >= 0) & (places + offset < extent)
        total = total + jnp.where(inside, tap(offset), 0.0)
    return 1.0 / jnp.maximum(total, tap(REACH))


def matrices(layers, rows, cols):
    depth = depth_matrix(layers)
    up, down = band(REACH, REACH, REACH), band(REACH, REACH, -REACH)
    below = np.kron(depth, up)
    near = np.concatenate([np.zeros((REACH, REACH)), down], axis=1)
    line = band(1, 2 * REACH, 1 - 2 * REACH)
    above = np.concatenate([np.kron(depth, near), np.kron(depth, line)], axis=0)
    rows_band = np.concatenate([np.zeros((REACH - 1, rows)), band(1, rows, 1), band(rows, rows)])
    slots = cols // REACH
    low, high, ahead = np.zeros((cols, 2 * cols)), np.zeros((cols, 2 * cols)), np.zeros((cols, cols))
    for layer in range(layers):
        own = slice(layer * REACH, (layer + 1) * REACH)
        previous = (layer - 1) % slots
        other = slice(previous * REACH, (previous + 1) * REACH)
        low[own, other] = up.T
        high[other, own] = down.T
        low[own, cols + layer] = [tap(j + 1) for j in range(REACH)]
        high[other, cols + layer] = [tap(REACH - 1 - j) for j in range(REACH)]
        ahead[((layer - 2) % slots) * REACH + REACH - 1, layer] = tap(REACH)
    constants = (below, above, rows_band, band(cols, cols), low, high, ahead)
    return depth, [jnp.asarray(matrix, jnp.float32) for matrix in constants]


def local(trial_stress, old_strain, yield_mask, newton_count, damage_threshold):
    layers, rows, cols = trial_stress.shape
    assert layers * REACH == cols == rows and layers % 2 == 0
    total, strip = rows + REACH, layers * REACH
    depth, (below, above, rows_band, cols_band, low, high, ahead) = matrices(layers, rows, cols)

    across_rows = inverse_weights("gx", -REACH, total, rows)[:, None]
    across_cols = inverse_weights("gy", -1, cols + 1, cols)[None, :]
    norm = across_rows * across_cols[:, 1:]
    norm_last = jnp.broadcast_to(across_rows * across_cols[:, cols:], (total, cols))
    norm_before = jnp.broadcast_to(across_rows * across_cols[:, :1], (total, cols))

    inputs = (trial_stress, old_strain, yield_mask, newton_count)
    whole, wide = (layers, rows, cols), (layers, total, cols)
    sent_rows = (strip + 3 * layers, cols)
    sent_cols = (total + rows // 4 + REACH, cols)
    packed, packed_two = (total, cols), (total, 2 * cols)
    work = layers * rows * cols
    columns = (low, high, ahead)

    for outer_no in range(OUTER):
        if outer_no == 0:
            edge = [pltpu.VMEM((2, layers, REACH, cols), kind) for kind in
                    (jnp.float32, jnp.float32, jnp.int32, jnp.int32)]
            row_even, row_odd = call(
                first_edge_kernel, [sent_rows] * 2,
                edge + [(strip, cols), pltpu.SemaphoreType.DMA((2, 4))], work * 16,
                (*inputs, below, above[:strip].reshape(strip, layers, 2, REACH)[:, :, 1].reshape(strip, strip)),
                anywhere=True,
            )
        else:
            row_even, row_odd = call(
                functools.partial(edge_kernel, 8), [sent_rows] * 2,
                [(strip, cols), (2 * strip, cols), (2 * layers, cols)], work * 16,
                (*inputs, damage_threshold, smooth, col_even, col_odd, norm, below, above),
            )
        row_even, row_odd = exchange("gx", row_even, row_odd)
        if outer_no == 0:
            across, low_cols, high_cols = call(
                functools.partial(main_kernel, depth, True), [wide, packed_two, packed_two],
                [wide, packed, packed, packed], work * 400,
                (*inputs, rows_band, *columns),
            )
        else:
            across, low_cols, high_cols, plastic = call(
                functools.partial(main_kernel, depth, False), [wide, packed_two, packed_two, whole],
                [wide, packed, packed, packed, packed, packed], work * 400,
                (*inputs, damage_threshold, smooth, col_even, col_odd, norm, norm_last,
                 rows_band, *columns),
            )
        col_even, col_odd, own_cols = call(
            corner_kernel, [sent_cols, sent_cols, packed], [], work * 16,
            (row_even, row_odd, low_cols, high_cols, norm_last, *columns),
        )
        col_even, col_odd = exchange("gy", col_even, col_odd)
        (smooth,) = call(
            column_kernel, [wide], [], work * 100, (across, row_even, row_odd, cols_band)
        )
    return tuple(call(
        final_kernel, [whole, whole, (2, *whole)],
        [packed, whole, (2, *whole), pltpu.SemaphoreType.DMA(()), pltpu.SemaphoreType.DMA((3, layers))],
        work * 100,
        (trial_stress, old_strain, plastic, damage_threshold, smooth, col_even, col_odd,
         row_even, row_odd, norm, norm_before, own_cols),
        outs_anywhere=True,
    ))


def solution(mesh):
    split_in = P(None, "gx", "gy")
    return jax.shard_map(
        local,
        mesh=mesh,
        in_specs=(split_in,) * 5,
        out_specs=(split_in, split_in, P(None, None, "gx", "gy")),
        check_vma=False,
    )
```

time: 160 us -> 79 us (0.49)
  the two profiles are of different devices: /device:TPU:0 before, /device:TPU:3 now
where the time goes in v2:
time: 79 us; the launch traced here: 78.4 us
  Pallas kernels  41.2 us (52%)
  starting transfers between devices  25.2 us (32%)
  local copies, waits for them, and re-layouts  8.65 us (11%)
  other arithmetic  1.46 us (2%)
  between operations  1.05 us (1%)
    pallas_call x13, Pallas kernels, call(): pl.pallas_call(kernel, out_shape=[jax.ShapeDtypeStruct(shape, jnp.float32...  41.2 us
    ppermute x12, starting transfers between devices, exchange(): results.append(lax.ppermute(value, axis, pairs))  25.2 us
    unnamed x38, local copies, waits for them, and re-layouts  7.85 us
  transfers between devices with their start and end apart: 12, of which 1 were waited for; matrix products, arithmetic and copies ran while one was open for 3% of the time, Pallas kernels for 38%

profile of v2, /device:TPU:3, one launch (start us, length us, event | category | flops | bytes accessed | tf_op | source)
XLA Modules:
  0.0 78.4 jit_solution(500805810761331219)
XLA Ops:
  0.6 0.0 copy-start
  0.6 1.2 %copy-done = f32[16,128,128]{2,1,0:T(8,128)S(1)} copy-done((f32[16,128,128]{2,1,0:T(8,128)S(1)}, f32[16,128,128]{2,1,0:T(8,128)}, u32[]{:S(2)}) %copy-start) | copy-done | bytes 1048600
  1.9 1.2 %copy-done.2 = f32[16,128,128]{2,1,0:T(8,128)S(1)} copy-done((f32[16,128,128]{2,1,0:T(8,128)S(1)}, f32[16,128,128]{2,1,0:T(8,128)}, u32[]{:S(2)}) %copy-start.2) | copy-done | bytes 1048600
  3.1 1.2 %copy-done.4 = s32[16,128,128]{2,1,0:T(8,128)S(1)} copy-done((s32[16,128,128]{2,1,0:T(8,128)S(1)}, s32[16,128,128]{2,1,0:T(8,128)}, u32[]{:S(2)}) %copy-start.4) | copy-done | bytes 1048600
  4.3 1.2 %copy-done.6 = s32[16,128,128]{2,1,0:T(8,128)S(1)} copy-done((s32[16,128,128]{2,1,0:T(8,128)S(1)}, s32[16,128,128]{2,1,0:T(8,128)}, u32[]{:S(2)}) %copy-start.6) | copy-done | bytes 1048600
  5.5 0.8 %copy-done.14 = f32[128,128]{1,0:T(8,128)S(1)} copy-done((f32[128,128]{1,0:T(8,128)S(1)}, f32[128,128]{1,0:T(8,128)}, u32[]{:S(2)}) %copy-start.14) | copy-done | bytes 65560
  6.4 0.8 %copy-done.18 = f32[128,128]{1,0:T(8,128)S(1)} copy-done((f32[128,128]{1,0:T(8,128)S(1)}, f32[128,128]{1,0:T(8,128)}, u32[]{:S(2)}) %copy-start.18) | copy-done | bytes 65560
  7.2 0.0 copy-start.11
  7.2 0.0 copy-start.12
  7.2 0.0 copy-start.13
  7.3 1.6 %shard_map.140 = (f32[176,128]{1,0:T(8,128)}, f32[176,128]{1,0:T(8,128)}) custom-call(f32[16,128,128]{2,1,0:T(8,128)S(1)} %copy-done, f32[16,128,128]{2,1,0:T(8,128)S(1)} %copy-done.2, s32[16,128,128]{2,1,0:T(8,128)S(1)} %copy-done.4, s32[16,128,128]{2,1,0:T(8,128)S(1)} %copy-done.6, f32[128,128]{1,0:T(8,128)S(1)} %copy-done.14, f32[128,128]{1,0:T(8,128)S(1)} %copy-done.18), custom_call_target="tpu_custom_call" | custom-call | flops 4194304 | bytes 262144 | tf_op jit(solution)/shard_map/pallas_call | solution.py:445
  8.8 0.1 collective-permute-start
  8.9 4.4 %collective-permute-start.1 = (f32[176,128]{1,0:T(8,128)}, f32[176,128]{1,0:T(8,128)}, u32[]{:S(2)}, u32[]{:S(2)}) collective-permute-start(f32[176,128]{1,0:T(8,128)} %get-tuple-element.28), channel_id=1, source_target_pairs={{4,8},{8,4},{12,16},{16,12},{20,24},{24,20},{5,9},{9,5},{13,17},{1... | collective-permute-start | bytes 270344 | tf_op jit(solution)/shard_map/ppermute | solution.py:463
  13.3 0.1 slice_bitcast_fusion
  13.4 0.6 fusion.32
  14.1 0.0 copy-start.7
  14.1 1.2 %copy-done.7 = s32[16,128,128]{2,1,0:T(8,128)S(1)} copy-done((s32[16,128,128]{2,1,0:T(8,128)S(1)}, s32[16,128,128]{2,1,0:T(8,128)}, u32[]{:S(2)}) %copy-start.7) | copy-done | bytes 1048600
  15.3 5.9 %shard_map.139 = (f32[16,136,128]{2,1,0:T(8,128)S(1)}, f32[136,256]{1,0:T(8,128)S(1)}, f32[136,256]{1,0:T(8,128)S(1)}) custom-call(f32[16,128,128]{2,1,0:T(8,128)S(1)} %copy-done.1, f32[16,128,128]{2,1,0:T(8,128)S(1)} %copy-done.3, s32[16,128,128]{2,1,0:T(8,128)S(1)} %copy-done.5, s32[16,128,128]{2,1,0:T(8,128)S(1)} %copy-done.7, f32[136,128]{1,0:T(8,128)S(1)} %copy-done.13, ...), custom_call_target="tpu_custom_call" | custom-call | flops 104857600 | bytes 6553600 | tf_op jit(solution)/shard_map/pallas_call | solution.py:445
  21.2 0.6 broadcast_multiply_fusion.2
  21.9 0.0 collective-permute-done.row_even
  21.9 0.0 collective-permute-done.1.row_odd
  21.9 0.1 broadcast_in_dim.138.norm_last.refs_9_
  22.0 1.9 %shard_map.142 = (f32[176,128]{1,0:T(8,128)S(1)}, f32[176,128]{1,0:T(8,128)S(1)}, f32[136,128]{1,0:T(8,128)}) custom-call(f32[176,128]{1,0:T(8,128)} %collective-permute-done.row_even, f32[176,128]{1,0:T(8,128)} %collective-permute-done.1.row_odd, f32[136,256]{1,0:T(8,128)S(1)} %get-tuple-element.29.low_cols, f32[136,256]{1,0:T(8,128)S(1)} %get-tuple-element.30.high_cols, ...), custom_call_target="tpu_custom_call" | custom-call | flops 4194304 | bytes 262144 | tf_op jit(solution)/shard_map/pallas_call | solution.py:445
  23.9 1.2 %collective-permute-start.2 = (f32[176,128]{1,0:T(8,128)S(1)}, f32[176,128]{1,0:T(8,128)S(1)}, u32[]{:S(2)}, u32[]{:S(2)}) collective-permute-start(f32[176,128]{1,0:T(8,128)S(1)} %get-tuple-element.31), channel_id=1, source_target_pairs={{0,1},{1,0},{2,3},{3,2},{4,5},{5,4},{6,7},{7,6},{8,9},{9,8},{10,11... | collective-permute-start | bytes 270344 | tf_op jit(solution)/shard_map/ppermute | solution.py:463
  25.1 3.0 %collective-permute-start.3 = (f32[176,128]{1,0:T(8,128)S(1)}, f32[176,128]{1,0:T(8,128)S(1)}, u32[]{:S(2)}, u32[]{:S(2)}) collective-permute-start(f32[176,128]{1,0:T(8,128)S(1)} %get-tuple-element.32), channel_id=1, source_target_pairs={{1,2},{2,1},{5,6},{6,5},{9,10},{10,9},{13,14},{14,13},{17,18},{18,... | collective-permute-start | bytes 270344 | tf_op jit(solution)/shard_map/ppermute | solution.py:463
  28.1 0.1 broadcast_multiply_fusion.refs_8_.norm
  28.2 0.0 copy-done.17
  28.2 0.0 copy-start.8
  28.3 0.0 copy-start.9
  28.3 0.0 copy-start.15
  28.3 0.0 copy-start.16
  28.3 2.7 %shard_map.141.refs_5_.smooth = f32[16,136,128]{2,1,0:T(8,128)S(1)} custom-call(f32[16,136,128]{2,1,0:T(8,128)S(1)} %get-tuple-element.26.across, f32[176,128]{1,0:T(8,128)} %collective-permute-done.row_even, f32[176,128]{1,0:T(8,128)} %collective-permute-done.1.row_odd, f32[128,128]{1,0:T(8,128)S(1)} %copy-done.17), custom_call_target="tpu_custom_call" | custom-call | flops 26214400 | bytes 1638400 | tf_op jit(solution)/shard_map/pallas_call | solution.py:445
  31.0 0.0 collective-permute-done.2.refs_6_.col_even
  31.0 0.0 collective-permute-done.3.refs_7_.col_odd
  31.0 0.0 copy-done.8
  31.0 0.0 copy-done.9
  31.0 0.0 copy-done.15
  31.0 1.0 %shard_map.144 = (f32[176,128]{1,0:T(8,128)S(1)}, f32[176,128]{1,0:T(8,128)S(1)}) custom-call(f32[16,128,128]{2,1,0:T(8,128)S(1)} %copy-done.1, f32[16,128,128]{2,1,0:T(8,128)S(1)} %copy-done.3, s32[16,128,128]{2,1,0:T(8,128)S(1)} %copy-done.5, s32[16,128,128]{2,1,0:T(8,128)S(1)} %copy-done.8, f32[16,128,128]{2,1,0:T(8,128)S(1)} %copy-done.9, ...), custom_call_target="tpu_custom_call" | custom-call | flops 4194304 | bytes 262144 | tf_op jit(solution)/shard_map/pallas_call | solution.py:445
  32.0 0.1 collective-permute-start.4
  32.1 4.4 %collective-permute-start.5 = (f32[176,128]{1,0:T(8,128)S(1)}, f32[176,128]{1,0:T(8,128)S(1)}, u32[]{:S(2)}, u32[]{:S(2)}) collective-permute-start(f32[176,128]{1,0:T(8,128)S(1)} %get-tuple-element.35), channel_id=1, source_target_pairs={{4,8},{8,4},{12,16},{16,12},{20,24},{24,20},{5,9},{9,5},{13,17},{1... | collective-permute-start | bytes 270344 | tf_op jit(solution)/shard_map/ppermute | solution.py:463
  36.5 9.6 %shard_map.143 = (f32[16,136,128]{2,1,0:T(8,128)S(1)}, f32[136,256]{1,0:T(8,128)S(1)}, f32[136,256]{1,0:T(8,128)S(1)}, f32[16,128,128]{2,1,0:T(8,128)}) custom-call(f32[16,128,128]{2,1,0:T(8,128)S(1)} %copy-done.1, f32[16,128,128]{2,1,0:T(8,128)S(1)} %copy-done.3, s32[16,128,128]{2,1,0:T(8,128)S(1)} %copy-done.5, s32[16,128,128]{2,1,0:T(8,128)S(1)} %copy-done.8, ...), custom_call_target="tpu_custom_call" | custom-call | flops 104857600 | bytes 6553600 | tf_op jit(solution)/shard_map/pallas_call | solution.py:445
  46.1 0.0 collective-permute-done.4.row_even
  46.1 0.0 collective-permute-done.5.row_odd
  46.1 0.9 %shard_map.146 = (f32[176,128]{1,0:T(8,128)S(1)}, f32[176,128]{1,0:T(8,128)S(1)}, f32[136,128]{1,0:T(8,128)}) custom-call(f32[176,128]{1,0:T(8,128)S(1)} %collective-permute-done.4.row_even, f32[176,128]{1,0:T(8,128)S(1)} %collective-permute-done.5.row_odd, f32[136,256]{1,0:T(8,128)S(1)} %get-tuple-element.36.low_cols, ...), custom_call_target="tpu_custom_call" | custom-call | flops 4194304 | bytes 262144 | tf_op jit(solution)/shard_map/pallas_call | solution.py:445
  47.0 0.0 collective-permute-start.6
  47.0 3.5 %collective-permute-start.7 = (f32[176,128]{1,0:T(8,128)S(1)}, f32[176,128]{1,0:T(8,128)S(1)}, u32[]{:S(2)}, u32[]{:S(2)}) collective-permute-start(f32[176,128]{1,0:T(8,128)S(1)} %get-tuple-element.39), channel_id=1, source_target_pairs={{1,2},{2,1},{5,6},{6,5},{9,10},{10,9},{13,14},{14,13},{17,18},{18,... | collective-permute-start | bytes 270344 | tf_op jit(solution)/shard_map/ppermute | solution.py:463
  50.6 1.6 %shard_map.145.refs_5_.smooth = f32[16,136,128]{2,1,0:T(8,128)S(1)} custom-call(f32[16,136,128]{2,1,0:T(8,128)S(1)} %get-tuple-element.33.across, f32[176,128]{1,0:T(8,128)S(1)} %collective-permute-done.4.row_even, f32[176,128]{1,0:T(8,128)S(1)} %collective-permute-done.5.row_odd, f32[128,128]{1,0:T(8,128)S(1)} %copy-done.17), custom_call_target="tpu_custom_call" | custom-call | flops 26214400 | bytes 1638400 | tf_op jit(solution)/shard_map/pallas_call | solution.py:445
  52.1 0.0 collective-permute-done.6.refs_6_.col_even
  52.1 0.7 collective-permute-done.7.refs_7_.col_odd
  52.9 1.0 %shard_map.148 = (f32[176,128]{1,0:T(8,128)S(1)}, f32[176,128]{1,0:T(8,128)S(1)}) custom-call(f32[16,128,128]{2,1,0:T(8,128)S(1)} %copy-done.1, f32[16,128,128]{2,1,0:T(8,128)S(1)} %copy-done.3, s32[16,128,128]{2,1,0:T(8,128)S(1)} %copy-done.5, s32[16,128,128]{2,1,0:T(8,128)S(1)} %copy-done.8, f32[16,128,128]{2,1,0:T(8,128)S(1)} %copy-done.9, ...), custom_call_target="tpu_custom_call" | custom-call | flops 4194304 | bytes 262144 | tf_op jit(solution)/shard_map/pallas_call | solution.py:445
  53.9 0.1 collective-permute-start.8
  53.9 4.4 %collective-permute-start.9 = (f32[176,128]{1,0:T(8,128)S(1)}, f32[176,128]{1,0:T(8,128)S(1)}, u32[]{:S(2)}, u32[]{:S(2)}) collective-permute-start(f32[176,128]{1,0:T(8,128)S(1)} %get-tuple-element.43), channel_id=1, source_target_pairs={{4,8},{8,4},{12,16},{16,12},{20,24},{24,20},{5,9},{9,5},{13,17},{1... | collective-permute-start | bytes 270344 | tf_op jit(solution)/shard_map/ppermute | solution.py:463
  58.3 8.7 %shard_map.147 = (f32[16,136,128]{2,1,0:T(8,128)S(1)}, f32[136,256]{1,0:T(8,128)S(1)}, f32[136,256]{1,0:T(8,128)S(1)}, f32[16,128,128]{2,1,0:T(8,128)S(1)}) custom-call(f32[16,128,128]{2,1,0:T(8,128)S(1)} %copy-done.1, f32[16,128,128]{2,1,0:T(8,128)S(1)} %copy-done.3, s32[16,128,128]{2,1,0:T(8,128)S(1)} %copy-done.5, s32[16,128,128]{2,1,0:T(8,128)S(1)} %copy-done.8, ...), custom_call_target="tpu_custom_call" | custom-call | flops 104857600 | bytes 6553600 | tf_op jit(solution)/shard_map/pallas_call | solution.py:445
  67.0 0.0 collective-permute-done.8.row_even
  67.0 0.0 collective-permute-done.9.row_odd
  67.0 0.4 shard_map.150
  67.4 0.0 collective-permute-start.10
  67.5 4.1 %collective-permute-start.11 = (f32[176,128]{1,0:T(8,128)S(1)}, f32[176,128]{1,0:T(8,128)S(1)}, u32[]{:S(2)}, u32[]{:S(2)}) collective-permute-start(f32[176,128]{1,0:T(8,128)S(1)} %get-tuple-element.47), channel_id=1, source_target_pairs={{1,2},{2,1},{5,6},{6,5},{9,10},{10,9},{13,14},{14,13},{17,18},{18,... | collective-permute-start | bytes 270344 | tf_op jit(solution)/shard_map/ppermute | solution.py:463
  71.6 0.7 broadcast_multiply_fusion.1
  72.2 1.6 %shard_map.149.smooth = f32[16,136,128]{2,1,0:T(8,128)S(1)} custom-call(f32[16,136,128]{2,1,0:T(8,128)S(1)} %get-tuple-element.41.across, f32[176,128]{1,0:T(8,128)S(1)} %collective-permute-done.8.row_even, f32[176,128]{1,0:T(8,128)S(1)} %collective-permute-done.9.row_odd, f32[128,128]{1,0:T(8,128)S(1)} %copy-done.17), custom_call_target="tpu_custom_call" | custom-call | flops 26214400 | bytes 1638400 | tf_op jit(solution)/shard_map/pallas_call | solution.py:445
  73.8 0.0 collective-permute-done.10.col_even
  73.8 0.0 collective-permute-done.11.col_odd
  73.8 0.1 broadcast_in_dim.139.norm_before
  73.9 4.5 %shard_map.151 = (f32[16,128,128]{2,1,0:T(8,128)}, f32[16,128,128]{2,1,0:T(8,128)}, f32[2,16,128,128]{3,2,1,0:T(8,128)}) custom-call(f32[16,128,128]{2,1,0:T(8,128)S(1)} %copy-done.1, f32[16,128,128]{2,1,0:T(8,128)S(1)} %copy-done.3, f32[16,128,128]{2,1,0:T(8,128)S(1)} %get-tuple-element.40.plastic, f32[16,128,128]{2,1,0:T(8,128)S(1)} %copy-done.9, ...), custom_call_target="tpu_custom_call" | custom-call | flops 26214400 | bytes 1638400 | tf_op jit(solution)/shard_map/pallas_call | solution.py:445
  (20 shorter events, 0.1 us)
Async XLA Ops:
  0.6 1.2 %copy-start = (f32[16,128,128]{2,1,0:T(8,128)S(1)}, f32[16,128,128]{2,1,0:T(8,128)}, u32[]{:S(2)}) copy-start(f32[16,128,128]{2,1,0:T(8,128)} %stress.7) | copy-start | bytes 3145732
  1.9 1.2 %copy-start.2 = (f32[16,128,128]{2,1,0:T(8,128)S(1)}, f32[16,128,128]{2,1,0:T(8,128)}, u32[]{:S(2)}) copy-start(f32[16,128,128]{2,1,0:T(8,128)} %strain.7) | copy-start | bytes 3145732
  3.1 1.2 %copy-start.4 = (s32[16,128,128]{2,1,0:T(8,128)S(1)}, s32[16,128,128]{2,1,0:T(8,128)}, u32[]{:S(2)}) copy-start(s32[16,128,128]{2,1,0:T(8,128)} %yields.5) | copy-start | bytes 3145732
  4.3 1.2 %copy-start.6 = (s32[16,128,128]{2,1,0:T(8,128)S(1)}, s32[16,128,128]{2,1,0:T(8,128)}, u32[]{:S(2)}) copy-start(s32[16,128,128]{2,1,0:T(8,128)} %count.5) | copy-start | bytes 3145732
  5.5 0.8 %copy-start.14 = (f32[128,128]{1,0:T(8,128)S(1)}, f32[128,128]{1,0:T(8,128)}, u32[]{:S(2)}) copy-start(f32[128,128]{1,0:T(8,128)} %constant.20.clone.below) | copy-start | bytes 196612
  6.4 0.8 %copy-start.18 = (f32[128,128]{1,0:T(8,128)S(1)}, f32[128,128]{1,0:T(8,128)}, u32[]{:S(2)}) copy-start(f32[128,128]{1,0:T(8,128)} %constant.30.above) | copy-start | bytes 196612
  7.2 6.8 %copy-start.1 = (f32[16,128,128]{2,1,0:T(8,128)S(1)}, f32[16,128,128]{2,1,0:T(8,128)}, u32[]{:S(2)}) copy-start(f32[16,128,128]{2,1,0:T(8,128)} %stress.7) | copy-start | bytes 3145732
  7.2 6.8 %copy-start.3 = (f32[16,128,128]{2,1,0:T(8,128)S(1)}, f32[16,128,128]{2,1,0:T(8,128)}, u32[]{:S(2)}) copy-start(f32[16,128,128]{2,1,0:T(8,128)} %strain.7) | copy-start | bytes 3145732
  7.2 6.8 %copy-start.5 = (s32[16,128,128]{2,1,0:T(8,128)S(1)}, s32[16,128,128]{2,1,0:T(8,128)}, u32[]{:S(2)}) copy-start(s32[16,128,128]{2,1,0:T(8,128)} %yields.5) | copy-start | bytes 3145732
  7.2 6.8 %copy-start.10 = (f32[128,256]{1,0:T(8,128)S(1)}, f32[128,256]{1,0:T(8,128)}, u32[]{:S(2)}) copy-start(f32[128,256]{1,0:T(8,128)} %constant.25.clone.refs_6_.high_ref.refs_12_) | copy-start | bytes 393220
  7.2 6.8 %copy-start.11 = (f32[128,256]{1,0:T(8,128)S(1)}, f32[128,256]{1,0:T(8,128)}, u32[]{:S(2)}) copy-start(f32[128,256]{1,0:T(8,128)} %constant.24.clone.refs_5_.low_ref.refs_11_) | copy-start | bytes 393220
  7.2 6.8 %copy-start.12 = (f32[128,128]{1,0:T(8,128)S(1)}, f32[128,128]{1,0:T(8,128)}, u32[]{:S(2)}) copy-start(f32[128,128]{1,0:T(8,128)} %constant.26.clone.refs_7_.next_ref.refs_13_) | copy-start | bytes 196612
  7.2 6.8 %copy-start.13 = (f32[136,128]{1,0:T(8,128)S(1)}, f32[136,128]{1,0:T(8,128)}, u32[]{:S(2)}) copy-start(f32[136,128]{1,0:T(8,128)} %constant.22.clone.refs_4_.refs_10_) | copy-start | bytes 208900
  8.8 13.1 %collective-permute-start = (f32[176,128]{1,0:T(8,128)}, f32[176,128]{1,0:T(8,128)}, u32[]{:S(2)}, u32[]{:S(2)}) collective-permute-start(f32[176,128]{1,0:T(8,128)} %get-tuple-element.27), channel_id=1, source_target_pairs={{0,4},{4,0},{8,12},{12,8},{16,20},{20,16},{24,28},{28,24},{1,5},{5... | collective-permute-start | bytes 270344 | tf_op jit(solution)/shard_map/ppermute | solution.py:463
  8.9 13.0 %collective-permute-start.1 = (f32[176,128]{1,0:T(8,128)}, f32[176,128]{1,0:T(8,128)}, u32[]{:S(2)}, u32[]{:S(2)}) collective-permute-start(f32[176,128]{1,0:T(8,128)} %get-tuple-element.28), channel_id=1, source_target_pairs={{4,8},{8,4},{12,16},{16,12},{20,24},{24,20},{5,9},{9,5},{13,17},{1... | collective-permute-start | bytes 270344 | tf_op jit(solution)/shard_map/ppermute | solution.py:463
  14.1 1.2 %copy-start.7 = (s32[16,128,128]{2,1,0:T(8,128)S(1)}, s32[16,128,128]{2,1,0:T(8,128)}, u32[]{:S(2)}) copy-start(s32[16,128,128]{2,1,0:T(8,128)} %count.5) | copy-start | bytes 3145732
  15.3 12.9 %copy-start.17 = (f32[128,128]{1,0:T(8,128)S(1)}, f32[128,128]{1,0:T(8,128)}, u32[]{:S(2)}) copy-start(f32[128,128]{1,0:T(8,128)} %constant.23.clone.band_ref) | copy-start | bytes 196612
  23.9 7.1 %collective-permute-start.2 = (f32[176,128]{1,0:T(8,128)S(1)}, f32[176,128]{1,0:T(8,128)S(1)}, u32[]{:S(2)}, u32[]{:S(2)}) collective-permute-start(f32[176,128]{1,0:T(8,128)S(1)} %get-tuple-element.31), channel_id=1, source_target_pairs={{0,1},{1,0},{2,3},{3,2},{4,5},{5,4},{6,7},{7,6},{8,9},{9,8},{10,11... | collective-permute-start | bytes 270344 | tf_op jit(solution)/shard_map/ppermute | solution.py:463
  25.1 5.9 %collective-permute-start.3 = (f32[176,128]{1,0:T(8,128)S(1)}, f32[176,128]{1,0:T(8,128)S(1)}, u32[]{:S(2)}, u32[]{:S(2)}) collective-permute-start(f32[176,128]{1,0:T(8,128)S(1)} %get-tuple-element.32), channel_id=1, source_target_pairs={{1,2},{2,1},{5,6},{6,5},{9,10},{10,9},{13,14},{14,13},{17,18},{18,... | collective-permute-start | bytes 270344 | tf_op jit(solution)/shard_map/ppermute | solution.py:463
  28.2 2.7 %copy-start.8 = (s32[16,128,128]{2,1,0:T(8,128)S(1)}, s32[16,128,128]{2,1,0:T(8,128)}, u32[]{:S(2)}) copy-start(s32[16,128,128]{2,1,0:T(8,128)} %count.5) | copy-start | bytes 3145732
  28.3 2.7 %copy-start.9 = (f32[16,128,128]{2,1,0:T(8,128)S(1)}, f32[16,128,128]{2,1,0:T(8,128)}, u32[]{:S(2)}) copy-start(f32[16,128,128]{2,1,0:T(8,128)} %threshold.5) | copy-start | bytes 3145732
  28.3 2.7 %copy-start.15 = (f32[128,128]{1,0:T(8,128)S(1)}, f32[128,128]{1,0:T(8,128)}, u32[]{:S(2)}) copy-start(f32[128,128]{1,0:T(8,128)} %constant.20.clone.below) | copy-start | bytes 196612
  28.3 2.7 %copy-start.16 = (f32[144,256]{1,0:T(8,128)S(1)}, f32[144,256]{1,0:T(8,128)}, u32[]{:S(2)}) copy-start(f32[144,256]{1,0:T(8,128)} %constant.21.clone.above) | copy-start | bytes 442372
  32.0 14.1 %collective-permute-start.4 = (f32[176,128]{1,0:T(8,128)S(1)}, f32[176,128]{1,0:T(8,128)S(1)}, u32[]{:S(2)}, u32[]{:S(2)}) collective-permute-start(f32[176,128]{1,0:T(8,128)S(1)} %get-tuple-element.34), channel_id=1, source_target_pairs={{0,4},{4,0},{8,12},{12,8},{16,20},{20,16},{24,28},{28,24},{1,5},{5... | collective-permute-start | bytes 270344 | tf_op jit(solution)/shard_map/ppermute | solution.py:463
  32.1 14.0 %collective-permute-start.5 = (f32[176,128]{1,0:T(8,128)S(1)}, f32[176,128]{1,0:T(8,128)S(1)}, u32[]{:S(2)}, u32[]{:S(2)}) collective-permute-start(f32[176,128]{1,0:T(8,128)S(1)} %get-tuple-element.35), channel_id=1, source_target_pairs={{4,8},{8,4},{12,16},{16,12},{20,24},{24,20},{5,9},{9,5},{13,17},{1... | collective-permute-start | bytes 270344 | tf_op jit(solution)/shard_map/ppermute | solution.py:463
  47.0 5.1 %collective-permute-start.6 = (f32[176,128]{1,0:T(8,128)S(1)}, f32[176,128]{1,0:T(8,128)S(1)}, u32[]{:S(2)}, u32[]{:S(2)}) collective-permute-start(f32[176,128]{1,0:T(8,128)S(1)} %get-tuple-element.38), channel_id=1, source_target_pairs={{0,1},{1,0},{2,3},{3,2},{4,5},{5,4},{6,7},{7,6},{8,9},{9,8},{10,11... | collective-permute-start | bytes 270344 | tf_op jit(solution)/shard_map/ppermute | solution.py:463
  47.0 5.8 %collective-permute-start.7 = (f32[176,128]{1,0:T(8,128)S(1)}, f32[176,128]{1,0:T(8,128)S(1)}, u32[]{:S(2)}, u32[]{:S(2)}) collective-permute-start(f32[176,128]{1,0:T(8,128)S(1)} %get-tuple-element.39), channel_id=1, source_target_pairs={{1,2},{2,1},{5,6},{6,5},{9,10},{10,9},{13,14},{14,13},{17,18},{18,... | collective-permute-start | bytes 270344 | tf_op jit(solution)/shard_map/ppermute | solution.py:463
  53.9 13.2 %collective-permute-start.8 = (f32[176,128]{1,0:T(8,128)S(1)}, f32[176,128]{1,0:T(8,128)S(1)}, u32[]{:S(2)}, u32[]{:S(2)}) collective-permute-start(f32[176,128]{1,0:T(8,128)S(1)} %get-tuple-element.42), channel_id=1, source_target_pairs={{0,4},{4,0},{8,12},{12,8},{16,20},{20,16},{24,28},{28,24},{1,5},{5... | collective-permute-start | bytes 270344 | tf_op jit(solution)/shard_map/ppermute | solution.py:463
  53.9 13.1 %collective-permute-start.9 = (f32[176,128]{1,0:T(8,128)S(1)}, f32[176,128]{1,0:T(8,128)S(1)}, u32[]{:S(2)}, u32[]{:S(2)}) collective-permute-start(f32[176,128]{1,0:T(8,128)S(1)} %get-tuple-element.43), channel_id=1, source_target_pairs={{4,8},{8,4},{12,16},{16,12},{20,24},{24,20},{5,9},{9,5},{13,17},{1... | collective-permute-start | bytes 270344 | tf_op jit(solution)/shard_map/ppermute | solution.py:463
  67.4 6.4 %collective-permute-start.10 = (f32[176,128]{1,0:T(8,128)S(1)}, f32[176,128]{1,0:T(8,128)S(1)}, u32[]{:S(2)}, u32[]{:S(2)}) collective-permute-start(f32[176,128]{1,0:T(8,128)S(1)} %get-tuple-element.46), channel_id=1, source_target_pairs={{0,1},{1,0},{2,3},{3,2},{4,5},{5,4},{6,7},{7,6},{8,9},{9,8},{10,11... | collective-permute-start | bytes 270344 | tf_op jit(solution)/shard_map/ppermute | solution.py:463
  67.5 6.4 %collective-permute-start.11 = (f32[176,128]{1,0:T(8,128)S(1)}, f32[176,128]{1,0:T(8,128)S(1)}, u32[]{:S(2)}, u32[]{:S(2)}) collective-permute-start(f32[176,128]{1,0:T(8,128)S(1)} %get-tuple-element.47), channel_id=1, source_target_pairs={{1,2},{2,1},{5,6},{6,5},{9,10},{10,9},{13,14},{14,13},{17,18},{18,... | collective-permute-start | bytes 270344 | tf_op jit(solution)/shard_map/ppermute | solution.py:463

commit v3 on v2

--- a/solution.py
+++ b/solution.py
@@ -112,7 +112,7 @@
 
 def add_columns(value, layer, low, high):
     cols = value.shape[1]
-    slots = lane_ids(value.shape) // REACH
+    slots = lane_ids(value.shape) >> (REACH.bit_length() - 1)
     packed = jnp.where(slots == layer, low, high)
     shift = (cols - layer * REACH) % cols
     moved = packed if isinstance(layer, int) and layer == 0 else pltpu.roll(packed, shift, 1)
@@ -123,8 +123,9 @@
     return jnp.exp2(jnp.minimum(threshold - full * norm, 0.0) * RATE)
 
 
-def first_edge_kernel(stress, strain, yields, count, below, above, even_ref, odd_ref,
-                      stress_s, strain_s, yields_s, count_s, block, sems):
+def first_edge_kernel(stress, strain, yields, count, below, above,
+                      even_ref, odd_ref, norm, norm_last, norm_before, *refs):
+    blank_smooth, blank_even, blank_odd, stress_s, strain_s, yields_s, count_s, block, sems = refs
     layers, rows, cols = stress.shape
     pairs = ((stress, stress_s), (strain, strain_s), (yields, yields_s), (count, count_s))
     starts = (0, rows - REACH)
@@ -137,6 +138,12 @@
                 )
             )
             copies[-1].start()
+    total = rows + REACH
+    ids = lax.broadcasted_iota(jnp.int32, (total, cols), 0)
+    down = inverse_weights("gx", ids - REACH, rows)
+    lanes = lane_ids((REACH, cols))
+    for ref, place in ((norm, lanes), (norm_last, 0 * lanes + (cols - 1)), (norm_before, 0 * lanes - 1)):
+        ref[...] = down * inverse_weights("gy", place, cols)[:1]
     sent = []
     extra = jnp.zeros((even_ref.shape[0] - layers * REACH, cols), jnp.float32)
     for side, matrix in enumerate((below, above)):
@@ -152,7 +159,7 @@
     send("gx", *sent, even_ref, odd_ref)
 
 
-def edge_kernel(group, stress, strain, yields, count, threshold, smooth, col_even, col_odd, norm,
+def edge_kernel(stress, strain, yields, count, threshold, smooth, col_even, col_odd, norm,
                 below, above, even_ref, odd_ref, low_block, high_block, rest):
     layers, rows, cols = stress.shape
     starts = (0, rows - 2 * REACH, rows - REACH)
@@ -169,21 +176,16 @@
             soften = 0.5 + 0.5 * retained(full, norm[extended, :], threshold[at])
             value = newton(stress[at], strain[at], yields[at], count[at], soften)
             if index == 0:
-                low_block[pl.ds(pl.multiple_of(layer * REACH, REACH), REACH), :] = value
+                low_block[pl.ds(layer * REACH, REACH), :] = value
             else:
-                row = pl.multiple_of((2 * layer + index - 1) * REACH, REACH)
-                high_block[pl.ds(row, REACH), :] = value
+                high_block[pl.ds((2 * layer + index - 1) * REACH, REACH), :] = value
             if index == 2:
                 kept = (stress[at] + strain[at]) - value
                 rest[pl.ds(layer, 1), :] = kept[REACH - 1 :]
                 rest[pl.ds(layers + layer, 1), :] = threshold[at][REACH - 1 :]
 
-    def step(index, carry):
-        for inner in range(group):
-            layer_step(index * group + inner)
-        return carry
-
-    lax.fori_loop(0, layers // group, step, 0)
+    for layer in range(layers):
+        layer_step(layer)
     low = left_product(left_constant(below[...]), low_block[...])
     high = left_product(left_constant(above[...]), high_block[...])
     extra = jnp.zeros((even_ref.shape[0] - low.shape[0], cols), jnp.float32)
@@ -193,89 +195,87 @@
     )
 
 
-def main_kernel(depth, fresh, *refs):
-    if fresh:
-        (stress, strain, yields, count, band_ref, low_ref, high_ref, next_ref,
-         across, low_cols, high_cols, deep, pack_low, pack_high, pack_next) = refs
-    else:
-        (stress, strain, yields, count, threshold, smooth, col_even, col_odd, norm, norm_last,
-         band_ref, low_ref, high_ref, next_ref,
-         across, low_cols, high_cols, plastic,
-         deep, pack_low, pack_high, pack_next, pack_threshold, pack_kept) = refs
+def main_kernel(turn, stress, strain, yields, count, threshold, smooth, col_even, col_odd, norm,
+                norm_last, band_ref, low_ref, high_ref, next_ref,
+                across, low_cols, high_cols, plastic,
+                soften, pack_low, pack_high, pack_next, pack_last):
     layers, rows, cols = stress.shape
-    blocks = rows // REACH
+    step_rows = 2 * REACH
+    steps = rows // step_rows
+
+    @pl.when(turn[0] == 0)
+    def _():
+        soften[...] = jnp.ones_like(soften)
+
+    @pl.when(turn[0] > 0)
+    def _():
+        def soften_step(index, carry):
+            part = pl.ds(pl.multiple_of(index * step_rows, step_rows), step_rows)
+            extended = pl.ds(pl.multiple_of(index * step_rows + REACH, REACH), step_rows)
+            low, high = sides("gy", col_even[extended, :], col_odd[extended, :])
+            for layer in range(layers):
+                at = (layer, part, slice(None))
+                full = add_columns(smooth[layer, extended, :], layer, low, high)
+                soften[at] = 0.5 + 0.5 * retained(full, norm[extended, :], threshold[at])
+            return carry
+
+        lax.fori_loop(0, steps, soften_step, 0)
+
+    def newton_step(index, carry):
+        part = pl.ds(pl.multiple_of(index * step_rows, step_rows), step_rows)
+        for layer in range(layers):
+            at = (layer, part, slice(None))
+            plastic[at] = newton(stress[at], strain[at], yields[at], count[at], soften[at])
+        return carry
+
+    lax.fori_loop(0, steps, newton_step, 0)
+
     constant = left_constant(band_ref[...])
-
-    def layer_pair(index, carry):
-        pair = []
-        for inner in range(2):
-            layer = 2 * index + inner
-            values = []
-            for block in range(blocks):
-                at = (layer, pl.ds(block * REACH, REACH), slice(None))
-                if fresh:
-                    soften = jnp.ones((REACH, cols), jnp.float32)
-                else:
-                    extended = pl.ds((block + 1) * REACH, REACH)
-                    low, high = sides("gy", col_even[extended, :], col_odd[extended, :])
-                    full = add_columns(smooth[layer, extended, :], layer, low, high)
-                    soften = 0.5 + 0.5 * retained(full, norm[extended, :], threshold[at])
-                value = newton(stress[at], strain[at], yields[at], count[at], soften)
-                values.append(value)
-                if not fresh:
-                    plastic[at] = value
-            pair.append(jnp.concatenate(values, axis=0))
-        result = left_product(constant, jnp.concatenate(pair, axis=1))
-        deep[2 * index] = result[:, :cols]
-        deep[2 * index + 1] = result[:, cols:]
-        return carry
-
-    lax.fori_loop(0, layers // 2, layer_pair, 0)
-
-    def row_block(index, carry):
+    for layer in range(0, layers, 2):
+        pair = jnp.concatenate([plastic[layer], plastic[layer + 1]], axis=1)
+        result = left_product(constant, pair)
+        across[layer] = result[:, :cols]
+        across[layer + 1] = result[:, cols:]
+
+    def pack(index, carry):
         part = pl.ds(pl.multiple_of(index * REACH, REACH), REACH)
-        values = depth_smooth([deep[layer, part, :] for layer in range(layers)], depth)
-        for layer, value in enumerate(values):
-            across[layer, part, :] = value
-        for ref, packed in zip((pack_low, pack_high, pack_next), pack_edges(values)):
+        packs = pack_edges([across[layer, part, :] for layer in range(layers)])
+        for ref, packed in zip((pack_low, pack_high, pack_next), packs):
             ref[part, :] = packed
         return carry
 
-    lax.fori_loop(0, blocks + 1, row_block, 0)
+    lax.fori_loop(0, rows // REACH + 1, pack, 0)
     low_cols[...] = right_product(pack_low[...], right_constant(low_ref[...]))
     high = right_product(pack_high[...], right_constant(high_ref[...]))
     behind = right_product(pack_next[...], right_constant(next_ref[...]))
-    if fresh:
-        high_cols[...] = high
-        return
-
-    def last_column(index, carry):
-        part = pl.ds(pl.multiple_of(index * REACH, REACH), REACH)
-        lanes = lane_ids((REACH, cols))
-        limit = kept = jnp.zeros((REACH, cols), jnp.float32)
-        for layer in range(layers):
-            at = (layer, part, slice(None))
-            limit = jnp.where(lanes == layer, pltpu.roll(threshold[at], layer + 1, 1), limit)
-            rest = (stress[at] + strain[at]) - plastic[at]
-            kept = jnp.where(lanes == layers + layer, pltpu.roll(rest, layers + layer + 1, 1), kept)
-        extended = pl.ds(pl.multiple_of((index + 1) * REACH, REACH), REACH)
-        pack_threshold[extended, :] = limit
-        pack_kept[extended, :] = kept
-        return carry
-
-    pack_threshold[pl.ds(0, REACH), :] = jnp.zeros((REACH, cols), jnp.float32)
-    pack_kept[pl.ds(0, REACH), :] = jnp.zeros((REACH, cols), jnp.float32)
-    lax.fori_loop(0, blocks, last_column, 0)
-    lanes = lane_ids(pack_kept.shape)
-    column = pack_threshold[...] - (high[:, cols:] + behind) * norm_last[...]
     high_cols[:, :cols] = high[:, :cols]
-    high_cols[:, cols:] = jnp.where(lanes < layers, column, pack_kept[...])
+
+    @pl.when(turn[0] == OUTER - 1)
+    def _():
+        def last_column(index, carry):
+            part = pl.ds(pl.multiple_of(index * step_rows, step_rows), step_rows)
+            lanes = lane_ids((step_rows, cols))
+            packed = jnp.zeros((step_rows, cols), jnp.float32)
+            for layer in range(layers):
+                at = (layer, part, slice(None))
+                packed = jnp.where(lanes == layer, pltpu.roll(threshold[at], layer + 1, 1), packed)
+                rest = (stress[at] + strain[at]) - plastic[at]
+                turned = pltpu.roll(rest, layers + layer + 1, 1)
+                packed = jnp.where(lanes == layers + layer, turned, packed)
+            pack_last[pl.ds(pl.multiple_of(index * step_rows + REACH, REACH), step_rows), :] = packed
+            return carry
+
+        pack_last[pl.ds(0, REACH), :] = jnp.zeros((REACH, cols), jnp.float32)
+        lax.fori_loop(0, steps, last_column, 0)
+        lanes = lane_ids(pack_last.shape)
+        drop = (high[:, cols:] + behind) * norm_last[...]
+        high_cols[:, cols:] = pack_last[...] - jnp.where(lanes < layers, drop, 0.0)
 
 
 def pack_edges(values):
     cols = values[0].shape[1]
     count = cols // REACH
-    slots = lane_ids(values[0].shape) // REACH
+    slots = lane_ids(values[0].shape) >> (REACH.bit_length() - 1)
     low = high = ahead = jnp.zeros_like(values[0])
     for layer, value in enumerate(values):
         moved = pltpu.roll(value, layer * REACH, 1) if layer else value
@@ -342,28 +342,33 @@
     own_ref[...] = low_all[:, cols:]
 
 
-def column_kernel(across, row_even, row_odd, band_ref, smooth):
+def column_kernel(depth, across, row_even, row_odd, band_ref, smooth, deep):
     layers, total, cols = across.shape
     strip = layers * REACH
-    constant = right_constant(band_ref[...])
+    edges = (0, REACH, total - REACH)
+
+    def depth_sums(part, values):
+        for layer, value in enumerate(depth_smooth(values, depth)):
+            deep[layer, part, :] = value
 
     def step(index, carry):
         for inner in range(2):
-            layer = 2 * index + inner
-            part = pl.ds(pl.multiple_of(layer * REACH, REACH), REACH)
-            low, high = sides("gx", row_even[part, :], row_odd[part, :])
-            line = pl.ds(strip + layer, 1)
-            before, _ = sides("gx", row_even[line, :], row_odd[line, :])
-            value = across[layer]
-            value = jnp.concatenate(
-                [value[:REACH] + before, value[REACH : 2 * REACH] + low,
-                 value[2 * REACH : total - REACH], value[total - REACH :] + high],
-                axis=0,
-            )
-            smooth[layer] = right_product(value, constant)
+            part = pl.ds(pl.multiple_of((2 * index + inner + 2) * REACH, REACH), REACH)
+            depth_sums(part, [across[layer, part, :] for layer in range(layers)])
         return carry
 
-    lax.fori_loop(0, layers // 2, step, 0)
+    lax.fori_loop(0, (total // REACH - 3) // 2, step, 0)
+    for first_row in edges:
+        part = pl.ds(first_row, REACH)
+        values = []
+        for layer in range(layers):
+            line = pl.ds(strip + layer, 1) if first_row == 0 else pl.ds(layer * REACH, REACH)
+            both = sides("gx", row_even[line, :], row_odd[line, :])
+            values.append(across[layer, part, :] + both[first_row > REACH])
+        depth_sums(part, values)
+    constant = right_constant(band_ref[...])
+    for layer in range(layers):
+        smooth[layer] = right_product(deep[layer], constant)
 
 
 def final_kernel(stress, strain, plastic, threshold, smooth, col_even, col_odd, row_even, row_odd,
@@ -393,7 +398,7 @@
             pltpu.make_async_copy(force_s.at[1, layer], force_out.at[1, layer], sems.at[2, layer]),
         )
 
-    def step(layer, carry):
+    def layer_step(layer):
         lanes = lane_ids((REACH, cols))
         top = lax.broadcasted_iota(jnp.int32, (REACH, cols), 0) == 0
         above_sum = above_diff = None
@@ -424,11 +429,16 @@
                 force_s[(0, *at)] = 0.5 * (jnp.where(top, above_sum, both) - (left + value))
                 force_s[(1, *at)] = 0.5 * (jnp.where(top, above_diff, diff) + (left - value))
             above_sum, above_diff = both, diff
-        for copy in copies(layer):
-            copy.start()
+
+    def step(index, carry):
+        for inner in range(2):
+            layer_step(2 * index + inner)
+        for inner in range(2):
+            for copy in copies(2 * index + inner):
+                copy.start()
         return carry
 
-    lax.fori_loop(0, layers, step, 0)
+    lax.fori_loop(0, layers // 2, step, 0)
 
     def drain(layer, carry):
         for copy in copies(layer):
@@ -439,14 +449,13 @@
     whole.wait()
 
 
-def call(kernel, outs, scratch, cost, operands, anywhere=False, outs_anywhere=False):
-    inside, outside = pl.BlockSpec(memory_space=pltpu.VMEM), pl.BlockSpec(memory_space=pl.ANY)
-    far = 4 if anywhere else 0
+def call(kernel, outs, scratch, cost, operands, spaces=None, outs_space=pltpu.VMEM):
+    spaces = spaces or [pltpu.VMEM] * len(operands)
     return pl.pallas_call(
         kernel,
         out_shape=[jax.ShapeDtypeStruct(shape, jnp.float32) for shape in outs],
-        in_specs=[outside] * far + [inside] * (len(operands) - far),
-        out_specs=[outside if outs_anywhere else inside] * len(outs),
+        in_specs=[pl.BlockSpec(memory_space=space) for space in spaces],
+        out_specs=[pl.BlockSpec(memory_space=outs_space)] * len(outs),
         scratch_shapes=[pltpu.VMEM(s, jnp.float32) if isinstance(s, tuple) else s for s in scratch],
         compiler_params=pltpu.CompilerParams(vmem_limit_bytes=VMEM_BYTES),
         cost_estimate=pl.CostEstimate(flops=cost, bytes_accessed=cost // 16, transcendentals=0),
@@ -456,18 +465,18 @@
 def exchange(axis, even, odd):
     count = lax.axis_size(axis)
     results = []
-    for start, value in ((0, even), (1, odd)):
+    for start, value in ((1, odd), (0, even)):
         pairs = []
         for low in range(start, count - 1, 2):
             pairs += [(low, low + 1), (low + 1, low)]
         results.append(lax.ppermute(value, axis, pairs))
-    return results
-
-
-def inverse_weights(axis, first, positions, length):
+    return results[::-1]
+
+
+def inverse_weights(axis, places, length):
     extent = length * lax.axis_size(axis)
-    places = lax.axis_index(axis) * length + first + jnp.arange(positions, dtype=jnp.int32)
-    total = jnp.zeros((positions,), jnp.float32)
+    places = places + lax.axis_index(axis) * length
+    total = jnp.zeros(places.shape, jnp.float32)
     for offset in range(-REACH, REACH + 1):
         inside = (places + offset >= 0) & (places + offset < extent)
         total = total + jnp.where(inside, tap(offset), 0.0)
@@ -477,23 +486,27 @@
 def matrices(layers, rows, cols):
     depth = depth_matrix(layers)
     up, down = band(REACH, REACH, REACH), band(REACH, REACH, -REACH)
-    below = np.kron(depth, up)
+    same = np.eye(layers)
+    below = np.kron(same, up)
     near = np.concatenate([np.zeros((REACH, REACH)), down], axis=1)
     line = band(1, 2 * REACH, 1 - 2 * REACH)
-    above = np.concatenate([np.kron(depth, near), np.kron(depth, line)], axis=0)
+    above = np.concatenate([np.kron(same, near), np.kron(same, line)], axis=0)
     rows_band = np.concatenate([np.zeros((REACH - 1, rows)), band(1, rows, 1), band(rows, rows)])
     slots = cols // REACH
     low, high, ahead = np.zeros((cols, 2 * cols)), np.zeros((cols, 2 * cols)), np.zeros((cols, cols))
-    for layer in range(layers):
-        own = slice(layer * REACH, (layer + 1) * REACH)
-        previous = (layer - 1) % slots
-        other = slice(previous * REACH, (previous + 1) * REACH)
-        low[own, other] = up.T
-        high[other, own] = down.T
-        low[own, cols + layer] = [tap(j + 1) for j in range(REACH)]
-        high[other, cols + layer] = [tap(REACH - 1 - j) for j in range(REACH)]
-        ahead[((layer - 2) % slots) * REACH + REACH - 1, layer] = tap(REACH)
-    constants = (below, above, rows_band, band(cols, cols), low, high, ahead)
+    for source in range(layers):
+        own = slice(source * REACH, (source + 1) * REACH)
+        first = (source - 1) % slots * REACH
+        other = slice(first, first + REACH)
+        for layer in range(layers):
+            weight = depth[layer, source]
+            first = (layer - 1) % slots * REACH
+            low[own, first : first + REACH] = weight * up.T
+            high[other, layer * REACH : (layer + 1) * REACH] = weight * down.T
+            low[own, cols + layer] = [weight * tap(j + 1) for j in range(REACH)]
+            high[other, cols + layer] = [weight * tap(REACH - 1 - j) for j in range(REACH)]
+            ahead[((source - 2) % slots) * REACH + REACH - 1, layer] = weight * tap(REACH)
+    constants = (below, above, np.kron(same, down), rows_band, band(cols, cols), low, high, ahead)
     return depth, [jnp.asarray(matrix, jnp.float32) for matrix in constants]
 
 
@@ -501,13 +514,8 @@
     layers, rows, cols = trial_stress.shape
     assert layers * REACH == cols == rows and layers % 2 == 0
     total, strip = rows + REACH, layers * REACH
-    depth, (below, above, rows_band, cols_band, low, high, ahead) = matrices(layers, rows, cols)
-
-    across_rows = inverse_weights("gx", -REACH, total, rows)[:, None]
-    across_cols = inverse_weights("gy", -1, cols + 1, cols)[None, :]
-    norm = across_rows * across_cols[:, 1:]
-    norm_last = jnp.broadcast_to(across_rows * across_cols[:, cols:], (total, cols))
-    norm_before = jnp.broadcast_to(across_rows * across_cols[:, :1], (total, cols))
+    depth, constants = matrices(layers, rows, cols)
+    below, above, above_first, rows_band, cols_band, *columns = constants
 
     inputs = (trial_stress, old_strain, yield_mask, newton_count)
     whole, wide = (layers, rows, cols), (layers, total, cols)
@@ -515,45 +523,40 @@
     sent_cols = (total + rows // 4 + REACH, cols)
     packed, packed_two = (total, cols), (total, 2 * cols)
     work = layers * rows * cols
-    columns = (low, high, ahead)
 
     for outer_no in range(OUTER):
         if outer_no == 0:
             edge = [pltpu.VMEM((2, layers, REACH, cols), kind) for kind in
                     (jnp.float32, jnp.float32, jnp.int32, jnp.int32)]
-            row_even, row_odd = call(
-                first_edge_kernel, [sent_rows] * 2,
+            row_even, row_odd, norm, norm_last, norm_before, smooth, col_even, col_odd = call(
+                first_edge_kernel,
+                [sent_rows, sent_rows, packed, packed, packed, wide, sent_cols, sent_cols],
                 edge + [(strip, cols), pltpu.SemaphoreType.DMA((2, 4))], work * 16,
-                (*inputs, below, above[:strip].reshape(strip, layers, 2, REACH)[:, :, 1].reshape(strip, strip)),
-                anywhere=True,
+                (*inputs, below, above_first), [pltpu.HBM] * 4 + [pltpu.VMEM] * 2,
             )
         else:
             row_even, row_odd = call(
-                functools.partial(edge_kernel, 8), [sent_rows] * 2,
+                edge_kernel, [sent_rows] * 2,
                 [(strip, cols), (2 * strip, cols), (2 * layers, cols)], work * 16,
                 (*inputs, damage_threshold, smooth, col_even, col_odd, norm, below, above),
             )
         row_even, row_odd = exchange("gx", row_even, row_odd)
-        if outer_no == 0:
-            across, low_cols, high_cols = call(
-                functools.partial(main_kernel, depth, True), [wide, packed_two, packed_two],
-                [wide, packed, packed, packed], work * 400,
-                (*inputs, rows_band, *columns),
-            )
-        else:
-            across, low_cols, high_cols, plastic = call(
-                functools.partial(main_kernel, depth, False), [wide, packed_two, packed_two, whole],
-                [wide, packed, packed, packed, packed, packed], work * 400,
-                (*inputs, damage_threshold, smooth, col_even, col_odd, norm, norm_last,
-                 rows_band, *columns),
-            )
+        turn = jnp.full((1,), outer_no, jnp.int32)
+        across, low_cols, high_cols, plastic = call(
+            main_kernel, [wide, packed_two, packed_two, whole],
+            [whole, packed, packed, packed, packed], work * 400,
+            (turn, *inputs, damage_threshold, smooth, col_even, col_odd, norm, norm_last,
+             rows_band, *columns),
+            [pltpu.SMEM] + [pltpu.VMEM] * 14,
+        )
         col_even, col_odd, own_cols = call(
             corner_kernel, [sent_cols, sent_cols, packed], [], work * 16,
             (row_even, row_odd, low_cols, high_cols, norm_last, *columns),
         )
         col_even, col_odd = exchange("gy", col_even, col_odd)
         (smooth,) = call(
-            column_kernel, [wide], [], work * 100, (across, row_even, row_odd, cols_band)
+            functools.partial(column_kernel, depth), [wide], [wide], work * 100,
+            (across, row_even, row_odd, cols_band),
         )
     return tuple(call(
         final_kernel, [whole, whole, (2, *whole)],
@@ -561,7 +564,7 @@
         work * 100,
         (trial_stress, old_strain, plastic, damage_threshold, smooth, col_even, col_odd,
          row_even, row_odd, norm, norm_before, own_cols),
-        outs_anywhere=True,
+        outs_space=pltpu.HBM,
     ))
 
 

time: 79 us -> 67.7 us (0.86)
  Pallas kernels: 41.2 us -> 30.4 us
  waiting for transfers between devices: 0.76 us -> 3.91 us
  local copies, waits for them, and re-layouts: 8.65 us -> 6.62 us
  other arithmetic: 1.46 us -> 0 us
    pallas_call x13, Pallas kernels: 41.2 us -> 30.4 us  [call(): pl.pallas_call(kernel, out_shape=[jax.ShapeDtypeStruct(shape, jnp.float32...]
    ppermute x12, waiting for transfers between devices: 0.76 us -> 3.91 us  [exchange(): results.append(lax.ppermute(value, axis, pairs))]
    mul x3 -> x0, other arithmetic: 1.4 us -> none  [the longest x1 0.67 us: local(): across_rows * across_cols[:, :1]]
    unnamed x38 -> x32, local copies, waits for them, and re-layouts: 7.85 us -> 6.62 us
  transfers between devices with their start and end apart: 12 -> 12, of which waited for: 1 -> 3; matrix products, arithmetic and copies ran while one was open for 3% -> 0% of each run, Pallas kernels for 38% -> 33%
where the time goes in v3:
time: 67.7 us; the launch traced here: 67.2 us
  Pallas kernels  30.4 us (45%)
  starting transfers between devices  25.3 us (37%)
  local copies, waits for them, and re-layouts  6.62 us (10%)
  waiting for transfers between devices  3.91 us (6%)
  between operations  0.93 us (1%)
    pallas_call x13, Pallas kernels, call(): pl.pallas_call(kernel, out_shape=[jax.ShapeDtypeStruct(shape, jnp.float32...  30.4 us
    ppermute x12, starting transfers between devices, exchange(): results.append(lax.ppermute(value, axis, pairs))  25.3 us
    unnamed x32, local copies, waits for them, and re-layouts  6.62 us
    ppermute x12, waiting for transfers between devices, exchange(): results.append(lax.ppermute(value, axis, pairs))  3.91 us
  transfers between devices with their start and end apart: 12, of which 3 were waited for; matrix products, arithmetic and copies ran while one was open for 0% of the time, Pallas kernels for 33%

profile of v3, /device:TPU:3, one launch (start us, length us, event | category | flops | bytes accessed | tf_op | source)
XLA Modules:
  0.0 67.2 jit_solution(15595950796489516505)
XLA Ops:
  0.6 0.0 copy-start
  0.6 1.2 %copy-done = f32[16,128,128]{2,1,0:T(8,128)S(1)} copy-done((f32[16,128,128]{2,1,0:T(8,128)S(1)}, f32[16,128,128]{2,1,0:T(8,128)}, u32[]{:S(2)}) %copy-start) | copy-done | bytes 1048600
  1.9 0.0 copy-start.2
  1.9 1.2 %copy-done.2 = f32[16,128,128]{2,1,0:T(8,128)S(1)} copy-done((f32[16,128,128]{2,1,0:T(8,128)S(1)}, f32[16,128,128]{2,1,0:T(8,128)}, u32[]{:S(2)}) %copy-start.2) | copy-done | bytes 1048600
  3.1 0.0 copy-start.5
  3.1 1.2 %copy-done.5 = s32[16,128,128]{2,1,0:T(8,128)S(1)} copy-done((s32[16,128,128]{2,1,0:T(8,128)S(1)}, s32[16,128,128]{2,1,0:T(8,128)}, u32[]{:S(2)}) %copy-start.5) | copy-done | bytes 1048600
  4.3 0.0 copy-start.7
  4.3 1.2 %copy-done.7 = s32[16,128,128]{2,1,0:T(8,128)S(1)} copy-done((s32[16,128,128]{2,1,0:T(8,128)S(1)}, s32[16,128,128]{2,1,0:T(8,128)}, u32[]{:S(2)}) %copy-start.7) | copy-done | bytes 1048600
  5.5 0.8 %copy-done.12 = f32[128,128]{1,0:T(8,128)S(1)} copy-done((f32[128,128]{1,0:T(8,128)S(1)}, f32[128,128]{1,0:T(8,128)}, u32[]{:S(2)}) %copy-start.12) | copy-done | bytes 65560
  6.4 0.8 %copy-done.15 = f32[128,128]{1,0:T(8,128)S(1)} copy-done((f32[128,128]{1,0:T(8,128)S(1)}, f32[128,128]{1,0:T(8,128)}, u32[]{:S(2)}) %copy-start.15) | copy-done | bytes 65560
  7.2 0.0 copy-start.8
  7.2 0.0 copy-start.9
  7.2 0.0 copy-start.11
  7.2 1.2 %shard_map.148 = (f32[176,128]{1,0:T(8,128)S(1)}, f32[176,128]{1,0:T(8,128)S(1)}, f32[136,128]{1,0:T(8,128)S(1)}, f32[136,128]{1,0:T(8,128)S(1)}, f32[136,128]{1...) custom-call(f32[16,128,128]{2,1,0:T(8,128)S(1)} %copy-done, ...), custom_call_target="tpu_custom_call" | custom-call | flops 4194304 | bytes 262144 | tf_op jit(solution)/shard_map/pallas_call | solution.py:454
  8.4 0.1 collective-permute-start
  8.5 4.4 %collective-permute-start.1 = (f32[176,128]{1,0:T(8,128)S(1)}, f32[176,128]{1,0:T(8,128)S(1)}, u32[]{:S(2)}, u32[]{:S(2)}) collective-permute-start(f32[176,128]{1,0:T(8,128)S(1)} %get-tuple-element.39), channel_id=1, source_target_pairs={{4,8},{8,4},{12,16},{16,12},{20,24},{24,20},{5,9},{9,5},{13,17},{1... | collective-permute-start | bytes 270344 | tf_op jit(solution)/shard_map/ppermute | solution.py:472
  12.9 0.0 copy-done.4
  12.9 0.0 copy-done.8
  12.9 0.0 copy-done.9
  12.9 0.0 copy-done.10
  12.9 0.0 copy-done.11
  12.9 0.0 copy-start.14
  12.9 5.6 %shard_map.149 = (f32[16,136,128]{2,1,0:T(8,128)S(1)}, f32[136,256]{1,0:T(8,128)S(1)}, f32[136,256]{1,0:T(8,128)S(1)}, f32[16,128,128]{2,1,0:T(8,128)}) custom-call(s32[1]{0:T(128)} %constant.10.clone.1.turn, f32[16,128,128]{2,1,0:T(8,128)S(1)} %copy-done, f32[16,128,128]{2,1,0:T(8,128)S(1)} %copy-done.2, s32[16,128,128]{2,1,0:T(8,128)S(1)} %copy-done.5, ...), custom_call_target="tpu_custom_call" | custom-call | flops 104857600 | bytes 6553600 | tf_op jit(solution)/shard_map/pallas_call | solution.py:454
  18.6 0.0 collective-permute-done.row_even
  18.6 0.0 collective-permute-done.1.row_odd
  18.6 1.0 %shard_map.151 = (f32[176,128]{1,0:T(8,128)S(1)}, f32[176,128]{1,0:T(8,128)S(1)}, f32[136,128]{1,0:T(8,128)}) custom-call(f32[176,128]{1,0:T(8,128)S(1)} %collective-permute-done.row_even, f32[176,128]{1,0:T(8,128)S(1)} %collective-permute-done.1.row_odd, f32[136,256]{1,0:T(8,128)S(1)} %get-tuple-element.40.low_cols, ...), custom_call_target="tpu_custom_call" | custom-call | flops 4194304 | bytes 262144 | tf_op jit(solution)/shard_map/pallas_call | solution.py:454
  19.5 1.2 %collective-permute-start.2 = (f32[176,128]{1,0:T(8,128)S(1)}, f32[176,128]{1,0:T(8,128)S(1)}, u32[]{:S(2)}, u32[]{:S(2)}) collective-permute-start(f32[176,128]{1,0:T(8,128)S(1)} %get-tuple-element.42), channel_id=1, source_target_pairs={{0,1},{1,0},{2,3},{3,2},{4,5},{5,4},{6,7},{7,6},{8,9},{9,8},{10,11... | collective-permute-start | bytes 270344 | tf_op jit(solution)/shard_map/ppermute | solution.py:472
  20.8 3.0 %collective-permute-start.3 = (f32[176,128]{1,0:T(8,128)S(1)}, f32[176,128]{1,0:T(8,128)S(1)}, u32[]{:S(2)}, u32[]{:S(2)}) collective-permute-start(f32[176,128]{1,0:T(8,128)S(1)} %get-tuple-element.43), channel_id=1, source_target_pairs={{1,2},{2,1},{5,6},{6,5},{9,10},{10,9},{13,14},{14,13},{17,18},{18,... | collective-permute-start | bytes 270344 | tf_op jit(solution)/shard_map/ppermute | solution.py:472
  23.8 0.0 copy-done.14
  23.8 0.0 copy-start.1
  23.8 0.0 copy-start.3
  23.8 0.0 copy-start.13
  23.8 1.1 %shard_map.150.smooth = f32[16,136,128]{2,1,0:T(8,128)S(1)} custom-call(f32[16,136,128]{2,1,0:T(8,128)S(1)} %get-tuple-element.37.across, f32[176,128]{1,0:T(8,128)S(1)} %collective-permute-done.row_even, f32[176,128]{1,0:T(8,128)S(1)} %collective-permute-done.1.row_odd, f32[128,128]{1,0:T(8,128)S(1)} %copy-done.14), custom_call_target="tpu_custom_call" | custom-call | flops 26214400 | bytes 1638400 | tf_op jit(solution)/shard_map/pallas_call | solution.py:454
  24.9 0.0 collective-permute-done.2.col_even
  24.9 1.7 %collective-permute-done.3.col_odd = f32[176,128]{1,0:T(8,128)S(1)} collective-permute-done((f32[176,128]{1,0:T(8,128)S(1)}, f32[176,128]{1,0:T(8,128)S(1)}, u32[]{:S(2)}, u32[]{:S(2)}) %collective-permute-start.3) | collective-permute-done | bytes 90144 | tf_op jit(solution)/shard_map/ppermute | solution.py:472
  26.6 0.0 copy-done.6
  26.6 0.0 copy-done.1
  26.6 0.0 copy-done.3
  26.6 0.0 copy-done.13
  26.6 0.8 %shard_map.153 = (f32[176,128]{1,0:T(8,128)S(1)}, f32[176,128]{1,0:T(8,128)S(1)}) custom-call(f32[16,128,128]{2,1,0:T(8,128)S(1)} %copy-done.1, f32[16,128,128]{2,1,0:T(8,128)S(1)} %copy-done.3, s32[16,128,128]{2,1,0:T(8,128)S(1)} %copy-done.6, s32[16,128,128]{2,1,0:T(8,128)S(1)} %copy-done.7, f32[16,128,128]{2,1,0:T(8,128)S(1)} %copy-done.4, ...), custom_call_target="tpu_custom_call" | custom-call | flops 4194304 | bytes 262144 | tf_op jit(solution)/shard_map/pallas_call | solution.py:454
  27.4 0.1 collective-permute-start.4
  27.5 4.4 %collective-permute-start.5 = (f32[176,128]{1,0:T(8,128)S(1)}, f32[176,128]{1,0:T(8,128)S(1)}, u32[]{:S(2)}, u32[]{:S(2)}) collective-permute-start(f32[176,128]{1,0:T(8,128)S(1)} %get-tuple-element.46), channel_id=1, source_target_pairs={{4,8},{8,4},{12,16},{16,12},{20,24},{24,20},{5,9},{9,5},{13,17},{1... | collective-permute-start | bytes 270344 | tf_op jit(solution)/shard_map/ppermute | solution.py:472
  31.9 6.6 %shard_map.152 = (f32[16,136,128]{2,1,0:T(8,128)S(1)}, f32[136,256]{1,0:T(8,128)S(1)}, f32[136,256]{1,0:T(8,128)S(1)}, f32[16,128,128]{2,1,0:T(8,128)}) custom-call(s32[1]{0:T(128)} %constant.9.clone.1.turn, f32[16,128,128]{2,1,0:T(8,128)S(1)} %copy-done.1, f32[16,128,128]{2,1,0:T(8,128)S(1)} %copy-done.3, s32[16,128,128]{2,1,0:T(8,128)S(1)} %copy-done.6, ...), custom_call_target="tpu_custom_call" | custom-call | flops 104857600 | bytes 6553600 | tf_op jit(solution)/shard_map/pallas_call | solution.py:454
  38.5 0.0 collective-permute-done.4.row_even
  38.5 0.0 collective-permute-done.5.row_odd
  38.5 0.9 %shard_map.155 = (f32[176,128]{1,0:T(8,128)S(1)}, f32[176,128]{1,0:T(8,128)S(1)}, f32[136,128]{1,0:T(8,128)}) custom-call(f32[176,128]{1,0:T(8,128)S(1)} %collective-permute-done.4.row_even, f32[176,128]{1,0:T(8,128)S(1)} %collective-permute-done.5.row_odd, f32[136,256]{1,0:T(8,128)S(1)} %get-tuple-element.47.low_cols, ...), custom_call_target="tpu_custom_call" | custom-call | flops 4194304 | bytes 262144 | tf_op jit(solution)/shard_map/pallas_call | solution.py:454
  39.4 0.0 collective-permute-start.6
  39.4 3.6 %collective-permute-start.7 = (f32[176,128]{1,0:T(8,128)S(1)}, f32[176,128]{1,0:T(8,128)S(1)}, u32[]{:S(2)}, u32[]{:S(2)}) collective-permute-start(f32[176,128]{1,0:T(8,128)S(1)} %get-tuple-element.50), channel_id=1, source_target_pairs={{1,2},{2,1},{5,6},{6,5},{9,10},{10,9},{13,14},{14,13},{17,18},{18,... | collective-permute-start | bytes 270344 | tf_op jit(solution)/shard_map/ppermute | solution.py:472
  43.0 1.1 %shard_map.154.smooth = f32[16,136,128]{2,1,0:T(8,128)S(1)} custom-call(f32[16,136,128]{2,1,0:T(8,128)S(1)} %get-tuple-element.44.across, f32[176,128]{1,0:T(8,128)S(1)} %collective-permute-done.4.row_even, f32[176,128]{1,0:T(8,128)S(1)} %collective-permute-done.5.row_odd, f32[128,128]{1,0:T(8,128)S(1)} %copy-done.14), custom_call_target="tpu_custom_call" | custom-call | flops 26214400 | bytes 1638400 | tf_op jit(solution)/shard_map/pallas_call | solution.py:454
  44.1 0.0 collective-permute-done.6.col_even
  44.1 1.1 %collective-permute-done.7.col_odd = f32[176,128]{1,0:T(8,128)S(1)} collective-permute-done((f32[176,128]{1,0:T(8,128)S(1)}, f32[176,128]{1,0:T(8,128)S(1)}, u32[]{:S(2)}, u32[]{:S(2)}) %collective-permute-start.7) | collective-permute-done | bytes 90144 | tf_op jit(solution)/shard_map/ppermute | solution.py:472
  45.2 0.8 %shard_map.157 = (f32[176,128]{1,0:T(8,128)S(1)}, f32[176,128]{1,0:T(8,128)S(1)}) custom-call(f32[16,128,128]{2,1,0:T(8,128)S(1)} %copy-done.1, f32[16,128,128]{2,1,0:T(8,128)S(1)} %copy-done.3, s32[16,128,128]{2,1,0:T(8,128)S(1)} %copy-done.6, s32[16,128,128]{2,1,0:T(8,128)S(1)} %copy-done.7, f32[16,128,128]{2,1,0:T(8,128)S(1)} %copy-done.4, ...), custom_call_target="tpu_custom_call" | custom-call | flops 4194304 | bytes 262144 | tf_op jit(solution)/shard_map/pallas_call | solution.py:454
  46.1 0.1 collective-permute-start.8
  46.1 4.4 %collective-permute-start.9 = (f32[176,128]{1,0:T(8,128)S(1)}, f32[176,128]{1,0:T(8,128)S(1)}, u32[]{:S(2)}, u32[]{:S(2)}) collective-permute-start(f32[176,128]{1,0:T(8,128)S(1)} %get-tuple-element.54), channel_id=1, source_target_pairs={{4,8},{8,4},{12,16},{16,12},{20,24},{24,20},{5,9},{9,5},{13,17},{1... | collective-permute-start | bytes 270344 | tf_op jit(solution)/shard_map/ppermute | solution.py:472
  50.5 6.7 %shard_map.156 = (f32[16,136,128]{2,1,0:T(8,128)S(1)}, f32[136,256]{1,0:T(8,128)S(1)}, f32[136,256]{1,0:T(8,128)S(1)}, f32[16,128,128]{2,1,0:T(8,128)S(1)}) custom-call(s32[1]{0:T(128)} %constant.8.clone.1.turn, f32[16,128,128]{2,1,0:T(8,128)S(1)} %copy-done.1, f32[16,128,128]{2,1,0:T(8,128)S(1)} %copy-done.3, s32[16,128,128]{2,1,0:T(8,128)S(1)} %copy-done.6, ...), custom_call_target="tpu_custom_call" | custom-call | flops 104857600 | bytes 6553600 | tf_op jit(solution)/shard_map/pallas_call | solution.py:454
  57.2 0.0 collective-permute-done.8.row_even
  57.2 0.0 collective-permute-done.9.row_odd
  57.2 0.4 shard_map.159
  57.6 0.0 collective-permute-start.10
  57.6 4.2 %collective-permute-start.11 = (f32[176,128]{1,0:T(8,128)S(1)}, f32[176,128]{1,0:T(8,128)S(1)}, u32[]{:S(2)}, u32[]{:S(2)}) collective-permute-start(f32[176,128]{1,0:T(8,128)S(1)} %get-tuple-element.58), channel_id=1, source_target_pairs={{1,2},{2,1},{5,6},{6,5},{9,10},{10,9},{13,14},{14,13},{17,18},{18,... | collective-permute-start | bytes 270344 | tf_op jit(solution)/shard_map/ppermute | solution.py:472
  61.8 1.1 %shard_map.158.smooth = f32[16,136,128]{2,1,0:T(8,128)S(1)} custom-call(f32[16,136,128]{2,1,0:T(8,128)S(1)} %get-tuple-element.52.across, f32[176,128]{1,0:T(8,128)S(1)} %collective-permute-done.8.row_even, f32[176,128]{1,0:T(8,128)S(1)} %collective-permute-done.9.row_odd, f32[128,128]{1,0:T(8,128)S(1)} %copy-done.14), custom_call_target="tpu_custom_call" | custom-call | flops 26214400 | bytes 1638400 | tf_op jit(solution)/shard_map/pallas_call | solution.py:454
  62.9 0.0 collective-permute-done.10.col_even
  62.9 1.1 %collective-permute-done.11.col_odd = f32[176,128]{1,0:T(8,128)S(1)} collective-permute-done((f32[176,128]{1,0:T(8,128)S(1)}, f32[176,128]{1,0:T(8,128)S(1)}, u32[]{:S(2)}, u32[]{:S(2)}) %collective-permute-start.11) | collective-permute-done | bytes 90144 | tf_op jit(solution)/shard_map/ppermute | solution.py:472
  64.0 3.2 %shard_map.160 = (f32[16,128,128]{2,1,0:T(8,128)}, f32[16,128,128]{2,1,0:T(8,128)}, f32[2,16,128,128]{3,2,1,0:T(8,128)}) custom-call(f32[16,128,128]{2,1,0:T(8,128)S(1)} %copy-done.1, f32[16,128,128]{2,1,0:T(8,128)S(1)} %copy-done.3, f32[16,128,128]{2,1,0:T(8,128)S(1)} %get-tuple-element.51.plastic, f32[16,128,128]{2,1,0:T(8,128)S(1)} %copy-done.4, ...), custom_call_target="tpu_custom_call" | custom-call | flops 26214400 | bytes 1638400 | tf_op jit(solution)/shard_map/pallas_call | solution.py:454
  (5 shorter events, 0.0 us)
Async XLA Ops:
  0.6 1.2 %copy-start = (f32[16,128,128]{2,1,0:T(8,128)S(1)}, f32[16,128,128]{2,1,0:T(8,128)}, u32[]{:S(2)}) copy-start(f32[16,128,128]{2,1,0:T(8,128)} %stress.13) | copy-start | bytes 3145732
  1.9 1.2 %copy-start.2 = (f32[16,128,128]{2,1,0:T(8,128)S(1)}, f32[16,128,128]{2,1,0:T(8,128)}, u32[]{:S(2)}) copy-start(f32[16,128,128]{2,1,0:T(8,128)} %strain.13) | copy-start | bytes 3145732
  3.1 1.2 %copy-start.5 = (s32[16,128,128]{2,1,0:T(8,128)S(1)}, s32[16,128,128]{2,1,0:T(8,128)}, u32[]{:S(2)}) copy-start(s32[16,128,128]{2,1,0:T(8,128)} %yields.11) | copy-start | bytes 3145732
  4.3 1.2 %copy-start.7 = (s32[16,128,128]{2,1,0:T(8,128)S(1)}, s32[16,128,128]{2,1,0:T(8,128)}, u32[]{:S(2)}) copy-start(s32[16,128,128]{2,1,0:T(8,128)} %count.11) | copy-start | bytes 3145732
  5.5 0.8 %copy-start.12 = (f32[128,128]{1,0:T(8,128)S(1)}, f32[128,128]{1,0:T(8,128)}, u32[]{:S(2)}) copy-start(f32[128,128]{1,0:T(8,128)} %constant.22.clone.below) | copy-start | bytes 196612
  6.4 0.8 %copy-start.15 = (f32[128,128]{1,0:T(8,128)S(1)}, f32[128,128]{1,0:T(8,128)}, u32[]{:S(2)}) copy-start(f32[128,128]{1,0:T(8,128)} %constant.24.clone.above) | copy-start | bytes 196612
  7.2 5.7 %copy-start.4 = (f32[16,128,128]{2,1,0:T(8,128)S(1)}, f32[16,128,128]{2,1,0:T(8,128)}, u32[]{:S(2)}) copy-start(f32[16,128,128]{2,1,0:T(8,128)} %threshold.11) | copy-start | bytes 3145732
  7.2 5.7 %copy-start.8 = (f32[128,256]{1,0:T(8,128)S(1)}, f32[128,256]{1,0:T(8,128)}, u32[]{:S(2)}) copy-start(f32[128,256]{1,0:T(8,128)} %constant.28.clone.high_ref) | copy-start | bytes 393220
  7.2 5.7 %copy-start.9 = (f32[128,256]{1,0:T(8,128)S(1)}, f32[128,256]{1,0:T(8,128)}, u32[]{:S(2)}) copy-start(f32[128,256]{1,0:T(8,128)} %constant.27.clone.low_ref) | copy-start | bytes 393220
  7.2 5.7 %copy-start.10 = (f32[128,128]{1,0:T(8,128)S(1)}, f32[128,128]{1,0:T(8,128)}, u32[]{:S(2)}) copy-start(f32[128,128]{1,0:T(8,128)} %constant.29.clone.next_ref) | copy-start | bytes 196612
  7.2 5.7 %copy-start.11 = (f32[136,128]{1,0:T(8,128)S(1)}, f32[136,128]{1,0:T(8,128)}, u32[]{:S(2)}) copy-start(f32[136,128]{1,0:T(8,128)} %constant.25.clone.band_ref) | copy-start | bytes 208900
  8.4 10.1 %collective-permute-start = (f32[176,128]{1,0:T(8,128)S(1)}, f32[176,128]{1,0:T(8,128)S(1)}, u32[]{:S(2)}, u32[]{:S(2)}) collective-permute-start(f32[176,128]{1,0:T(8,128)S(1)} %get-tuple-element.38), channel_id=1, source_target_pairs={{0,4},{4,0},{8,12},{12,8},{16,20},{20,16},{24,28},{28,24},{1,5},{5... | collective-permute-start | bytes 270344 | tf_op jit(solution)/shard_map/ppermute | solution.py:472
  8.5 10.1 %collective-permute-start.1 = (f32[176,128]{1,0:T(8,128)S(1)}, f32[176,128]{1,0:T(8,128)S(1)}, u32[]{:S(2)}, u32[]{:S(2)}) collective-permute-start(f32[176,128]{1,0:T(8,128)S(1)} %get-tuple-element.39), channel_id=1, source_target_pairs={{4,8},{8,4},{12,16},{16,12},{20,24},{24,20},{5,9},{9,5},{13,17},{1... | collective-permute-start | bytes 270344 | tf_op jit(solution)/shard_map/ppermute | solution.py:472
  12.9 10.9 %copy-start.14 = (f32[128,128]{1,0:T(8,128)S(1)}, f32[128,128]{1,0:T(8,128)}, u32[]{:S(2)}) copy-start(f32[128,128]{1,0:T(8,128)} %constant.26.clone.band_ref) | copy-start | bytes 196612
  18.6 8.0 %copy-start.6 = (s32[16,128,128]{2,1,0:T(8,128)S(1)}, s32[16,128,128]{2,1,0:T(8,128)}, u32[]{:S(2)}) copy-start(s32[16,128,128]{2,1,0:T(8,128)} %yields.11) | copy-start | bytes 3145732
  19.5 5.4 %collective-permute-start.2 = (f32[176,128]{1,0:T(8,128)S(1)}, f32[176,128]{1,0:T(8,128)S(1)}, u32[]{:S(2)}, u32[]{:S(2)}) collective-permute-start(f32[176,128]{1,0:T(8,128)S(1)} %get-tuple-element.42), channel_id=1, source_target_pairs={{0,1},{1,0},{2,3},{3,2},{4,5},{5,4},{6,7},{7,6},{8,9},{9,8},{10,11... | collective-permute-start | bytes 270344 | tf_op jit(solution)/shard_map/ppermute | solution.py:472
  20.8 5.8 %collective-permute-start.3 = (f32[176,128]{1,0:T(8,128)S(1)}, f32[176,128]{1,0:T(8,128)S(1)}, u32[]{:S(2)}, u32[]{:S(2)}) collective-permute-start(f32[176,128]{1,0:T(8,128)S(1)} %get-tuple-element.43), channel_id=1, source_target_pairs={{1,2},{2,1},{5,6},{6,5},{9,10},{10,9},{13,14},{14,13},{17,18},{18,... | collective-permute-start | bytes 270344 | tf_op jit(solution)/shard_map/ppermute | solution.py:472
  23.8 2.8 %copy-start.1 = (f32[16,128,128]{2,1,0:T(8,128)S(1)}, f32[16,128,128]{2,1,0:T(8,128)}, u32[]{:S(2)}) copy-start(f32[16,128,128]{2,1,0:T(8,128)} %stress.13) | copy-start | bytes 3145732
  23.8 2.8 %copy-start.3 = (f32[16,128,128]{2,1,0:T(8,128)S(1)}, f32[16,128,128]{2,1,0:T(8,128)}, u32[]{:S(2)}) copy-start(f32[16,128,128]{2,1,0:T(8,128)} %strain.13) | copy-start | bytes 3145732
  23.8 2.8 %copy-start.13 = (f32[144,256]{1,0:T(8,128)S(1)}, f32[144,256]{1,0:T(8,128)}, u32[]{:S(2)}) copy-start(f32[144,256]{1,0:T(8,128)} %constant.23.clone.above) | copy-start | bytes 442372
  27.4 11.0 %collective-permute-start.4 = (f32[176,128]{1,0:T(8,128)S(1)}, f32[176,128]{1,0:T(8,128)S(1)}, u32[]{:S(2)}, u32[]{:S(2)}) collective-permute-start(f32[176,128]{1,0:T(8,128)S(1)} %get-tuple-element.45), channel_id=1, source_target_pairs={{0,4},{4,0},{8,12},{12,8},{16,20},{20,16},{24,28},{28,24},{1,5},{5... | collective-permute-start | bytes 270344 | tf_op jit(solution)/shard_map/ppermute | solution.py:472
  27.5 10.9 %collective-permute-start.5 = (f32[176,128]{1,0:T(8,128)S(1)}, f32[176,128]{1,0:T(8,128)S(1)}, u32[]{:S(2)}, u32[]{:S(2)}) collective-permute-start(f32[176,128]{1,0:T(8,128)S(1)} %get-tuple-element.46), channel_id=1, source_target_pairs={{4,8},{8,4},{12,16},{16,12},{20,24},{24,20},{5,9},{9,5},{13,17},{1... | collective-permute-start | bytes 270344 | tf_op jit(solution)/shard_map/ppermute | solution.py:472
  39.4 4.7 %collective-permute-start.6 = (f32[176,128]{1,0:T(8,128)S(1)}, f32[176,128]{1,0:T(8,128)S(1)}, u32[]{:S(2)}, u32[]{:S(2)}) collective-permute-start(f32[176,128]{1,0:T(8,128)S(1)} %get-tuple-element.49), channel_id=1, source_target_pairs={{0,1},{1,0},{2,3},{3,2},{4,5},{5,4},{6,7},{7,6},{8,9},{9,8},{10,11... | collective-permute-start | bytes 270344 | tf_op jit(solution)/shard_map/ppermute | solution.py:472
  39.4 5.8 %collective-permute-start.7 = (f32[176,128]{1,0:T(8,128)S(1)}, f32[176,128]{1,0:T(8,128)S(1)}, u32[]{:S(2)}, u32[]{:S(2)}) collective-permute-start(f32[176,128]{1,0:T(8,128)S(1)} %get-tuple-element.50), channel_id=1, source_target_pairs={{1,2},{2,1},{5,6},{6,5},{9,10},{10,9},{13,14},{14,13},{17,18},{18,... | collective-permute-start | bytes 270344 | tf_op jit(solution)/shard_map/ppermute | solution.py:472
  46.1 11.2 %collective-permute-start.8 = (f32[176,128]{1,0:T(8,128)S(1)}, f32[176,128]{1,0:T(8,128)S(1)}, u32[]{:S(2)}, u32[]{:S(2)}) collective-permute-start(f32[176,128]{1,0:T(8,128)S(1)} %get-tuple-element.53), channel_id=1, source_target_pairs={{0,4},{4,0},{8,12},{12,8},{16,20},{20,16},{24,28},{28,24},{1,5},{5... | collective-permute-start | bytes 270344 | tf_op jit(solution)/shard_map/ppermute | solution.py:472
  46.1 11.1 %collective-permute-start.9 = (f32[176,128]{1,0:T(8,128)S(1)}, f32[176,128]{1,0:T(8,128)S(1)}, u32[]{:S(2)}, u32[]{:S(2)}) collective-permute-start(f32[176,128]{1,0:T(8,128)S(1)} %get-tuple-element.54), channel_id=1, source_target_pairs={{4,8},{8,4},{12,16},{16,12},{20,24},{24,20},{5,9},{9,5},{13,17},{1... | collective-permute-start | bytes 270344 | tf_op jit(solution)/shard_map/ppermute | solution.py:472
  57.6 5.3 %collective-permute-start.10 = (f32[176,128]{1,0:T(8,128)S(1)}, f32[176,128]{1,0:T(8,128)S(1)}, u32[]{:S(2)}, u32[]{:S(2)}) collective-permute-start(f32[176,128]{1,0:T(8,128)S(1)} %get-tuple-element.57), channel_id=1, source_target_pairs={{0,1},{1,0},{2,3},{3,2},{4,5},{5,4},{6,7},{7,6},{8,9},{9,8},{10,11... | collective-permute-start | bytes 270344 | tf_op jit(solution)/shard_map/ppermute | solution.py:472
  57.6 6.4 %collective-permute-start.11 = (f32[176,128]{1,0:T(8,128)S(1)}, f32[176,128]{1,0:T(8,128)S(1)}, u32[]{:S(2)}, u32[]{:S(2)}) collective-permute-start(f32[176,128]{1,0:T(8,128)S(1)} %get-tuple-element.58), channel_id=1, source_target_pairs={{1,2},{2,1},{5,6},{6,5},{9,10},{10,9},{13,14},{14,13},{17,18},{18,... | collective-permute-start | bytes 270344 | tf_op jit(solution)/shard_map/ppermute | solution.py:472

commit v4 on v3

--- a/solution.py
+++ b/solution.py
@@ -123,38 +123,35 @@
     return jnp.exp2(jnp.minimum(threshold - full * norm, 0.0) * RATE)
 
 
-def first_edge_kernel(stress, strain, yields, count, below, above,
+def first_edge_kernel(stress, strain, yields, count,
                       even_ref, odd_ref, norm, norm_last, norm_before, *refs):
-    blank_smooth, blank_even, blank_odd, stress_s, strain_s, yields_s, count_s, block, sems = refs
-    layers, rows, cols = stress.shape
-    pairs = ((stress, stress_s), (strain, strain_s), (yields, yields_s), (count, count_s))
-    starts = (0, rows - REACH)
-    copies = []
-    for side, first_row in enumerate(starts):
-        for index, (source, target) in enumerate(pairs):
-            copies.append(
-                pltpu.make_async_copy(
-                    source.at[:, pl.ds(first_row, REACH), :], target.at[side], sems.at[side, index]
-                )
-            )
-            copies[-1].start()
+    block = refs[-1]
+    layers, cols = stress.shape[0], stress.shape[2]
+    rows = norm.shape[0] - REACH
     total = rows + REACH
     ids = lax.broadcasted_iota(jnp.int32, (total, cols), 0)
     down = inverse_weights("gx", ids - REACH, rows)
     lanes = lane_ids((REACH, cols))
     for ref, place in ((norm, lanes), (norm_last, 0 * lanes + (cols - 1)), (norm_before, 0 * lanes - 1)):
         ref[...] = down * inverse_weights("gy", place, cols)[:1]
+    square = (layers * REACH, layers * REACH)
+    line, lane = lax.broadcasted_iota(jnp.int32, square, 0), lane_ids(square)
+    steps = (lane & (REACH - 1)) - (line & (REACH - 1))
+    band_part = jnp.zeros(square, jnp.float32)
+    for step in range(REACH):
+        band_part = jnp.where(abs(steps) == step, tap(REACH - step), band_part)
+    band_part = jnp.where((line ^ lane) < REACH, band_part, 0.0)
     sent = []
     extra = jnp.zeros((even_ref.shape[0] - layers * REACH, cols), jnp.float32)
-    for side, matrix in enumerate((below, above)):
-        for copy in copies[side * len(pairs) : (side + 1) * len(pairs)]:
-            copy.wait()
+    for side, matrix in enumerate(
+        (jnp.where(steps <= 0, band_part, 0.0), jnp.where(steps >= 0, band_part, 0.0))
+    ):
         for layer in range(layers):
-            at = (side, layer)
+            at = (layer, pl.ds(side * REACH, REACH), slice(None))
             block[pl.ds(layer * REACH, REACH), :] = newton(
-                stress_s[at], strain_s[at], yields_s[at], count_s[at], jnp.ones((REACH, cols), jnp.float32)
+                stress[at], strain[at], yields[at], count[at], jnp.ones((REACH, cols), jnp.float32)
             )
-        product = left_product(left_constant(matrix[...]), block[...])
+        product = left_product(left_constant(matrix), block[...])
         sent.append(jnp.concatenate([product, extra], axis=0))
     send("gx", *sent, even_ref, odd_ref)
 
@@ -195,56 +192,59 @@
     )
 
 
-def main_kernel(turn, stress, strain, yields, count, threshold, smooth, col_even, col_odd, norm,
-                norm_last, band_ref, low_ref, high_ref, next_ref,
-                across, low_cols, high_cols, plastic,
-                soften, pack_low, pack_high, pack_next, pack_last):
+def newton_kernel(turn, stress, strain, yields, count, threshold, smooth, col_even, col_odd, norm,
+                  waiting, plastic, ready):
     layers, rows, cols = stress.shape
     step_rows = 2 * REACH
     steps = rows // step_rows
+    ready[...] = waiting[...]
 
     @pl.when(turn[0] == 0)
     def _():
-        soften[...] = jnp.ones_like(soften)
+        def step(index, carry):
+            part = pl.ds(pl.multiple_of(index * step_rows, step_rows), step_rows)
+            soften = jnp.ones((step_rows, cols), jnp.float32)
+            for layer in range(layers):
+                at = (layer, part, slice(None))
+                plastic[at] = newton(stress[at], strain[at], yields[at], count[at], soften)
+            return carry
+
+        lax.fori_loop(0, steps, step, 0)
 
     @pl.when(turn[0] > 0)
     def _():
-        def soften_step(index, carry):
+        def step(index, carry):
             part = pl.ds(pl.multiple_of(index * step_rows, step_rows), step_rows)
             extended = pl.ds(pl.multiple_of(index * step_rows + REACH, REACH), step_rows)
             low, high = sides("gy", col_even[extended, :], col_odd[extended, :])
             for layer in range(layers):
                 at = (layer, part, slice(None))
                 full = add_columns(smooth[layer, extended, :], layer, low, high)
-                soften[at] = 0.5 + 0.5 * retained(full, norm[extended, :], threshold[at])
+                soften = 0.5 + 0.5 * retained(full, norm[extended, :], threshold[at])
+                plastic[at] = newton(stress[at], strain[at], yields[at], count[at], soften)
             return carry
 
-        lax.fori_loop(0, steps, soften_step, 0)
-
-    def newton_step(index, carry):
-        part = pl.ds(pl.multiple_of(index * step_rows, step_rows), step_rows)
-        for layer in range(layers):
-            at = (layer, part, slice(None))
-            plastic[at] = newton(stress[at], strain[at], yields[at], count[at], soften[at])
-        return carry
-
-    lax.fori_loop(0, steps, newton_step, 0)
-
+        lax.fori_loop(0, steps, step, 0)
+
+
+def across_kernel(turn, stress, strain, threshold, plastic, norm_last, band_ref, low_ref, high_ref,
+                  next_ref, _, across, low_cols, high_cols, pack_low, pack_high, pack_next, pack_last):
+    layers, rows, cols = stress.shape
+    total = rows + REACH
+    step_rows = 2 * REACH
     constant = left_constant(band_ref[...])
+    slots = lane_ids((total, cols)) >> (REACH.bit_length() - 1)
     for layer in range(0, layers, 2):
         pair = jnp.concatenate([plastic[layer], plastic[layer + 1]], axis=1)
         result = left_product(constant, pair)
-        across[layer] = result[:, :cols]
-        across[layer + 1] = result[:, cols:]
-
-    def pack(index, carry):
-        part = pl.ds(pl.multiple_of(index * REACH, REACH), REACH)
-        packs = pack_edges([across[layer, part, :] for layer in range(layers)])
-        for ref, packed in zip((pack_low, pack_high, pack_next), packs):
-            ref[part, :] = packed
-        return carry
-
-    lax.fori_loop(0, rows // REACH + 1, pack, 0)
+        for inner in range(2):
+            value = result[:, inner * cols : (inner + 1) * cols]
+            across[layer + inner] = value
+            moved = pltpu.roll(value, (layer + inner) * REACH, 1) if layer + inner else value
+            for behind, ref in enumerate((pack_low, pack_high, pack_next)):
+                mask = slots == (layer + inner - behind) % (cols // REACH)
+                pltpu.store(ref, moved, mask=mask)
+
     low_cols[...] = right_product(pack_low[...], right_constant(low_ref[...]))
     high = right_product(pack_high[...], right_constant(high_ref[...]))
     behind = right_product(pack_next[...], right_constant(next_ref[...]))
@@ -266,7 +266,7 @@
             return carry
 
         pack_last[pl.ds(0, REACH), :] = jnp.zeros((REACH, cols), jnp.float32)
-        lax.fori_loop(0, steps, last_column, 0)
+        lax.fori_loop(0, rows // step_rows, last_column, 0)
         lanes = lane_ids(pack_last.shape)
         drop = (high[:, cols:] + behind) * norm_last[...]
         high_cols[:, cols:] = pack_last[...] - jnp.where(lanes < layers, drop, 0.0)
@@ -342,10 +342,10 @@
     own_ref[...] = low_all[:, cols:]
 
 
-def column_kernel(depth, across, row_even, row_odd, band_ref, smooth, deep):
+def depth_kernel(depth, across, row_even, row_odd, waiting, _, deep, ready):
     layers, total, cols = across.shape
     strip = layers * REACH
-    edges = (0, REACH, total - REACH)
+    ready[...] = waiting[...]
 
     def depth_sums(part, values):
         for layer, value in enumerate(depth_smooth(values, depth)):
@@ -358,7 +358,7 @@
         return carry
 
     lax.fori_loop(0, (total // REACH - 3) // 2, step, 0)
-    for first_row in edges:
+    for first_row in (0, REACH, total - REACH):
         part = pl.ds(first_row, REACH)
         values = []
         for layer in range(layers):
@@ -366,8 +366,11 @@
             both = sides("gx", row_even[line, :], row_odd[line, :])
             values.append(across[layer, part, :] + both[first_row > REACH])
         depth_sums(part, values)
+
+
+def column_kernel(deep, band_ref, _, smooth):
     constant = right_constant(band_ref[...])
-    for layer in range(layers):
+    for layer in range(deep.shape[0]):
         smooth[layer] = right_product(deep[layer], constant)
 
 
@@ -449,28 +452,29 @@
     whole.wait()
 
 
-def call(kernel, outs, scratch, cost, operands, spaces=None, outs_space=pltpu.VMEM):
+def call(kernel, outs, scratch, nanoseconds, operands, spaces=None, outs_space=pltpu.VMEM):
     spaces = spaces or [pltpu.VMEM] * len(operands)
+    shapes = [out if isinstance(out, jax.ShapeDtypeStruct) else jax.ShapeDtypeStruct(out, jnp.float32)
+              for out in outs]
     return pl.pallas_call(
         kernel,
-        out_shape=[jax.ShapeDtypeStruct(shape, jnp.float32) for shape in outs],
+        out_shape=shapes,
         in_specs=[pl.BlockSpec(memory_space=space) for space in spaces],
         out_specs=[pl.BlockSpec(memory_space=outs_space)] * len(outs),
         scratch_shapes=[pltpu.VMEM(s, jnp.float32) if isinstance(s, tuple) else s for s in scratch],
         compiler_params=pltpu.CompilerParams(vmem_limit_bytes=VMEM_BYTES),
-        cost_estimate=pl.CostEstimate(flops=cost, bytes_accessed=cost // 16, transcendentals=0),
+        cost_estimate=pl.CostEstimate(
+            flops=nanoseconds * 1_000_000, bytes_accessed=nanoseconds * 1000, transcendentals=0
+        ),
     )(*operands)
 
 
-def exchange(axis, even, odd):
+def exchange(axis, start, value):
     count = lax.axis_size(axis)
-    results = []
-    for start, value in ((1, odd), (0, even)):
-        pairs = []
-        for low in range(start, count - 1, 2):
-            pairs += [(low, low + 1), (low + 1, low)]
-        results.append(lax.ppermute(value, axis, pairs))
-    return results[::-1]
+    pairs = []
+    for low in range(start, count - 1, 2):
+        pairs += [(low, low + 1), (low + 1, low)]
+    return lax.ppermute(value, axis, pairs)
 
 
 def inverse_weights(axis, places, length):
@@ -506,7 +510,7 @@
             low[own, cols + layer] = [weight * tap(j + 1) for j in range(REACH)]
             high[other, cols + layer] = [weight * tap(REACH - 1 - j) for j in range(REACH)]
             ahead[((source - 2) % slots) * REACH + REACH - 1, layer] = weight * tap(REACH)
-    constants = (below, above, np.kron(same, down), rows_band, band(cols, cols), low, high, ahead)
+    constants = (below, above, rows_band, band(cols, cols), low, high, ahead)
     return depth, [jnp.asarray(matrix, jnp.float32) for matrix in constants]
 
 
@@ -515,54 +519,58 @@
     assert layers * REACH == cols == rows and layers % 2 == 0
     total, strip = rows + REACH, layers * REACH
     depth, constants = matrices(layers, rows, cols)
-    below, above, above_first, rows_band, cols_band, *columns = constants
-
-    inputs = (trial_stress, old_strain, yield_mask, newton_count)
+    below, above, rows_band, cols_band, *columns = constants
+
     whole, wide = (layers, rows, cols), (layers, total, cols)
     sent_rows = (strip + 3 * layers, cols)
     sent_cols = (total + rows // 4 + REACH, cols)
     packed, packed_two = (total, cols), (total, 2 * cols)
-    work = layers * rows * cols
-
+
+    inputs = (trial_stress, old_strain, yield_mask, newton_count, damage_threshold)
+    stress, strain, _, _, threshold = inputs
+    edges = [jnp.concatenate([value[:, :REACH], value[:, rows - REACH :]], axis=1) for value in inputs[:4]]
+    row_even, row_odd, norm, norm_last, norm_before, smooth, col_even, col_odd = call(
+        first_edge_kernel,
+        [sent_rows, sent_rows, packed, packed, packed, wide, sent_cols, sent_cols],
+        [(strip, cols)], 6000, edges,
+    )
     for outer_no in range(OUTER):
-        if outer_no == 0:
-            edge = [pltpu.VMEM((2, layers, REACH, cols), kind) for kind in
-                    (jnp.float32, jnp.float32, jnp.int32, jnp.int32)]
-            row_even, row_odd, norm, norm_last, norm_before, smooth, col_even, col_odd = call(
-                first_edge_kernel,
-                [sent_rows, sent_rows, packed, packed, packed, wide, sent_cols, sent_cols],
-                edge + [(strip, cols), pltpu.SemaphoreType.DMA((2, 4))], work * 16,
-                (*inputs, below, above_first), [pltpu.HBM] * 4 + [pltpu.VMEM] * 2,
-            )
-        else:
+        if outer_no:
             row_even, row_odd = call(
                 edge_kernel, [sent_rows] * 2,
-                [(strip, cols), (2 * strip, cols), (2 * layers, cols)], work * 16,
-                (*inputs, damage_threshold, smooth, col_even, col_odd, norm, below, above),
+                [(strip, cols), (2 * strip, cols), (2 * layers, cols)], 800,
+                (*inputs, smooth, col_even, col_odd, norm, below, above),
             )
-        row_even, row_odd = exchange("gx", row_even, row_odd)
         turn = jnp.full((1,), outer_no, jnp.int32)
-        across, low_cols, high_cols, plastic = call(
-            main_kernel, [wide, packed_two, packed_two, whole],
-            [whole, packed, packed, packed, packed], work * 400,
-            (turn, *inputs, damage_threshold, smooth, col_even, col_odd, norm, norm_last,
-             rows_band, *columns),
-            [pltpu.SMEM] + [pltpu.VMEM] * 14,
+        row_even = exchange("gx", 0, row_even)
+        plastic, row_odd = call(
+            newton_kernel, [whole, sent_rows], [], 3000,
+            (turn, *inputs, smooth, col_even, col_odd, norm, row_odd),
+            [pltpu.SMEM] + [pltpu.VMEM] * 10,
+        )
+        row_odd = exchange("gx", 1, row_odd)
+        across, low_cols, high_cols = call(
+            across_kernel, [wide, packed_two, packed_two],
+            [packed, packed, packed, packed], 2000,
+            (turn, stress, strain, threshold, plastic, norm_last, rows_band, *columns, row_even),
+            [pltpu.SMEM] + [pltpu.VMEM] * 10,
         )
         col_even, col_odd, own_cols = call(
-            corner_kernel, [sent_cols, sent_cols, packed], [], work * 16,
+            corner_kernel, [sent_cols, sent_cols, packed], [], 400,
             (row_even, row_odd, low_cols, high_cols, norm_last, *columns),
         )
-        col_even, col_odd = exchange("gy", col_even, col_odd)
-        (smooth,) = call(
-            functools.partial(column_kernel, depth), [wide], [wide], work * 100,
-            (across, row_even, row_odd, cols_band),
+        col_even = exchange("gy", 0, col_even)
+        deep, col_odd = call(
+            functools.partial(depth_kernel, depth), [wide, sent_cols], [], 700,
+            (across, row_even, row_odd, col_odd, own_cols),
         )
+        col_odd = exchange("gy", 1, col_odd)
+        (smooth,) = call(column_kernel, [wide], [], 500, (deep, cols_band, col_even))
     return tuple(call(
         final_kernel, [whole, whole, (2, *whole)],
         [packed, whole, (2, *whole), pltpu.SemaphoreType.DMA(()), pltpu.SemaphoreType.DMA((3, layers))],
-        work * 100,
-        (trial_stress, old_strain, plastic, damage_threshold, smooth, col_even, col_odd,
+        3000,
+        (stress, strain, plastic, threshold, smooth, col_even, col_odd,
          row_even, row_odd, norm, norm_before, own_cols),
         outs_space=pltpu.HBM,
     ))

time: 67.7 us -> 65.8 us (0.972)
  the two profiles are of different devices: /device:TPU:3 before, /device:TPU:19 now
where the time goes in v4:
time: 65.8 us; the launch traced here: 65.4 us
  starting transfers between devices  23.9 us (36%)
  Pallas kernels  22.6 us (34%)
  waiting for transfers between devices  13 us (20%)
  local copies, waits for them, and re-layouts  4.94 us (8%)
  between operations  0.97 us (1%)
    ppermute x12, starting transfers between devices, exchange(): return lax.ppermute(value, axis, pairs)  23.9 us
    pallas_call x19, Pallas kernels, call(): pl.pallas_call(kernel, out_shape=shapes, in_specs=[pl.BlockSpec(memory_sp...  22.6 us
    ppermute x12, waiting for transfers between devices, exchange(): return lax.ppermute(value, axis, pairs)  13 us
    slice x4, local copies, waits for them, and re-layouts, local(): value[:, :REACH]  3.54 us
    unnamed x24, local copies, waits for them, and re-layouts  1.4 us
  transfers between devices with their start and end apart: 12, of which 6 were waited for; matrix products, arithmetic and copies ran while one was open for 0% of the time, Pallas kernels for 24%

profile of v4, /device:TPU:19, one launch (start us, length us, event | category | flops | bytes accessed | tf_op | source)
XLA Modules:
  0.0 65.4 jit_solution(6445851145486429014)
XLA Ops:
  0.6 0.9 %fusion.1 = (s32[16,8,128]{2,1,0:T(8,128)S(1)}, s32[16,8,128]{2,1,0:T(8,128)S(1)}) fusion(s32[16,128,128]{2,1,0:T(8,128)} %yields.9), kind=kLoop, calls=%fused_computation.5 | loop fusion | bytes 262144 | tf_op jit(solution)/shard_map/slice | solution.py:531
  1.5 0.9 %fusion = (s32[16,8,128]{2,1,0:T(8,128)S(1)}, s32[16,8,128]{2,1,0:T(8,128)S(1)}) fusion(s32[16,128,128]{2,1,0:T(8,128)} %count.9), kind=kLoop, calls=%fused_computation.4 | loop fusion | bytes 262144 | tf_op jit(solution)/shard_map/slice | solution.py:531
  2.4 0.9 %fusion.3 = (f32[16,8,128]{2,1,0:T(8,128)S(1)}, f32[16,8,128]{2,1,0:T(8,128)S(1)}) fusion(f32[16,128,128]{2,1,0:T(8,128)} %stress.17), kind=kLoop, calls=%fused_computation.7 | loop fusion | bytes 262144 | tf_op jit(solution)/shard_map/slice | solution.py:531
  3.3 0.9 %fusion.2 = (f32[16,8,128]{2,1,0:T(8,128)S(1)}, f32[16,8,128]{2,1,0:T(8,128)S(1)}) fusion(f32[16,128,128]{2,1,0:T(8,128)} %strain.17), kind=kLoop, calls=%fused_computation.6 | loop fusion | bytes 262144 | tf_op jit(solution)/shard_map/slice | solution.py:531
  4.2 0.0 copy-start
  4.2 0.0 copy-start.1
  4.3 0.0 copy-start.2
  4.3 0.0 copy-start.3
  4.3 0.0 copy-start.4
  4.3 0.8 %shard_map.139 = (f32[176,128]{1,0:T(8,128)S(1)}, f32[176,128]{1,0:T(8,128)S(1)}, f32[136,128]{1,0:T(8,128)S(1)}, f32[136,128]{1,0:T(8,128)S(1)}, f32[136,128]{1...) custom-call(f32[16,16,128]{2,1,0:T(8,128)S(1)} %get-tuple-element.95.stress, ...), custom_call_target="tpu_custom_call" | custom-call | flops 6000000000 | bytes 6000000 | tf_op jit(solution)/shard_map/pallas_call | solution.py:459
  5.1 0.3 collective-permute-start
  5.4 0.1 copy-done
  5.5 0.3 copy-done.1
  5.8 0.3 copy-done.2
  6.1 0.3 copy-done.3
  6.4 0.3 copy-done.4
  6.8 2.2 %shard_map.140 = (f32[16,128,128]{2,1,0:T(8,128)S(1)}, f32[176,128]{1,0:T(8,128)S(1)}) custom-call(s32[1]{0:T(128)} %constant.9.clone.1.turn, f32[16,128,128]{2,1,0:T(8,128)S(1)} %copy-done.2, f32[16,128,128]{2,1,0:T(8,128)S(1)} %copy-done.3, s32[16,128,128]{2,1,0:T(8,128)S(1)} %copy-done, s32[16,128,128]{2,1,0:T(8,128)S(1)} %copy-done.1, ...), custom_call_target="tpu_custom_call" | custom-call | flops 3000000000 | bytes 3000000 | tf_op jit(solution)/shard_map/pallas_call | solution.py:459
  8.9 3.2 %collective-permute-start.1 = (f32[176,128]{1,0:T(8,128)S(1)}, f32[176,128]{1,0:T(8,128)S(1)}, u32[]{:S(2)}, u32[]{:S(2)}) collective-permute-start(f32[176,128]{1,0:T(8,128)S(1)} %get-tuple-element.54), channel_id=1, source_target_pairs={{4,8},{8,4},{12,16},{16,12},{20,24},{24,20},{5,9},{9,5},{13,17},{1... | collective-permute-start | bytes 270344 | tf_op jit(solution)/shard_map/ppermute | solution.py:477
  12.1 0.0 collective-permute-done._.row_even
  12.1 0.0 copy-done.8
  12.1 0.0 copy-done.9
  12.2 0.0 copy-done.10
  12.2 0.0 copy-done.11
  12.2 0.8 %shard_map.141 = (f32[16,136,128]{2,1,0:T(8,128)S(1)}, f32[136,256]{1,0:T(8,128)S(1)}, f32[136,256]{1,0:T(8,128)S(1)}) custom-call(s32[1]{0:T(128)} %constant.9.clone.1.turn, f32[16,128,128]{2,1,0:T(8,128)S(1)} %copy-done.2, f32[16,128,128]{2,1,0:T(8,128)S(1)} %copy-done.3, f32[16,128,128]{2,1,0:T(8,128)S(1)} %copy-done.4, ...), custom_call_target="tpu_custom_call" | custom-call | flops 2000000000 | bytes 2000000 | tf_op jit(solution)/shard_map/pallas_call | solution.py:459
  13.0 2.1 %collective-permute-done.1.row_odd = f32[176,128]{1,0:T(8,128)S(1)} collective-permute-done((f32[176,128]{1,0:T(8,128)S(1)}, f32[176,128]{1,0:T(8,128)S(1)}, u32[]{:S(2)}, u32[]{:S(2)}) %collective-permute-start.1) | collective-permute-done | bytes 90144 | tf_op jit(solution)/shard_map/ppermute | solution.py:477
  15.1 0.4 shard_map.142
  15.5 1.8 %collective-permute-start.2 = (f32[176,128]{1,0:T(8,128)S(1)}, f32[176,128]{1,0:T(8,128)S(1)}, u32[]{:S(2)}, u32[]{:S(2)}) collective-permute-start(f32[176,128]{1,0:T(8,128)S(1)} %get-tuple-element.60), channel_id=1, source_target_pairs={{0,1},{1,0},{2,3},{3,2},{4,5},{5,4},{6,7},{7,6},{8,9},{9,8},{10,11... | collective-permute-start | bytes 270344 | tf_op jit(solution)/shard_map/ppermute | solution.py:477
  17.3 0.7 %shard_map.143 = (f32[16,136,128]{2,1,0:T(8,128)S(1)}, f32[176,128]{1,0:T(8,128)S(1)}) custom-call(f32[16,136,128]{2,1,0:T(8,128)S(1)} %get-tuple-element.53.across, f32[176,128]{1,0:T(8,128)S(1)} %collective-permute-done._.row_even, f32[176,128]{1,0:T(8,128)S(1)} %collective-permute-done.1.row_odd, f32[176,128]{1,0:T(8,128)S(1)} %get-tuple-element.57.waiting, ...), custom_call_target="tpu_custom_call" | custom-call | flops 700000000 | bytes 700000 | tf_op jit(solution)/shard_map/pallas_call | solution.py:459
  18.0 3.1 %collective-permute-start.3 = (f32[176,128]{1,0:T(8,128)S(1)}, f32[176,128]{1,0:T(8,128)S(1)}, u32[]{:S(2)}, u32[]{:S(2)}) collective-permute-start(f32[176,128]{1,0:T(8,128)S(1)} %get-tuple-element.61), channel_id=1, source_target_pairs={{1,2},{2,1},{5,6},{6,5},{9,10},{10,9},{13,14},{14,13},{17,18},{18,... | collective-permute-start | bytes 270344 | tf_op jit(solution)/shard_map/ppermute | solution.py:477
  21.1 0.0 collective-permute-done.2._.col_even
  21.1 0.0 copy-done.6
  21.1 0.0 copy-start.5
  21.1 0.0 copy-start.7
  21.1 0.5 shard_map.144.smooth
  21.6 2.5 %collective-permute-done.3.col_odd = f32[176,128]{1,0:T(8,128)S(1)} collective-permute-done((f32[176,128]{1,0:T(8,128)S(1)}, f32[176,128]{1,0:T(8,128)S(1)}, u32[]{:S(2)}, u32[]{:S(2)}) %collective-permute-start.3) | collective-permute-done | bytes 90144 | tf_op jit(solution)/shard_map/ppermute | solution.py:477
  24.2 0.8 %shard_map.145 = (f32[176,128]{1,0:T(8,128)S(1)}, f32[176,128]{1,0:T(8,128)S(1)}) custom-call(f32[16,128,128]{2,1,0:T(8,128)S(1)} %copy-done.2, f32[16,128,128]{2,1,0:T(8,128)S(1)} %copy-done.3, s32[16,128,128]{2,1,0:T(8,128)S(1)} %copy-done, s32[16,128,128]{2,1,0:T(8,128)S(1)} %copy-done.1, f32[16,128,128]{2,1,0:T(8,128)S(1)} %copy-done.4, ...), custom_call_target="tpu_custom_call" | custom-call | flops 800000000 | bytes 800000 | tf_op jit(solution)/shard_map/pallas_call | solution.py:459
  25.0 0.3 collective-permute-start.4
  25.3 3.2 %shard_map.146 = (f32[16,128,128]{2,1,0:T(8,128)S(1)}, f32[176,128]{1,0:T(8,128)S(1)}) custom-call(s32[1]{0:T(128)} %constant.8.clone.1.turn, f32[16,128,128]{2,1,0:T(8,128)S(1)} %copy-done.2, f32[16,128,128]{2,1,0:T(8,128)S(1)} %copy-done.3, s32[16,128,128]{2,1,0:T(8,128)S(1)} %copy-done, s32[16,128,128]{2,1,0:T(8,128)S(1)} %copy-done.1, ...), custom_call_target="tpu_custom_call" | custom-call | flops 3000000000 | bytes 3000000 | tf_op jit(solution)/shard_map/pallas_call | solution.py:459
  28.5 2.9 %collective-permute-start.5 = (f32[176,128]{1,0:T(8,128)S(1)}, f32[176,128]{1,0:T(8,128)S(1)}, u32[]{:S(2)}, u32[]{:S(2)}) collective-permute-start(f32[176,128]{1,0:T(8,128)S(1)} %get-tuple-element.66), channel_id=1, source_target_pairs={{4,8},{8,4},{12,16},{16,12},{20,24},{24,20},{5,9},{9,5},{13,17},{1... | collective-permute-start | bytes 270344 | tf_op jit(solution)/shard_map/ppermute | solution.py:477
  31.5 0.0 collective-permute-done.4._.row_even
  31.5 0.8 %shard_map.147 = (f32[16,136,128]{2,1,0:T(8,128)S(1)}, f32[136,256]{1,0:T(8,128)S(1)}, f32[136,256]{1,0:T(8,128)S(1)}) custom-call(s32[1]{0:T(128)} %constant.8.clone.1.turn, f32[16,128,128]{2,1,0:T(8,128)S(1)} %copy-done.2, f32[16,128,128]{2,1,0:T(8,128)S(1)} %copy-done.3, f32[16,128,128]{2,1,0:T(8,128)S(1)} %copy-done.4, ...), custom_call_target="tpu_custom_call" | custom-call | flops 2000000000 | bytes 2000000 | tf_op jit(solution)/shard_map/pallas_call | solution.py:459
  32.3 2.4 %collective-permute-done.5.row_odd = f32[176,128]{1,0:T(8,128)S(1)} collective-permute-done((f32[176,128]{1,0:T(8,128)S(1)}, f32[176,128]{1,0:T(8,128)S(1)}, u32[]{:S(2)}, u32[]{:S(2)}) %collective-permute-start.5) | collective-permute-done | bytes 90144 | tf_op jit(solution)/shard_map/ppermute | solution.py:477
  34.7 0.4 shard_map.148
  35.1 0.0 collective-permute-start.6
  35.1 0.7 %shard_map.149 = (f32[16,136,128]{2,1,0:T(8,128)S(1)}, f32[176,128]{1,0:T(8,128)S(1)}) custom-call(f32[16,136,128]{2,1,0:T(8,128)S(1)} %get-tuple-element.65.across, f32[176,128]{1,0:T(8,128)S(1)} %collective-permute-done.4._.row_even, f32[176,128]{1,0:T(8,128)S(1)} %collective-permute-done.5.row_odd, f32[176,128]{1,0:T(8,128)S(1)} %get-tuple-element.69.waiting, ...), custom_call_target="tpu_custom_call" | custom-call | flops 700000000 | bytes 700000 | tf_op jit(solution)/shard_map/pallas_call | solution.py:459
  35.8 4.2 %collective-permute-start.7 = (f32[176,128]{1,0:T(8,128)S(1)}, f32[176,128]{1,0:T(8,128)S(1)}, u32[]{:S(2)}, u32[]{:S(2)}) collective-permute-start(f32[176,128]{1,0:T(8,128)S(1)} %get-tuple-element.73), channel_id=1, source_target_pairs={{1,2},{2,1},{5,6},{6,5},{9,10},{10,9},{13,14},{14,13},{17,18},{18,... | collective-permute-start | bytes 270344 | tf_op jit(solution)/shard_map/ppermute | solution.py:477
  40.0 0.0 collective-permute-done.6._.col_even
  40.0 0.5 shard_map.150.smooth
  40.5 2.0 %collective-permute-done.7.col_odd = f32[176,128]{1,0:T(8,128)S(1)} collective-permute-done((f32[176,128]{1,0:T(8,128)S(1)}, f32[176,128]{1,0:T(8,128)S(1)}, u32[]{:S(2)}, u32[]{:S(2)}) %collective-permute-start.7) | collective-permute-done | bytes 90144 | tf_op jit(solution)/shard_map/ppermute | solution.py:477
  42.5 0.8 %shard_map.151 = (f32[176,128]{1,0:T(8,128)S(1)}, f32[176,128]{1,0:T(8,128)S(1)}) custom-call(f32[16,128,128]{2,1,0:T(8,128)S(1)} %copy-done.2, f32[16,128,128]{2,1,0:T(8,128)S(1)} %copy-done.3, s32[16,128,128]{2,1,0:T(8,128)S(1)} %copy-done, s32[16,128,128]{2,1,0:T(8,128)S(1)} %copy-done.1, f32[16,128,128]{2,1,0:T(8,128)S(1)} %copy-done.4, ...), custom_call_target="tpu_custom_call" | custom-call | flops 800000000 | bytes 800000 | tf_op jit(solution)/shard_map/pallas_call | solution.py:459
  43.3 1.3 %collective-permute-start.8 = (f32[176,128]{1,0:T(8,128)S(1)}, f32[176,128]{1,0:T(8,128)S(1)}, u32[]{:S(2)}, u32[]{:S(2)}) collective-permute-start(f32[176,128]{1,0:T(8,128)S(1)} %get-tuple-element.76), channel_id=1, source_target_pairs={{0,4},{4,0},{8,12},{12,8},{16,20},{20,16},{24,28},{28,24},{1,5},{5... | collective-permute-start | bytes 270344 | tf_op jit(solution)/shard_map/ppermute | solution.py:477
  44.6 3.2 %shard_map.152 = (f32[16,128,128]{2,1,0:T(8,128)S(1)}, f32[176,128]{1,0:T(8,128)S(1)}) custom-call(s32[1]{0:T(128)} %constant.7.clone.1.turn, f32[16,128,128]{2,1,0:T(8,128)S(1)} %copy-done.2, f32[16,128,128]{2,1,0:T(8,128)S(1)} %copy-done.3, s32[16,128,128]{2,1,0:T(8,128)S(1)} %copy-done, s32[16,128,128]{2,1,0:T(8,128)S(1)} %copy-done.1, ...), custom_call_target="tpu_custom_call" | custom-call | flops 3000000000 | bytes 3000000 | tf_op jit(solution)/shard_map/pallas_call | solution.py:459
  47.8 1.9 %collective-permute-start.9 = (f32[176,128]{1,0:T(8,128)S(1)}, f32[176,128]{1,0:T(8,128)S(1)}, u32[]{:S(2)}, u32[]{:S(2)}) collective-permute-start(f32[176,128]{1,0:T(8,128)S(1)} %get-tuple-element.78), channel_id=1, source_target_pairs={{4,8},{8,4},{12,16},{16,12},{20,24},{24,20},{5,9},{9,5},{13,17},{1... | collective-permute-start | bytes 270344 | tf_op jit(solution)/shard_map/ppermute | solution.py:477
  49.7 0.0 collective-permute-done.8._.row_even
  49.7 1.9 %shard_map.153 = (f32[16,136,128]{2,1,0:T(8,128)S(1)}, f32[136,256]{1,0:T(8,128)S(1)}, f32[136,256]{1,0:T(8,128)S(1)}) custom-call(s32[1]{0:T(128)} %constant.7.clone.1.turn, f32[16,128,128]{2,1,0:T(8,128)S(1)} %copy-done.2, f32[16,128,128]{2,1,0:T(8,128)S(1)} %copy-done.3, f32[16,128,128]{2,1,0:T(8,128)S(1)} %copy-done.4, ...), custom_call_target="tpu_custom_call" | custom-call | flops 2000000000 | bytes 2000000 | tf_op jit(solution)/shard_map/pallas_call | solution.py:459
  51.7 2.3 %collective-permute-done.9.row_odd = f32[176,128]{1,0:T(8,128)S(1)} collective-permute-done((f32[176,128]{1,0:T(8,128)S(1)}, f32[176,128]{1,0:T(8,128)S(1)}, u32[]{:S(2)}, u32[]{:S(2)}) %collective-permute-start.9) | collective-permute-done | bytes 90144 | tf_op jit(solution)/shard_map/ppermute | solution.py:477
  54.0 0.4 shard_map.154
  54.4 0.0 collective-permute-start.10
  54.4 0.7 %shard_map.155 = (f32[16,136,128]{2,1,0:T(8,128)S(1)}, f32[176,128]{1,0:T(8,128)S(1)}) custom-call(f32[16,136,128]{2,1,0:T(8,128)S(1)} %get-tuple-element.77.across, f32[176,128]{1,0:T(8,128)S(1)} %collective-permute-done.8._.row_even, f32[176,128]{1,0:T(8,128)S(1)} %collective-permute-done.9.row_odd, f32[176,128]{1,0:T(8,128)S(1)} %get-tuple-element.81.waiting, ...), custom_call_target="tpu_custom_call" | custom-call | flops 700000000 | bytes 700000 | tf_op jit(solution)/shard_map/pallas_call | solution.py:459
  55.1 4.8 %collective-permute-start.11 = (f32[176,128]{1,0:T(8,128)S(1)}, f32[176,128]{1,0:T(8,128)S(1)}, u32[]{:S(2)}, u32[]{:S(2)}) collective-permute-start(f32[176,128]{1,0:T(8,128)S(1)} %get-tuple-element.85), channel_id=1, source_target_pairs={{1,2},{2,1},{5,6},{6,5},{9,10},{10,9},{13,14},{14,13},{17,18},{18,... | collective-permute-start | bytes 270344 | tf_op jit(solution)/shard_map/ppermute | solution.py:477
  59.9 0.0 collective-permute-done.10._.col_even
  59.9 0.5 shard_map.156.smooth
  60.4 1.7 %collective-permute-done.11.col_odd = f32[176,128]{1,0:T(8,128)S(1)} collective-permute-done((f32[176,128]{1,0:T(8,128)S(1)}, f32[176,128]{1,0:T(8,128)S(1)}, u32[]{:S(2)}, u32[]{:S(2)}) %collective-permute-start.11) | collective-permute-done | bytes 90144 | tf_op jit(solution)/shard_map/ppermute | solution.py:477
  62.1 3.3 %shard_map.157 = (f32[16,128,128]{2,1,0:T(8,128)}, f32[16,128,128]{2,1,0:T(8,128)}, f32[2,16,128,128]{3,2,1,0:T(8,128)}) custom-call(f32[16,128,128]{2,1,0:T(8,128)S(1)} %copy-done.2, f32[16,128,128]{2,1,0:T(8,128)S(1)} %copy-done.3, f32[16,128,128]{2,1,0:T(8,128)S(1)} %get-tuple-element.75.plastic, f32[16,128,128]{2,1,0:T(8,128)S(1)} %copy-done.4, ...), custom_call_target="tpu_custom_call" | custom-call | flops 3000000000 | bytes 3000000 | tf_op jit(solution)/shard_map/pallas_call | solution.py:459
  (9 shorter events, 0.1 us)
Async XLA Ops:
  4.2 1.2 %copy-start = (s32[16,128,128]{2,1,0:T(8,128)S(1)}, s32[16,128,128]{2,1,0:T(8,128)}, u32[]{:S(2)}) copy-start(s32[16,128,128]{2,1,0:T(8,128)} %yields.9) | copy-start | bytes 3145732
  4.2 1.5 %copy-start.1 = (s32[16,128,128]{2,1,0:T(8,128)S(1)}, s32[16,128,128]{2,1,0:T(8,128)}, u32[]{:S(2)}) copy-start(s32[16,128,128]{2,1,0:T(8,128)} %count.9) | copy-start | bytes 3145732
  4.3 1.8 %copy-start.2 = (f32[16,128,128]{2,1,0:T(8,128)S(1)}, f32[16,128,128]{2,1,0:T(8,128)}, u32[]{:S(2)}) copy-start(f32[16,128,128]{2,1,0:T(8,128)} %stress.17) | copy-start | bytes 3145732
  4.3 2.1 %copy-start.3 = (f32[16,128,128]{2,1,0:T(8,128)S(1)}, f32[16,128,128]{2,1,0:T(8,128)}, u32[]{:S(2)}) copy-start(f32[16,128,128]{2,1,0:T(8,128)} %strain.17) | copy-start | bytes 3145732
  4.3 2.5 %copy-start.4 = (f32[16,128,128]{2,1,0:T(8,128)S(1)}, f32[16,128,128]{2,1,0:T(8,128)}, u32[]{:S(2)}) copy-start(f32[16,128,128]{2,1,0:T(8,128)} %threshold.17) | copy-start | bytes 3145732
  5.1 7.1 %collective-permute-start = (f32[176,128]{1,0:T(8,128)S(1)}, f32[176,128]{1,0:T(8,128)S(1)}, u32[]{:S(2)}, u32[]{:S(2)}) collective-permute-start(f32[176,128]{1,0:T(8,128)S(1)} %get-tuple-element.52), channel_id=1, source_target_pairs={{0,4},{4,0},{8,12},{12,8},{16,20},{20,16},{24,28},{28,24},{1,5},{5... | collective-permute-start | bytes 270344 | tf_op jit(solution)/shard_map/ppermute | solution.py:477
  6.7 5.4 %copy-start.8 = (f32[128,256]{1,0:T(8,128)S(1)}, f32[128,256]{1,0:T(8,128)}, u32[]{:S(2)}) copy-start(f32[128,256]{1,0:T(8,128)} %constant.25.clone.high_ref) | copy-start | bytes 393220
  6.7 5.4 %copy-start.9 = (f32[128,256]{1,0:T(8,128)S(1)}, f32[128,256]{1,0:T(8,128)}, u32[]{:S(2)}) copy-start(f32[128,256]{1,0:T(8,128)} %constant.24.clone.low_ref) | copy-start | bytes 393220
  6.7 5.4 %copy-start.10 = (f32[136,128]{1,0:T(8,128)S(1)}, f32[136,128]{1,0:T(8,128)}, u32[]{:S(2)}) copy-start(f32[136,128]{1,0:T(8,128)} %constant.22.clone.band_ref) | copy-start | bytes 208900
  6.7 5.4 %copy-start.11 = (f32[128,128]{1,0:T(8,128)S(1)}, f32[128,128]{1,0:T(8,128)}, u32[]{:S(2)}) copy-start(f32[128,128]{1,0:T(8,128)} %constant.26.clone.next_ref) | copy-start | bytes 196612
  8.9 6.2 %collective-permute-start.1 = (f32[176,128]{1,0:T(8,128)S(1)}, f32[176,128]{1,0:T(8,128)S(1)}, u32[]{:S(2)}, u32[]{:S(2)}) collective-permute-start(f32[176,128]{1,0:T(8,128)S(1)} %get-tuple-element.54), channel_id=1, source_target_pairs={{4,8},{8,4},{12,16},{16,12},{20,24},{24,20},{5,9},{9,5},{13,17},{1... | collective-permute-start | bytes 270344 | tf_op jit(solution)/shard_map/ppermute | solution.py:477
  15.5 5.6 %collective-permute-start.2 = (f32[176,128]{1,0:T(8,128)S(1)}, f32[176,128]{1,0:T(8,128)S(1)}, u32[]{:S(2)}, u32[]{:S(2)}) collective-permute-start(f32[176,128]{1,0:T(8,128)S(1)} %get-tuple-element.60), channel_id=1, source_target_pairs={{0,1},{1,0},{2,3},{3,2},{4,5},{5,4},{6,7},{7,6},{8,9},{9,8},{10,11... | collective-permute-start | bytes 270344 | tf_op jit(solution)/shard_map/ppermute | solution.py:477
  17.3 3.8 %copy-start.6 = (f32[128,128]{1,0:T(8,128)S(1)}, f32[128,128]{1,0:T(8,128)}, u32[]{:S(2)}) copy-start(f32[128,128]{1,0:T(8,128)} %constant.23.clone.band_ref) | copy-start | bytes 196612
  18.0 6.1 %collective-permute-start.3 = (f32[176,128]{1,0:T(8,128)S(1)}, f32[176,128]{1,0:T(8,128)S(1)}, u32[]{:S(2)}, u32[]{:S(2)}) collective-permute-start(f32[176,128]{1,0:T(8,128)S(1)} %get-tuple-element.61), channel_id=1, source_target_pairs={{1,2},{2,1},{5,6},{6,5},{9,10},{10,9},{13,14},{14,13},{17,18},{18,... | collective-permute-start | bytes 270344 | tf_op jit(solution)/shard_map/ppermute | solution.py:477
  21.1 3.1 %copy-start.5 = (f32[144,256]{1,0:T(8,128)S(1)}, f32[144,256]{1,0:T(8,128)}, u32[]{:S(2)}) copy-start(f32[144,256]{1,0:T(8,128)} %constant.21.clone.above) | copy-start | bytes 442372
  21.1 3.0 %copy-start.7 = (f32[128,128]{1,0:T(8,128)S(1)}, f32[128,128]{1,0:T(8,128)}, u32[]{:S(2)}) copy-start(f32[128,128]{1,0:T(8,128)} %constant.20.clone.below) | copy-start | bytes 196612
  25.0 6.5 %collective-permute-start.4 = (f32[176,128]{1,0:T(8,128)S(1)}, f32[176,128]{1,0:T(8,128)S(1)}, u32[]{:S(2)}, u32[]{:S(2)}) collective-permute-start(f32[176,128]{1,0:T(8,128)S(1)} %get-tuple-element.64), channel_id=1, source_target_pairs={{0,4},{4,0},{8,12},{12,8},{16,20},{20,16},{24,28},{28,24},{1,5},{5... | collective-permute-start | bytes 270344 | tf_op jit(solution)/shard_map/ppermute | solution.py:477
  28.5 6.2 %collective-permute-start.5 = (f32[176,128]{1,0:T(8,128)S(1)}, f32[176,128]{1,0:T(8,128)S(1)}, u32[]{:S(2)}, u32[]{:S(2)}) collective-permute-start(f32[176,128]{1,0:T(8,128)S(1)} %get-tuple-element.66), channel_id=1, source_target_pairs={{4,8},{8,4},{12,16},{16,12},{20,24},{24,20},{5,9},{9,5},{13,17},{1... | collective-permute-start | bytes 270344 | tf_op jit(solution)/shard_map/ppermute | solution.py:477
  35.1 5.0 %collective-permute-start.6 = (f32[176,128]{1,0:T(8,128)S(1)}, f32[176,128]{1,0:T(8,128)S(1)}, u32[]{:S(2)}, u32[]{:S(2)}) collective-permute-start(f32[176,128]{1,0:T(8,128)S(1)} %get-tuple-element.72), channel_id=1, source_target_pairs={{0,1},{1,0},{2,3},{3,2},{4,5},{5,4},{6,7},{7,6},{8,9},{9,8},{10,11... | collective-permute-start | bytes 270344 | tf_op jit(solution)/shard_map/ppermute | solution.py:477
  35.8 6.7 %collective-permute-start.7 = (f32[176,128]{1,0:T(8,128)S(1)}, f32[176,128]{1,0:T(8,128)S(1)}, u32[]{:S(2)}, u32[]{:S(2)}) collective-permute-start(f32[176,128]{1,0:T(8,128)S(1)} %get-tuple-element.73), channel_id=1, source_target_pairs={{1,2},{2,1},{5,6},{6,5},{9,10},{10,9},{13,14},{14,13},{17,18},{18,... | collective-permute-start | bytes 270344 | tf_op jit(solution)/shard_map/ppermute | solution.py:477
  43.3 6.4 %collective-permute-start.8 = (f32[176,128]{1,0:T(8,128)S(1)}, f32[176,128]{1,0:T(8,128)S(1)}, u32[]{:S(2)}, u32[]{:S(2)}) collective-permute-start(f32[176,128]{1,0:T(8,128)S(1)} %get-tuple-element.76), channel_id=1, source_target_pairs={{0,4},{4,0},{8,12},{12,8},{16,20},{20,16},{24,28},{28,24},{1,5},{5... | collective-permute-start | bytes 270344 | tf_op jit(solution)/shard_map/ppermute | solution.py:477
  47.8 6.2 %collective-permute-start.9 = (f32[176,128]{1,0:T(8,128)S(1)}, f32[176,128]{1,0:T(8,128)S(1)}, u32[]{:S(2)}, u32[]{:S(2)}) collective-permute-start(f32[176,128]{1,0:T(8,128)S(1)} %get-tuple-element.78), channel_id=1, source_target_pairs={{4,8},{8,4},{12,16},{16,12},{20,24},{24,20},{5,9},{9,5},{13,17},{1... | collective-permute-start | bytes 270344 | tf_op jit(solution)/shard_map/ppermute | solution.py:477
  54.4 5.5 %collective-permute-start.10 = (f32[176,128]{1,0:T(8,128)S(1)}, f32[176,128]{1,0:T(8,128)S(1)}, u32[]{:S(2)}, u32[]{:S(2)}) collective-permute-start(f32[176,128]{1,0:T(8,128)S(1)} %get-tuple-element.84), channel_id=1, source_target_pairs={{0,1},{1,0},{2,3},{3,2},{4,5},{5,4},{6,7},{7,6},{8,9},{9,8},{10,11... | collective-permute-start | bytes 270344 | tf_op jit(solution)/shard_map/ppermute | solution.py:477
  55.1 7.0 %collective-permute-start.11 = (f32[176,128]{1,0:T(8,128)S(1)}, f32[176,128]{1,0:T(8,128)S(1)}, u32[]{:S(2)}, u32[]{:S(2)}) collective-permute-start(f32[176,128]{1,0:T(8,128)S(1)} %get-tuple-element.85), channel_id=1, source_target_pairs={{1,2},{2,1},{5,6},{6,5},{9,10},{10,9},{13,14},{14,13},{17,18},{18,... | collective-permute-start | bytes 270344 | tf_op jit(solution)/shard_map/ppermute | solution.py:477

commit v5 on v4

--- a/solution.py
+++ b/solution.py
@@ -14,6 +14,7 @@
 RATE = math.log2(math.e) / 0.3
 HALF_LN2 = 0.5 * math.log(2.0)
 VMEM_BYTES = 24 * 1024 * 1024
+FIRST_VMEM_BYTES = 48 * 1024 * 1024
 
 
 def tap(offset):
@@ -106,6 +107,9 @@
 
 
 def send(axis, low, high, even_ref, odd_ref):
+    place = lax.axis_index(axis)
+    low = jnp.where(place == 0, 0.0, low)
+    high = jnp.where(place == lax.axis_size(axis) - 1, 0.0, high)
     even_ref[...] = jnp.where(on_even(axis), high, low)
     odd_ref[...] = jnp.where(on_even(axis), low, high)
 
@@ -123,11 +127,22 @@
     return jnp.exp2(jnp.minimum(threshold - full * norm, 0.0) * RATE)
 
 
-def first_edge_kernel(stress, strain, yields, count,
-                      even_ref, odd_ref, norm, norm_last, norm_before, *refs):
-    block = refs[-1]
-    layers, cols = stress.shape[0], stress.shape[2]
-    rows = norm.shape[0] - REACH
+def first_edge_kernel(*refs):
+    sources, refs = refs[:5], refs[5:]
+    even_ref, odd_ref, norm, norm_last, norm_before, _, _, *refs = refs
+    targets, (block, sems) = refs[:5], refs[5:]
+    stress, strain, yields, count, _ = targets
+    layers, rows, cols = stress.shape
+    parts = (pl.ds(0, REACH), pl.ds(rows - REACH, REACH), pl.ds(REACH, rows - 2 * REACH))
+    copies = []
+    for side, part in enumerate(parts):
+        for index, (source, target) in enumerate(zip(sources, targets)):
+            copies.append(
+                pltpu.make_async_copy(
+                    source.at[:, part, :], target.at[:, part, :], sems.at[side, index]
+                )
+            )
+            copies[-1].start()
     total = rows + REACH
     ids = lax.broadcasted_iota(jnp.int32, (total, cols), 0)
     down = inverse_weights("gx", ids - REACH, rows)
@@ -146,17 +161,21 @@
     for side, matrix in enumerate(
         (jnp.where(steps <= 0, band_part, 0.0), jnp.where(steps >= 0, band_part, 0.0))
     ):
+        for copy in copies[side * 5 : side * 5 + 5]:
+            copy.wait()
         for layer in range(layers):
-            at = (layer, pl.ds(side * REACH, REACH), slice(None))
+            at = (layer, parts[side], slice(None))
             block[pl.ds(layer * REACH, REACH), :] = newton(
                 stress[at], strain[at], yields[at], count[at], jnp.ones((REACH, cols), jnp.float32)
             )
         product = left_product(left_constant(matrix), block[...])
         sent.append(jnp.concatenate([product, extra], axis=0))
     send("gx", *sent, even_ref, odd_ref)
-
-
-def edge_kernel(stress, strain, yields, count, threshold, smooth, col_even, col_odd, norm,
+    for copy in copies[10:]:
+        copy.wait()
+
+
+def edge_kernel(stress, strain, yields, count, threshold, smooth, _, col_even, col_odd, norm,
                 below, above, even_ref, odd_ref, low_block, high_block, rest):
     layers, rows, cols = stress.shape
     starts = (0, rows - 2 * REACH, rows - REACH)
@@ -169,7 +188,7 @@
         for index, first_row in enumerate(starts):
             at = (layer, pl.ds(first_row, REACH), slice(None))
             extended = pl.ds(first_row + REACH, REACH)
-            full = add_columns(smooth[layer, extended, :], layer, *received[index])
+            full = add_columns(smooth[at], layer, *received[index])
             soften = 0.5 + 0.5 * retained(full, norm[extended, :], threshold[at])
             value = newton(stress[at], strain[at], yields[at], count[at], soften)
             if index == 0:
@@ -192,12 +211,13 @@
     )
 
 
-def newton_kernel(turn, stress, strain, yields, count, threshold, smooth, col_even, col_odd, norm,
-                  waiting, plastic, ready):
+def main_kernel(turn, stress, strain, yields, count, threshold, smooth, col_even, col_odd, norm,
+                norm_last, band_ref, low_ref, high_ref, next_ref,
+                across, low_cols, high_cols, plastic, pack_low, pack_high, pack_next, pack_last):
     layers, rows, cols = stress.shape
+    total = rows + REACH
     step_rows = 2 * REACH
     steps = rows // step_rows
-    ready[...] = waiting[...]
 
     @pl.when(turn[0] == 0)
     def _():
@@ -219,19 +239,13 @@
             low, high = sides("gy", col_even[extended, :], col_odd[extended, :])
             for layer in range(layers):
                 at = (layer, part, slice(None))
-                full = add_columns(smooth[layer, extended, :], layer, low, high)
+                full = add_columns(smooth[at], layer, low, high)
                 soften = 0.5 + 0.5 * retained(full, norm[extended, :], threshold[at])
                 plastic[at] = newton(stress[at], strain[at], yields[at], count[at], soften)
             return carry
 
         lax.fori_loop(0, steps, step, 0)
 
-
-def across_kernel(turn, stress, strain, threshold, plastic, norm_last, band_ref, low_ref, high_ref,
-                  next_ref, _, across, low_cols, high_cols, pack_low, pack_high, pack_next, pack_last):
-    layers, rows, cols = stress.shape
-    total = rows + REACH
-    step_rows = 2 * REACH
     constant = left_constant(band_ref[...])
     slots = lane_ids((total, cols)) >> (REACH.bit_length() - 1)
     for layer in range(0, layers, 2):
@@ -266,7 +280,7 @@
             return carry
 
         pack_last[pl.ds(0, REACH), :] = jnp.zeros((REACH, cols), jnp.float32)
-        lax.fori_loop(0, rows // step_rows, last_column, 0)
+        lax.fori_loop(0, steps, last_column, 0)
         lanes = lane_ids(pack_last.shape)
         drop = (high[:, cols:] + behind) * norm_last[...]
         high_cols[:, cols:] = pack_last[...] - jnp.where(lanes < layers, drop, 0.0)
@@ -285,7 +299,7 @@
     return low, high, ahead
 
 
-def corner_kernel(row_even, row_odd, low_cols, high_cols, norm_last, low_ref, high_ref, next_ref,
+def corner_kernel(row_even, row_odd, low_cols, high_cols, norm_last, _, low_ref, high_ref, next_ref,
                   even_ref, odd_ref, own_ref):
     cols = low_ref.shape[0]
     total = low_cols.shape[0]
@@ -342,10 +356,9 @@
     own_ref[...] = low_all[:, cols:]
 
 
-def depth_kernel(depth, across, row_even, row_odd, waiting, _, deep, ready):
+def column_kernel(depth, across, row_even, row_odd, band_ref, _, smooth, before, deep):
     layers, total, cols = across.shape
     strip = layers * REACH
-    ready[...] = waiting[...]
 
     def depth_sums(part, values):
         for layer, value in enumerate(depth_smooth(values, depth)):
@@ -366,15 +379,14 @@
             both = sides("gx", row_even[line, :], row_odd[line, :])
             values.append(across[layer, part, :] + both[first_row > REACH])
         depth_sums(part, values)
-
-
-def column_kernel(deep, band_ref, _, smooth):
     constant = right_constant(band_ref[...])
-    for layer in range(deep.shape[0]):
-        smooth[layer] = right_product(deep[layer], constant)
-
-
-def final_kernel(stress, strain, plastic, threshold, smooth, col_even, col_odd, row_even, row_odd,
+    for layer in range(layers):
+        result = right_product(deep[layer], constant)
+        before[layer] = result[:REACH]
+        smooth[layer] = result[REACH:]
+
+
+def final_kernel(stress, strain, plastic, threshold, smooth, before, col_even, col_odd, row_even, row_odd,
                  norm, norm_before, own_cols, plastic_out, damage_out, force_out,
                  columns, damage_s, force_s, copy_sem, sems):
     layers, rows, cols = stress.shape
@@ -408,8 +420,8 @@
         for block in range(rows // REACH + 1):
             extended = pl.ds(block * REACH, REACH)
             low, high = sides("gy", col_even[extended, :], col_odd[extended, :])
-            full = add_columns(smooth[layer, extended, :], layer, low, high)
             if block == 0:
+                summed = before[layer]
                 line = pl.ds(strip + layers + layer, 1)
                 rest, _ = sides("gx", row_even[line, :], row_odd[line, :])
                 line = pl.ds(strip + 2 * layers + layer, 1)
@@ -418,6 +430,8 @@
                 at = (layer, pl.ds((block - 1) * REACH, REACH), slice(None))
                 rest = (stress[at] + strain[at]) - plastic[at]
                 limit = threshold[at]
+                summed = smooth[at]
+            full = add_columns(summed, layer, low, high)
             ratio = retained(full, norm[extended, :], limit)
             value = ratio * rest
             left = jnp.where(
@@ -452,7 +466,7 @@
     whole.wait()
 
 
-def call(kernel, outs, scratch, nanoseconds, operands, spaces=None, outs_space=pltpu.VMEM):
+def call(kernel, outs, scratch, nanoseconds, operands, spaces=None, outs_space=pltpu.VMEM, limit=VMEM_BYTES):
     spaces = spaces or [pltpu.VMEM] * len(operands)
     shapes = [out if isinstance(out, jax.ShapeDtypeStruct) else jax.ShapeDtypeStruct(out, jnp.float32)
               for out in outs]
@@ -462,19 +476,22 @@
         in_specs=[pl.BlockSpec(memory_space=space) for space in spaces],
         out_specs=[pl.BlockSpec(memory_space=outs_space)] * len(outs),
         scratch_shapes=[pltpu.VMEM(s, jnp.float32) if isinstance(s, tuple) else s for s in scratch],
-        compiler_params=pltpu.CompilerParams(vmem_limit_bytes=VMEM_BYTES),
+        compiler_params=pltpu.CompilerParams(vmem_limit_bytes=limit),
         cost_estimate=pl.CostEstimate(
             flops=nanoseconds * 1_000_000, bytes_accessed=nanoseconds * 1000, transcendentals=0
         ),
     )(*operands)
 
 
-def exchange(axis, start, value):
+def exchange(axis, even, odd):
     count = lax.axis_size(axis)
-    pairs = []
-    for low in range(start, count - 1, 2):
-        pairs += [(low, low + 1), (low + 1, low)]
-    return lax.ppermute(value, axis, pairs)
+    results = []
+    for start, value in ((0, even), (1, odd)):
+        partner = list(range(count))
+        for low in range(start, count - 1, 2):
+            partner[low], partner[low + 1] = low + 1, low
+        results.append(lax.ppermute(value, axis, list(enumerate(partner))))
+    return results
 
 
 def inverse_weights(axis, places, length):
@@ -526,51 +543,45 @@
     sent_cols = (total + rows // 4 + REACH, cols)
     packed, packed_two = (total, cols), (total, 2 * cols)
 
-    inputs = (trial_stress, old_strain, yield_mask, newton_count, damage_threshold)
+    sources = (trial_stress, old_strain, yield_mask, newton_count, damage_threshold)
+    row_even, row_odd, norm, norm_last, norm_before, col_even, col_odd, *inputs = call(
+        first_edge_kernel,
+        [sent_rows, sent_rows, packed, packed, packed, sent_cols, sent_cols]
+        + [jax.ShapeDtypeStruct(whole, source.dtype) for source in sources],
+        [(strip, cols), pltpu.SemaphoreType.DMA((3, len(sources)))], 2500,
+        sources, [pltpu.HBM] * len(sources), limit=FIRST_VMEM_BYTES,
+    )
     stress, strain, _, _, threshold = inputs
-    edges = [jnp.concatenate([value[:, :REACH], value[:, rows - REACH :]], axis=1) for value in inputs[:4]]
-    row_even, row_odd, norm, norm_last, norm_before, smooth, col_even, col_odd = call(
-        first_edge_kernel,
-        [sent_rows, sent_rows, packed, packed, packed, wide, sent_cols, sent_cols],
-        [(strip, cols)], 6000, edges,
-    )
+    smooth = stress
     for outer_no in range(OUTER):
         if outer_no:
             row_even, row_odd = call(
                 edge_kernel, [sent_rows] * 2,
                 [(strip, cols), (2 * strip, cols), (2 * layers, cols)], 800,
-                (*inputs, smooth, col_even, col_odd, norm, below, above),
+                (*inputs, smooth, before, col_even, col_odd, norm, below, above),
             )
+        row_even, row_odd = exchange("gx", row_even, row_odd)
         turn = jnp.full((1,), outer_no, jnp.int32)
-        row_even = exchange("gx", 0, row_even)
-        plastic, row_odd = call(
-            newton_kernel, [whole, sent_rows], [], 3000,
-            (turn, *inputs, smooth, col_even, col_odd, norm, row_odd),
-            [pltpu.SMEM] + [pltpu.VMEM] * 10,
-        )
-        row_odd = exchange("gx", 1, row_odd)
-        across, low_cols, high_cols = call(
-            across_kernel, [wide, packed_two, packed_two],
-            [packed, packed, packed, packed], 2000,
-            (turn, stress, strain, threshold, plastic, norm_last, rows_band, *columns, row_even),
-            [pltpu.SMEM] + [pltpu.VMEM] * 10,
+        across, low_cols, high_cols, plastic = call(
+            main_kernel, [wide, packed_two, packed_two, whole],
+            [packed, packed, packed, packed], 4500,
+            (turn, *inputs, smooth, col_even, col_odd, norm, norm_last, rows_band, *columns),
+            [pltpu.SMEM] + [pltpu.VMEM] * 14,
         )
         col_even, col_odd, own_cols = call(
             corner_kernel, [sent_cols, sent_cols, packed], [], 400,
-            (row_even, row_odd, low_cols, high_cols, norm_last, *columns),
+            (row_even, row_odd, low_cols, high_cols, norm_last, plastic, *columns),
         )
-        col_even = exchange("gy", 0, col_even)
-        deep, col_odd = call(
-            functools.partial(depth_kernel, depth), [wide, sent_cols], [], 700,
-            (across, row_even, row_odd, col_odd, own_cols),
+        col_even, col_odd = exchange("gy", col_even, col_odd)
+        smooth, before = call(
+            functools.partial(column_kernel, depth), [whole, (layers, REACH, cols)], [wide], 1200,
+            (across, row_even, row_odd, cols_band, own_cols),
         )
-        col_odd = exchange("gy", 1, col_odd)
-        (smooth,) = call(column_kernel, [wide], [], 500, (deep, cols_band, col_even))
     return tuple(call(
         final_kernel, [whole, whole, (2, *whole)],
         [packed, whole, (2, *whole), pltpu.SemaphoreType.DMA(()), pltpu.SemaphoreType.DMA((3, layers))],
         3000,
-        (stress, strain, plastic, threshold, smooth, col_even, col_odd,
+        (stress, strain, plastic, threshold, smooth, before, col_even, col_odd,
          row_even, row_odd, norm, norm_before, own_cols),
         outs_space=pltpu.HBM,
     ))

time: 65.8 us -> 55 us (0.84)
  the two profiles are of different devices: /device:TPU:19 before, /device:TPU:3 now
where the time goes in v5:
time: 55 us; the launch traced here: 54.7 us
  starting transfers between devices  24.8 us (45%)
  Pallas kernels  24.4 us (44%)
  waiting for transfers between devices  4.48 us (8%)
  between operations  0.96 us (2%)
    ppermute x12, starting transfers between devices, exchange(): results.append(lax.ppermute(value, axis, list(enumerate(partner))))  24.8 us
    pallas_call x13, Pallas kernels, call(): pl.pallas_call(kernel, out_shape=shapes, in_specs=[pl.BlockSpec(memory_sp...  24.4 us
    ppermute x12, waiting for transfers between devices, exchange(): results.append(lax.ppermute(value, axis, list(enumerate(partner))))  4.48 us
  transfers between devices with their start and end apart: 12, of which 3 were waited for; matrix products, arithmetic and copies ran while one was open for 0% of the time, Pallas kernels for 28%

profile of v5, /device:TPU:3, one launch (start us, length us, event | category | flops | bytes accessed | tf_op | source)
XLA Modules:
  0.0 54.7 jit_solution(10109832841496594315)
XLA Ops:
  0.6 0.0 copy-start
  0.6 0.0 copy-start.1
  0.7 0.0 copy-start.3
  0.7 0.0 copy-start.5
  0.7 2.8 %shard_map.139 = (f32[176,128]{1,0:T(8,128)S(1)}, f32[176,128]{1,0:T(8,128)S(1)}, f32[136,128]{1,0:T(8,128)S(1)}, f32[136,128]{1,0:T(8,128)S(1)}, f32[136,128]{1...) custom-call(f32[16,128,128]{2,1,0:T(8,128)} %refs_0_.1, ...), custom_call_target="tpu_custom_call" | custom-call | flops 2500000000 | bytes 2500000 | tf_op jit(solution)/shard_map/pallas_call | solution.py:473
  3.5 0.1 collective-permute-start
  3.6 4.4 %collective-permute-start.1 = (f32[176,128]{1,0:T(8,128)S(1)}, f32[176,128]{1,0:T(8,128)S(1)}, u32[]{:S(2)}, u32[]{:S(2)}) collective-permute-start(f32[176,128]{1,0:T(8,128)S(1)} %get-tuple-element.57), channel_id=1, source_target_pairs={{0,0},{4,8},{8,4},{12,16},{16,12},{20,24},{24,20},{28,28},{1,1},{5... | collective-permute-start | bytes 270344 | tf_op jit(solution)/shard_map/ppermute | solution.py:493
  7.9 0.0 copy-done
  8.0 0.0 copy-done.1
  8.0 0.0 copy-done.3
  8.0 0.0 copy-done.5
  8.0 3.0 %shard_map.140 = (f32[16,136,128]{2,1,0:T(8,128)S(1)}, f32[136,256]{1,0:T(8,128)S(1)}, f32[136,256]{1,0:T(8,128)S(1)}, f32[16,128,128]{2,1,0:T(8,128)S(1)}) custom-call(s32[1]{0:T(128)} %constant.9.clone.1.turn, f32[16,128,128]{2,1,0:T(8,128)S(1)} %get-tuple-element.46.stress.smooth, f32[16,128,128]{2,1,0:T(8,128)S(1)} %get-tuple-element.47.strain, ...), custom_call_target="tpu_custom_call" | custom-call | flops 4499999744 | bytes 4500000 | tf_op jit(solution)/shard_map/pallas_call | solution.py:473
  11.0 0.0 copy-start.6
  11.0 0.0 collective-permute-done.row_even
  11.0 0.0 collective-permute-done.1.row_odd
  11.0 0.4 shard_map.141
  11.4 1.2 %collective-permute-start.2 = (f32[176,128]{1,0:T(8,128)S(1)}, f32[176,128]{1,0:T(8,128)S(1)}, u32[]{:S(2)}, u32[]{:S(2)}) collective-permute-start(f32[176,128]{1,0:T(8,128)S(1)} %get-tuple-element.63), channel_id=1, source_target_pairs={{0,1},{1,0},{2,3},{3,2},{4,5},{5,4},{6,7},{7,6},{8,9},{9,8},{10,11... | collective-permute-start | bytes 270344 | tf_op jit(solution)/shard_map/ppermute | solution.py:493
  12.7 3.0 %collective-permute-start.3 = (f32[176,128]{1,0:T(8,128)S(1)}, f32[176,128]{1,0:T(8,128)S(1)}, u32[]{:S(2)}, u32[]{:S(2)}) collective-permute-start(f32[176,128]{1,0:T(8,128)S(1)} %get-tuple-element.64), channel_id=1, source_target_pairs={{0,0},{1,2},{2,1},{3,3},{4,4},{5,6},{6,5},{7,7},{8,8},{9,10},{10,9... | collective-permute-start | bytes 270344 | tf_op jit(solution)/shard_map/ppermute | solution.py:493
  15.7 0.0 copy-done.6
  15.7 0.0 copy-start.2
  15.7 0.0 copy-start.4
  15.8 1.1 %shard_map.142 = (f32[16,128,128]{2,1,0:T(8,128)S(1)}, f32[16,8,128]{2,1,0:T(8,128)S(1)}) custom-call(f32[16,136,128]{2,1,0:T(8,128)S(1)} %get-tuple-element.55.across, f32[176,128]{1,0:T(8,128)S(1)} %collective-permute-done.row_even, f32[176,128]{1,0:T(8,128)S(1)} %collective-permute-done.1.row_odd, f32[128,128]{1,0:T(8,128)S(1)} %copy-done.6, ...), custom_call_target="tpu_custom_call" | custom-call | flops 1200000000 | bytes 1200000 | tf_op jit(solution)/shard_map/pallas_call | solution.py:473
  16.8 0.0 collective-permute-done.2.col_even
  16.8 1.9 %collective-permute-done.3.col_odd = f32[176,128]{1,0:T(8,128)S(1)} collective-permute-done((f32[176,128]{1,0:T(8,128)S(1)}, f32[176,128]{1,0:T(8,128)S(1)}, u32[]{:S(2)}, u32[]{:S(2)}) %collective-permute-start.3) | collective-permute-done | bytes 90144 | tf_op jit(solution)/shard_map/ppermute | solution.py:493
  18.8 0.0 copy-done.2
  18.8 0.0 copy-done.4
  18.8 0.8 %shard_map.144 = (f32[176,128]{1,0:T(8,128)S(1)}, f32[176,128]{1,0:T(8,128)S(1)}) custom-call(f32[16,128,128]{2,1,0:T(8,128)S(1)} %get-tuple-element.46.stress.smooth, f32[16,128,128]{2,1,0:T(8,128)S(1)} %get-tuple-element.47.strain, s32[16,128,128]{2,1,0:T(8,128)S(1)} %get-tuple-element.48.yields, s32[16,128,128]{2,1,0:T(8,128)S(1)} %get-tuple-element.49.count, ...), custom_call_target="tpu_custom_call" | custom-call | flops 800000000 | bytes 800000 | tf_op jit(solution)/shard_map/pallas_call | solution.py:473
  19.6 0.1 collective-permute-start.4
  19.7 4.4 %collective-permute-start.5 = (f32[176,128]{1,0:T(8,128)S(1)}, f32[176,128]{1,0:T(8,128)S(1)}, u32[]{:S(2)}, u32[]{:S(2)}) collective-permute-start(f32[176,128]{1,0:T(8,128)S(1)} %get-tuple-element.68), channel_id=1, source_target_pairs={{0,0},{4,8},{8,4},{12,16},{16,12},{20,24},{24,20},{28,28},{1,1},{5... | collective-permute-start | bytes 270344 | tf_op jit(solution)/shard_map/ppermute | solution.py:493
  24.1 4.1 %shard_map.143 = (f32[16,136,128]{2,1,0:T(8,128)S(1)}, f32[136,256]{1,0:T(8,128)S(1)}, f32[136,256]{1,0:T(8,128)S(1)}, f32[16,128,128]{2,1,0:T(8,128)S(1)}) custom-call(s32[1]{0:T(128)} %constant.8.clone.1.turn, f32[16,128,128]{2,1,0:T(8,128)S(1)} %get-tuple-element.46.stress.smooth, f32[16,128,128]{2,1,0:T(8,128)S(1)} %get-tuple-element.47.strain, ...), custom_call_target="tpu_custom_call" | custom-call | flops 4499999744 | bytes 4500000 | tf_op jit(solution)/shard_map/pallas_call | solution.py:473
  28.1 0.0 collective-permute-done.4.row_even
  28.2 0.0 collective-permute-done.5.row_odd
  28.2 0.4 shard_map.145
  28.5 0.0 collective-permute-start.6
  28.6 3.3 %collective-permute-start.7 = (f32[176,128]{1,0:T(8,128)S(1)}, f32[176,128]{1,0:T(8,128)S(1)}, u32[]{:S(2)}, u32[]{:S(2)}) collective-permute-start(f32[176,128]{1,0:T(8,128)S(1)} %get-tuple-element.75), channel_id=1, source_target_pairs={{0,0},{1,2},{2,1},{3,3},{4,4},{5,6},{6,5},{7,7},{8,8},{9,10},{10,9... | collective-permute-start | bytes 270344 | tf_op jit(solution)/shard_map/ppermute | solution.py:493
  31.9 1.1 %shard_map.146 = (f32[16,128,128]{2,1,0:T(8,128)S(1)}, f32[16,8,128]{2,1,0:T(8,128)S(1)}) custom-call(f32[16,136,128]{2,1,0:T(8,128)S(1)} %get-tuple-element.65.across, f32[176,128]{1,0:T(8,128)S(1)} %collective-permute-done.4.row_even, f32[176,128]{1,0:T(8,128)S(1)} %collective-permute-done.5.row_odd, f32[128,128]{1,0:T(8,128)S(1)} %copy-done.6, ...), custom_call_target="tpu_custom_call" | custom-call | flops 1200000000 | bytes 1200000 | tf_op jit(solution)/shard_map/pallas_call | solution.py:473
  33.0 0.0 collective-permute-done.6.col_even
  33.0 1.4 %collective-permute-done.7.col_odd = f32[176,128]{1,0:T(8,128)S(1)} collective-permute-done((f32[176,128]{1,0:T(8,128)S(1)}, f32[176,128]{1,0:T(8,128)S(1)}, u32[]{:S(2)}, u32[]{:S(2)}) %collective-permute-start.7) | collective-permute-done | bytes 90144 | tf_op jit(solution)/shard_map/ppermute | solution.py:493
  34.4 0.8 %shard_map.148 = (f32[176,128]{1,0:T(8,128)S(1)}, f32[176,128]{1,0:T(8,128)S(1)}) custom-call(f32[16,128,128]{2,1,0:T(8,128)S(1)} %get-tuple-element.46.stress.smooth, f32[16,128,128]{2,1,0:T(8,128)S(1)} %get-tuple-element.47.strain, s32[16,128,128]{2,1,0:T(8,128)S(1)} %get-tuple-element.48.yields, s32[16,128,128]{2,1,0:T(8,128)S(1)} %get-tuple-element.49.count, ...), custom_call_target="tpu_custom_call" | custom-call | flops 800000000 | bytes 800000 | tf_op jit(solution)/shard_map/pallas_call | solution.py:473
  35.2 0.1 collective-permute-start.8
  35.3 4.4 %collective-permute-start.9 = (f32[176,128]{1,0:T(8,128)S(1)}, f32[176,128]{1,0:T(8,128)S(1)}, u32[]{:S(2)}, u32[]{:S(2)}) collective-permute-start(f32[176,128]{1,0:T(8,128)S(1)} %get-tuple-element.80), channel_id=1, source_target_pairs={{0,0},{4,8},{8,4},{12,16},{16,12},{20,24},{24,20},{28,28},{1,1},{5... | collective-permute-start | bytes 270344 | tf_op jit(solution)/shard_map/ppermute | solution.py:493
  39.7 5.2 %shard_map.147 = (f32[16,136,128]{2,1,0:T(8,128)S(1)}, f32[136,256]{1,0:T(8,128)S(1)}, f32[136,256]{1,0:T(8,128)S(1)}, f32[16,128,128]{2,1,0:T(8,128)S(1)}) custom-call(s32[1]{0:T(128)} %constant.7.clone.1.turn, f32[16,128,128]{2,1,0:T(8,128)S(1)} %get-tuple-element.46.stress.smooth, f32[16,128,128]{2,1,0:T(8,128)S(1)} %get-tuple-element.47.strain, ...), custom_call_target="tpu_custom_call" | custom-call | flops 4499999744 | bytes 4500000 | tf_op jit(solution)/shard_map/pallas_call | solution.py:473
  44.9 0.0 collective-permute-done.8.row_even
  44.9 0.0 collective-permute-done.9.row_odd
  44.9 0.4 shard_map.149
  45.3 0.0 collective-permute-start.10
  45.3 3.9 %collective-permute-start.11 = (f32[176,128]{1,0:T(8,128)S(1)}, f32[176,128]{1,0:T(8,128)S(1)}, u32[]{:S(2)}, u32[]{:S(2)}) collective-permute-start(f32[176,128]{1,0:T(8,128)S(1)} %get-tuple-element.87), channel_id=1, source_target_pairs={{0,0},{1,2},{2,1},{3,3},{4,4},{5,6},{6,5},{7,7},{8,8},{9,10},{10,9... | collective-permute-start | bytes 270344 | tf_op jit(solution)/shard_map/ppermute | solution.py:493
  49.2 1.1 %shard_map.150 = (f32[16,128,128]{2,1,0:T(8,128)S(1)}, f32[16,8,128]{2,1,0:T(8,128)S(1)}) custom-call(f32[16,136,128]{2,1,0:T(8,128)S(1)} %get-tuple-element.77.across, f32[176,128]{1,0:T(8,128)S(1)} %collective-permute-done.8.row_even, f32[176,128]{1,0:T(8,128)S(1)} %collective-permute-done.9.row_odd, f32[128,128]{1,0:T(8,128)S(1)} %copy-done.6, ...), custom_call_target="tpu_custom_call" | custom-call | flops 1200000000 | bytes 1200000 | tf_op jit(solution)/shard_map/pallas_call | solution.py:473
  50.3 0.0 collective-permute-done.10.col_even
  50.3 1.1 %collective-permute-done.11.col_odd = f32[176,128]{1,0:T(8,128)S(1)} collective-permute-done((f32[176,128]{1,0:T(8,128)S(1)}, f32[176,128]{1,0:T(8,128)S(1)}, u32[]{:S(2)}, u32[]{:S(2)}) %collective-permute-start.11) | collective-permute-done | bytes 90144 | tf_op jit(solution)/shard_map/ppermute | solution.py:493
  51.4 3.3 %shard_map.151 = (f32[16,128,128]{2,1,0:T(8,128)}, f32[16,128,128]{2,1,0:T(8,128)}, f32[2,16,128,128]{3,2,1,0:T(8,128)}) custom-call(f32[16,128,128]{2,1,0:T(8,128)S(1)} %get-tuple-element.46.stress.smooth, f32[16,128,128]{2,1,0:T(8,128)S(1)} %get-tuple-element.47.strain, f32[16,128,128]{2,1,0:T(8,128)S(1)} %get-tuple-element.76._.plastic, ...), custom_call_target="tpu_custom_call" | custom-call | flops 3000000000 | bytes 3000000 | tf_op jit(solution)/shard_map/pallas_call | solution.py:473
Async XLA Ops:
  0.6 7.3 %copy-start = (f32[128,256]{1,0:T(8,128)S(1)}, f32[128,256]{1,0:T(8,128)}, u32[]{:S(2)}) copy-start(f32[128,256]{1,0:T(8,128)} %constant.25.clone.high_ref) | copy-start | bytes 393220
  0.6 7.3 %copy-start.1 = (f32[128,256]{1,0:T(8,128)S(1)}, f32[128,256]{1,0:T(8,128)}, u32[]{:S(2)}) copy-start(f32[128,256]{1,0:T(8,128)} %constant.24.clone.low_ref) | copy-start | bytes 393220
  0.7 7.3 %copy-start.3 = (f32[128,128]{1,0:T(8,128)S(1)}, f32[128,128]{1,0:T(8,128)}, u32[]{:S(2)}) copy-start(f32[128,128]{1,0:T(8,128)} %constant.26.clone.next_ref) | copy-start | bytes 196612
  0.7 7.3 %copy-start.5 = (f32[136,128]{1,0:T(8,128)S(1)}, f32[136,128]{1,0:T(8,128)}, u32[]{:S(2)}) copy-start(f32[136,128]{1,0:T(8,128)} %constant.22.clone.band_ref) | copy-start | bytes 208900
  3.5 7.5 %collective-permute-start = (f32[176,128]{1,0:T(8,128)S(1)}, f32[176,128]{1,0:T(8,128)S(1)}, u32[]{:S(2)}, u32[]{:S(2)}) collective-permute-start(f32[176,128]{1,0:T(8,128)S(1)} %get-tuple-element.56), channel_id=1, source_target_pairs={{0,4},{4,0},{8,12},{12,8},{16,20},{20,16},{24,28},{28,24},{1,5},{5... | collective-permute-start | bytes 270344 | tf_op jit(solution)/shard_map/ppermute | solution.py:493
  3.6 7.5 %collective-permute-start.1 = (f32[176,128]{1,0:T(8,128)S(1)}, f32[176,128]{1,0:T(8,128)S(1)}, u32[]{:S(2)}, u32[]{:S(2)}) collective-permute-start(f32[176,128]{1,0:T(8,128)S(1)} %get-tuple-element.57), channel_id=1, source_target_pairs={{0,0},{4,8},{8,4},{12,16},{16,12},{20,24},{24,20},{28,28},{1,1},{5... | collective-permute-start | bytes 270344 | tf_op jit(solution)/shard_map/ppermute | solution.py:493
  11.0 4.7 %copy-start.6 = (f32[128,128]{1,0:T(8,128)S(1)}, f32[128,128]{1,0:T(8,128)}, u32[]{:S(2)}) copy-start(f32[128,128]{1,0:T(8,128)} %constant.23.clone.band_ref) | copy-start | bytes 196612
  11.4 5.4 %collective-permute-start.2 = (f32[176,128]{1,0:T(8,128)S(1)}, f32[176,128]{1,0:T(8,128)S(1)}, u32[]{:S(2)}, u32[]{:S(2)}) collective-permute-start(f32[176,128]{1,0:T(8,128)S(1)} %get-tuple-element.63), channel_id=1, source_target_pairs={{0,1},{1,0},{2,3},{3,2},{4,5},{5,4},{6,7},{7,6},{8,9},{9,8},{10,11... | collective-permute-start | bytes 270344 | tf_op jit(solution)/shard_map/ppermute | solution.py:493
  12.7 6.1 %collective-permute-start.3 = (f32[176,128]{1,0:T(8,128)S(1)}, f32[176,128]{1,0:T(8,128)S(1)}, u32[]{:S(2)}, u32[]{:S(2)}) collective-permute-start(f32[176,128]{1,0:T(8,128)S(1)} %get-tuple-element.64), channel_id=1, source_target_pairs={{0,0},{1,2},{2,1},{3,3},{4,4},{5,6},{6,5},{7,7},{8,8},{9,10},{10,9... | collective-permute-start | bytes 270344 | tf_op jit(solution)/shard_map/ppermute | solution.py:493
  15.7 3.1 %copy-start.2 = (f32[144,256]{1,0:T(8,128)S(1)}, f32[144,256]{1,0:T(8,128)}, u32[]{:S(2)}) copy-start(f32[144,256]{1,0:T(8,128)} %constant.21.clone.above) | copy-start | bytes 442372
  15.7 3.1 %copy-start.4 = (f32[128,128]{1,0:T(8,128)S(1)}, f32[128,128]{1,0:T(8,128)}, u32[]{:S(2)}) copy-start(f32[128,128]{1,0:T(8,128)} %constant.20.clone.below) | copy-start | bytes 196612
  19.6 8.5 %collective-permute-start.4 = (f32[176,128]{1,0:T(8,128)S(1)}, f32[176,128]{1,0:T(8,128)S(1)}, u32[]{:S(2)}, u32[]{:S(2)}) collective-permute-start(f32[176,128]{1,0:T(8,128)S(1)} %get-tuple-element.67), channel_id=1, source_target_pairs={{0,4},{4,0},{8,12},{12,8},{16,20},{20,16},{24,28},{28,24},{1,5},{5... | collective-permute-start | bytes 270344 | tf_op jit(solution)/shard_map/ppermute | solution.py:493
  19.7 8.5 %collective-permute-start.5 = (f32[176,128]{1,0:T(8,128)S(1)}, f32[176,128]{1,0:T(8,128)S(1)}, u32[]{:S(2)}, u32[]{:S(2)}) collective-permute-start(f32[176,128]{1,0:T(8,128)S(1)} %get-tuple-element.68), channel_id=1, source_target_pairs={{0,0},{4,8},{8,4},{12,16},{16,12},{20,24},{24,20},{28,28},{1,1},{5... | collective-permute-start | bytes 270344 | tf_op jit(solution)/shard_map/ppermute | solution.py:493
  28.5 4.5 %collective-permute-start.6 = (f32[176,128]{1,0:T(8,128)S(1)}, f32[176,128]{1,0:T(8,128)S(1)}, u32[]{:S(2)}, u32[]{:S(2)}) collective-permute-start(f32[176,128]{1,0:T(8,128)S(1)} %get-tuple-element.74), channel_id=1, source_target_pairs={{0,1},{1,0},{2,3},{3,2},{4,5},{5,4},{6,7},{7,6},{8,9},{9,8},{10,11... | collective-permute-start | bytes 270344 | tf_op jit(solution)/shard_map/ppermute | solution.py:493
  28.6 5.8 %collective-permute-start.7 = (f32[176,128]{1,0:T(8,128)S(1)}, f32[176,128]{1,0:T(8,128)S(1)}, u32[]{:S(2)}, u32[]{:S(2)}) collective-permute-start(f32[176,128]{1,0:T(8,128)S(1)} %get-tuple-element.75), channel_id=1, source_target_pairs={{0,0},{1,2},{2,1},{3,3},{4,4},{5,6},{6,5},{7,7},{8,8},{9,10},{10,9... | collective-permute-start | bytes 270344 | tf_op jit(solution)/shard_map/ppermute | solution.py:493
  35.2 9.7 %collective-permute-start.8 = (f32[176,128]{1,0:T(8,128)S(1)}, f32[176,128]{1,0:T(8,128)S(1)}, u32[]{:S(2)}, u32[]{:S(2)}) collective-permute-start(f32[176,128]{1,0:T(8,128)S(1)} %get-tuple-element.79), channel_id=1, source_target_pairs={{0,4},{4,0},{8,12},{12,8},{16,20},{20,16},{24,28},{28,24},{1,5},{5... | collective-permute-start | bytes 270344 | tf_op jit(solution)/shard_map/ppermute | solution.py:493
  35.3 9.6 %collective-permute-start.9 = (f32[176,128]{1,0:T(8,128)S(1)}, f32[176,128]{1,0:T(8,128)S(1)}, u32[]{:S(2)}, u32[]{:S(2)}) collective-permute-start(f32[176,128]{1,0:T(8,128)S(1)} %get-tuple-element.80), channel_id=1, source_target_pairs={{0,0},{4,8},{8,4},{12,16},{16,12},{20,24},{24,20},{28,28},{1,1},{5... | collective-permute-start | bytes 270344 | tf_op jit(solution)/shard_map/ppermute | solution.py:493
  45.3 5.0 %collective-permute-start.10 = (f32[176,128]{1,0:T(8,128)S(1)}, f32[176,128]{1,0:T(8,128)S(1)}, u32[]{:S(2)}, u32[]{:S(2)}) collective-permute-start(f32[176,128]{1,0:T(8,128)S(1)} %get-tuple-element.86), channel_id=1, source_target_pairs={{0,1},{1,0},{2,3},{3,2},{4,5},{5,4},{6,7},{7,6},{8,9},{9,8},{10,11... | collective-permute-start | bytes 270344 | tf_op jit(solution)/shard_map/ppermute | solution.py:493
  45.3 6.1 %collective-permute-start.11 = (f32[176,128]{1,0:T(8,128)S(1)}, f32[176,128]{1,0:T(8,128)S(1)}, u32[]{:S(2)}, u32[]{:S(2)}) collective-permute-start(f32[176,128]{1,0:T(8,128)S(1)} %get-tuple-element.87), channel_id=1, source_target_pairs={{0,0},{1,2},{2,1},{3,3},{4,4},{5,6},{6,5},{7,7},{8,8},{9,10},{10,9... | collective-permute-start | bytes 270344 | tf_op jit(solution)/shard_map/ppermute | solution.py:493

commit v6 on v5

--- a/solution.py
+++ b/solution.py
@@ -216,7 +216,7 @@
                 across, low_cols, high_cols, plastic, pack_low, pack_high, pack_next, pack_last):
     layers, rows, cols = stress.shape
     total = rows + REACH
-    step_rows = 2 * REACH
+    step_rows = 4 * REACH
     steps = rows // step_rows
 
     @pl.when(turn[0] == 0)
@@ -448,14 +448,14 @@
             above_sum, above_diff = both, diff
 
     def step(index, carry):
-        for inner in range(2):
-            layer_step(2 * index + inner)
-        for inner in range(2):
-            for copy in copies(2 * index + inner):
+        for inner in range(4):
+            layer_step(4 * index + inner)
+        for inner in range(4):
+            for copy in copies(4 * index + inner):
                 copy.start()
         return carry
 
-    lax.fori_loop(0, layers // 2, step, 0)
+    lax.fori_loop(0, layers // 4, step, 0)
 
     def drain(layer, carry):
         for copy in copies(layer):
@@ -488,8 +488,8 @@
     results = []
     for start, value in ((0, even), (1, odd)):
         partner = list(range(count))
-        for low in range(start, count - 1, 2):
-            partner[low], partner[low + 1] = low + 1, low
+        for low in range(start, count + start - 1, 2):
+            partner[low], partner[(low + 1) % count] = (low + 1) % count, low
         results.append(lax.ppermute(value, axis, list(enumerate(partner))))
     return results
 

time: 55 us -> 50.6 us (0.920)
  the two profiles are of different devices: /device:TPU:3 before, /device:TPU:0 now
where the time goes in v6:
time: 50.6 us; the launch traced here: 50.4 us
  Pallas kernels  24.3 us (48%)
  starting transfers between devices  19 us (38%)
  waiting for transfers between devices  6.26 us (12%)
  between operations  0.84 us (2%)
    pallas_call x13, Pallas kernels, call(): pl.pallas_call(kernel, out_shape=shapes, in_specs=[pl.BlockSpec(memory_sp...  24.3 us
    ppermute x12, starting transfers between devices, exchange(): results.append(lax.ppermute(value, axis, list(enumerate(partner))))  19 us
    ppermute x12, waiting for transfers between devices, exchange(): results.append(lax.ppermute(value, axis, list(enumerate(partner))))  6.26 us
  transfers between devices with their start and end apart: 12, of which 5 were waited for; matrix products, arithmetic and copies ran while one was open for 0% of the time, Pallas kernels for 28%

profile of v6, /device:TPU:0, one launch (start us, length us, event | category | flops | bytes accessed | tf_op | source)
XLA Modules:
  0.0 50.4 jit_solution(1219471924499955072)
XLA Ops:
  0.6 0.0 copy-start
  0.6 0.0 copy-start.1
  0.7 0.0 copy-start.3
  0.7 0.0 copy-start.5
  0.7 2.8 %shard_map.139 = (f32[176,128]{1,0:T(8,128)S(1)}, f32[176,128]{1,0:T(8,128)S(1)}, f32[136,128]{1,0:T(8,128)S(1)}, f32[136,128]{1,0:T(8,128)S(1)}, f32[136,128]{1...) custom-call(f32[16,128,128]{2,1,0:T(8,128)} %refs_0_.1, ...), custom_call_target="tpu_custom_call" | custom-call | flops 2500000000 | bytes 2500000 | tf_op jit(solution)/shard_map/pallas_call | solution.py:473
  3.5 3.0 %collective-permute-start = (f32[176,128]{1,0:T(8,128)S(1)}, f32[176,128]{1,0:T(8,128)S(1)}, u32[]{:S(2)}, u32[]{:S(2)}) collective-permute-start(f32[176,128]{1,0:T(8,128)S(1)} %get-tuple-element.56), channel_id=1, source_target_pairs={{0,4},{4,0},{8,12},{12,8},{16,20},{20,16},{24,28},{28,24},{1,5},{5... | collective-permute-start | bytes 270344 | tf_op jit(solution)/shard_map/ppermute | solution.py:493
  6.5 3.6 %collective-permute-start.1 = (f32[176,128]{1,0:T(8,128)S(1)}, f32[176,128]{1,0:T(8,128)S(1)}, u32[]{:S(2)}, u32[]{:S(2)}) collective-permute-start(f32[176,128]{1,0:T(8,128)S(1)} %get-tuple-element.57), channel_id=1, source_target_pairs={{0,28},{4,8},{8,4},{12,16},{16,12},{20,24},{24,20},{28,0},{1,29},{... | collective-permute-start | bytes 270344 | tf_op jit(solution)/shard_map/ppermute | solution.py:493
  10.1 0.0 copy-done
  10.1 0.0 copy-done.1
  10.1 0.0 copy-done.3
  10.1 0.0 copy-done.5
  10.1 2.8 %shard_map.140 = (f32[16,136,128]{2,1,0:T(8,128)S(1)}, f32[136,256]{1,0:T(8,128)S(1)}, f32[136,256]{1,0:T(8,128)S(1)}, f32[16,128,128]{2,1,0:T(8,128)S(1)}) custom-call(s32[1]{0:T(128)} %constant.9.clone.1.turn, f32[16,128,128]{2,1,0:T(8,128)S(1)} %get-tuple-element.46.stress.smooth, f32[16,128,128]{2,1,0:T(8,128)S(1)} %get-tuple-element.47.strain, ...), custom_call_target="tpu_custom_call" | custom-call | flops 4499999744 | bytes 4500000 | tf_op jit(solution)/shard_map/pallas_call | solution.py:473
  12.9 0.0 copy-start.6
  12.9 0.0 collective-permute-done.row_even
  13.0 0.8 %collective-permute-done.1.row_odd = f32[176,128]{1,0:T(8,128)S(1)} collective-permute-done((f32[176,128]{1,0:T(8,128)S(1)}, f32[176,128]{1,0:T(8,128)S(1)}, u32[]{:S(2)}, u32[]{:S(2)}) %collective-permute-start.1) | collective-permute-done | bytes 90144 | tf_op jit(solution)/shard_map/ppermute | solution.py:493
  13.7 0.4 shard_map.141
  14.1 0.0 collective-permute-start.2
  14.1 1.6 %collective-permute-start.3 = (f32[176,128]{1,0:T(8,128)S(1)}, f32[176,128]{1,0:T(8,128)S(1)}, u32[]{:S(2)}, u32[]{:S(2)}) collective-permute-start(f32[176,128]{1,0:T(8,128)S(1)} %get-tuple-element.64), channel_id=1, source_target_pairs={{0,3},{1,2},{2,1},{3,0},{4,7},{5,6},{6,5},{7,4},{8,11},{9,10},{10,... | collective-permute-start | bytes 270344 | tf_op jit(solution)/shard_map/ppermute | solution.py:493
  15.8 0.0 copy-done.6
  15.8 0.0 copy-start.2
  15.8 0.0 copy-start.4
  15.8 1.1 %shard_map.142 = (f32[16,128,128]{2,1,0:T(8,128)S(1)}, f32[16,8,128]{2,1,0:T(8,128)S(1)}) custom-call(f32[16,136,128]{2,1,0:T(8,128)S(1)} %get-tuple-element.55.across, f32[176,128]{1,0:T(8,128)S(1)} %collective-permute-done.row_even, f32[176,128]{1,0:T(8,128)S(1)} %collective-permute-done.1.row_odd, f32[128,128]{1,0:T(8,128)S(1)} %copy-done.6, ...), custom_call_target="tpu_custom_call" | custom-call | flops 1200000000 | bytes 1200000 | tf_op jit(solution)/shard_map/pallas_call | solution.py:473
  16.8 0.0 collective-permute-done.2.col_even
  16.9 1.7 %collective-permute-done.3.col_odd = f32[176,128]{1,0:T(8,128)S(1)} collective-permute-done((f32[176,128]{1,0:T(8,128)S(1)}, f32[176,128]{1,0:T(8,128)S(1)}, u32[]{:S(2)}, u32[]{:S(2)}) %collective-permute-start.3) | collective-permute-done | bytes 90144 | tf_op jit(solution)/shard_map/ppermute | solution.py:493
  18.5 0.0 copy-done.2
  18.5 0.0 copy-done.4
  18.5 0.8 %shard_map.144 = (f32[176,128]{1,0:T(8,128)S(1)}, f32[176,128]{1,0:T(8,128)S(1)}) custom-call(f32[16,128,128]{2,1,0:T(8,128)S(1)} %get-tuple-element.46.stress.smooth, f32[16,128,128]{2,1,0:T(8,128)S(1)} %get-tuple-element.47.strain, s32[16,128,128]{2,1,0:T(8,128)S(1)} %get-tuple-element.48.yields, s32[16,128,128]{2,1,0:T(8,128)S(1)} %get-tuple-element.49.count, ...), custom_call_target="tpu_custom_call" | custom-call | flops 800000000 | bytes 800000 | tf_op jit(solution)/shard_map/pallas_call | solution.py:473
  19.4 0.1 collective-permute-start.4
  19.4 3.7 %collective-permute-start.5 = (f32[176,128]{1,0:T(8,128)S(1)}, f32[176,128]{1,0:T(8,128)S(1)}, u32[]{:S(2)}, u32[]{:S(2)}) collective-permute-start(f32[176,128]{1,0:T(8,128)S(1)} %get-tuple-element.68), channel_id=1, source_target_pairs={{0,28},{4,8},{8,4},{12,16},{16,12},{20,24},{24,20},{28,0},{1,29},{... | collective-permute-start | bytes 270344 | tf_op jit(solution)/shard_map/ppermute | solution.py:493
  23.1 3.6 %shard_map.143 = (f32[16,136,128]{2,1,0:T(8,128)S(1)}, f32[136,256]{1,0:T(8,128)S(1)}, f32[136,256]{1,0:T(8,128)S(1)}, f32[16,128,128]{2,1,0:T(8,128)S(1)}) custom-call(s32[1]{0:T(128)} %constant.8.clone.1.turn, f32[16,128,128]{2,1,0:T(8,128)S(1)} %get-tuple-element.46.stress.smooth, f32[16,128,128]{2,1,0:T(8,128)S(1)} %get-tuple-element.47.strain, ...), custom_call_target="tpu_custom_call" | custom-call | flops 4499999744 | bytes 4500000 | tf_op jit(solution)/shard_map/pallas_call | solution.py:473
  26.7 0.0 collective-permute-done.4.row_even
  26.7 0.4 collective-permute-done.5.row_odd
  27.1 0.4 shard_map.145
  27.5 0.0 collective-permute-start.6
  27.5 1.6 %collective-permute-start.7 = (f32[176,128]{1,0:T(8,128)S(1)}, f32[176,128]{1,0:T(8,128)S(1)}, u32[]{:S(2)}, u32[]{:S(2)}) collective-permute-start(f32[176,128]{1,0:T(8,128)S(1)} %get-tuple-element.75), channel_id=1, source_target_pairs={{0,3},{1,2},{2,1},{3,0},{4,7},{5,6},{6,5},{7,4},{8,11},{9,10},{10,... | collective-permute-start | bytes 270344 | tf_op jit(solution)/shard_map/ppermute | solution.py:493
  29.2 1.1 %shard_map.146 = (f32[16,128,128]{2,1,0:T(8,128)S(1)}, f32[16,8,128]{2,1,0:T(8,128)S(1)}) custom-call(f32[16,136,128]{2,1,0:T(8,128)S(1)} %get-tuple-element.65.across, f32[176,128]{1,0:T(8,128)S(1)} %collective-permute-done.4.row_even, f32[176,128]{1,0:T(8,128)S(1)} %collective-permute-done.5.row_odd, f32[128,128]{1,0:T(8,128)S(1)} %copy-done.6, ...), custom_call_target="tpu_custom_call" | custom-call | flops 1200000000 | bytes 1200000 | tf_op jit(solution)/shard_map/pallas_call | solution.py:473
  30.2 0.0 collective-permute-done.6.col_even
  30.2 1.7 %collective-permute-done.7.col_odd = f32[176,128]{1,0:T(8,128)S(1)} collective-permute-done((f32[176,128]{1,0:T(8,128)S(1)}, f32[176,128]{1,0:T(8,128)S(1)}, u32[]{:S(2)}, u32[]{:S(2)}) %collective-permute-start.7) | collective-permute-done | bytes 90144 | tf_op jit(solution)/shard_map/ppermute | solution.py:493
  31.9 0.8 %shard_map.148 = (f32[176,128]{1,0:T(8,128)S(1)}, f32[176,128]{1,0:T(8,128)S(1)}) custom-call(f32[16,128,128]{2,1,0:T(8,128)S(1)} %get-tuple-element.46.stress.smooth, f32[16,128,128]{2,1,0:T(8,128)S(1)} %get-tuple-element.47.strain, s32[16,128,128]{2,1,0:T(8,128)S(1)} %get-tuple-element.48.yields, s32[16,128,128]{2,1,0:T(8,128)S(1)} %get-tuple-element.49.count, ...), custom_call_target="tpu_custom_call" | custom-call | flops 800000000 | bytes 800000 | tf_op jit(solution)/shard_map/pallas_call | solution.py:473
  32.8 0.1 collective-permute-start.8
  32.8 3.7 %collective-permute-start.9 = (f32[176,128]{1,0:T(8,128)S(1)}, f32[176,128]{1,0:T(8,128)S(1)}, u32[]{:S(2)}, u32[]{:S(2)}) collective-permute-start(f32[176,128]{1,0:T(8,128)S(1)} %get-tuple-element.80), channel_id=1, source_target_pairs={{0,28},{4,8},{8,4},{12,16},{16,12},{20,24},{24,20},{28,0},{1,29},{... | collective-permute-start | bytes 270344 | tf_op jit(solution)/shard_map/ppermute | solution.py:493
  36.5 4.4 %shard_map.147 = (f32[16,136,128]{2,1,0:T(8,128)S(1)}, f32[136,256]{1,0:T(8,128)S(1)}, f32[136,256]{1,0:T(8,128)S(1)}, f32[16,128,128]{2,1,0:T(8,128)S(1)}) custom-call(s32[1]{0:T(128)} %constant.7.clone.1.turn, f32[16,128,128]{2,1,0:T(8,128)S(1)} %get-tuple-element.46.stress.smooth, f32[16,128,128]{2,1,0:T(8,128)S(1)} %get-tuple-element.47.strain, ...), custom_call_target="tpu_custom_call" | custom-call | flops 4499999744 | bytes 4500000 | tf_op jit(solution)/shard_map/pallas_call | solution.py:473
  40.9 0.0 collective-permute-done.8.row_even
  40.9 0.0 collective-permute-done.9.row_odd
  40.9 0.4 shard_map.149
  41.3 0.1 collective-permute-start.10
  41.4 1.6 %collective-permute-start.11 = (f32[176,128]{1,0:T(8,128)S(1)}, f32[176,128]{1,0:T(8,128)S(1)}, u32[]{:S(2)}, u32[]{:S(2)}) collective-permute-start(f32[176,128]{1,0:T(8,128)S(1)} %get-tuple-element.87), channel_id=1, source_target_pairs={{0,3},{1,2},{2,1},{3,0},{4,7},{5,6},{6,5},{7,4},{8,11},{9,10},{10,... | collective-permute-start | bytes 270344 | tf_op jit(solution)/shard_map/ppermute | solution.py:493
  43.0 1.1 %shard_map.150 = (f32[16,128,128]{2,1,0:T(8,128)S(1)}, f32[16,8,128]{2,1,0:T(8,128)S(1)}) custom-call(f32[16,136,128]{2,1,0:T(8,128)S(1)} %get-tuple-element.77.across, f32[176,128]{1,0:T(8,128)S(1)} %collective-permute-done.8.row_even, f32[176,128]{1,0:T(8,128)S(1)} %collective-permute-done.9.row_odd, f32[128,128]{1,0:T(8,128)S(1)} %copy-done.6, ...), custom_call_target="tpu_custom_call" | custom-call | flops 1200000000 | bytes 1200000 | tf_op jit(solution)/shard_map/pallas_call | solution.py:473
  44.1 0.0 collective-permute-done.10.col_even
  44.1 1.7 %collective-permute-done.11.col_odd = f32[176,128]{1,0:T(8,128)S(1)} collective-permute-done((f32[176,128]{1,0:T(8,128)S(1)}, f32[176,128]{1,0:T(8,128)S(1)}, u32[]{:S(2)}, u32[]{:S(2)}) %collective-permute-start.11) | collective-permute-done | bytes 90144 | tf_op jit(solution)/shard_map/ppermute | solution.py:493
  45.8 4.7 %shard_map.151 = (f32[16,128,128]{2,1,0:T(8,128)}, f32[16,128,128]{2,1,0:T(8,128)}, f32[2,16,128,128]{3,2,1,0:T(8,128)}) custom-call(f32[16,128,128]{2,1,0:T(8,128)S(1)} %get-tuple-element.46.stress.smooth, f32[16,128,128]{2,1,0:T(8,128)S(1)} %get-tuple-element.47.strain, f32[16,128,128]{2,1,0:T(8,128)S(1)} %get-tuple-element.76._.plastic, ...), custom_call_target="tpu_custom_call" | custom-call | flops 3000000000 | bytes 3000000 | tf_op jit(solution)/shard_map/pallas_call | solution.py:473
Async XLA Ops:
  0.6 9.4 %copy-start = (f32[128,256]{1,0:T(8,128)S(1)}, f32[128,256]{1,0:T(8,128)}, u32[]{:S(2)}) copy-start(f32[128,256]{1,0:T(8,128)} %constant.25.clone.high_ref) | copy-start | bytes 393220
  0.6 9.4 %copy-start.1 = (f32[128,256]{1,0:T(8,128)S(1)}, f32[128,256]{1,0:T(8,128)}, u32[]{:S(2)}) copy-start(f32[128,256]{1,0:T(8,128)} %constant.24.clone.low_ref) | copy-start | bytes 393220
  0.7 9.4 %copy-start.3 = (f32[128,128]{1,0:T(8,128)S(1)}, f32[128,128]{1,0:T(8,128)}, u32[]{:S(2)}) copy-start(f32[128,128]{1,0:T(8,128)} %constant.26.clone.next_ref) | copy-start | bytes 196612
  0.7 9.4 %copy-start.5 = (f32[136,128]{1,0:T(8,128)S(1)}, f32[136,128]{1,0:T(8,128)}, u32[]{:S(2)}) copy-start(f32[136,128]{1,0:T(8,128)} %constant.22.clone.band_ref) | copy-start | bytes 208900
  3.5 9.5 %collective-permute-start = (f32[176,128]{1,0:T(8,128)S(1)}, f32[176,128]{1,0:T(8,128)S(1)}, u32[]{:S(2)}, u32[]{:S(2)}) collective-permute-start(f32[176,128]{1,0:T(8,128)S(1)} %get-tuple-element.56), channel_id=1, source_target_pairs={{0,4},{4,0},{8,12},{12,8},{16,20},{20,16},{24,28},{28,24},{1,5},{5... | collective-permute-start | bytes 270344 | tf_op jit(solution)/shard_map/ppermute | solution.py:493
  6.5 7.2 %collective-permute-start.1 = (f32[176,128]{1,0:T(8,128)S(1)}, f32[176,128]{1,0:T(8,128)S(1)}, u32[]{:S(2)}, u32[]{:S(2)}) collective-permute-start(f32[176,128]{1,0:T(8,128)S(1)} %get-tuple-element.57), channel_id=1, source_target_pairs={{0,28},{4,8},{8,4},{12,16},{16,12},{20,24},{24,20},{28,0},{1,29},{... | collective-permute-start | bytes 270344 | tf_op jit(solution)/shard_map/ppermute | solution.py:493
  12.9 2.8 %copy-start.6 = (f32[128,128]{1,0:T(8,128)S(1)}, f32[128,128]{1,0:T(8,128)}, u32[]{:S(2)}) copy-start(f32[128,128]{1,0:T(8,128)} %constant.23.clone.band_ref) | copy-start | bytes 196612
  14.1 2.7 %collective-permute-start.2 = (f32[176,128]{1,0:T(8,128)S(1)}, f32[176,128]{1,0:T(8,128)S(1)}, u32[]{:S(2)}, u32[]{:S(2)}) collective-permute-start(f32[176,128]{1,0:T(8,128)S(1)} %get-tuple-element.63), channel_id=1, source_target_pairs={{0,1},{1,0},{2,3},{3,2},{4,5},{5,4},{6,7},{7,6},{8,9},{9,8},{10,11... | collective-permute-start | bytes 270344 | tf_op jit(solution)/shard_map/ppermute | solution.py:493
  14.1 4.4 %collective-permute-start.3 = (f32[176,128]{1,0:T(8,128)S(1)}, f32[176,128]{1,0:T(8,128)S(1)}, u32[]{:S(2)}, u32[]{:S(2)}) collective-permute-start(f32[176,128]{1,0:T(8,128)S(1)} %get-tuple-element.64), channel_id=1, source_target_pairs={{0,3},{1,2},{2,1},{3,0},{4,7},{5,6},{6,5},{7,4},{8,11},{9,10},{10,... | collective-permute-start | bytes 270344 | tf_op jit(solution)/shard_map/ppermute | solution.py:493
  15.8 2.8 %copy-start.2 = (f32[144,256]{1,0:T(8,128)S(1)}, f32[144,256]{1,0:T(8,128)}, u32[]{:S(2)}) copy-start(f32[144,256]{1,0:T(8,128)} %constant.21.clone.above) | copy-start | bytes 442372
  15.8 2.8 %copy-start.4 = (f32[128,128]{1,0:T(8,128)S(1)}, f32[128,128]{1,0:T(8,128)}, u32[]{:S(2)}) copy-start(f32[128,128]{1,0:T(8,128)} %constant.20.clone.below) | copy-start | bytes 196612
  19.4 7.3 %collective-permute-start.4 = (f32[176,128]{1,0:T(8,128)S(1)}, f32[176,128]{1,0:T(8,128)S(1)}, u32[]{:S(2)}, u32[]{:S(2)}) collective-permute-start(f32[176,128]{1,0:T(8,128)S(1)} %get-tuple-element.67), channel_id=1, source_target_pairs={{0,4},{4,0},{8,12},{12,8},{16,20},{20,16},{24,28},{28,24},{1,5},{5... | collective-permute-start | bytes 270344 | tf_op jit(solution)/shard_map/ppermute | solution.py:493
  19.4 7.7 %collective-permute-start.5 = (f32[176,128]{1,0:T(8,128)S(1)}, f32[176,128]{1,0:T(8,128)S(1)}, u32[]{:S(2)}, u32[]{:S(2)}) collective-permute-start(f32[176,128]{1,0:T(8,128)S(1)} %get-tuple-element.68), channel_id=1, source_target_pairs={{0,28},{4,8},{8,4},{12,16},{16,12},{20,24},{24,20},{28,0},{1,29},{... | collective-permute-start | bytes 270344 | tf_op jit(solution)/shard_map/ppermute | solution.py:493
  27.5 2.7 %collective-permute-start.6 = (f32[176,128]{1,0:T(8,128)S(1)}, f32[176,128]{1,0:T(8,128)S(1)}, u32[]{:S(2)}, u32[]{:S(2)}) collective-permute-start(f32[176,128]{1,0:T(8,128)S(1)} %get-tuple-element.74), channel_id=1, source_target_pairs={{0,1},{1,0},{2,3},{3,2},{4,5},{5,4},{6,7},{7,6},{8,9},{9,8},{10,11... | collective-permute-start | bytes 270344 | tf_op jit(solution)/shard_map/ppermute | solution.py:493
  27.5 4.4 %collective-permute-start.7 = (f32[176,128]{1,0:T(8,128)S(1)}, f32[176,128]{1,0:T(8,128)S(1)}, u32[]{:S(2)}, u32[]{:S(2)}) collective-permute-start(f32[176,128]{1,0:T(8,128)S(1)} %get-tuple-element.75), channel_id=1, source_target_pairs={{0,3},{1,2},{2,1},{3,0},{4,7},{5,6},{6,5},{7,4},{8,11},{9,10},{10,... | collective-permute-start | bytes 270344 | tf_op jit(solution)/shard_map/ppermute | solution.py:493
  32.8 8.2 %collective-permute-start.8 = (f32[176,128]{1,0:T(8,128)S(1)}, f32[176,128]{1,0:T(8,128)S(1)}, u32[]{:S(2)}, u32[]{:S(2)}) collective-permute-start(f32[176,128]{1,0:T(8,128)S(1)} %get-tuple-element.79), channel_id=1, source_target_pairs={{0,4},{4,0},{8,12},{12,8},{16,20},{20,16},{24,28},{28,24},{1,5},{5... | collective-permute-start | bytes 270344 | tf_op jit(solution)/shard_map/ppermute | solution.py:493
  32.8 8.1 %collective-permute-start.9 = (f32[176,128]{1,0:T(8,128)S(1)}, f32[176,128]{1,0:T(8,128)S(1)}, u32[]{:S(2)}, u32[]{:S(2)}) collective-permute-start(f32[176,128]{1,0:T(8,128)S(1)} %get-tuple-element.80), channel_id=1, source_target_pairs={{0,28},{4,8},{8,4},{12,16},{16,12},{20,24},{24,20},{28,0},{1,29},{... | collective-permute-start | bytes 270344 | tf_op jit(solution)/shard_map/ppermute | solution.py:493
  41.3 2.7 %collective-permute-start.10 = (f32[176,128]{1,0:T(8,128)S(1)}, f32[176,128]{1,0:T(8,128)S(1)}, u32[]{:S(2)}, u32[]{:S(2)}) collective-permute-start(f32[176,128]{1,0:T(8,128)S(1)} %get-tuple-element.86), channel_id=1, source_target_pairs={{0,1},{1,0},{2,3},{3,2},{4,5},{5,4},{6,7},{7,6},{8,9},{9,8},{10,11... | collective-permute-start | bytes 270344 | tf_op jit(solution)/shard_map/ppermute | solution.py:493
  41.4 4.3 %collective-permute-start.11 = (f32[176,128]{1,0:T(8,128)S(1)}, f32[176,128]{1,0:T(8,128)S(1)}, u32[]{:S(2)}, u32[]{:S(2)}) collective-permute-start(f32[176,128]{1,0:T(8,128)S(1)} %get-tuple-element.87), channel_id=1, source_target_pairs={{0,3},{1,2},{2,1},{3,0},{4,7},{5,6},{6,5},{7,4},{8,11},{9,10},{10,... | collective-permute-start | bytes 270344 | tf_op jit(solution)/shard_map/ppermute | solution.py:493

commit v7 on v6

--- a/solution.py
+++ b/solution.py
@@ -114,22 +114,34 @@
     odd_ref[...] = jnp.where(on_even(axis), low, high)
 
 
-def add_columns(value, layer, low, high):
-    cols = value.shape[1]
-    slots = lane_ids(value.shape) >> (REACH.bit_length() - 1)
+def layer_slots(shape):
+    return lane_ids(shape) >> (REACH.bit_length() - 1)
+
+
+def ratio(limit):
+    return jnp.exp2(jnp.minimum(limit, 0.0) * RATE)
+
+
+def edge_ratios(edges, received, norms, part, extended):
+    both = sides("gy", *(ref[part, :] for ref in received))
+    return [
+        ratio(edge[extended, :] - value * norm[extended, :])
+        for edge, value, norm in zip(edges, both, norms)
+    ]
+
+
+def with_edges(inner, layer, low, high):
+    cols = inner.shape[1]
+    slots = layer_slots(inner.shape)
     packed = jnp.where(slots == layer, low, high)
     shift = (cols - layer * REACH) % cols
     moved = packed if isinstance(layer, int) and layer == 0 else pltpu.roll(packed, shift, 1)
-    return value + jnp.where((slots == 0) | (slots == cols // REACH - 1), moved, 0.0)
-
-
-def retained(full, norm, threshold):
-    return jnp.exp2(jnp.minimum(threshold - full * norm, 0.0) * RATE)
+    return jnp.where((slots == 0) | (slots == cols // REACH - 1), moved, inner)
 
 
 def first_edge_kernel(*refs):
     sources, refs = refs[:5], refs[5:]
-    even_ref, odd_ref, norm, norm_last, norm_before, _, _, *refs = refs
+    even_ref, odd_ref, norm, norm_low, norm_high, norm_last, norm_before, _, _, _, *refs = refs
     targets, (block, sems) = refs[:5], refs[5:]
     stress, strain, yields, count, _ = targets
     layers, rows, cols = stress.shape
@@ -147,7 +159,9 @@
     ids = lax.broadcasted_iota(jnp.int32, (total, cols), 0)
     down = inverse_weights("gx", ids - REACH, rows)
     lanes = lane_ids((REACH, cols))
-    for ref, place in ((norm, lanes), (norm_last, 0 * lanes + (cols - 1)), (norm_before, 0 * lanes - 1)):
+    within = lanes & (REACH - 1)
+    places = (lanes, within, within + (cols - REACH), 0 * lanes + (cols - 1), 0 * lanes - 1)
+    for ref, place in zip((norm, norm_low, norm_high, norm_last, norm_before), places):
         ref[...] = down * inverse_weights("gy", place, cols)[:1]
     square = (layers * REACH, layers * REACH)
     line, lane = lax.broadcasted_iota(jnp.int32, square, 0), lane_ids(square)
@@ -157,7 +171,6 @@
         band_part = jnp.where(abs(steps) == step, tap(REACH - step), band_part)
     band_part = jnp.where((line ^ lane) < REACH, band_part, 0.0)
     sent = []
-    extra = jnp.zeros((even_ref.shape[0] - layers * REACH, cols), jnp.float32)
     for side, matrix in enumerate(
         (jnp.where(steps <= 0, band_part, 0.0), jnp.where(steps >= 0, band_part, 0.0))
     ):
@@ -168,36 +181,37 @@
             block[pl.ds(layer * REACH, REACH), :] = newton(
                 stress[at], strain[at], yields[at], count[at], jnp.ones((REACH, cols), jnp.float32)
             )
-        product = left_product(left_constant(matrix), block[...])
-        sent.append(jnp.concatenate([product, extra], axis=0))
+        sent.append(left_product(left_constant(matrix), block[...]))
     send("gx", *sent, even_ref, odd_ref)
     for copy in copies[10:]:
         copy.wait()
 
 
-def edge_kernel(stress, strain, yields, count, threshold, smooth, _, col_even, col_odd, norm,
-                below, above, even_ref, odd_ref, low_block, high_block, rest):
+def edge_kernel(stress, strain, yields, count, threshold, kept, _, edge_low, edge_high, norm_low,
+                norm_high, col_even, col_odd, below, above,
+                even_ref, odd_ref, low_block, high_block, rest):
     layers, rows, cols = stress.shape
     starts = (0, rows - 2 * REACH, rows - REACH)
-    received = []
-    for first_row in starts:
-        part = pl.ds(first_row + REACH, REACH)
-        received.append(sides("gy", col_even[part, :], col_odd[part, :]))
+    packed = [
+        edge_ratios(
+            (edge_low, edge_high), (col_even, col_odd), (norm_low, norm_high),
+            pl.ds(first_row, REACH), pl.ds(first_row + REACH, REACH),
+        )
+        for first_row in starts
+    ]
 
     def layer_step(layer):
         for index, first_row in enumerate(starts):
             at = (layer, pl.ds(first_row, REACH), slice(None))
-            extended = pl.ds(first_row + REACH, REACH)
-            full = add_columns(smooth[at], layer, *received[index])
-            soften = 0.5 + 0.5 * retained(full, norm[extended, :], threshold[at])
+            soften = 0.5 + 0.5 * with_edges(kept[at], layer, *packed[index])
             value = newton(stress[at], strain[at], yields[at], count[at], soften)
             if index == 0:
                 low_block[pl.ds(layer * REACH, REACH), :] = value
             else:
                 high_block[pl.ds((2 * layer + index - 1) * REACH, REACH), :] = value
             if index == 2:
-                kept = (stress[at] + strain[at]) - value
-                rest[pl.ds(layer, 1), :] = kept[REACH - 1 :]
+                left = (stress[at] + strain[at]) - value
+                rest[pl.ds(layer, 1), :] = left[REACH - 1 :]
                 rest[pl.ds(layers + layer, 1), :] = threshold[at][REACH - 1 :]
 
     for layer in range(layers):
@@ -211,8 +225,8 @@
     )
 
 
-def main_kernel(turn, stress, strain, yields, count, threshold, smooth, col_even, col_odd, norm,
-                norm_last, band_ref, low_ref, high_ref, next_ref,
+def main_kernel(turn, stress, strain, yields, count, threshold, kept, edge_low, edge_high, norm_low,
+                norm_high, col_even, col_odd, norm_last, band_ref, low_ref, high_ref, next_ref,
                 across, low_cols, high_cols, plastic, pack_low, pack_high, pack_next, pack_last):
     layers, rows, cols = stress.shape
     total = rows + REACH
@@ -236,18 +250,19 @@
         def step(index, carry):
             part = pl.ds(pl.multiple_of(index * step_rows, step_rows), step_rows)
             extended = pl.ds(pl.multiple_of(index * step_rows + REACH, REACH), step_rows)
-            low, high = sides("gy", col_even[extended, :], col_odd[extended, :])
+            packed = edge_ratios(
+                (edge_low, edge_high), (col_even, col_odd), (norm_low, norm_high), part, extended
+            )
             for layer in range(layers):
                 at = (layer, part, slice(None))
-                full = add_columns(smooth[at], layer, low, high)
-                soften = 0.5 + 0.5 * retained(full, norm[extended, :], threshold[at])
+                soften = 0.5 + 0.5 * with_edges(kept[at], layer, *packed)
                 plastic[at] = newton(stress[at], strain[at], yields[at], count[at], soften)
             return carry
 
         lax.fori_loop(0, steps, step, 0)
 
     constant = left_constant(band_ref[...])
-    slots = lane_ids((total, cols)) >> (REACH.bit_length() - 1)
+    slots = layer_slots((total, cols))
     for layer in range(0, layers, 2):
         pair = jnp.concatenate([plastic[layer], plastic[layer + 1]], axis=1)
         result = left_product(constant, pair)
@@ -289,7 +304,7 @@
 def pack_edges(values):
     cols = values[0].shape[1]
     count = cols // REACH
-    slots = lane_ids(values[0].shape) >> (REACH.bit_length() - 1)
+    slots = layer_slots(values[0].shape)
     low = high = ahead = jnp.zeros_like(values[0])
     for layer, value in enumerate(values):
         moved = pltpu.roll(value, layer * REACH, 1) if layer else value
@@ -299,16 +314,15 @@
     return low, high, ahead
 
 
-def corner_kernel(row_even, row_odd, low_cols, high_cols, norm_last, _, low_ref, high_ref, next_ref,
+def corner_kernel(row_even, row_odd, rest_even, rest_odd, low_cols, high_cols, norm_last, _, low_ref, high_ref, next_ref,
                   even_ref, odd_ref, own_ref):
     cols = low_ref.shape[0]
     total = low_cols.shape[0]
     layers = (total - REACH) // REACH
     strip = layers * REACH
     from_low, from_high = sides("gx", row_even[...], row_odd[...])
-    partial = from_low[strip : strip + layers]
-    kept = from_low[strip + layers : strip + 2 * layers]
-    limit = from_low[strip + 2 * layers : strip + 3 * layers]
+    rest, _ = sides("gx", rest_even[...], rest_odd[...])
+    partial, kept, limit = rest[:layers], rest[layers : 2 * layers], rest[2 * layers :]
     before = [jnp.broadcast_to(partial[layer : layer + 1], (REACH, cols)) for layer in range(layers)]
     packs = [pack_edges(before)] + [
         pack_edges([block[layer * REACH : (layer + 1) * REACH] for layer in range(layers)])
@@ -350,15 +364,16 @@
         folded = jnp.where(lanes // (2 * layers) == part, moved, folded)
     extra = jnp.zeros((quarter + REACH, cols), jnp.float32)
     send(
-        "gy", jnp.concatenate([low_all[:, :cols], extra], axis=0),
-        jnp.concatenate([high_all, folded, first], axis=0), even_ref, odd_ref,
+        "gy", jnp.concatenate([low_all[REACH:, :cols], low_all[:REACH, :cols], extra], axis=0),
+        jnp.concatenate([high_all[REACH:], high_all[:REACH], folded, first], axis=0),
+        even_ref, odd_ref,
     )
     own_ref[...] = low_all[:, cols:]
 
 
-def column_kernel(depth, across, row_even, row_odd, band_ref, _, smooth, before, deep):
+def column_kernel(depth, across, row_even, row_odd, rest_even, rest_odd, threshold, norm, band_ref, _,
+                  kept, kept_before, edge_low, edge_high, deep):
     layers, total, cols = across.shape
-    strip = layers * REACH
 
     def depth_sums(part, values):
         for layer, value in enumerate(depth_smooth(values, depth)):
@@ -375,35 +390,44 @@
         part = pl.ds(first_row, REACH)
         values = []
         for layer in range(layers):
-            line = pl.ds(strip + layer, 1) if first_row == 0 else pl.ds(layer * REACH, REACH)
-            both = sides("gx", row_even[line, :], row_odd[line, :])
+            if first_row:
+                line = pl.ds(layer * REACH, REACH)
+                both = sides("gx", row_even[line, :], row_odd[line, :])
+            else:
+                both = sides("gx", rest_even[pl.ds(layer, 1), :], rest_odd[pl.ds(layer, 1), :])
             values.append(across[layer, part, :] + both[first_row > REACH])
         depth_sums(part, values)
+
     constant = right_constant(band_ref[...])
+    slots = layer_slots((total, cols))
     for layer in range(layers):
-        result = right_product(deep[layer], constant)
-        before[layer] = result[:REACH]
-        smooth[layer] = result[REACH:]
-
-
-def final_kernel(stress, strain, plastic, threshold, smooth, before, col_even, col_odd, row_even, row_odd,
-                 norm, norm_before, own_cols, plastic_out, damage_out, force_out,
-                 columns, damage_s, force_s, copy_sem, sems):
+        nonlocal_strain = right_product(deep[layer], constant) * norm[...]
+        line = pl.ds(2 * layers + layer, 1)
+        limit, _ = sides("gx", rest_even[line, :], rest_odd[line, :])
+        first = limit - nonlocal_strain[:REACH]
+        others = threshold[layer] - nonlocal_strain[REACH:]
+        kept_before[layer] = ratio(first)
+        kept[layer] = ratio(others)
+        moved = jnp.concatenate([first, others], axis=0)
+        moved = pltpu.roll(moved, layer * REACH, 1) if layer else moved
+        pltpu.store(edge_low, moved, mask=slots == layer)
+        pltpu.store(edge_high, moved, mask=slots == (layer - 1) % (cols // REACH))
+
+
+def final_kernel(stress, strain, plastic, inner, inner_before, edge_low, edge_high, norm_low, norm_high,
+                 col_even, col_odd, last_even, last_odd, rest_even, rest_odd, norm_before, own_cols,
+                 plastic_out, damage_out, force_out, columns, damage_s, force_s, copy_sem, sems):
     layers, rows, cols = stress.shape
-    total = rows + REACH
-    strip = layers * REACH
     whole = pltpu.make_async_copy(plastic, plastic_out, copy_sem)
     whole.start()
 
-    from_low, _ = sides("gy", col_even[...], col_odd[...])
-    quarter = rows // 4
-    folded = from_low[total : total + quarter]
-    pieces = [from_low[total + quarter :], folded]
+    from_low, _ = sides("gy", last_even[...], last_odd[...])
+    folded = from_low[REACH : REACH + rows // 4]
+    pieces = [from_low[REACH + rows // 4 :], folded]
     for part in range(1, 4):
         pieces.append(pltpu.roll(folded, cols - part * 2 * layers, 1))
     column = jnp.concatenate(pieces, axis=0)
-    limit = column - own_cols[...] * norm_before[...]
-    kept = jnp.exp2(jnp.minimum(limit, 0.0) * RATE)
+    kept = ratio(column - own_cols[...] * norm_before[...])
     columns[...] = kept * pltpu.roll(column, cols - layers, 1)
 
     def copies(layer):
@@ -419,21 +443,19 @@
         above_sum = above_diff = None
         for block in range(rows // REACH + 1):
             extended = pl.ds(block * REACH, REACH)
-            low, high = sides("gy", col_even[extended, :], col_odd[extended, :])
-            if block == 0:
-                summed = before[layer]
-                line = pl.ds(strip + layers + layer, 1)
-                rest, _ = sides("gx", row_even[line, :], row_odd[line, :])
-                line = pl.ds(strip + 2 * layers + layer, 1)
-                limit, _ = sides("gx", row_even[line, :], row_odd[line, :])
+            part = pl.ds((block - 1) * REACH if block else 0, REACH)
+            received = (col_even, col_odd) if block else (last_even, last_odd)
+            packed = edge_ratios(
+                (edge_low, edge_high), received, (norm_low, norm_high), part, extended
+            )
+            at = (layer, part, slice(None))
+            if block:
+                rest = (stress[at] + strain[at]) - plastic[at]
             else:
-                at = (layer, pl.ds((block - 1) * REACH, REACH), slice(None))
-                rest = (stress[at] + strain[at]) - plastic[at]
-                limit = threshold[at]
-                summed = smooth[at]
-            full = add_columns(summed, layer, low, high)
-            ratio = retained(full, norm[extended, :], limit)
-            value = ratio * rest
+                line = pl.ds(layers + layer, 1)
+                rest, _ = sides("gx", rest_even[line, :], rest_odd[line, :])
+            kept = with_edges(inner[at] if block else inner_before[layer], layer, *packed)
+            value = kept * rest
             left = jnp.where(
                 lanes == 0,
                 pltpu.roll(columns[extended, :], (cols - layer) % cols, 1),
@@ -442,20 +464,20 @@
             both = pltpu.roll(left + value, 1, 0)
             diff = pltpu.roll(left - value, 1, 0)
             if block:
-                damage_s[at] = 1.0 - ratio
+                damage_s[at] = 1.0 - kept
                 force_s[(0, *at)] = 0.5 * (jnp.where(top, above_sum, both) - (left + value))
                 force_s[(1, *at)] = 0.5 * (jnp.where(top, above_diff, diff) + (left - value))
             above_sum, above_diff = both, diff
 
     def step(index, carry):
-        for inner in range(4):
-            layer_step(4 * index + inner)
-        for inner in range(4):
-            for copy in copies(4 * index + inner):
+        for near in range(2):
+            layer_step(2 * index + near)
+        for near in range(2):
+            for copy in copies(2 * index + near):
                 copy.start()
         return carry
 
-    lax.fori_loop(0, layers // 4, step, 0)
+    lax.fori_loop(0, layers // 2, step, 0)
 
     def drain(layer, carry):
         for copy in copies(layer):
@@ -483,14 +505,24 @@
     )(*operands)
 
 
-def exchange(axis, even, odd):
-    count = lax.axis_size(axis)
+def exchange(axis, other, even, odd):
+    names = ("gx", "gy")
+    count, across = lax.axis_size(axis), lax.axis_size(other)
+    stride = {"gx": lax.axis_size("gy"), "gy": 1}
     results = []
     for start, value in ((0, even), (1, odd)):
-        partner = list(range(count))
-        for low in range(start, count + start - 1, 2):
-            partner[low], partner[(low + 1) % count] = (low + 1) % count, low
-        results.append(lax.ppermute(value, axis, list(enumerate(partner))))
+        pairs = []
+        for place in range(count):
+            partner = place + 1 if (place - start) % 2 == 0 else place - 1
+            for line in range(across):
+                target = (partner, line)
+                if not 0 <= partner < count:
+                    target = (place, line ^ 1 if line ^ 1 < across else line)
+                pairs.append((
+                    place * stride[axis] + line * stride[other],
+                    target[0] * stride[axis] + target[1] * stride[other],
+                ))
+        results.append(lax.ppermute(value, names, pairs))
     return results
 
 
@@ -538,51 +570,66 @@
     depth, constants = matrices(layers, rows, cols)
     below, above, rows_band, cols_band, *columns = constants
 
-    whole, wide = (layers, rows, cols), (layers, total, cols)
+    whole, wide, top = (layers, rows, cols), (layers, total, cols), (layers, REACH, cols)
     sent_rows = (strip + 3 * layers, cols)
     sent_cols = (total + rows // 4 + REACH, cols)
+    spare = (3 * layers, cols)
     packed, packed_two = (total, cols), (total, 2 * cols)
 
     sources = (trial_stress, old_strain, yield_mask, newton_count, damage_threshold)
-    row_even, row_odd, norm, norm_last, norm_before, col_even, col_odd, *inputs = call(
+    row_even, row_odd, norm, norm_low, norm_high, norm_last, norm_before, col_even, col_odd, rest, *inputs = call(
         first_edge_kernel,
-        [sent_rows, sent_rows, packed, packed, packed, sent_cols, sent_cols]
+        [(strip, cols)] * 2 + [packed] * 5 + [(rows, cols)] * 2 + [spare]
         + [jax.ShapeDtypeStruct(whole, source.dtype) for source in sources],
         [(strip, cols), pltpu.SemaphoreType.DMA((3, len(sources)))], 2500,
         sources, [pltpu.HBM] * len(sources), limit=FIRST_VMEM_BYTES,
     )
     stress, strain, _, _, threshold = inputs
-    smooth = stress
+    kept, edge_low, edge_high, norms = stress, norm_low, norm_high, (norm_low, norm_high)
+    rest_even = rest_odd = rest
     for outer_no in range(OUTER):
+        last = outer_no == OUTER - 1
         if outer_no:
             row_even, row_odd = call(
                 edge_kernel, [sent_rows] * 2,
                 [(strip, cols), (2 * strip, cols), (2 * layers, cols)], 800,
-                (*inputs, smooth, before, col_even, col_odd, norm, below, above),
+                (*inputs, kept, kept_before, edge_low, edge_high, *norms, col_even, col_odd,
+                 below, above),
             )
-        row_even, row_odd = exchange("gx", row_even, row_odd)
+        if not last:
+            row_even, row_odd = row_even[:strip], row_odd[:strip]
+        row_even, row_odd = exchange("gx", "gy", row_even, row_odd)
+        if last:
+            rest_even, rest_odd = row_even[strip:], row_odd[strip:]
+            row_even, row_odd = row_even[:strip], row_odd[:strip]
         turn = jnp.full((1,), outer_no, jnp.int32)
         across, low_cols, high_cols, plastic = call(
             main_kernel, [wide, packed_two, packed_two, whole],
             [packed, packed, packed, packed], 4500,
-            (turn, *inputs, smooth, col_even, col_odd, norm, norm_last, rows_band, *columns),
-            [pltpu.SMEM] + [pltpu.VMEM] * 14,
+            (turn, *inputs, kept, edge_low, edge_high, *norms, col_even, col_odd, norm_last,
+             rows_band, *columns),
+            [pltpu.SMEM] + [pltpu.VMEM] * 17,
         )
         col_even, col_odd, own_cols = call(
             corner_kernel, [sent_cols, sent_cols, packed], [], 400,
-            (row_even, row_odd, low_cols, high_cols, norm_last, plastic, *columns),
+            (row_even, row_odd, rest_even, rest_odd, low_cols, high_cols, norm_last, plastic, *columns),
         )
-        col_even, col_odd = exchange("gy", col_even, col_odd)
-        smooth, before = call(
-            functools.partial(column_kernel, depth), [whole, (layers, REACH, cols)], [wide], 1200,
-            (across, row_even, row_odd, cols_band, own_cols),
+        if not last:
+            col_even, col_odd = col_even[:rows], col_odd[:rows]
+        col_even, col_odd = exchange("gy", "gx", col_even, col_odd)
+        if last:
+            last_even, last_odd = col_even[rows:], col_odd[rows:]
+            col_even, col_odd = col_even[:rows], col_odd[:rows]
+        kept, kept_before, edge_low, edge_high = call(
+            functools.partial(column_kernel, depth), [whole, top, packed, packed], [wide], 1800,
+            (across, row_even, row_odd, rest_even, rest_odd, threshold, norm, cols_band, own_cols),
         )
     return tuple(call(
         final_kernel, [whole, whole, (2, *whole)],
         [packed, whole, (2, *whole), pltpu.SemaphoreType.DMA(()), pltpu.SemaphoreType.DMA((3, layers))],
         3000,
-        (stress, strain, plastic, threshold, smooth, before, col_even, col_odd,
-         row_even, row_odd, norm, norm_before, own_cols),
+        (stress, strain, plastic, kept, kept_before, edge_low, edge_high, *norms, col_even, col_odd,
+         last_even, last_odd, rest_even, rest_odd, norm_before, own_cols),
         outs_space=pltpu.HBM,
     ))
 

time: 50.6 us -> 43.9 us (0.87)
  starting transfers between devices: 19 us -> 15.4 us
  waiting for transfers between devices: 6.26 us -> 4.48 us
  Pallas kernels: 24.3 us -> 22.8 us
    ppermute x12, starting transfers between devices: 19 us -> 15.4 us  [exchange(): results.append(lax.ppermute(value, names, pairs))]
    ppermute x12, waiting for transfers between devices: 6.26 us -> 4.48 us  [exchange(): results.append(lax.ppermute(value, names, pairs))]
    pallas_call x13, Pallas kernels: 24.3 us -> 22.8 us  [call(): pl.pallas_call(kernel, out_shape=shapes, in_specs=[pl.BlockSpec(memory_sp...]
  transfers between devices with their start and end apart: 12 -> 12, of which waited for: 5 -> 4; matrix products, arithmetic and copies ran while one was open for 0% -> 0% of each run, Pallas kernels for 28% -> 32%
where the time goes in v7:
time: 43.9 us; the launch traced here: 43.7 us
  Pallas kernels  22.8 us (52%)
  starting transfers between devices  15.4 us (35%)
  waiting for transfers between devices  4.48 us (10%)
  between operations  0.91 us (2%)
    pallas_call x13, Pallas kernels, call(): pl.pallas_call(kernel, out_shape=shapes, in_specs=[pl.BlockSpec(memory_sp...  22.8 us
    ppermute x12, starting transfers between devices, exchange(): results.append(lax.ppermute(value, names, pairs))  15.4 us
    ppermute x12, waiting for transfers between devices, exchange(): results.append(lax.ppermute(value, names, pairs))  4.48 us
  transfers between devices with their start and end apart: 12, of which 4 were waited for; matrix products, arithmetic and copies ran while one was open for 0% of the time, Pallas kernels for 32%

profile of v7, /device:TPU:0, one launch (start us, length us, event | category | flops | bytes accessed | tf_op | source)
XLA Modules:
  0.0 43.7 jit_solution(15410524847676660799)
XLA Ops:
  0.6 0.0 copy-start
  0.6 0.0 copy-start.1
  0.7 0.0 copy-start.3
  0.7 0.0 copy-start.5
  0.7 2.8 %shard_map.139 = (f32[128,128]{1,0:T(8,128)S(1)}, f32[128,128]{1,0:T(8,128)S(1)}, f32[136,128]{1,0:T(8,128)S(1)}, f32[136,128]{1,0:T(8,128)S(1)}, f32[136,128]{1...) custom-call(f32[16,128,128]{2,1,0:T(8,128)} %refs_0_.1, ...), custom_call_target="tpu_custom_call" | custom-call | flops 2500000000 | bytes 2500000 | tf_op jit(solution)/shard_map/pallas_call | solution.py:495
  3.5 3.0 %collective-permute-start = (f32[128,128]{1,0:T(8,128)S(1)}, f32[128,128]{1,0:T(8,128)S(1)}, u32[]{:S(2)}, u32[]{:S(2)}) collective-permute-start(f32[128,128]{1,0:T(8,128)S(1)} %get-tuple-element.66), channel_id=1, source_target_pairs={{0,4},{1,5},{2,6},{3,7},{4,0},{5,1},{6,2},{7,3},{8,12},{9,13},{10,... | collective-permute-start | bytes 196616 | tf_op jit(solution)/shard_map/ppermute | solution.py:525
  6.5 0.0 collective-permute-start.1
  6.5 0.0 copy-done
  6.5 0.0 copy-done.1
  6.5 0.0 copy-done.3
  6.5 0.0 copy-done.5
  6.5 2.8 %shard_map.140 = (f32[16,136,128]{2,1,0:T(8,128)S(1)}, f32[136,256]{1,0:T(8,128)S(1)}, f32[136,256]{1,0:T(8,128)S(1)}, f32[16,128,128]{2,1,0:T(8,128)S(1)}) custom-call(s32[1]{0:T(128)} %constant.9.clone.1.turn, f32[16,128,128]{2,1,0:T(8,128)S(1)} %get-tuple-element.55.stress.kept, f32[16,128,128]{2,1,0:T(8,128)S(1)} %get-tuple-element.56.strain, ...), custom_call_target="tpu_custom_call" | custom-call | flops 4499999744 | bytes 4500000 | tf_op jit(solution)/shard_map/pallas_call | solution.py:495
  9.4 0.0 copy-start.6
  9.4 0.2 collective-permute-done.row_even
  9.6 0.0 collective-permute-done.1.row_odd
  9.6 0.4 shard_map.141
  10.0 2.9 %collective-permute-start.3 = (f32[128,128]{1,0:T(8,128)S(1)}, f32[128,128]{1,0:T(8,128)S(1)}, u32[]{:S(2)}, u32[]{:S(2)}) collective-permute-start(f32[128,128]{1,0:T(8,128)S(1)} %slice.43), channel_id=1, source_target_pairs={{0,4},{4,0},{8,12},{12,8},{16,20},{20,16},{24,28},{28,24},{1,2},{5... | collective-permute-start | bytes 196616 | tf_op jit(solution)/shard_map/ppermute | solution.py:525
  12.9 0.0 collective-permute-start.2
  12.9 0.0 copy-done.6
  12.9 0.0 copy-start.2
  12.9 0.0 copy-start.4
  12.9 1.2 %shard_map.142 = (f32[16,128,128]{2,1,0:T(8,128)S(1)}, f32[16,8,128]{2,1,0:T(8,128)S(1)}, f32[136,128]{1,0:T(8,128)S(1)}, f32[136,128]{1,0:T(8,128)S(1)}) custom-call(f32[16,136,128]{2,1,0:T(8,128)S(1)} %get-tuple-element.65.across, f32[128,128]{1,0:T(8,128)S(1)} %collective-permute-done.row_even, f32[128,128]{1,0:T(8,128)S(1)} %collective-permute-done.1.row_odd, ...), custom_call_target="tpu_custom_call" | custom-call | flops 1800000000 | bytes 1800000 | tf_op jit(solution)/shard_map/pallas_call | solution.py:495
  14.1 1.0 %collective-permute-done.3.col_odd = f32[128,128]{1,0:T(8,128)S(1)} collective-permute-done((f32[128,128]{1,0:T(8,128)S(1)}, f32[128,128]{1,0:T(8,128)S(1)}, u32[]{:S(2)}, u32[]{:S(2)}) %collective-permute-start.3) | collective-permute-done | bytes 65568 | tf_op jit(solution)/shard_map/ppermute | solution.py:525
  15.1 0.0 collective-permute-done.2.col_even
  15.1 0.0 copy-done.2
  15.2 0.0 copy-done.4
  15.2 0.8 %shard_map.144 = (f32[176,128]{1,0:T(8,128)S(1)}, f32[176,128]{1,0:T(8,128)S(1)}) custom-call(f32[16,128,128]{2,1,0:T(8,128)S(1)} %get-tuple-element.55.stress.kept, f32[16,128,128]{2,1,0:T(8,128)S(1)} %get-tuple-element.56.strain, s32[16,128,128]{2,1,0:T(8,128)S(1)} %get-tuple-element.57.yields, s32[16,128,128]{2,1,0:T(8,128)S(1)} %get-tuple-element.58.count, ...), custom_call_target="tpu_custom_call" | custom-call | flops 800000000 | bytes 800000 | tf_op jit(solution)/shard_map/pallas_call | solution.py:495
  16.0 0.1 collective-permute-start.5
  16.0 4.3 %collective-permute-start.4 = (f32[128,128]{1,0:T(8,128)S(1)}, f32[128,128]{1,0:T(8,128)S(1)}, u32[]{:S(2)}, u32[]{:S(2)}) collective-permute-start(f32[128,128]{1,0:T(8,128)S(1)} %slice.44), channel_id=1, source_target_pairs={{0,4},{1,5},{2,6},{3,7},{4,0},{5,1},{6,2},{7,3},{8,12},{9,13},{10,... | collective-permute-start | bytes 196616 | tf_op jit(solution)/shard_map/ppermute | solution.py:525
  20.3 3.4 %shard_map.143 = (f32[16,136,128]{2,1,0:T(8,128)S(1)}, f32[136,256]{1,0:T(8,128)S(1)}, f32[136,256]{1,0:T(8,128)S(1)}, f32[16,128,128]{2,1,0:T(8,128)S(1)}) custom-call(s32[1]{0:T(128)} %constant.8.clone.1.turn, f32[16,128,128]{2,1,0:T(8,128)S(1)} %get-tuple-element.55.stress.kept, f32[16,128,128]{2,1,0:T(8,128)S(1)} %get-tuple-element.56.strain, ...), custom_call_target="tpu_custom_call" | custom-call | flops 4499999744 | bytes 4500000 | tf_op jit(solution)/shard_map/pallas_call | solution.py:495
  23.7 0.0 collective-permute-done.5.row_odd
  23.7 0.0 collective-permute-done.4.row_even
  23.7 0.4 shard_map.145
  24.1 0.9 %collective-permute-start.7 = (f32[128,128]{1,0:T(8,128)S(1)}, f32[128,128]{1,0:T(8,128)S(1)}, u32[]{:S(2)}, u32[]{:S(2)}) collective-permute-start(f32[128,128]{1,0:T(8,128)S(1)} %slice.47), channel_id=1, source_target_pairs={{0,4},{4,0},{8,12},{12,8},{16,20},{20,16},{24,28},{28,24},{1,2},{5... | collective-permute-start | bytes 196616 | tf_op jit(solution)/shard_map/ppermute | solution.py:525
  25.0 0.2 collective-permute-start.6
  25.3 1.2 %shard_map.146 = (f32[16,128,128]{2,1,0:T(8,128)S(1)}, f32[16,8,128]{2,1,0:T(8,128)S(1)}, f32[136,128]{1,0:T(8,128)S(1)}, f32[136,128]{1,0:T(8,128)S(1)}) custom-call(f32[16,136,128]{2,1,0:T(8,128)S(1)} %get-tuple-element.79.across, f32[128,128]{1,0:T(8,128)S(1)} %collective-permute-done.4.row_even, f32[128,128]{1,0:T(8,128)S(1)} %collective-permute-done.5.row_odd, ...), custom_call_target="tpu_custom_call" | custom-call | flops 1800000000 | bytes 1800000 | tf_op jit(solution)/shard_map/pallas_call | solution.py:495
  26.5 2.0 %collective-permute-done.7.col_odd = f32[128,128]{1,0:T(8,128)S(1)} collective-permute-done((f32[128,128]{1,0:T(8,128)S(1)}, f32[128,128]{1,0:T(8,128)S(1)}, u32[]{:S(2)}, u32[]{:S(2)}) %collective-permute-start.7) | collective-permute-done | bytes 65568 | tf_op jit(solution)/shard_map/ppermute | solution.py:525
  28.5 0.0 collective-permute-done.6.col_even
  28.5 0.8 %shard_map.148 = (f32[176,128]{1,0:T(8,128)S(1)}, f32[176,128]{1,0:T(8,128)S(1)}) custom-call(f32[16,128,128]{2,1,0:T(8,128)S(1)} %get-tuple-element.55.stress.kept, f32[16,128,128]{2,1,0:T(8,128)S(1)} %get-tuple-element.56.strain, s32[16,128,128]{2,1,0:T(8,128)S(1)} %get-tuple-element.57.yields, s32[16,128,128]{2,1,0:T(8,128)S(1)} %get-tuple-element.58.count, ...), custom_call_target="tpu_custom_call" | custom-call | flops 800000000 | bytes 800000 | tf_op jit(solution)/shard_map/pallas_call | solution.py:495
  29.2 0.9 %collective-permute-start.8 = (f32[176,128]{1,0:T(8,128)S(1)}, f32[176,128]{1,0:T(8,128)S(1)}, u32[]{:S(2)}, u32[]{:S(2)}) collective-permute-start(f32[176,128]{1,0:T(8,128)S(1)} %get-tuple-element.95), channel_id=1, source_target_pairs={{0,4},{1,5},{2,6},{3,7},{4,0},{5,1},{6,2},{7,3},{8,12},{9,13},{10,... | collective-permute-start | bytes 270344 | tf_op jit(solution)/shard_map/ppermute | solution.py:525
  30.1 0.0 collective-permute-start.9
  30.1 4.2 %shard_map.147 = (f32[16,136,128]{2,1,0:T(8,128)S(1)}, f32[136,256]{1,0:T(8,128)S(1)}, f32[136,256]{1,0:T(8,128)S(1)}, f32[16,128,128]{2,1,0:T(8,128)S(1)}) custom-call(s32[1]{0:T(128)} %constant.7.clone.1.turn, f32[16,128,128]{2,1,0:T(8,128)S(1)} %get-tuple-element.55.stress.kept, f32[16,128,128]{2,1,0:T(8,128)S(1)} %get-tuple-element.56.strain, ...), custom_call_target="tpu_custom_call" | custom-call | flops 4499999744 | bytes 4500000 | tf_op jit(solution)/shard_map/pallas_call | solution.py:495
  34.4 0.0 collective-permute-done.8
  34.4 0.0 collective-permute-done.9
  34.4 0.4 shard_map.149
  34.8 0.5 %collective-permute-start.10 = (f32[176,128]{1,0:T(8,128)S(1)}, f32[176,128]{1,0:T(8,128)S(1)}, u32[]{:S(2)}, u32[]{:S(2)}) collective-permute-start(f32[176,128]{1,0:T(8,128)S(1)} %get-tuple-element.104), channel_id=1, source_target_pairs={{0,1},{4,5},{8,9},{12,13},{16,17},{20,21},{24,25},{28,29},{1,0},{5... | collective-permute-start | bytes 270344 | tf_op jit(solution)/shard_map/ppermute | solution.py:525
  35.3 2.6 %collective-permute-start.11 = (f32[176,128]{1,0:T(8,128)S(1)}, f32[176,128]{1,0:T(8,128)S(1)}, u32[]{:S(2)}, u32[]{:S(2)}) collective-permute-start(f32[176,128]{1,0:T(8,128)S(1)} %get-tuple-element.105), channel_id=1, source_target_pairs={{0,4},{4,0},{8,12},{12,8},{16,20},{20,16},{24,28},{28,24},{1,2},{5... | collective-permute-start | bytes 270344 | tf_op jit(solution)/shard_map/ppermute | solution.py:525
  38.0 1.2 %shard_map.150 = (f32[16,128,128]{2,1,0:T(8,128)S(1)}, f32[16,8,128]{2,1,0:T(8,128)S(1)}, f32[136,128]{1,0:T(8,128)S(1)}, f32[136,128]{1,0:T(8,128)S(1)}) custom-call(f32[16,136,128]{2,1,0:T(8,128)S(1)} %get-tuple-element.93.across, f32[128,128]{1,0:T(8,128)S(1)} %slice.56.row_even, f32[128,128]{1,0:T(8,128)S(1)} %slice.57.row_odd, ...), custom_call_target="tpu_custom_call" | custom-call | flops 1800000000 | bytes 1800000 | tf_op jit(solution)/shard_map/pallas_call | solution.py:495
  39.2 0.0 collective-permute-done.10
  39.2 1.2 %collective-permute-done.11 = f32[176,128]{1,0:T(8,128)S(1)} collective-permute-done((f32[176,128]{1,0:T(8,128)S(1)}, f32[176,128]{1,0:T(8,128)S(1)}, u32[]{:S(2)}, u32[]{:S(2)}) %collective-permute-start.11) | collective-permute-done | bytes 90144 | tf_op jit(solution)/shard_map/ppermute | solution.py:525
  40.5 3.3 %shard_map.151 = (f32[16,128,128]{2,1,0:T(8,128)}, f32[16,128,128]{2,1,0:T(8,128)}, f32[2,16,128,128]{3,2,1,0:T(8,128)}) custom-call(f32[16,128,128]{2,1,0:T(8,128)S(1)} %get-tuple-element.55.stress.kept, f32[16,128,128]{2,1,0:T(8,128)S(1)} %get-tuple-element.56.strain, f32[16,128,128]{2,1,0:T(8,128)S(1)} %get-tuple-element.92._.plastic, ...), custom_call_target="tpu_custom_call" | custom-call | flops 3000000000 | bytes 3000000 | tf_op jit(solution)/shard_map/pallas_call | solution.py:495
  (14 shorter events, 0.1 us)
Async XLA Ops:
  0.6 5.9 %copy-start = (f32[128,256]{1,0:T(8,128)S(1)}, f32[128,256]{1,0:T(8,128)}, u32[]{:S(2)}) copy-start(f32[128,256]{1,0:T(8,128)} %constant.25.clone.high_ref) | copy-start | bytes 393220
  0.6 5.9 %copy-start.1 = (f32[128,256]{1,0:T(8,128)S(1)}, f32[128,256]{1,0:T(8,128)}, u32[]{:S(2)}) copy-start(f32[128,256]{1,0:T(8,128)} %constant.24.clone.low_ref) | copy-start | bytes 393220
  0.7 5.9 %copy-start.3 = (f32[128,128]{1,0:T(8,128)S(1)}, f32[128,128]{1,0:T(8,128)}, u32[]{:S(2)}) copy-start(f32[128,128]{1,0:T(8,128)} %constant.26.clone.next_ref) | copy-start | bytes 196612
  0.7 5.9 %copy-start.5 = (f32[136,128]{1,0:T(8,128)S(1)}, f32[136,128]{1,0:T(8,128)}, u32[]{:S(2)}) copy-start(f32[136,128]{1,0:T(8,128)} %constant.22.clone.band_ref) | copy-start | bytes 208900
  3.5 6.1 %collective-permute-start = (f32[128,128]{1,0:T(8,128)S(1)}, f32[128,128]{1,0:T(8,128)S(1)}, u32[]{:S(2)}, u32[]{:S(2)}) collective-permute-start(f32[128,128]{1,0:T(8,128)S(1)} %get-tuple-element.66), channel_id=1, source_target_pairs={{0,4},{1,5},{2,6},{3,7},{4,0},{5,1},{6,2},{7,3},{8,12},{9,13},{10,... | collective-permute-start | bytes 196616 | tf_op jit(solution)/shard_map/ppermute | solution.py:525
  6.5 3.1 %collective-permute-start.1 = (f32[128,128]{1,0:T(8,128)S(1)}, f32[128,128]{1,0:T(8,128)S(1)}, u32[]{:S(2)}, u32[]{:S(2)}) collective-permute-start(f32[128,128]{1,0:T(8,128)S(1)} %get-tuple-element.67), channel_id=1, source_target_pairs={{0,1},{1,0},{2,3},{3,2},{4,8},{5,9},{6,10},{7,11},{8,4},{9,5},{10,... | collective-permute-start | bytes 196616 | tf_op jit(solution)/shard_map/ppermute | solution.py:525
  9.4 3.5 %copy-start.6 = (f32[128,128]{1,0:T(8,128)S(1)}, f32[128,128]{1,0:T(8,128)}, u32[]{:S(2)}) copy-start(f32[128,128]{1,0:T(8,128)} %constant.23.clone.band_ref) | copy-start | bytes 196612
  10.0 5.1 %collective-permute-start.3 = (f32[128,128]{1,0:T(8,128)S(1)}, f32[128,128]{1,0:T(8,128)S(1)}, u32[]{:S(2)}, u32[]{:S(2)}) collective-permute-start(f32[128,128]{1,0:T(8,128)S(1)} %slice.43), channel_id=1, source_target_pairs={{0,4},{4,0},{8,12},{12,8},{16,20},{20,16},{24,28},{28,24},{1,2},{5... | collective-permute-start | bytes 196616 | tf_op jit(solution)/shard_map/ppermute | solution.py:525
  12.9 2.2 %collective-permute-start.2 = (f32[128,128]{1,0:T(8,128)S(1)}, f32[128,128]{1,0:T(8,128)S(1)}, u32[]{:S(2)}, u32[]{:S(2)}) collective-permute-start(f32[128,128]{1,0:T(8,128)S(1)} %slice.42), channel_id=1, source_target_pairs={{0,1},{4,5},{8,9},{12,13},{16,17},{20,21},{24,25},{28,29},{1,0},{5... | collective-permute-start | bytes 196616 | tf_op jit(solution)/shard_map/ppermute | solution.py:525
  12.9 2.2 %copy-start.2 = (f32[144,256]{1,0:T(8,128)S(1)}, f32[144,256]{1,0:T(8,128)}, u32[]{:S(2)}) copy-start(f32[144,256]{1,0:T(8,128)} %constant.21.clone.above) | copy-start | bytes 442372
  12.9 2.2 %copy-start.4 = (f32[128,128]{1,0:T(8,128)S(1)}, f32[128,128]{1,0:T(8,128)}, u32[]{:S(2)}) copy-start(f32[128,128]{1,0:T(8,128)} %constant.20.clone.below) | copy-start | bytes 196612
  16.0 7.8 %collective-permute-start.5 = (f32[128,128]{1,0:T(8,128)S(1)}, f32[128,128]{1,0:T(8,128)S(1)}, u32[]{:S(2)}, u32[]{:S(2)}) collective-permute-start(f32[128,128]{1,0:T(8,128)S(1)} %slice.45), channel_id=1, source_target_pairs={{0,1},{1,0},{2,3},{3,2},{4,8},{5,9},{6,10},{7,11},{8,4},{9,5},{10,... | collective-permute-start | bytes 196616 | tf_op jit(solution)/shard_map/ppermute | solution.py:525
  16.0 7.7 %collective-permute-start.4 = (f32[128,128]{1,0:T(8,128)S(1)}, f32[128,128]{1,0:T(8,128)S(1)}, u32[]{:S(2)}, u32[]{:S(2)}) collective-permute-start(f32[128,128]{1,0:T(8,128)S(1)} %slice.44), channel_id=1, source_target_pairs={{0,4},{1,5},{2,6},{3,7},{4,0},{5,1},{6,2},{7,3},{8,12},{9,13},{10,... | collective-permute-start | bytes 196616 | tf_op jit(solution)/shard_map/ppermute | solution.py:525
  24.1 4.3 %collective-permute-start.7 = (f32[128,128]{1,0:T(8,128)S(1)}, f32[128,128]{1,0:T(8,128)S(1)}, u32[]{:S(2)}, u32[]{:S(2)}) collective-permute-start(f32[128,128]{1,0:T(8,128)S(1)} %slice.47), channel_id=1, source_target_pairs={{0,4},{4,0},{8,12},{12,8},{16,20},{20,16},{24,28},{28,24},{1,2},{5... | collective-permute-start | bytes 196616 | tf_op jit(solution)/shard_map/ppermute | solution.py:525
  25.0 3.4 %collective-permute-start.6 = (f32[128,128]{1,0:T(8,128)S(1)}, f32[128,128]{1,0:T(8,128)S(1)}, u32[]{:S(2)}, u32[]{:S(2)}) collective-permute-start(f32[128,128]{1,0:T(8,128)S(1)} %slice.46), channel_id=1, source_target_pairs={{0,1},{4,5},{8,9},{12,13},{16,17},{20,21},{24,25},{28,29},{1,0},{5... | collective-permute-start | bytes 196616 | tf_op jit(solution)/shard_map/ppermute | solution.py:525
  29.2 5.1 %collective-permute-start.8 = (f32[176,128]{1,0:T(8,128)S(1)}, f32[176,128]{1,0:T(8,128)S(1)}, u32[]{:S(2)}, u32[]{:S(2)}) collective-permute-start(f32[176,128]{1,0:T(8,128)S(1)} %get-tuple-element.95), channel_id=1, source_target_pairs={{0,4},{1,5},{2,6},{3,7},{4,0},{5,1},{6,2},{7,3},{8,12},{9,13},{10,... | collective-permute-start | bytes 270344 | tf_op jit(solution)/shard_map/ppermute | solution.py:525
  30.1 4.3 %collective-permute-start.9 = (f32[176,128]{1,0:T(8,128)S(1)}, f32[176,128]{1,0:T(8,128)S(1)}, u32[]{:S(2)}, u32[]{:S(2)}) collective-permute-start(f32[176,128]{1,0:T(8,128)S(1)} %get-tuple-element.96), channel_id=1, source_target_pairs={{0,1},{1,0},{2,3},{3,2},{4,8},{5,9},{6,10},{7,11},{8,4},{9,5},{10,... | collective-permute-start | bytes 270344 | tf_op jit(solution)/shard_map/ppermute | solution.py:525
  34.8 4.4 %collective-permute-start.10 = (f32[176,128]{1,0:T(8,128)S(1)}, f32[176,128]{1,0:T(8,128)S(1)}, u32[]{:S(2)}, u32[]{:S(2)}) collective-permute-start(f32[176,128]{1,0:T(8,128)S(1)} %get-tuple-element.104), channel_id=1, source_target_pairs={{0,1},{4,5},{8,9},{12,13},{16,17},{20,21},{24,25},{28,29},{1,0},{5... | collective-permute-start | bytes 270344 | tf_op jit(solution)/shard_map/ppermute | solution.py:525
  35.3 5.1 %collective-permute-start.11 = (f32[176,128]{1,0:T(8,128)S(1)}, f32[176,128]{1,0:T(8,128)S(1)}, u32[]{:S(2)}, u32[]{:S(2)}) collective-permute-start(f32[176,128]{1,0:T(8,128)S(1)} %get-tuple-element.105), channel_id=1, source_target_pairs={{0,4},{4,0},{8,12},{12,8},{16,20},{20,16},{24,28},{28,24},{1,2},{5... | collective-permute-start | bytes 270344 | tf_op jit(solution)/shard_map/ppermute | solution.py:525

commit v8 on v7

--- a/solution.py
+++ b/solution.py
@@ -62,16 +62,15 @@
     return both[:, :cols] + both[:, cols:]
 
 
-def newton(stress, strain, yields, count, soften):
-    start = 2.0 * stress - 3.5 * soften
-    shift = start + (2.0 * strain - HALF_LN2)
-    drop = 0.2 * soften
-    state = start
+def newton(stress, strain, yields, count, kept):
+    top = (stress + strain) - (0.875 + 0.875 * kept)
+    shift = 2.0 * top - HALF_LN2
+    state = 2.0 * (top - strain)
+    drop = 0.1 + 0.1 * kept
     for sweep_no in range(1, 7):
         update = state * (0.8 - 0.2 * jnp.tanh(shift - state)) - drop
         state = update if sweep_no <= 3 else jnp.where(count >= sweep_no, update, state)
-    moved = (strain + (stress - 1.75 * soften)) - 0.5 * state
-    return jnp.where(yields > 0, moved, strain)
+    return jnp.where(yields > 0, top - 0.5 * state, strain)
 
 
 def depth_smooth(layers, matrix):
@@ -181,7 +180,8 @@
             block[pl.ds(layer * REACH, REACH), :] = newton(
                 stress[at], strain[at], yields[at], count[at], jnp.ones((REACH, cols), jnp.float32)
             )
-        sent.append(left_product(left_constant(matrix), block[...]))
+        product = left_product(left_constant(matrix), block[...])
+        sent.append(jnp.concatenate([product, product[:REACH]], axis=0))
     send("gx", *sent, even_ref, odd_ref)
     for copy in copies[10:]:
         copy.wait()
@@ -203,8 +203,8 @@
     def layer_step(layer):
         for index, first_row in enumerate(starts):
             at = (layer, pl.ds(first_row, REACH), slice(None))
-            soften = 0.5 + 0.5 * with_edges(kept[at], layer, *packed[index])
-            value = newton(stress[at], strain[at], yields[at], count[at], soften)
+            ratios = with_edges(kept[at], layer, *packed[index])
+            value = newton(stress[at], strain[at], yields[at], count[at], ratios)
             if index == 0:
                 low_block[pl.ds(layer * REACH, REACH), :] = value
             else:
@@ -226,40 +226,50 @@
 
 
 def main_kernel(turn, stress, strain, yields, count, threshold, kept, edge_low, edge_high, norm_low,
-                norm_high, col_even, col_odd, norm_last, band_ref, low_ref, high_ref, next_ref,
-                across, low_cols, high_cols, plastic, pack_low, pack_high, pack_next, pack_last):
+                norm_high, col_even, col_odd, norm_last, fixed, band_ref, low_ref, high_ref, next_ref,
+                across, low_cols, high_cols, plastic, fixed_out,
+                pack_low, pack_high, pack_next, pack_last):
     layers, rows, cols = stress.shape
     total = rows + REACH
     step_rows = 4 * REACH
-    steps = rows // step_rows
+    lanes = lane_ids((REACH, cols))
+    pack_last[pl.ds(0, REACH), :] = jnp.zeros((REACH, cols), jnp.float32)
+
+    def newton_blocks(index, fresh):
+        for near in range(step_rows // REACH):
+            first = index * step_rows + near * REACH
+            part = pl.ds(pl.multiple_of(first, REACH), REACH)
+            extended = pl.ds(pl.multiple_of(first + REACH, REACH), REACH)
+            if not fresh:
+                packed = edge_ratios(
+                    (edge_low, edge_high), (col_even, col_odd), (norm_low, norm_high), part, extended
+                )
+            for layer in range(layers):
+                at = (layer, part, slice(None))
+                if fresh:
+                    ratios = jnp.ones((REACH, cols), jnp.float32)
+                else:
+                    ratios = with_edges(kept[at], layer, *packed)
+                value = newton(stress[at], strain[at], yields[at], count[at], ratios)
+                plastic[at] = value
+                lane = layers + layer
+                if fresh:
+                    both = stress[at] + strain[at]
+                    pltpu.store(fixed_out.at[extended, :], pltpu.roll(both, lane + 1, 1), mask=lanes == lane)
+                    turned = pltpu.roll(threshold[at], layer + 1, 1)
+                    pltpu.store(fixed_out.at[extended, :], turned, mask=lanes == layer)
+                else:
+                    pltpu.store(pack_last.at[extended, :], pltpu.roll(value, lane + 1, 1), mask=lanes == lane)
 
     @pl.when(turn[0] == 0)
     def _():
-        def step(index, carry):
-            part = pl.ds(pl.multiple_of(index * step_rows, step_rows), step_rows)
-            soften = jnp.ones((step_rows, cols), jnp.float32)
-            for layer in range(layers):
-                at = (layer, part, slice(None))
-                plastic[at] = newton(stress[at], strain[at], yields[at], count[at], soften)
-            return carry
-
-        lax.fori_loop(0, steps, step, 0)
+        fixed_out[...] = jnp.zeros_like(fixed_out)
+        lax.fori_loop(0, rows // step_rows, lambda index, _: newton_blocks(index, True), None)
 
     @pl.when(turn[0] > 0)
     def _():
-        def step(index, carry):
-            part = pl.ds(pl.multiple_of(index * step_rows, step_rows), step_rows)
-            extended = pl.ds(pl.multiple_of(index * step_rows + REACH, REACH), step_rows)
-            packed = edge_ratios(
-                (edge_low, edge_high), (col_even, col_odd), (norm_low, norm_high), part, extended
-            )
-            for layer in range(layers):
-                at = (layer, part, slice(None))
-                soften = 0.5 + 0.5 * with_edges(kept[at], layer, *packed)
-                plastic[at] = newton(stress[at], strain[at], yields[at], count[at], soften)
-            return carry
-
-        lax.fori_loop(0, steps, step, 0)
+        fixed_out[...] = fixed[...]
+        lax.fori_loop(0, rows // step_rows, lambda index, _: newton_blocks(index, False), None)
 
     constant = left_constant(band_ref[...])
     slots = layer_slots((total, cols))
@@ -279,26 +289,9 @@
     behind = right_product(pack_next[...], right_constant(next_ref[...]))
     high_cols[:, :cols] = high[:, :cols]
 
-    @pl.when(turn[0] == OUTER - 1)
-    def _():
-        def last_column(index, carry):
-            part = pl.ds(pl.multiple_of(index * step_rows, step_rows), step_rows)
-            lanes = lane_ids((step_rows, cols))
-            packed = jnp.zeros((step_rows, cols), jnp.float32)
-            for layer in range(layers):
-                at = (layer, part, slice(None))
-                packed = jnp.where(lanes == layer, pltpu.roll(threshold[at], layer + 1, 1), packed)
-                rest = (stress[at] + strain[at]) - plastic[at]
-                turned = pltpu.roll(rest, layers + layer + 1, 1)
-                packed = jnp.where(lanes == layers + layer, turned, packed)
-            pack_last[pl.ds(pl.multiple_of(index * step_rows + REACH, REACH), step_rows), :] = packed
-            return carry
-
-        pack_last[pl.ds(0, REACH), :] = jnp.zeros((REACH, cols), jnp.float32)
-        lax.fori_loop(0, steps, last_column, 0)
-        lanes = lane_ids(pack_last.shape)
-        drop = (high[:, cols:] + behind) * norm_last[...]
-        high_cols[:, cols:] = pack_last[...] - jnp.where(lanes < layers, drop, 0.0)
+    drop = (high[:, cols:] + behind) * norm_last[...]
+    first_lanes = lane_ids((total, cols)) < layers
+    high_cols[:, cols:] = fixed_out[...] - jnp.where(first_lanes, drop, pack_last[...])
 
 
 def pack_edges(values):
@@ -314,8 +307,8 @@
     return low, high, ahead
 
 
-def corner_kernel(row_even, row_odd, rest_even, rest_odd, low_cols, high_cols, norm_last, _, low_ref, high_ref, next_ref,
-                  even_ref, odd_ref, own_ref):
+def corner_kernel(row_even, row_odd, rest_even, rest_odd, low_cols, high_cols, norm_last,
+                  _, __, low_ref, high_ref, next_ref, even_ref, odd_ref, own_ref):
     cols = low_ref.shape[0]
     total = low_cols.shape[0]
     layers = (total - REACH) // REACH
@@ -362,10 +355,11 @@
     for part in range(1, 4):
         moved = pltpu.roll(main[part * quarter : (part + 1) * quarter], part * 2 * layers, 1)
         folded = jnp.where(lanes // (2 * layers) == part, moved, folded)
+    spare = jnp.zeros((REACH, cols), jnp.float32)
     extra = jnp.zeros((quarter + REACH, cols), jnp.float32)
     send(
-        "gy", jnp.concatenate([low_all[REACH:, :cols], low_all[:REACH, :cols], extra], axis=0),
-        jnp.concatenate([high_all[REACH:], high_all[:REACH], folded, first], axis=0),
+        "gy", jnp.concatenate([low_all[REACH:, :cols], low_all[:REACH, :cols], extra, spare], axis=0),
+        jnp.concatenate([high_all[REACH:], high_all[:REACH], folded, first, spare], axis=0),
         even_ref, odd_ref,
     )
     own_ref[...] = low_all[:, cols:]
@@ -416,11 +410,11 @@
 
 def final_kernel(stress, strain, plastic, inner, inner_before, edge_low, edge_high, norm_low, norm_high,
                  col_even, col_odd, last_even, last_odd, rest_even, rest_odd, norm_before, own_cols,
-                 plastic_out, damage_out, force_out, columns, damage_s, force_s, copy_sem, sems):
+                 plastic_out, damage_out, force_out, columns, damage_s, force_s, sums, diffs,
+                 copy_sem, sems):
     layers, rows, cols = stress.shape
     whole = pltpu.make_async_copy(plastic, plastic_out, copy_sem)
     whole.start()
-
     from_low, _ = sides("gy", last_even[...], last_odd[...])
     folded = from_low[REACH : REACH + rows // 4]
     pieces = [from_low[REACH + rows // 4 :], folded]
@@ -428,7 +422,7 @@
         pieces.append(pltpu.roll(folded, cols - part * 2 * layers, 1))
     column = jnp.concatenate(pieces, axis=0)
     kept = ratio(column - own_cols[...] * norm_before[...])
-    columns[...] = kept * pltpu.roll(column, cols - layers, 1)
+    columns[...] = (0.5 * kept) * pltpu.roll(column, cols - layers, 1)
 
     def copies(layer):
         return (
@@ -437,10 +431,8 @@
             pltpu.make_async_copy(force_s.at[1, layer], force_out.at[1, layer], sems.at[2, layer]),
         )
 
-    def layer_step(layer):
+    def layer_step(layer, near):
         lanes = lane_ids((REACH, cols))
-        top = lax.broadcasted_iota(jnp.int32, (REACH, cols), 0) == 0
-        above_sum = above_diff = None
         for block in range(rows // REACH + 1):
             extended = pl.ds(block * REACH, REACH)
             part = pl.ds((block - 1) * REACH if block else 0, REACH)
@@ -455,23 +447,24 @@
                 line = pl.ds(layers + layer, 1)
                 rest, _ = sides("gx", rest_even[line, :], rest_odd[line, :])
             kept = with_edges(inner[at] if block else inner_before[layer], layer, *packed)
-            value = kept * rest
+            value = (0.5 * kept) * rest
             left = jnp.where(
                 lanes == 0,
                 pltpu.roll(columns[extended, :], (cols - layer) % cols, 1),
                 pltpu.roll(value, 1, 1),
             )
-            both = pltpu.roll(left + value, 1, 0)
-            diff = pltpu.roll(left - value, 1, 0)
+            both, diff = left + value, left - value
+            sums[near, extended, :] = both
+            diffs[near, extended, :] = diff
             if block:
+                behind = pl.ds(block * REACH - 1, REACH)
                 damage_s[at] = 1.0 - kept
-                force_s[(0, *at)] = 0.5 * (jnp.where(top, above_sum, both) - (left + value))
-                force_s[(1, *at)] = 0.5 * (jnp.where(top, above_diff, diff) + (left - value))
-            above_sum, above_diff = both, diff
+                force_s[(0, *at)] = sums[near, behind, :] - both
+                force_s[(1, *at)] = diffs[near, behind, :] + diff
 
     def step(index, carry):
         for near in range(2):
-            layer_step(2 * index + near)
+            layer_step(2 * index + near, near)
         for near in range(2):
             for copy in copies(2 * index + near):
                 copy.start()
@@ -572,14 +565,15 @@
 
     whole, wide, top = (layers, rows, cols), (layers, total, cols), (layers, REACH, cols)
     sent_rows = (strip + 3 * layers, cols)
-    sent_cols = (total + rows // 4 + REACH, cols)
+    sent_cols = (total + rows // 4 + 2 * REACH, cols)
+    last_cols = total + rows // 4 + REACH
     spare = (3 * layers, cols)
     packed, packed_two = (total, cols), (total, 2 * cols)
 
     sources = (trial_stress, old_strain, yield_mask, newton_count, damage_threshold)
     row_even, row_odd, norm, norm_low, norm_high, norm_last, norm_before, col_even, col_odd, rest, *inputs = call(
         first_edge_kernel,
-        [(strip, cols)] * 2 + [packed] * 5 + [(rows, cols)] * 2 + [spare]
+        [(strip + REACH, cols)] * 2 + [packed] * 5 + [(rows, cols)] * 2 + [spare]
         + [jax.ShapeDtypeStruct(whole, source.dtype) for source in sources],
         [(strip, cols), pltpu.SemaphoreType.DMA((3, len(sources)))], 2500,
         sources, [pltpu.HBM] * len(sources), limit=FIRST_VMEM_BYTES,
@@ -587,6 +581,7 @@
     stress, strain, _, _, threshold = inputs
     kept, edge_low, edge_high, norms = stress, norm_low, norm_high, (norm_low, norm_high)
     rest_even = rest_odd = rest
+    fixed = norm_last
     for outer_no in range(OUTER):
         last = outer_no == OUTER - 1
         if outer_no:
@@ -603,19 +598,19 @@
             rest_even, rest_odd = row_even[strip:], row_odd[strip:]
             row_even, row_odd = row_even[:strip], row_odd[:strip]
         turn = jnp.full((1,), outer_no, jnp.int32)
-        across, low_cols, high_cols, plastic = call(
-            main_kernel, [wide, packed_two, packed_two, whole],
+        across, low_cols, high_cols, plastic, fixed = call(
+            main_kernel, [wide, packed_two, packed_two, whole, packed],
             [packed, packed, packed, packed], 4500,
             (turn, *inputs, kept, edge_low, edge_high, *norms, col_even, col_odd, norm_last,
-             rows_band, *columns),
-            [pltpu.SMEM] + [pltpu.VMEM] * 17,
+             fixed, rows_band, *columns),
+            [pltpu.SMEM] + [pltpu.VMEM] * 18,
         )
         col_even, col_odd, own_cols = call(
             corner_kernel, [sent_cols, sent_cols, packed], [], 400,
-            (row_even, row_odd, rest_even, rest_odd, low_cols, high_cols, norm_last, plastic, *columns),
+            (row_even, row_odd, rest_even, rest_odd, low_cols, high_cols, norm_last, plastic, fixed, *columns),
         )
-        if not last:
-            col_even, col_odd = col_even[:rows], col_odd[:rows]
+        used = last_cols if last else rows
+        col_even, col_odd = col_even[:used], col_odd[:used]
         col_even, col_odd = exchange("gy", "gx", col_even, col_odd)
         if last:
             last_even, last_odd = col_even[rows:], col_odd[rows:]
@@ -626,7 +621,8 @@
         )
     return tuple(call(
         final_kernel, [whole, whole, (2, *whole)],
-        [packed, whole, (2, *whole), pltpu.SemaphoreType.DMA(()), pltpu.SemaphoreType.DMA((3, layers))],
+        [packed, whole, (2, *whole), (2, *packed), (2, *packed),
+         pltpu.SemaphoreType.DMA(()), pltpu.SemaphoreType.DMA((3, layers))],
         3000,
         (stress, strain, plastic, kept, kept_before, edge_low, edge_high, *norms, col_even, col_odd,
          last_even, last_odd, rest_even, rest_odd, norm_before, own_cols),

time: 43.9 us -> 43.6 us (level)
  starting transfers between devices: 15.4 us -> 14.1 us
  Pallas kernels: 22.8 us -> 23.3 us
  waiting for transfers between devices: 4.48 us -> 4.98 us
    ppermute x12, starting transfers between devices: 15.4 us -> 14.1 us  [exchange(): results.append(lax.ppermute(value, names, pairs))]
    ppermute x12, waiting for transfers between devices: 4.48 us -> 4.98 us  [exchange(): results.append(lax.ppermute(value, names, pairs))]
    pallas_call x13, Pallas kernels: 22.8 us -> 23.3 us  [call(): pl.pallas_call(kernel, out_shape=shapes, in_specs=[pl.BlockSpec(memory_sp...]
  transfers between devices with their start and end apart: 12 -> 12, of which waited for: 4 -> 4; matrix products, arithmetic and copies ran while one was open for 0% -> 0% of each run, Pallas kernels for 32% -> 33%
where the time goes in v8:
time: 43.6 us; the launch traced here: 43.5 us
  Pallas kernels  23.3 us (53%)
  starting transfers between devices  14.1 us (32%)
  waiting for transfers between devices  4.98 us (11%)
  between operations  0.91 us (2%)
    pallas_call x13, Pallas kernels, call(): pl.pallas_call(kernel, out_shape=shapes, in_specs=[pl.BlockSpec(memory_sp...  23.3 us
    ppermute x12, starting transfers between devices, exchange(): results.append(lax.ppermute(value, names, pairs))  14.1 us
    ppermute x12, waiting for transfers between devices, exchange(): results.append(lax.ppermute(value, names, pairs))  4.98 us
  transfers between devices with their start and end apart: 12, of which 4 were waited for; matrix products, arithmetic and copies ran while one was open for 0% of the time, Pallas kernels for 33%

profile of v8, /device:TPU:0, one launch (start us, length us, event | category | flops | bytes accessed | tf_op | source)
XLA Modules:
  0.0 43.5 jit_solution(1082949345591713733)
XLA Ops:
  0.6 0.0 copy-start
  0.6 0.0 copy-start.1
  0.7 0.0 copy-start.3
  0.7 0.0 copy-start.5
  0.7 2.8 %shard_map.139 = (f32[136,128]{1,0:T(8,128)S(1)}, f32[136,128]{1,0:T(8,128)S(1)}, f32[136,128]{1,0:T(8,128)S(1)}, f32[136,128]{1,0:T(8,128)S(1)}, f32[136,128]{1...) custom-call(f32[16,128,128]{2,1,0:T(8,128)} %refs_0_.1, ...), custom_call_target="tpu_custom_call" | custom-call | flops 2500000000 | bytes 2500000 | tf_op jit(solution)/shard_map/pallas_call | solution.py:488
  3.5 0.5 %collective-permute-start.1 = (f32[128,128]{1,0:T(8,128)S(1)}, f32[128,128]{1,0:T(8,128)S(1)}, u32[]{:S(2)}, u32[]{:S(2)}) collective-permute-start(f32[128,128]{1,0:T(8,128)S(1)} %slice.55), channel_id=1, source_target_pairs={{0,1},{1,0},{2,3},{3,2},{4,8},{5,9},{6,10},{7,11},{8,4},{9,5},{10,... | collective-permute-start | bytes 196616 | tf_op jit(solution)/shard_map/ppermute | solution.py:518
  4.0 4.0 %collective-permute-start = (f32[128,128]{1,0:T(8,128)S(1)}, f32[128,128]{1,0:T(8,128)S(1)}, u32[]{:S(2)}, u32[]{:S(2)}) collective-permute-start(f32[128,128]{1,0:T(8,128)S(1)} %slice.54), channel_id=1, source_target_pairs={{0,4},{1,5},{2,6},{3,7},{4,0},{5,1},{6,2},{7,3},{8,12},{9,13},{10,... | collective-permute-start | bytes 196616 | tf_op jit(solution)/shard_map/ppermute | solution.py:518
  8.1 0.0 copy-done
  8.1 0.0 copy-done.1
  8.1 0.0 copy-done.3
  8.1 0.0 copy-done.5
  8.1 3.6 %shard_map.140 = (f32[16,136,128]{2,1,0:T(8,128)S(1)}, f32[136,256]{1,0:T(8,128)S(1)}, f32[136,256]{1,0:T(8,128)S(1)}, f32[16,128,128]{2,1,0:T(8,128)S(1)}, f32[136,128]{1,0:T(8,128)S(1)}) custom-call(s32[1]{0:T(128)} %constant.9.clone.1.turn, f32[16,128,128]{2,1,0:T(8,128)S(1)} %get-tuple-element.58.stress.kept, ...), custom_call_target="tpu_custom_call" | custom-call | flops 4499999744 | bytes 4500000 | tf_op jit(solution)/shard_map/pallas_call | solution.py:488
  11.7 0.0 collective-permute-done.1.row_odd
  11.7 0.0 collective-permute-done.row_even
  11.7 0.0 copy-start.6
  11.8 0.4 shard_map.141
  12.2 1.0 %collective-permute-start.3 = (f32[128,128]{1,0:T(8,128)S(1)}, f32[128,128]{1,0:T(8,128)S(1)}, u32[]{:S(2)}, u32[]{:S(2)}) collective-permute-start(f32[128,128]{1,0:T(8,128)S(1)} %slice.57), channel_id=1, source_target_pairs={{0,4},{4,0},{8,12},{12,8},{16,20},{20,16},{24,28},{28,24},{1,2},{5... | collective-permute-start | bytes 196616 | tf_op jit(solution)/shard_map/ppermute | solution.py:518
  13.1 0.7 %collective-permute-start.2 = (f32[128,128]{1,0:T(8,128)S(1)}, f32[128,128]{1,0:T(8,128)S(1)}, u32[]{:S(2)}, u32[]{:S(2)}) collective-permute-start(f32[128,128]{1,0:T(8,128)S(1)} %slice.56), channel_id=1, source_target_pairs={{0,1},{4,5},{8,9},{12,13},{16,17},{20,21},{24,25},{28,29},{1,0},{5... | collective-permute-start | bytes 196616 | tf_op jit(solution)/shard_map/ppermute | solution.py:518
  13.9 0.0 copy-done.6
  13.9 0.0 copy-start.2
  13.9 0.0 copy-start.4
  13.9 1.2 %shard_map.142 = (f32[16,128,128]{2,1,0:T(8,128)S(1)}, f32[16,8,128]{2,1,0:T(8,128)S(1)}, f32[136,128]{1,0:T(8,128)S(1)}, f32[136,128]{1,0:T(8,128)S(1)}) custom-call(f32[16,136,128]{2,1,0:T(8,128)S(1)} %get-tuple-element.68.across, f32[128,128]{1,0:T(8,128)S(1)} %collective-permute-done.row_even, f32[128,128]{1,0:T(8,128)S(1)} %collective-permute-done.1.row_odd, ...), custom_call_target="tpu_custom_call" | custom-call | flops 1800000000 | bytes 1800000 | tf_op jit(solution)/shard_map/pallas_call | solution.py:488
  15.1 1.4 %collective-permute-done.3.col_odd = f32[128,128]{1,0:T(8,128)S(1)} collective-permute-done((f32[128,128]{1,0:T(8,128)S(1)}, f32[128,128]{1,0:T(8,128)S(1)}, u32[]{:S(2)}, u32[]{:S(2)}) %collective-permute-start.3) | collective-permute-done | bytes 65568 | tf_op jit(solution)/shard_map/ppermute | solution.py:518
  16.5 0.0 collective-permute-done.2.col_even
  16.5 0.0 copy-done.2
  16.5 0.0 copy-done.4
  16.5 0.7 %shard_map.144 = (f32[176,128]{1,0:T(8,128)S(1)}, f32[176,128]{1,0:T(8,128)S(1)}) custom-call(f32[16,128,128]{2,1,0:T(8,128)S(1)} %get-tuple-element.58.stress.kept, f32[16,128,128]{2,1,0:T(8,128)S(1)} %get-tuple-element.59.strain, s32[16,128,128]{2,1,0:T(8,128)S(1)} %get-tuple-element.60.yields, s32[16,128,128]{2,1,0:T(8,128)S(1)} %get-tuple-element.61.count, ...), custom_call_target="tpu_custom_call" | custom-call | flops 800000000 | bytes 800000 | tf_op jit(solution)/shard_map/pallas_call | solution.py:488
  17.3 0.1 collective-permute-start.5
  17.4 3.0 %collective-permute-start.4 = (f32[128,128]{1,0:T(8,128)S(1)}, f32[128,128]{1,0:T(8,128)S(1)}, u32[]{:S(2)}, u32[]{:S(2)}) collective-permute-start(f32[128,128]{1,0:T(8,128)S(1)} %slice.58), channel_id=1, source_target_pairs={{0,4},{1,5},{2,6},{3,7},{4,0},{5,1},{6,2},{7,3},{8,12},{9,13},{10,... | collective-permute-start | bytes 196616 | tf_op jit(solution)/shard_map/ppermute | solution.py:518
  20.4 3.6 %shard_map.143 = (f32[16,136,128]{2,1,0:T(8,128)S(1)}, f32[136,256]{1,0:T(8,128)S(1)}, f32[136,256]{1,0:T(8,128)S(1)}, f32[16,128,128]{2,1,0:T(8,128)S(1)}, f32[136,128]{1,0:T(8,128)S(1)}) custom-call(s32[1]{0:T(128)} %constant.8.clone.1.turn, f32[16,128,128]{2,1,0:T(8,128)S(1)} %get-tuple-element.58.stress.kept, ...), custom_call_target="tpu_custom_call" | custom-call | flops 4499999744 | bytes 4500000 | tf_op jit(solution)/shard_map/pallas_call | solution.py:488
  24.0 0.0 collective-permute-done.5.row_odd
  24.0 0.0 collective-permute-done.4.row_even
  24.0 0.4 shard_map.145
  24.4 0.7 %collective-permute-start.7 = (f32[128,128]{1,0:T(8,128)S(1)}, f32[128,128]{1,0:T(8,128)S(1)}, u32[]{:S(2)}, u32[]{:S(2)}) collective-permute-start(f32[128,128]{1,0:T(8,128)S(1)} %slice.61), channel_id=1, source_target_pairs={{0,4},{4,0},{8,12},{12,8},{16,20},{20,16},{24,28},{28,24},{1,2},{5... | collective-permute-start | bytes 196616 | tf_op jit(solution)/shard_map/ppermute | solution.py:518
  25.1 0.4 collective-permute-start.6
  25.5 1.2 %shard_map.146 = (f32[16,128,128]{2,1,0:T(8,128)S(1)}, f32[16,8,128]{2,1,0:T(8,128)S(1)}, f32[136,128]{1,0:T(8,128)S(1)}, f32[136,128]{1,0:T(8,128)S(1)}) custom-call(f32[16,136,128]{2,1,0:T(8,128)S(1)} %get-tuple-element.83.across, f32[128,128]{1,0:T(8,128)S(1)} %collective-permute-done.4.row_even, f32[128,128]{1,0:T(8,128)S(1)} %collective-permute-done.5.row_odd, ...), custom_call_target="tpu_custom_call" | custom-call | flops 1800000000 | bytes 1800000 | tf_op jit(solution)/shard_map/pallas_call | solution.py:488
  26.7 2.0 %collective-permute-done.7.col_odd = f32[128,128]{1,0:T(8,128)S(1)} collective-permute-done((f32[128,128]{1,0:T(8,128)S(1)}, f32[128,128]{1,0:T(8,128)S(1)}, u32[]{:S(2)}, u32[]{:S(2)}) %collective-permute-start.7) | collective-permute-done | bytes 65568 | tf_op jit(solution)/shard_map/ppermute | solution.py:518
  28.7 0.0 collective-permute-done.6.col_even
  28.7 0.7 %shard_map.148 = (f32[176,128]{1,0:T(8,128)S(1)}, f32[176,128]{1,0:T(8,128)S(1)}) custom-call(f32[16,128,128]{2,1,0:T(8,128)S(1)} %get-tuple-element.58.stress.kept, f32[16,128,128]{2,1,0:T(8,128)S(1)} %get-tuple-element.59.strain, s32[16,128,128]{2,1,0:T(8,128)S(1)} %get-tuple-element.60.yields, s32[16,128,128]{2,1,0:T(8,128)S(1)} %get-tuple-element.61.count, ...), custom_call_target="tpu_custom_call" | custom-call | flops 800000000 | bytes 800000 | tf_op jit(solution)/shard_map/pallas_call | solution.py:488
  29.5 0.7 %collective-permute-start.8 = (f32[176,128]{1,0:T(8,128)S(1)}, f32[176,128]{1,0:T(8,128)S(1)}, u32[]{:S(2)}, u32[]{:S(2)}) collective-permute-start(f32[176,128]{1,0:T(8,128)S(1)} %get-tuple-element.100), channel_id=1, source_target_pairs={{0,4},{1,5},{2,6},{3,7},{4,0},{5,1},{6,2},{7,3},{8,12},{9,13},{10,... | collective-permute-start | bytes 270344 | tf_op jit(solution)/shard_map/ppermute | solution.py:518
  30.2 0.0 collective-permute-start.9
  30.2 3.6 %shard_map.147 = (f32[16,136,128]{2,1,0:T(8,128)S(1)}, f32[136,256]{1,0:T(8,128)S(1)}, f32[136,256]{1,0:T(8,128)S(1)}, f32[16,128,128]{2,1,0:T(8,128)S(1)}, f32[136,128]{1,0:T(8,128)S(1)}) custom-call(s32[1]{0:T(128)} %constant.7.clone.1.turn, f32[16,128,128]{2,1,0:T(8,128)S(1)} %get-tuple-element.58.stress.kept, ...), custom_call_target="tpu_custom_call" | custom-call | flops 4499999744 | bytes 4500000 | tf_op jit(solution)/shard_map/pallas_call | solution.py:488
  33.8 0.3 collective-permute-done.8
  34.1 0.0 collective-permute-done.9
  34.1 0.4 shard_map.149
  34.5 3.0 %collective-permute-start.11 = (f32[176,128]{1,0:T(8,128)S(1)}, f32[176,128]{1,0:T(8,128)S(1)}, u32[]{:S(2)}, u32[]{:S(2)}) collective-permute-start(f32[176,128]{1,0:T(8,128)S(1)} %slice.68), channel_id=1, source_target_pairs={{0,4},{4,0},{8,12},{12,8},{16,20},{20,16},{24,28},{28,24},{1,2},{5... | collective-permute-start | bytes 270344 | tf_op jit(solution)/shard_map/ppermute | solution.py:518
  37.5 0.0 collective-permute-start.10
  37.5 1.2 %shard_map.150 = (f32[16,128,128]{2,1,0:T(8,128)S(1)}, f32[16,8,128]{2,1,0:T(8,128)S(1)}, f32[136,128]{1,0:T(8,128)S(1)}, f32[136,128]{1,0:T(8,128)S(1)}) custom-call(f32[16,136,128]{2,1,0:T(8,128)S(1)} %get-tuple-element.98.across, f32[128,128]{1,0:T(8,128)S(1)} %slice.72.row_even, f32[128,128]{1,0:T(8,128)S(1)} %slice.73.row_odd, ...), custom_call_target="tpu_custom_call" | custom-call | flops 1800000000 | bytes 1800000 | tf_op jit(solution)/shard_map/pallas_call | solution.py:488
  38.7 1.3 %collective-permute-done.11 = f32[176,128]{1,0:T(8,128)S(1)} collective-permute-done((f32[176,128]{1,0:T(8,128)S(1)}, f32[176,128]{1,0:T(8,128)S(1)}, u32[]{:S(2)}, u32[]{:S(2)}) %collective-permute-start.11) | collective-permute-done | bytes 90144 | tf_op jit(solution)/shard_map/ppermute | solution.py:518
  40.0 0.0 collective-permute-done.10
  40.0 3.4 %shard_map.151 = (f32[16,128,128]{2,1,0:T(8,128)}, f32[16,128,128]{2,1,0:T(8,128)}, f32[2,16,128,128]{3,2,1,0:T(8,128)}) custom-call(f32[16,128,128]{2,1,0:T(8,128)S(1)} %get-tuple-element.58.stress.kept, f32[16,128,128]{2,1,0:T(8,128)S(1)} %get-tuple-element.59.strain, f32[16,128,128]{2,1,0:T(8,128)S(1)} %get-tuple-element.97._.plastic, ...), custom_call_target="tpu_custom_call" | custom-call | flops 3000000000 | bytes 3000000 | tf_op jit(solution)/shard_map/pallas_call | solution.py:488
  (18 shorter events, 0.1 us)
Async XLA Ops:
  0.6 7.4 %copy-start = (f32[128,256]{1,0:T(8,128)S(1)}, f32[128,256]{1,0:T(8,128)}, u32[]{:S(2)}) copy-start(f32[128,256]{1,0:T(8,128)} %constant.25.clone.high_ref) | copy-start | bytes 393220
  0.6 7.4 %copy-start.1 = (f32[128,256]{1,0:T(8,128)S(1)}, f32[128,256]{1,0:T(8,128)}, u32[]{:S(2)}) copy-start(f32[128,256]{1,0:T(8,128)} %constant.24.clone.low_ref) | copy-start | bytes 393220
  0.7 7.4 %copy-start.3 = (f32[128,128]{1,0:T(8,128)S(1)}, f32[128,128]{1,0:T(8,128)}, u32[]{:S(2)}) copy-start(f32[128,128]{1,0:T(8,128)} %constant.26.clone.next_ref) | copy-start | bytes 196612
  0.7 7.4 %copy-start.5 = (f32[136,128]{1,0:T(8,128)S(1)}, f32[136,128]{1,0:T(8,128)}, u32[]{:S(2)}) copy-start(f32[136,128]{1,0:T(8,128)} %constant.22.clone.band_ref) | copy-start | bytes 208900
  3.5 8.2 %collective-permute-start.1 = (f32[128,128]{1,0:T(8,128)S(1)}, f32[128,128]{1,0:T(8,128)S(1)}, u32[]{:S(2)}, u32[]{:S(2)}) collective-permute-start(f32[128,128]{1,0:T(8,128)S(1)} %slice.55), channel_id=1, source_target_pairs={{0,1},{1,0},{2,3},{3,2},{4,8},{5,9},{6,10},{7,11},{8,4},{9,5},{10,... | collective-permute-start | bytes 196616 | tf_op jit(solution)/shard_map/ppermute | solution.py:518
  4.0 7.7 %collective-permute-start = (f32[128,128]{1,0:T(8,128)S(1)}, f32[128,128]{1,0:T(8,128)S(1)}, u32[]{:S(2)}, u32[]{:S(2)}) collective-permute-start(f32[128,128]{1,0:T(8,128)S(1)} %slice.54), channel_id=1, source_target_pairs={{0,4},{1,5},{2,6},{3,7},{4,0},{5,1},{6,2},{7,3},{8,12},{9,13},{10,... | collective-permute-start | bytes 196616 | tf_op jit(solution)/shard_map/ppermute | solution.py:518
  11.7 2.1 %copy-start.6 = (f32[128,128]{1,0:T(8,128)S(1)}, f32[128,128]{1,0:T(8,128)}, u32[]{:S(2)}) copy-start(f32[128,128]{1,0:T(8,128)} %constant.23.clone.band_ref) | copy-start | bytes 196612
  12.2 4.3 %collective-permute-start.3 = (f32[128,128]{1,0:T(8,128)S(1)}, f32[128,128]{1,0:T(8,128)S(1)}, u32[]{:S(2)}, u32[]{:S(2)}) collective-permute-start(f32[128,128]{1,0:T(8,128)S(1)} %slice.57), channel_id=1, source_target_pairs={{0,4},{4,0},{8,12},{12,8},{16,20},{20,16},{24,28},{28,24},{1,2},{5... | collective-permute-start | bytes 196616 | tf_op jit(solution)/shard_map/ppermute | solution.py:518
  13.1 3.4 %collective-permute-start.2 = (f32[128,128]{1,0:T(8,128)S(1)}, f32[128,128]{1,0:T(8,128)S(1)}, u32[]{:S(2)}, u32[]{:S(2)}) collective-permute-start(f32[128,128]{1,0:T(8,128)S(1)} %slice.56), channel_id=1, source_target_pairs={{0,1},{4,5},{8,9},{12,13},{16,17},{20,21},{24,25},{28,29},{1,0},{5... | collective-permute-start | bytes 196616 | tf_op jit(solution)/shard_map/ppermute | solution.py:518
  13.9 2.6 %copy-start.2 = (f32[144,256]{1,0:T(8,128)S(1)}, f32[144,256]{1,0:T(8,128)}, u32[]{:S(2)}) copy-start(f32[144,256]{1,0:T(8,128)} %constant.21.clone.above) | copy-start | bytes 442372
  13.9 2.6 %copy-start.4 = (f32[128,128]{1,0:T(8,128)S(1)}, f32[128,128]{1,0:T(8,128)}, u32[]{:S(2)}) copy-start(f32[128,128]{1,0:T(8,128)} %constant.20.clone.below) | copy-start | bytes 196612
  17.3 6.7 %collective-permute-start.5 = (f32[128,128]{1,0:T(8,128)S(1)}, f32[128,128]{1,0:T(8,128)S(1)}, u32[]{:S(2)}, u32[]{:S(2)}) collective-permute-start(f32[128,128]{1,0:T(8,128)S(1)} %slice.59), channel_id=1, source_target_pairs={{0,1},{1,0},{2,3},{3,2},{4,8},{5,9},{6,10},{7,11},{8,4},{9,5},{10,... | collective-permute-start | bytes 196616 | tf_op jit(solution)/shard_map/ppermute | solution.py:518
  17.4 6.6 %collective-permute-start.4 = (f32[128,128]{1,0:T(8,128)S(1)}, f32[128,128]{1,0:T(8,128)S(1)}, u32[]{:S(2)}, u32[]{:S(2)}) collective-permute-start(f32[128,128]{1,0:T(8,128)S(1)} %slice.58), channel_id=1, source_target_pairs={{0,4},{1,5},{2,6},{3,7},{4,0},{5,1},{6,2},{7,3},{8,12},{9,13},{10,... | collective-permute-start | bytes 196616 | tf_op jit(solution)/shard_map/ppermute | solution.py:518
  24.4 4.3 %collective-permute-start.7 = (f32[128,128]{1,0:T(8,128)S(1)}, f32[128,128]{1,0:T(8,128)S(1)}, u32[]{:S(2)}, u32[]{:S(2)}) collective-permute-start(f32[128,128]{1,0:T(8,128)S(1)} %slice.61), channel_id=1, source_target_pairs={{0,4},{4,0},{8,12},{12,8},{16,20},{20,16},{24,28},{28,24},{1,2},{5... | collective-permute-start | bytes 196616 | tf_op jit(solution)/shard_map/ppermute | solution.py:518
  25.1 3.6 %collective-permute-start.6 = (f32[128,128]{1,0:T(8,128)S(1)}, f32[128,128]{1,0:T(8,128)S(1)}, u32[]{:S(2)}, u32[]{:S(2)}) collective-permute-start(f32[128,128]{1,0:T(8,128)S(1)} %slice.60), channel_id=1, source_target_pairs={{0,1},{4,5},{8,9},{12,13},{16,17},{20,21},{24,25},{28,29},{1,0},{5... | collective-permute-start | bytes 196616 | tf_op jit(solution)/shard_map/ppermute | solution.py:518
  29.5 4.6 %collective-permute-start.8 = (f32[176,128]{1,0:T(8,128)S(1)}, f32[176,128]{1,0:T(8,128)S(1)}, u32[]{:S(2)}, u32[]{:S(2)}) collective-permute-start(f32[176,128]{1,0:T(8,128)S(1)} %get-tuple-element.100), channel_id=1, source_target_pairs={{0,4},{1,5},{2,6},{3,7},{4,0},{5,1},{6,2},{7,3},{8,12},{9,13},{10,... | collective-permute-start | bytes 270344 | tf_op jit(solution)/shard_map/ppermute | solution.py:518
  30.2 3.9 %collective-permute-start.9 = (f32[176,128]{1,0:T(8,128)S(1)}, f32[176,128]{1,0:T(8,128)S(1)}, u32[]{:S(2)}, u32[]{:S(2)}) collective-permute-start(f32[176,128]{1,0:T(8,128)S(1)} %get-tuple-element.101), channel_id=1, source_target_pairs={{0,1},{1,0},{2,3},{3,2},{4,8},{5,9},{6,10},{7,11},{8,4},{9,5},{10,... | collective-permute-start | bytes 270344 | tf_op jit(solution)/shard_map/ppermute | solution.py:518
  34.5 5.5 %collective-permute-start.11 = (f32[176,128]{1,0:T(8,128)S(1)}, f32[176,128]{1,0:T(8,128)S(1)}, u32[]{:S(2)}, u32[]{:S(2)}) collective-permute-start(f32[176,128]{1,0:T(8,128)S(1)} %slice.68), channel_id=1, source_target_pairs={{0,4},{4,0},{8,12},{12,8},{16,20},{20,16},{24,28},{28,24},{1,2},{5... | collective-permute-start | bytes 270344 | tf_op jit(solution)/shard_map/ppermute | solution.py:518
  37.5 2.5 %collective-permute-start.10 = (f32[176,128]{1,0:T(8,128)S(1)}, f32[176,128]{1,0:T(8,128)S(1)}, u32[]{:S(2)}, u32[]{:S(2)}) collective-permute-start(f32[176,128]{1,0:T(8,128)S(1)} %slice.66), channel_id=1, source_target_pairs={{0,1},{4,5},{8,9},{12,13},{16,17},{20,21},{24,25},{28,29},{1,0},{5... | collective-permute-start | bytes 270344 | tf_op jit(solution)/shard_map/ppermute | solution.py:518

commit v9 on v8

--- a/solution.py
+++ b/solution.py
@@ -62,13 +62,19 @@
     return both[:, :cols] + both[:, cols:]
 
 
-def newton(stress, strain, yields, count, kept):
+def first_factor(strain):
+    return 0.8 - 0.2 * jnp.tanh(2.0 * strain - HALF_LN2)
+
+
+def newton(stress, strain, yields, count, kept, factor):
     top = (stress + strain) - (0.875 + 0.875 * kept)
     shift = 2.0 * top - HALF_LN2
     state = 2.0 * (top - strain)
     drop = 0.1 + 0.1 * kept
     for sweep_no in range(1, 7):
-        update = state * (0.8 - 0.2 * jnp.tanh(shift - state)) - drop
+        if sweep_no > 1:
+            factor = 0.8 - 0.2 * jnp.tanh(shift - state)
+        update = state * factor - drop
         state = update if sweep_no <= 3 else jnp.where(count >= sweep_no, update, state)
     return jnp.where(yields > 0, top - 0.5 * state, strain)
 
@@ -178,7 +184,8 @@
         for layer in range(layers):
             at = (layer, parts[side], slice(None))
             block[pl.ds(layer * REACH, REACH), :] = newton(
-                stress[at], strain[at], yields[at], count[at], jnp.ones((REACH, cols), jnp.float32)
+                stress[at], strain[at], yields[at], count[at], jnp.ones((REACH, cols), jnp.float32),
+                first_factor(strain[at]),
             )
         product = left_product(left_constant(matrix), block[...])
         sent.append(jnp.concatenate([product, product[:REACH]], axis=0))
@@ -187,7 +194,7 @@
         copy.wait()
 
 
-def edge_kernel(stress, strain, yields, count, threshold, kept, _, edge_low, edge_high, norm_low,
+def edge_kernel(stress, strain, yields, count, threshold, factor, kept, _, edge_low, edge_high, norm_low,
                 norm_high, col_even, col_odd, below, above,
                 even_ref, odd_ref, low_block, high_block, rest):
     layers, rows, cols = stress.shape
@@ -204,7 +211,7 @@
         for index, first_row in enumerate(starts):
             at = (layer, pl.ds(first_row, REACH), slice(None))
             ratios = with_edges(kept[at], layer, *packed[index])
-            value = newton(stress[at], strain[at], yields[at], count[at], ratios)
+            value = newton(stress[at], strain[at], yields[at], count[at], ratios, factor[at])
             if index == 0:
                 low_block[pl.ds(layer * REACH, REACH), :] = value
             else:
@@ -225,10 +232,9 @@
     )
 
 
-def main_kernel(turn, stress, strain, yields, count, threshold, kept, edge_low, edge_high, norm_low,
+def main_kernel(turn, stress, strain, yields, count, factor, kept, edge_low, edge_high, norm_low,
                 norm_high, col_even, col_odd, norm_last, fixed, band_ref, low_ref, high_ref, next_ref,
-                across, low_cols, high_cols, plastic, fixed_out,
-                pack_low, pack_high, pack_next, pack_last):
+                across, low_cols, high_cols, plastic, pack_last, *packs):
     layers, rows, cols = stress.shape
     total = rows + REACH
     step_rows = 4 * REACH
@@ -247,32 +253,26 @@
             for layer in range(layers):
                 at = (layer, part, slice(None))
                 if fresh:
-                    ratios = jnp.ones((REACH, cols), jnp.float32)
+                    ratios, lead = jnp.ones((REACH, cols), jnp.float32), first_factor(strain[at])
                 else:
-                    ratios = with_edges(kept[at], layer, *packed)
-                value = newton(stress[at], strain[at], yields[at], count[at], ratios)
+                    ratios, lead = with_edges(kept[at], layer, *packed), factor[at]
+                value = newton(stress[at], strain[at], yields[at], count[at], ratios, lead)
                 plastic[at] = value
-                lane = layers + layer
-                if fresh:
-                    both = stress[at] + strain[at]
-                    pltpu.store(fixed_out.at[extended, :], pltpu.roll(both, lane + 1, 1), mask=lanes == lane)
-                    turned = pltpu.roll(threshold[at], layer + 1, 1)
-                    pltpu.store(fixed_out.at[extended, :], turned, mask=lanes == layer)
-                else:
+                if not fresh:
+                    lane = layers + layer
                     pltpu.store(pack_last.at[extended, :], pltpu.roll(value, lane + 1, 1), mask=lanes == lane)
 
     @pl.when(turn[0] == 0)
     def _():
-        fixed_out[...] = jnp.zeros_like(fixed_out)
         lax.fori_loop(0, rows // step_rows, lambda index, _: newton_blocks(index, True), None)
 
     @pl.when(turn[0] > 0)
     def _():
-        fixed_out[...] = fixed[...]
         lax.fori_loop(0, rows // step_rows, lambda index, _: newton_blocks(index, False), None)
 
     constant = left_constant(band_ref[...])
     slots = layer_slots((total, cols))
+    spread = len(packs)
     for layer in range(0, layers, 2):
         pair = jnp.concatenate([plastic[layer], plastic[layer + 1]], axis=1)
         result = left_product(constant, pair)
@@ -280,18 +280,44 @@
             value = result[:, inner * cols : (inner + 1) * cols]
             across[layer + inner] = value
             moved = pltpu.roll(value, (layer + inner) * REACH, 1) if layer + inner else value
-            for behind, ref in enumerate((pack_low, pack_high, pack_next)):
-                mask = slots == (layer + inner - behind) % (cols // REACH)
-                pltpu.store(ref, moved, mask=mask)
-
-    low_cols[...] = right_product(pack_low[...], right_constant(low_ref[...]))
-    high = right_product(pack_high[...], right_constant(high_ref[...]))
-    behind = right_product(pack_next[...], right_constant(next_ref[...]))
+            mask = ((layer + inner - slots) & (layers - 1)) < 3
+            pltpu.store(packs[(layer + inner) % spread], moved, mask=mask)
+
+    def gathered(behind):
+        source = (slots + behind) & (spread - 1)
+        parts = packs[0][...]
+        for index in range(1, spread):
+            parts = jnp.where(source == index, packs[index][...], parts)
+        return parts
+
+    low_cols[...] = right_product(gathered(0), right_constant(low_ref[...]))
+    high = right_product(gathered(1), right_constant(high_ref[...]))
+    behind = right_product(gathered(2), right_constant(next_ref[...]))
     high_cols[:, :cols] = high[:, :cols]
-
     drop = (high[:, cols:] + behind) * norm_last[...]
     first_lanes = lane_ids((total, cols)) < layers
-    high_cols[:, cols:] = fixed_out[...] - jnp.where(first_lanes, drop, pack_last[...])
+    high_cols[:, cols:] = fixed[...] - jnp.where(first_lanes, drop, pack_last[...])
+
+
+def prepare_kernel(stress, strain, threshold, _, factor, fixed):
+    layers, rows, cols = stress.shape
+    lanes = lane_ids((REACH, cols))
+    fixed[...] = jnp.zeros_like(fixed)
+
+    def step(index, carry):
+        for near in range(2):
+            first = (2 * index + near) * REACH
+            part = pl.ds(pl.multiple_of(first, REACH), REACH)
+            extended = pl.ds(pl.multiple_of(first + REACH, REACH), REACH)
+            for layer in range(layers):
+                at = (layer, part, slice(None))
+                factor[at] = first_factor(strain[at])
+                for lane, value in ((layer, threshold[at]), (layers + layer, stress[at] + strain[at])):
+                    moved = pltpu.roll(value, lane + 1, 1)
+                    pltpu.store(fixed.at[extended, :], moved, mask=lanes == lane)
+        return carry
+
+    lax.fori_loop(0, rows // (2 * REACH), step, 0)
 
 
 def pack_edges(values):
@@ -308,7 +334,7 @@
 
 
 def corner_kernel(row_even, row_odd, rest_even, rest_odd, low_cols, high_cols, norm_last,
-                  _, __, low_ref, high_ref, next_ref, even_ref, odd_ref, own_ref):
+                  _, low_ref, high_ref, next_ref, even_ref, odd_ref, own_ref):
     cols = low_ref.shape[0]
     total = low_cols.shape[0]
     layers = (total - REACH) // REACH
@@ -410,7 +436,7 @@
 
 def final_kernel(stress, strain, plastic, inner, inner_before, edge_low, edge_high, norm_low, norm_high,
                  col_even, col_odd, last_even, last_odd, rest_even, rest_odd, norm_before, own_cols,
-                 plastic_out, damage_out, force_out, columns, damage_s, force_s, sums, diffs,
+                 plastic_out, damage_out, force_out, columns, lows, highs, damage_s, force_s, sums, diffs,
                  copy_sem, sems):
     layers, rows, cols = stress.shape
     whole = pltpu.make_async_copy(plastic, plastic_out, copy_sem)
@@ -424,6 +450,17 @@
     kept = ratio(column - own_cols[...] * norm_before[...])
     columns[...] = (0.5 * kept) * pltpu.roll(column, cols - layers, 1)
 
+    low, high = edge_ratios(
+        (edge_low, edge_high), (last_even, last_odd), (norm_low, norm_high),
+        pl.ds(0, REACH), pl.ds(0, REACH),
+    )
+    lows[pl.ds(0, REACH), :], highs[pl.ds(0, REACH), :] = low, high
+    low, high = edge_ratios(
+        (edge_low, edge_high), (col_even, col_odd), (norm_low, norm_high),
+        pl.ds(0, rows), pl.ds(REACH, rows),
+    )
+    lows[pl.ds(REACH, rows), :], highs[pl.ds(REACH, rows), :] = low, high
+
     def copies(layer):
         return (
             pltpu.make_async_copy(damage_s.at[layer], damage_out.at[layer], sems.at[0, layer]),
@@ -436,10 +473,7 @@
         for block in range(rows // REACH + 1):
             extended = pl.ds(block * REACH, REACH)
             part = pl.ds((block - 1) * REACH if block else 0, REACH)
-            received = (col_even, col_odd) if block else (last_even, last_odd)
-            packed = edge_ratios(
-                (edge_low, edge_high), received, (norm_low, norm_high), part, extended
-            )
+            packed = lows[extended, :], highs[extended, :]
             at = (layer, part, slice(None))
             if block:
                 rest = (stress[at] + strain[at]) - plastic[at]
@@ -558,7 +592,7 @@
 
 def local(trial_stress, old_strain, yield_mask, newton_count, damage_threshold):
     layers, rows, cols = trial_stress.shape
-    assert layers * REACH == cols == rows and layers % 2 == 0
+    assert layers * REACH == cols == rows and layers & (layers - 1) == 0
     total, strip = rows + REACH, layers * REACH
     depth, constants = matrices(layers, rows, cols)
     below, above, rows_band, cols_band, *columns = constants
@@ -581,14 +615,14 @@
     stress, strain, _, _, threshold = inputs
     kept, edge_low, edge_high, norms = stress, norm_low, norm_high, (norm_low, norm_high)
     rest_even = rest_odd = rest
-    fixed = norm_last
+    fixed, factor = norm_last, stress
     for outer_no in range(OUTER):
         last = outer_no == OUTER - 1
         if outer_no:
             row_even, row_odd = call(
                 edge_kernel, [sent_rows] * 2,
                 [(strip, cols), (2 * strip, cols), (2 * layers, cols)], 800,
-                (*inputs, kept, kept_before, edge_low, edge_high, *norms, col_even, col_odd,
+                (*inputs, factor, kept, kept_before, edge_low, edge_high, *norms, col_even, col_odd,
                  below, above),
             )
         if not last:
@@ -598,17 +632,21 @@
             rest_even, rest_odd = row_even[strip:], row_odd[strip:]
             row_even, row_odd = row_even[:strip], row_odd[:strip]
         turn = jnp.full((1,), outer_no, jnp.int32)
-        across, low_cols, high_cols, plastic, fixed = call(
-            main_kernel, [wide, packed_two, packed_two, whole, packed],
-            [packed, packed, packed, packed], 4500,
-            (turn, *inputs, kept, edge_low, edge_high, *norms, col_even, col_odd, norm_last,
+        across, low_cols, high_cols, plastic = call(
+            main_kernel, [wide, packed_two, packed_two, whole],
+            [packed] * 5, 4500,
+            (turn, *inputs[:4], factor, kept, edge_low, edge_high, *norms, col_even, col_odd, norm_last,
              fixed, rows_band, *columns),
             [pltpu.SMEM] + [pltpu.VMEM] * 18,
         )
         col_even, col_odd, own_cols = call(
             corner_kernel, [sent_cols, sent_cols, packed], [], 400,
-            (row_even, row_odd, rest_even, rest_odd, low_cols, high_cols, norm_last, plastic, fixed, *columns),
+            (row_even, row_odd, rest_even, rest_odd, low_cols, high_cols, norm_last, plastic, *columns),
         )
+        if not outer_no:
+            factor, fixed = call(
+                prepare_kernel, [whole, packed], [], 1200, (stress, strain, threshold, col_odd),
+            )
         used = last_cols if last else rows
         col_even, col_odd = col_even[:used], col_odd[:used]
         col_even, col_odd = exchange("gy", "gx", col_even, col_odd)
@@ -621,7 +659,7 @@
         )
     return tuple(call(
         final_kernel, [whole, whole, (2, *whole)],
-        [packed, whole, (2, *whole), (2, *packed), (2, *packed),
+        [packed] * 3 + [whole, (2, *whole), (2, *packed), (2, *packed),
          pltpu.SemaphoreType.DMA(()), pltpu.SemaphoreType.DMA((3, layers))],
         3000,
         (stress, strain, plastic, kept, kept_before, edge_low, edge_high, *norms, col_even, col_odd,

time: 43.6 us -> 43 us (0.986)
  waiting for transfers between devices: 4.98 us -> 3.19 us
  starting transfers between devices: 14.1 us -> 15.3 us
    ppermute x12, waiting for transfers between devices: 4.98 us -> 3.19 us  [exchange(): results.append(lax.ppermute(value, names, pairs))]
    ppermute x12, starting transfers between devices: 14.1 us -> 15.3 us  [exchange(): results.append(lax.ppermute(value, names, pairs))]
    pallas_call x13 -> x14, Pallas kernels: 23.3 us -> 23.3 us  [call(): pl.pallas_call(kernel, out_shape=shapes, in_specs=[pl.BlockSpec(memory_sp...]
  transfers between devices with their start and end apart: 12 -> 12, of which waited for: 4 -> 3; matrix products, arithmetic and copies ran while one was open for 0% -> 0% of each run, Pallas kernels for 33% -> 34%
where the time goes in v9:
time: 43 us; the launch traced here: 42.9 us
  Pallas kernels  23.3 us (54%)
  starting transfers between devices  15.3 us (36%)
  waiting for transfers between devices  3.19 us (7%)
  between operations  0.94 us (2%)
    pallas_call x14, Pallas kernels, call(): pl.pallas_call(kernel, out_shape=shapes, in_specs=[pl.BlockSpec(memory_sp...  23.3 us
    ppermute x12, starting transfers between devices, exchange(): results.append(lax.ppermute(value, names, pairs))  15.3 us
    ppermute x12, waiting for transfers between devices, exchange(): results.append(lax.ppermute(value, names, pairs))  3.19 us
  transfers between devices with their start and end apart: 12, of which 3 were waited for; matrix products, arithmetic and copies ran while one was open for 0% of the time, Pallas kernels for 34%

profile of v9, /device:TPU:0, one launch (start us, length us, event | category | flops | bytes accessed | tf_op | source)
XLA Modules:
  0.0 42.9 jit_solution(5828571073409147926)
XLA Ops:
  0.6 0.0 copy-start
  0.6 0.0 copy-start.1
  0.7 0.0 copy-start.3
  0.7 0.0 copy-start.5
  0.7 2.8 %shard_map.139 = (f32[136,128]{1,0:T(8,128)S(1)}, f32[136,128]{1,0:T(8,128)S(1)}, f32[136,128]{1,0:T(8,128)S(1)}, f32[136,128]{1,0:T(8,128)S(1)}, f32[136,128]{1...) custom-call(f32[16,128,128]{2,1,0:T(8,128)} %refs_0_.1, ...), custom_call_target="tpu_custom_call" | custom-call | flops 2500000000 | bytes 2500000 | tf_op jit(solution)/shard_map/pallas_call | solution.py:522
  3.5 0.5 %collective-permute-start.1 = (f32[128,128]{1,0:T(8,128)S(1)}, f32[128,128]{1,0:T(8,128)S(1)}, u32[]{:S(2)}, u32[]{:S(2)}) collective-permute-start(f32[128,128]{1,0:T(8,128)S(1)} %slice.55), channel_id=1, source_target_pairs={{0,1},{1,0},{2,3},{3,2},{4,8},{5,9},{6,10},{7,11},{8,4},{9,5},{10,... | collective-permute-start | bytes 196616 | tf_op jit(solution)/shard_map/ppermute | solution.py:552
  4.0 4.0 %collective-permute-start = (f32[128,128]{1,0:T(8,128)S(1)}, f32[128,128]{1,0:T(8,128)S(1)}, u32[]{:S(2)}, u32[]{:S(2)}) collective-permute-start(f32[128,128]{1,0:T(8,128)S(1)} %slice.54), channel_id=1, source_target_pairs={{0,4},{1,5},{2,6},{3,7},{4,0},{5,1},{6,2},{7,3},{8,12},{9,13},{10,... | collective-permute-start | bytes 196616 | tf_op jit(solution)/shard_map/ppermute | solution.py:552
  8.1 0.0 copy-done
  8.1 0.0 copy-done.1
  8.1 0.0 copy-done.3
  8.1 0.0 copy-done.5
  8.1 2.9 %shard_map.140 = (f32[16,136,128]{2,1,0:T(8,128)S(1)}, f32[136,256]{1,0:T(8,128)S(1)}, f32[136,256]{1,0:T(8,128)S(1)}, f32[16,128,128]{2,1,0:T(8,128)S(1)}) custom-call(s32[1]{0:T(128)} %constant.8.clone.1.turn, f32[16,128,128]{2,1,0:T(8,128)S(1)} %get-tuple-element.57.stress.factor.kept, f32[16,128,128]{2,1,0:T(8,128)S(1)} %get-tuple-element.58.strain, ...), custom_call_target="tpu_custom_call" | custom-call | flops 4499999744 | bytes 4500000 | tf_op jit(solution)/shard_map/pallas_call | solution.py:522
  11.0 0.0 copy-start.6
  11.0 0.0 collective-permute-done.1.row_odd
  11.0 0.0 collective-permute-done.row_even
  11.0 0.4 shard_map.141
  11.4 1.7 %collective-permute-start.3 = (f32[128,128]{1,0:T(8,128)S(1)}, f32[128,128]{1,0:T(8,128)S(1)}, u32[]{:S(2)}, u32[]{:S(2)}) collective-permute-start(f32[128,128]{1,0:T(8,128)S(1)} %slice.57), channel_id=1, source_target_pairs={{0,4},{4,0},{8,12},{12,8},{16,20},{20,16},{24,28},{28,24},{1,2},{5... | collective-permute-start | bytes 196616 | tf_op jit(solution)/shard_map/ppermute | solution.py:552
  13.1 0.0 collective-permute-start.2
  13.1 0.0 copy-done.6
  13.1 1.2 %shard_map.143 = (f32[16,128,128]{2,1,0:T(8,128)S(1)}, f32[16,8,128]{2,1,0:T(8,128)S(1)}, f32[136,128]{1,0:T(8,128)S(1)}, f32[136,128]{1,0:T(8,128)S(1)}) custom-call(f32[16,136,128]{2,1,0:T(8,128)S(1)} %get-tuple-element.75.across, f32[128,128]{1,0:T(8,128)S(1)} %collective-permute-done.row_even, f32[128,128]{1,0:T(8,128)S(1)} %collective-permute-done.1.row_odd, ...), custom_call_target="tpu_custom_call" | custom-call | flops 1800000000 | bytes 1800000 | tf_op jit(solution)/shard_map/pallas_call | solution.py:522
  14.3 0.0 copy-start.2
  14.4 0.0 copy-start.4
  14.4 1.2 %shard_map.142 = (f32[16,128,128]{2,1,0:T(8,128)S(1)}, f32[136,128]{1,0:T(8,128)S(1)}) custom-call(f32[16,128,128]{2,1,0:T(8,128)S(1)} %get-tuple-element.57.stress.factor.kept, f32[16,128,128]{2,1,0:T(8,128)S(1)} %get-tuple-element.58.strain, f32[16,128,128]{2,1,0:T(8,128)S(1)} %get-tuple-element.61.threshold, f32[184,128]{1,0:T(8,128)S(1)} %get-tuple-element.73._), custom_call_target="tpu_custom_call" | custom-call | flops 1200000000 | bytes 1200000 | tf_op jit(solution)/shard_map/pallas_call | solution.py:522
  15.6 0.1 collective-permute-done.3.col_odd
  15.8 0.0 collective-permute-done.2.col_even
  15.8 0.0 copy-done.2
  15.8 0.0 copy-done.4
  15.8 0.7 %shard_map.145 = (f32[176,128]{1,0:T(8,128)S(1)}, f32[176,128]{1,0:T(8,128)S(1)}) custom-call(f32[16,128,128]{2,1,0:T(8,128)S(1)} %get-tuple-element.57.stress.factor.kept, f32[16,128,128]{2,1,0:T(8,128)S(1)} %get-tuple-element.58.strain, s32[16,128,128]{2,1,0:T(8,128)S(1)} %get-tuple-element.59.yields, s32[16,128,128]{2,1,0:T(8,128)S(1)} %get-tuple-element.60.count, ...), custom_call_target="tpu_custom_call" | custom-call | flops 800000000 | bytes 800000 | tf_op jit(solution)/shard_map/pallas_call | solution.py:522
  16.5 0.5 %collective-permute-start.5 = (f32[128,128]{1,0:T(8,128)S(1)}, f32[128,128]{1,0:T(8,128)S(1)}, u32[]{:S(2)}, u32[]{:S(2)}) collective-permute-start(f32[128,128]{1,0:T(8,128)S(1)} %slice.59), channel_id=1, source_target_pairs={{0,1},{1,0},{2,3},{3,2},{4,8},{5,9},{6,10},{7,11},{8,4},{9,5},{10,... | collective-permute-start | bytes 196616 | tf_op jit(solution)/shard_map/ppermute | solution.py:552
  17.0 2.8 %collective-permute-start.4 = (f32[128,128]{1,0:T(8,128)S(1)}, f32[128,128]{1,0:T(8,128)S(1)}, u32[]{:S(2)}, u32[]{:S(2)}) collective-permute-start(f32[128,128]{1,0:T(8,128)S(1)} %slice.58), channel_id=1, source_target_pairs={{0,4},{1,5},{2,6},{3,7},{4,0},{5,1},{6,2},{7,3},{8,12},{9,13},{10,... | collective-permute-start | bytes 196616 | tf_op jit(solution)/shard_map/ppermute | solution.py:552
  19.8 3.4 %shard_map.144 = (f32[16,136,128]{2,1,0:T(8,128)S(1)}, f32[136,256]{1,0:T(8,128)S(1)}, f32[136,256]{1,0:T(8,128)S(1)}, f32[16,128,128]{2,1,0:T(8,128)S(1)}) custom-call(s32[1]{0:T(128)} %constant.9.clone.1.turn, f32[16,128,128]{2,1,0:T(8,128)S(1)} %get-tuple-element.57.stress.factor.kept, f32[16,128,128]{2,1,0:T(8,128)S(1)} %get-tuple-element.58.strain, ...), custom_call_target="tpu_custom_call" | custom-call | flops 4499999744 | bytes 4500000 | tf_op jit(solution)/shard_map/pallas_call | solution.py:522
  23.1 0.0 collective-permute-done.5.row_odd
  23.1 0.0 collective-permute-done.4.row_even
  23.2 0.4 shard_map.146
  23.6 1.3 %collective-permute-start.7 = (f32[128,128]{1,0:T(8,128)S(1)}, f32[128,128]{1,0:T(8,128)S(1)}, u32[]{:S(2)}, u32[]{:S(2)}) collective-permute-start(f32[128,128]{1,0:T(8,128)S(1)} %slice.61), channel_id=1, source_target_pairs={{0,4},{4,0},{8,12},{12,8},{16,20},{20,16},{24,28},{28,24},{1,2},{5... | collective-permute-start | bytes 196616 | tf_op jit(solution)/shard_map/ppermute | solution.py:552
  24.9 0.0 collective-permute-start.6
  24.9 1.2 %shard_map.147 = (f32[16,128,128]{2,1,0:T(8,128)S(1)}, f32[16,8,128]{2,1,0:T(8,128)S(1)}, f32[136,128]{1,0:T(8,128)S(1)}, f32[136,128]{1,0:T(8,128)S(1)}) custom-call(f32[16,136,128]{2,1,0:T(8,128)S(1)} %get-tuple-element.83.across, f32[128,128]{1,0:T(8,128)S(1)} %collective-permute-done.4.row_even, f32[128,128]{1,0:T(8,128)S(1)} %collective-permute-done.5.row_odd, ...), custom_call_target="tpu_custom_call" | custom-call | flops 1800000000 | bytes 1800000 | tf_op jit(solution)/shard_map/pallas_call | solution.py:522
  26.1 1.8 %collective-permute-done.7.col_odd = f32[128,128]{1,0:T(8,128)S(1)} collective-permute-done((f32[128,128]{1,0:T(8,128)S(1)}, f32[128,128]{1,0:T(8,128)S(1)}, u32[]{:S(2)}, u32[]{:S(2)}) %collective-permute-start.7) | collective-permute-done | bytes 65568 | tf_op jit(solution)/shard_map/ppermute | solution.py:552
  27.9 0.0 collective-permute-done.6.col_even
  27.9 0.7 %shard_map.149 = (f32[176,128]{1,0:T(8,128)S(1)}, f32[176,128]{1,0:T(8,128)S(1)}) custom-call(f32[16,128,128]{2,1,0:T(8,128)S(1)} %get-tuple-element.57.stress.factor.kept, f32[16,128,128]{2,1,0:T(8,128)S(1)} %get-tuple-element.58.strain, s32[16,128,128]{2,1,0:T(8,128)S(1)} %get-tuple-element.59.yields, s32[16,128,128]{2,1,0:T(8,128)S(1)} %get-tuple-element.60.count, ...), custom_call_target="tpu_custom_call" | custom-call | flops 800000000 | bytes 800000 | tf_op jit(solution)/shard_map/pallas_call | solution.py:522
  28.6 1.4 %collective-permute-start.8 = (f32[176,128]{1,0:T(8,128)S(1)}, f32[176,128]{1,0:T(8,128)S(1)}, u32[]{:S(2)}, u32[]{:S(2)}) collective-permute-start(f32[176,128]{1,0:T(8,128)S(1)} %get-tuple-element.99), channel_id=1, source_target_pairs={{0,4},{1,5},{2,6},{3,7},{4,0},{5,1},{6,2},{7,3},{8,12},{9,13},{10,... | collective-permute-start | bytes 270344 | tf_op jit(solution)/shard_map/ppermute | solution.py:552
  30.0 0.0 collective-permute-start.9
  30.0 3.4 %shard_map.148 = (f32[16,136,128]{2,1,0:T(8,128)S(1)}, f32[136,256]{1,0:T(8,128)S(1)}, f32[136,256]{1,0:T(8,128)S(1)}, f32[16,128,128]{2,1,0:T(8,128)S(1)}) custom-call(s32[1]{0:T(128)} %constant.7.clone.1.turn, f32[16,128,128]{2,1,0:T(8,128)S(1)} %get-tuple-element.57.stress.factor.kept, f32[16,128,128]{2,1,0:T(8,128)S(1)} %get-tuple-element.58.strain, ...), custom_call_target="tpu_custom_call" | custom-call | flops 4499999744 | bytes 4500000 | tf_op jit(solution)/shard_map/pallas_call | solution.py:522
  33.3 0.0 collective-permute-done.8
  33.4 0.0 collective-permute-done.9
  33.4 0.4 shard_map.150
  33.8 3.1 %collective-permute-start.11 = (f32[176,128]{1,0:T(8,128)S(1)}, f32[176,128]{1,0:T(8,128)S(1)}, u32[]{:S(2)}, u32[]{:S(2)}) collective-permute-start(f32[176,128]{1,0:T(8,128)S(1)} %slice.68), channel_id=1, source_target_pairs={{0,4},{4,0},{8,12},{12,8},{16,20},{20,16},{24,28},{28,24},{1,2},{5... | collective-permute-start | bytes 270344 | tf_op jit(solution)/shard_map/ppermute | solution.py:552
  36.9 0.0 collective-permute-start.10
  36.9 1.2 %shard_map.151 = (f32[16,128,128]{2,1,0:T(8,128)S(1)}, f32[16,8,128]{2,1,0:T(8,128)S(1)}, f32[136,128]{1,0:T(8,128)S(1)}, f32[136,128]{1,0:T(8,128)S(1)}) custom-call(f32[16,136,128]{2,1,0:T(8,128)S(1)} %get-tuple-element.97.across, f32[128,128]{1,0:T(8,128)S(1)} %slice.72.row_even, f32[128,128]{1,0:T(8,128)S(1)} %slice.73.row_odd, ...), custom_call_target="tpu_custom_call" | custom-call | flops 1800000000 | bytes 1800000 | tf_op jit(solution)/shard_map/pallas_call | solution.py:522
  38.2 1.3 %collective-permute-done.11 = f32[176,128]{1,0:T(8,128)S(1)} collective-permute-done((f32[176,128]{1,0:T(8,128)S(1)}, f32[176,128]{1,0:T(8,128)S(1)}, u32[]{:S(2)}, u32[]{:S(2)}) %collective-permute-start.11) | collective-permute-done | bytes 90144 | tf_op jit(solution)/shard_map/ppermute | solution.py:552
  39.5 0.0 collective-permute-done.10
  39.5 3.4 %shard_map.152 = (f32[16,128,128]{2,1,0:T(8,128)}, f32[16,128,128]{2,1,0:T(8,128)}, f32[2,16,128,128]{3,2,1,0:T(8,128)}) custom-call(f32[16,128,128]{2,1,0:T(8,128)S(1)} %get-tuple-element.57.stress.factor.kept, f32[16,128,128]{2,1,0:T(8,128)S(1)} %get-tuple-element.58.strain, f32[16,128,128]{2,1,0:T(8,128)S(1)} %get-tuple-element.96._.plastic, ...), custom_call_target="tpu_custom_call" | custom-call | flops 3000000000 | bytes 3000000 | tf_op jit(solution)/shard_map/pallas_call | solution.py:522
  (18 shorter events, 0.1 us)
Async XLA Ops:
  0.6 7.4 %copy-start = (f32[128,256]{1,0:T(8,128)S(1)}, f32[128,256]{1,0:T(8,128)}, u32[]{:S(2)}) copy-start(f32[128,256]{1,0:T(8,128)} %constant.25.clone.high_ref) | copy-start | bytes 393220
  0.6 7.4 %copy-start.1 = (f32[128,256]{1,0:T(8,128)S(1)}, f32[128,256]{1,0:T(8,128)}, u32[]{:S(2)}) copy-start(f32[128,256]{1,0:T(8,128)} %constant.24.clone.low_ref) | copy-start | bytes 393220
  0.7 7.4 %copy-start.3 = (f32[128,128]{1,0:T(8,128)S(1)}, f32[128,128]{1,0:T(8,128)}, u32[]{:S(2)}) copy-start(f32[128,128]{1,0:T(8,128)} %constant.26.clone.next_ref) | copy-start | bytes 196612
  0.7 7.4 %copy-start.5 = (f32[136,128]{1,0:T(8,128)S(1)}, f32[136,128]{1,0:T(8,128)}, u32[]{:S(2)}) copy-start(f32[136,128]{1,0:T(8,128)} %constant.22.clone.band_ref) | copy-start | bytes 208900
  3.5 7.5 %collective-permute-start.1 = (f32[128,128]{1,0:T(8,128)S(1)}, f32[128,128]{1,0:T(8,128)S(1)}, u32[]{:S(2)}, u32[]{:S(2)}) collective-permute-start(f32[128,128]{1,0:T(8,128)S(1)} %slice.55), channel_id=1, source_target_pairs={{0,1},{1,0},{2,3},{3,2},{4,8},{5,9},{6,10},{7,11},{8,4},{9,5},{10,... | collective-permute-start | bytes 196616 | tf_op jit(solution)/shard_map/ppermute | solution.py:552
  4.0 7.0 %collective-permute-start = (f32[128,128]{1,0:T(8,128)S(1)}, f32[128,128]{1,0:T(8,128)S(1)}, u32[]{:S(2)}, u32[]{:S(2)}) collective-permute-start(f32[128,128]{1,0:T(8,128)S(1)} %slice.54), channel_id=1, source_target_pairs={{0,4},{1,5},{2,6},{3,7},{4,0},{5,1},{6,2},{7,3},{8,12},{9,13},{10,... | collective-permute-start | bytes 196616 | tf_op jit(solution)/shard_map/ppermute | solution.py:552
  11.0 2.1 %copy-start.6 = (f32[128,128]{1,0:T(8,128)S(1)}, f32[128,128]{1,0:T(8,128)}, u32[]{:S(2)}) copy-start(f32[128,128]{1,0:T(8,128)} %constant.23.clone.band_ref) | copy-start | bytes 196612
  11.4 4.3 %collective-permute-start.3 = (f32[128,128]{1,0:T(8,128)S(1)}, f32[128,128]{1,0:T(8,128)S(1)}, u32[]{:S(2)}, u32[]{:S(2)}) collective-permute-start(f32[128,128]{1,0:T(8,128)S(1)} %slice.57), channel_id=1, source_target_pairs={{0,4},{4,0},{8,12},{12,8},{16,20},{20,16},{24,28},{28,24},{1,2},{5... | collective-permute-start | bytes 196616 | tf_op jit(solution)/shard_map/ppermute | solution.py:552
  13.1 2.6 %collective-permute-start.2 = (f32[128,128]{1,0:T(8,128)S(1)}, f32[128,128]{1,0:T(8,128)S(1)}, u32[]{:S(2)}, u32[]{:S(2)}) collective-permute-start(f32[128,128]{1,0:T(8,128)S(1)} %slice.56), channel_id=1, source_target_pairs={{0,1},{4,5},{8,9},{12,13},{16,17},{20,21},{24,25},{28,29},{1,0},{5... | collective-permute-start | bytes 196616 | tf_op jit(solution)/shard_map/ppermute | solution.py:552
  14.3 1.4 %copy-start.2 = (f32[144,256]{1,0:T(8,128)S(1)}, f32[144,256]{1,0:T(8,128)}, u32[]{:S(2)}) copy-start(f32[144,256]{1,0:T(8,128)} %constant.21.clone.above) | copy-start | bytes 442372
  14.4 1.4 %copy-start.4 = (f32[128,128]{1,0:T(8,128)S(1)}, f32[128,128]{1,0:T(8,128)}, u32[]{:S(2)}) copy-start(f32[128,128]{1,0:T(8,128)} %constant.20.clone.below) | copy-start | bytes 196612
  16.5 6.6 %collective-permute-start.5 = (f32[128,128]{1,0:T(8,128)S(1)}, f32[128,128]{1,0:T(8,128)S(1)}, u32[]{:S(2)}, u32[]{:S(2)}) collective-permute-start(f32[128,128]{1,0:T(8,128)S(1)} %slice.59), channel_id=1, source_target_pairs={{0,1},{1,0},{2,3},{3,2},{4,8},{5,9},{6,10},{7,11},{8,4},{9,5},{10,... | collective-permute-start | bytes 196616 | tf_op jit(solution)/shard_map/ppermute | solution.py:552
  17.0 6.2 %collective-permute-start.4 = (f32[128,128]{1,0:T(8,128)S(1)}, f32[128,128]{1,0:T(8,128)S(1)}, u32[]{:S(2)}, u32[]{:S(2)}) collective-permute-start(f32[128,128]{1,0:T(8,128)S(1)} %slice.58), channel_id=1, source_target_pairs={{0,4},{1,5},{2,6},{3,7},{4,0},{5,1},{6,2},{7,3},{8,12},{9,13},{10,... | collective-permute-start | bytes 196616 | tf_op jit(solution)/shard_map/ppermute | solution.py:552
  23.6 4.3 %collective-permute-start.7 = (f32[128,128]{1,0:T(8,128)S(1)}, f32[128,128]{1,0:T(8,128)S(1)}, u32[]{:S(2)}, u32[]{:S(2)}) collective-permute-start(f32[128,128]{1,0:T(8,128)S(1)} %slice.61), channel_id=1, source_target_pairs={{0,4},{4,0},{8,12},{12,8},{16,20},{20,16},{24,28},{28,24},{1,2},{5... | collective-permute-start | bytes 196616 | tf_op jit(solution)/shard_map/ppermute | solution.py:552
  24.9 3.0 %collective-permute-start.6 = (f32[128,128]{1,0:T(8,128)S(1)}, f32[128,128]{1,0:T(8,128)S(1)}, u32[]{:S(2)}, u32[]{:S(2)}) collective-permute-start(f32[128,128]{1,0:T(8,128)S(1)} %slice.60), channel_id=1, source_target_pairs={{0,1},{4,5},{8,9},{12,13},{16,17},{20,21},{24,25},{28,29},{1,0},{5... | collective-permute-start | bytes 196616 | tf_op jit(solution)/shard_map/ppermute | solution.py:552
  28.6 4.7 %collective-permute-start.8 = (f32[176,128]{1,0:T(8,128)S(1)}, f32[176,128]{1,0:T(8,128)S(1)}, u32[]{:S(2)}, u32[]{:S(2)}) collective-permute-start(f32[176,128]{1,0:T(8,128)S(1)} %get-tuple-element.99), channel_id=1, source_target_pairs={{0,4},{1,5},{2,6},{3,7},{4,0},{5,1},{6,2},{7,3},{8,12},{9,13},{10,... | collective-permute-start | bytes 270344 | tf_op jit(solution)/shard_map/ppermute | solution.py:552
  30.0 3.4 %collective-permute-start.9 = (f32[176,128]{1,0:T(8,128)S(1)}, f32[176,128]{1,0:T(8,128)S(1)}, u32[]{:S(2)}, u32[]{:S(2)}) collective-permute-start(f32[176,128]{1,0:T(8,128)S(1)} %get-tuple-element.100), channel_id=1, source_target_pairs={{0,1},{1,0},{2,3},{3,2},{4,8},{5,9},{6,10},{7,11},{8,4},{9,5},{10,... | collective-permute-start | bytes 270344 | tf_op jit(solution)/shard_map/ppermute | solution.py:552
  33.8 5.6 %collective-permute-start.11 = (f32[176,128]{1,0:T(8,128)S(1)}, f32[176,128]{1,0:T(8,128)S(1)}, u32[]{:S(2)}, u32[]{:S(2)}) collective-permute-start(f32[176,128]{1,0:T(8,128)S(1)} %slice.68), channel_id=1, source_target_pairs={{0,4},{4,0},{8,12},{12,8},{16,20},{20,16},{24,28},{28,24},{1,2},{5... | collective-permute-start | bytes 270344 | tf_op jit(solution)/shard_map/ppermute | solution.py:552
  36.9 2.5 %collective-permute-start.10 = (f32[176,128]{1,0:T(8,128)S(1)}, f32[176,128]{1,0:T(8,128)S(1)}, u32[]{:S(2)}, u32[]{:S(2)}) collective-permute-start(f32[176,128]{1,0:T(8,128)S(1)} %slice.66), channel_id=1, source_target_pairs={{0,1},{4,5},{8,9},{12,13},{16,17},{20,21},{24,25},{28,29},{1,0},{5... | collective-permute-start | bytes 270344 | tf_op jit(solution)/shard_map/ppermute | solution.py:552

commit v10 on v9

--- a/solution.py
+++ b/solution.py
@@ -14,7 +14,7 @@
 RATE = math.log2(math.e) / 0.3
 HALF_LN2 = 0.5 * math.log(2.0)
 VMEM_BYTES = 24 * 1024 * 1024
-FIRST_VMEM_BYTES = 48 * 1024 * 1024
+EDGE_VMEM_BYTES = 53 * 1024 * 1024
 
 
 def tap(offset):
@@ -145,18 +145,19 @@
 
 
 def first_edge_kernel(*refs):
-    sources, refs = refs[:5], refs[5:]
-    even_ref, odd_ref, norm, norm_low, norm_high, norm_last, norm_before, _, _, _, *refs = refs
-    targets, (block, sems) = refs[:5], refs[5:]
-    stress, strain, yields, count, _ = targets
-    layers, rows, cols = stress.shape
-    parts = (pl.ds(0, REACH), pl.ds(rows - REACH, REACH), pl.ds(REACH, rows - 2 * REACH))
+    sources, refs = refs[:4], refs[4:]
+    even_ref, odd_ref, norm, norm_low, norm_high, norm_last, norm_before, _, *refs = refs
+    targets, (block, sems) = refs[:4], refs[4:]
+    stress, strain, yields, count = targets
+    layers, rows, cols = sources[0].shape
     copies = []
-    for side, part in enumerate(parts):
+    for side, first_row in enumerate((0, rows - REACH)):
         for index, (source, target) in enumerate(zip(sources, targets)):
             copies.append(
                 pltpu.make_async_copy(
-                    source.at[:, part, :], target.at[:, part, :], sems.at[side, index]
+                    source.at[:, pl.ds(first_row, REACH), :],
+                    target.at[:, pl.ds(side * REACH, REACH), :],
+                    sems.at[side, index],
                 )
             )
             copies[-1].start()
@@ -179,10 +180,10 @@
     for side, matrix in enumerate(
         (jnp.where(steps <= 0, band_part, 0.0), jnp.where(steps >= 0, band_part, 0.0))
     ):
-        for copy in copies[side * 5 : side * 5 + 5]:
+        for copy in copies[side * 4 : side * 4 + 4]:
             copy.wait()
         for layer in range(layers):
-            at = (layer, parts[side], slice(None))
+            at = (layer, pl.ds(side * REACH, REACH), slice(None))
             block[pl.ds(layer * REACH, REACH), :] = newton(
                 stress[at], strain[at], yields[at], count[at], jnp.ones((REACH, cols), jnp.float32),
                 first_factor(strain[at]),
@@ -190,8 +191,6 @@
         product = left_product(left_constant(matrix), block[...])
         sent.append(jnp.concatenate([product, product[:REACH]], axis=0))
     send("gx", *sent, even_ref, odd_ref)
-    for copy in copies[10:]:
-        copy.wait()
 
 
 def edge_kernel(stress, strain, yields, count, threshold, factor, kept, _, edge_low, edge_high, norm_low,
@@ -232,8 +231,28 @@
     )
 
 
-def main_kernel(turn, stress, strain, yields, count, factor, kept, edge_low, edge_high, norm_low,
-                norm_high, col_even, col_odd, norm_last, fixed, band_ref, low_ref, high_ref, next_ref,
+def first_main_kernel(stress, strain, yields, count, band_ref, low_ref, high_ref, next_ref,
+                      across, low_cols, high_cols, plastic, *packs):
+    layers, rows, cols = stress.shape
+    step_rows = 4 * REACH
+
+    def step(index, carry):
+        for near in range(step_rows // REACH):
+            part = pl.ds(pl.multiple_of(index * step_rows + near * REACH, REACH), REACH)
+            for layer in range(layers):
+                at = (layer, part, slice(None))
+                plastic[at] = newton(
+                    stress[at], strain[at], yields[at], count[at],
+                    jnp.ones((REACH, cols), jnp.float32), first_factor(strain[at]),
+                )
+        return carry
+
+    lax.fori_loop(0, rows // step_rows, step, 0)
+    smooth_rows(plastic, (band_ref, low_ref, high_ref, next_ref), across, low_cols, high_cols, packs)
+
+
+def main_kernel(stress, strain, yields, count, factor, kept, edge_low, edge_high, norm_low, norm_high,
+                col_even, col_odd, norm_last, fixed, band_ref, low_ref, high_ref, next_ref,
                 across, low_cols, high_cols, plastic, pack_last, *packs):
     layers, rows, cols = stress.shape
     total = rows + REACH
@@ -241,35 +260,36 @@
     lanes = lane_ids((REACH, cols))
     pack_last[pl.ds(0, REACH), :] = jnp.zeros((REACH, cols), jnp.float32)
 
-    def newton_blocks(index, fresh):
+    def step(index, carry):
         for near in range(step_rows // REACH):
             first = index * step_rows + near * REACH
             part = pl.ds(pl.multiple_of(first, REACH), REACH)
             extended = pl.ds(pl.multiple_of(first + REACH, REACH), REACH)
-            if not fresh:
-                packed = edge_ratios(
-                    (edge_low, edge_high), (col_even, col_odd), (norm_low, norm_high), part, extended
-                )
+            packed = edge_ratios(
+                (edge_low, edge_high), (col_even, col_odd), (norm_low, norm_high), part, extended
+            )
             for layer in range(layers):
                 at = (layer, part, slice(None))
-                if fresh:
-                    ratios, lead = jnp.ones((REACH, cols), jnp.float32), first_factor(strain[at])
-                else:
-                    ratios, lead = with_edges(kept[at], layer, *packed), factor[at]
-                value = newton(stress[at], strain[at], yields[at], count[at], ratios, lead)
+                ratios = with_edges(kept[at], layer, *packed)
+                value = newton(stress[at], strain[at], yields[at], count[at], ratios, factor[at])
                 plastic[at] = value
-                if not fresh:
-                    lane = layers + layer
-                    pltpu.store(pack_last.at[extended, :], pltpu.roll(value, lane + 1, 1), mask=lanes == lane)
-
-    @pl.when(turn[0] == 0)
-    def _():
-        lax.fori_loop(0, rows // step_rows, lambda index, _: newton_blocks(index, True), None)
-
-    @pl.when(turn[0] > 0)
-    def _():
-        lax.fori_loop(0, rows // step_rows, lambda index, _: newton_blocks(index, False), None)
-
+                lane = layers + layer
+                pltpu.store(pack_last.at[extended, :], pltpu.roll(value, lane + 1, 1), mask=lanes == lane)
+        return carry
+
+    lax.fori_loop(0, rows // step_rows, step, 0)
+    behind = smooth_rows(
+        plastic, (band_ref, low_ref, high_ref, next_ref), across, low_cols, high_cols, packs
+    )
+    drop = behind * norm_last[...]
+    first_lanes = lane_ids((total, cols)) < layers
+    high_cols[:, cols:] = fixed[...] - jnp.where(first_lanes, drop, pack_last[...])
+
+
+def smooth_rows(plastic, tables, across, low_cols, high_cols, packs):
+    layers, rows, cols = plastic.shape
+    total = rows + REACH
+    band_ref, low_ref, high_ref, next_ref = tables
     constant = left_constant(band_ref[...])
     slots = layer_slots((total, cols))
     spread = len(packs)
@@ -294,9 +314,7 @@
     high = right_product(gathered(1), right_constant(high_ref[...]))
     behind = right_product(gathered(2), right_constant(next_ref[...]))
     high_cols[:, :cols] = high[:, :cols]
-    drop = (high[:, cols:] + behind) * norm_last[...]
-    first_lanes = lane_ids((total, cols)) < layers
-    high_cols[:, cols:] = fixed[...] - jnp.where(first_lanes, drop, pack_last[...])
+    return high[:, cols:] + behind
 
 
 def prepare_kernel(stress, strain, threshold, _, factor, fixed):
@@ -468,43 +486,56 @@
             pltpu.make_async_copy(force_s.at[1, layer], force_out.at[1, layer], sems.at[2, layer]),
         )
 
-    def layer_step(layer, near):
-        lanes = lane_ids((REACH, cols))
-        for block in range(rows // REACH + 1):
-            extended = pl.ds(block * REACH, REACH)
-            part = pl.ds((block - 1) * REACH if block else 0, REACH)
-            packed = lows[extended, :], highs[extended, :]
-            at = (layer, part, slice(None))
-            if block:
-                rest = (stress[at] + strain[at]) - plastic[at]
-            else:
-                line = pl.ds(layers + layer, 1)
-                rest, _ = sides("gx", rest_even[line, :], rest_odd[line, :])
-            kept = with_edges(inner[at] if block else inner_before[layer], layer, *packed)
-            value = (0.5 * kept) * rest
-            left = jnp.where(
-                lanes == 0,
-                pltpu.roll(columns[extended, :], (cols - layer) % cols, 1),
-                pltpu.roll(value, 1, 1),
-            )
-            both, diff = left + value, left - value
-            sums[near, extended, :] = both
-            diffs[near, extended, :] = diff
-            if block:
-                behind = pl.ds(block * REACH - 1, REACH)
-                damage_s[at] = 1.0 - kept
-                force_s[(0, *at)] = sums[near, behind, :] - both
-                force_s[(1, *at)] = diffs[near, behind, :] + diff
-
-    def step(index, carry):
+    lanes = lane_ids((REACH, cols))
+
+    def stresses(pair):
         for near in range(2):
-            layer_step(2 * index + near, near)
+            layer = 2 * pair + near
+            for block in range(rows // REACH + 1):
+                extended = pl.ds(block * REACH, REACH)
+                at = (layer, pl.ds((block - 1) * REACH if block else 0, REACH), slice(None))
+                if block:
+                    rest = (stress[at] + strain[at]) - plastic[at]
+                else:
+                    line = pl.ds(layers + layer, 1)
+                    rest, _ = sides("gx", rest_even[line, :], rest_odd[line, :])
+                kept = inner[at] if block else inner_before[layer]
+                kept = with_edges(kept, layer, lows[extended, :], highs[extended, :])
+                value = (0.5 * kept) * rest
+                left = jnp.where(
+                    lanes == 0,
+                    pltpu.roll(columns[extended, :], (cols - layer) % cols, 1),
+                    pltpu.roll(value, 1, 1),
+                )
+                sums[layer, extended, :] = left + value
+                diffs[layer, extended, :] = left - value
+                if block:
+                    damage_s[at] = 1.0 - kept
+
+    def forces(pair):
         for near in range(2):
-            for copy in copies(2 * index + near):
+            layer = 2 * pair + near
+            for block in range(rows // REACH):
+                at = (layer, pl.ds(block * REACH, REACH), slice(None))
+                here, behind = pl.ds((block + 1) * REACH, REACH), pl.ds((block + 1) * REACH - 1, REACH)
+                force_s[(0, *at)] = sums[layer, behind, :] - sums[layer, here, :]
+                force_s[(1, *at)] = diffs[layer, behind, :] + diffs[layer, here, :]
+
+    def start(pair):
+        for near in range(2):
+            for copy in copies(2 * pair + near):
                 copy.start()
+
+    def step(pair, carry):
+        forces(pair - 1)
+        stresses(pair)
+        start(pair - 1)
         return carry
 
-    lax.fori_loop(0, layers // 2, step, 0)
+    stresses(0)
+    lax.fori_loop(1, layers // 2, step, 0)
+    forces(layers // 2 - 1)
+    start(layers // 2 - 1)
 
     def drain(layer, carry):
         for copy in copies(layer):
@@ -604,26 +635,24 @@
     spare = (3 * layers, cols)
     packed, packed_two = (total, cols), (total, 2 * cols)
 
-    sources = (trial_stress, old_strain, yield_mask, newton_count, damage_threshold)
-    row_even, row_odd, norm, norm_low, norm_high, norm_last, norm_before, col_even, col_odd, rest, *inputs = call(
-        first_edge_kernel,
-        [(strip + REACH, cols)] * 2 + [packed] * 5 + [(rows, cols)] * 2 + [spare]
-        + [jax.ShapeDtypeStruct(whole, source.dtype) for source in sources],
-        [(strip, cols), pltpu.SemaphoreType.DMA((3, len(sources)))], 2500,
-        sources, [pltpu.HBM] * len(sources), limit=FIRST_VMEM_BYTES,
+    inputs = stress, strain, _, _ = (trial_stress, old_strain, yield_mask, newton_count)
+    threshold = damage_threshold
+    edge = [pltpu.VMEM((layers, 2 * REACH, cols), value.dtype) for value in inputs]
+    row_even, row_odd, norm, norm_low, norm_high, norm_last, norm_before, rest = call(
+        first_edge_kernel, [(strip + REACH, cols)] * 2 + [packed] * 5 + [spare],
+        edge + [(strip, cols), pltpu.SemaphoreType.DMA((2, 4))], 1500,
+        inputs, [pltpu.HBM] * 4, limit=EDGE_VMEM_BYTES,
     )
-    stress, strain, _, _, threshold = inputs
-    kept, edge_low, edge_high, norms = stress, norm_low, norm_high, (norm_low, norm_high)
+    norms = (norm_low, norm_high)
     rest_even = rest_odd = rest
-    fixed, factor = norm_last, stress
     for outer_no in range(OUTER):
         last = outer_no == OUTER - 1
         if outer_no:
             row_even, row_odd = call(
                 edge_kernel, [sent_rows] * 2,
                 [(strip, cols), (2 * strip, cols), (2 * layers, cols)], 800,
-                (*inputs, factor, kept, kept_before, edge_low, edge_high, *norms, col_even, col_odd,
-                 below, above),
+                (*inputs, threshold, factor, kept, kept_before, edge_low, edge_high, *norms,
+                 col_even, col_odd, below, above),
             )
         if not last:
             row_even, row_odd = row_even[:strip], row_odd[:strip]
@@ -631,14 +660,17 @@
         if last:
             rest_even, rest_odd = row_even[strip:], row_odd[strip:]
             row_even, row_odd = row_even[:strip], row_odd[:strip]
-        turn = jnp.full((1,), outer_no, jnp.int32)
-        across, low_cols, high_cols, plastic = call(
-            main_kernel, [wide, packed_two, packed_two, whole],
-            [packed] * 5, 4500,
-            (turn, *inputs[:4], factor, kept, edge_low, edge_high, *norms, col_even, col_odd, norm_last,
-             fixed, rows_band, *columns),
-            [pltpu.SMEM] + [pltpu.VMEM] * 18,
-        )
+        outs = [wide, packed_two, packed_two, whole]
+        if outer_no:
+            across, low_cols, high_cols, plastic = call(
+                main_kernel, outs, [packed] * 5, 4500,
+                (*inputs, factor, kept, edge_low, edge_high, *norms, col_even, col_odd, norm_last,
+                 fixed, rows_band, *columns),
+            )
+        else:
+            across, low_cols, high_cols, plastic = call(
+                first_main_kernel, outs, [packed] * 4, 4500, (*inputs, rows_band, *columns),
+            )
         col_even, col_odd, own_cols = call(
             corner_kernel, [sent_cols, sent_cols, packed], [], 400,
             (row_even, row_odd, rest_even, rest_odd, low_cols, high_cols, norm_last, plastic, *columns),
@@ -659,7 +691,7 @@
         )
     return tuple(call(
         final_kernel, [whole, whole, (2, *whole)],
-        [packed] * 3 + [whole, (2, *whole), (2, *packed), (2, *packed),
+        [packed] * 3 + [whole, (2, *whole), wide, wide,
          pltpu.SemaphoreType.DMA(()), pltpu.SemaphoreType.DMA((3, layers))],
         3000,
         (stress, strain, plastic, kept, kept_before, edge_low, edge_high, *norms, col_even, col_odd,

time: 43 us -> 41.9 us (0.974)
  Pallas kernels: 23.3 us -> 22.1 us
    pallas_call x14, Pallas kernels: 23.3 us -> 22.1 us  [call(): pl.pallas_call(kernel, out_shape=shapes, in_specs=[pl.BlockSpec(memory_sp...]
  transfers between devices with their start and end apart: 12 -> 12, of which waited for: 3 -> 3; matrix products, arithmetic and copies ran while one was open for 0% -> 0% of each run, Pallas kernels for 34% -> 35%
where the time goes in v10:
time: 41.9 us; the launch traced here: 41.8 us
  Pallas kernels  22.1 us (53%)
  starting transfers between devices  15.2 us (36%)
  waiting for transfers between devices  3.24 us (8%)
  between operations  1.01 us (2%)
    pallas_call x14, Pallas kernels, call(): pl.pallas_call(kernel, out_shape=shapes, in_specs=[pl.BlockSpec(memory_sp...  22.1 us
    ppermute x12, starting transfers between devices, exchange(): results.append(lax.ppermute(value, names, pairs))  15.2 us
    ppermute x12, waiting for transfers between devices, exchange(): results.append(lax.ppermute(value, names, pairs))  3.24 us
  transfers between devices with their start and end apart: 12, of which 3 were waited for; matrix products, arithmetic and copies ran while one was open for 0% of the time, Pallas kernels for 35%

profile of v10, /device:TPU:0, one launch (start us, length us, event | category | flops | bytes accessed | tf_op | source)
XLA Modules:
  0.0 41.8 jit_solution(16380873447484929375)
XLA Ops:
  0.6 0.0 copy-start.5
  0.6 0.0 copy-start.6
  0.7 0.0 copy-start.8
  0.7 0.0 copy-start.10
  0.7 0.0 copy-start.4
  0.7 0.0 copy-start.3
  0.7 0.0 copy-start.1
  0.7 0.0 copy-start
  0.7 1.9 %shard_map.139 = (f32[136,128]{1,0:T(8,128)S(1)}, f32[136,128]{1,0:T(8,128)S(1)}, f32[136,128]{1,0:T(8,128)S(1)}, f32[136,128]{1,0:T(8,128)S(1)}, f32[136,128]{1...) custom-call(f32[16,128,128]{2,1,0:T(8,128)} %stress.13, ...), custom_call_target="tpu_custom_call" | custom-call | flops 1500000000 | bytes 1500000 | tf_op jit(solution)/shard_map/pallas_call | solution.py:553
  2.6 0.5 %collective-permute-start.1 = (f32[128,128]{1,0:T(8,128)S(1)}, f32[128,128]{1,0:T(8,128)S(1)}, u32[]{:S(2)}, u32[]{:S(2)}) collective-permute-start(f32[128,128]{1,0:T(8,128)S(1)} %slice.55), channel_id=1, source_target_pairs={{0,1},{1,0},{2,3},{3,2},{4,8},{5,9},{6,10},{7,11},{8,4},{9,5},{10,... | collective-permute-start | bytes 196616 | tf_op jit(solution)/shard_map/ppermute | solution.py:583
  3.2 4.0 %collective-permute-start = (f32[128,128]{1,0:T(8,128)S(1)}, f32[128,128]{1,0:T(8,128)S(1)}, u32[]{:S(2)}, u32[]{:S(2)}) collective-permute-start(f32[128,128]{1,0:T(8,128)S(1)} %slice.54), channel_id=1, source_target_pairs={{0,4},{1,5},{2,6},{3,7},{4,0},{5,1},{6,2},{7,3},{8,12},{9,13},{10,... | collective-permute-start | bytes 196616 | tf_op jit(solution)/shard_map/ppermute | solution.py:583
  7.2 0.0 copy-done.5
  7.2 0.0 copy-done.6
  7.2 0.0 copy-done.8
  7.2 0.0 copy-done.10
  7.2 0.0 copy-done.4
  7.2 0.0 copy-done.3
  7.2 0.0 copy-done.1
  7.2 0.0 copy-done
  7.3 2.9 %shard_map.140 = (f32[16,136,128]{2,1,0:T(8,128)S(1)}, f32[136,256]{1,0:T(8,128)S(1)}, f32[136,256]{1,0:T(8,128)S(1)}, f32[16,128,128]{2,1,0:T(8,128)S(1)}) custom-call(f32[16,128,128]{2,1,0:T(8,128)S(1)} %copy-done.3, f32[16,128,128]{2,1,0:T(8,128)S(1)} %copy-done.4, s32[16,128,128]{2,1,0:T(8,128)S(1)} %copy-done, s32[16,128,128]{2,1,0:T(8,128)S(1)} %copy-done.1, ...), custom_call_target="tpu_custom_call" | custom-call | flops 4499999744 | bytes 4500000 | tf_op jit(solution)/shard_map/pallas_call | solution.py:553
  10.2 0.0 copy-start.2
  10.2 0.0 copy-start.11
  10.2 0.0 collective-permute-done.1.row_odd
  10.2 0.0 collective-permute-done.row_even
  10.2 0.4 shard_map.141
  10.6 1.6 %collective-permute-start.3 = (f32[128,128]{1,0:T(8,128)S(1)}, f32[128,128]{1,0:T(8,128)S(1)}, u32[]{:S(2)}, u32[]{:S(2)}) collective-permute-start(f32[128,128]{1,0:T(8,128)S(1)} %slice.57), channel_id=1, source_target_pairs={{0,4},{4,0},{8,12},{12,8},{16,20},{20,16},{24,28},{28,24},{1,2},{5... | collective-permute-start | bytes 196616 | tf_op jit(solution)/shard_map/ppermute | solution.py:583
  12.2 0.1 collective-permute-start.2
  12.3 0.0 copy-done.2
  12.3 0.0 copy-done.11
  12.3 1.2 %shard_map.143 = (f32[16,128,128]{2,1,0:T(8,128)S(1)}, f32[16,8,128]{2,1,0:T(8,128)S(1)}, f32[136,128]{1,0:T(8,128)S(1)}, f32[136,128]{1,0:T(8,128)S(1)}) custom-call(f32[16,136,128]{2,1,0:T(8,128)S(1)} %get-tuple-element.59.across, f32[128,128]{1,0:T(8,128)S(1)} %collective-permute-done.row_even, f32[128,128]{1,0:T(8,128)S(1)} %collective-permute-done.1.row_odd, ...), custom_call_target="tpu_custom_call" | custom-call | flops 1800000000 | bytes 1800000 | tf_op jit(solution)/shard_map/pallas_call | solution.py:553
  13.5 0.0 copy-start.7
  13.5 0.0 copy-start.9
  13.6 1.2 %shard_map.142 = (f32[16,128,128]{2,1,0:T(8,128)S(1)}, f32[136,128]{1,0:T(8,128)S(1)}) custom-call(f32[16,128,128]{2,1,0:T(8,128)S(1)} %copy-done.3, f32[16,128,128]{2,1,0:T(8,128)S(1)} %copy-done.4, f32[16,128,128]{2,1,0:T(8,128)S(1)} %copy-done.2, f32[184,128]{1,0:T(8,128)S(1)} %get-tuple-element.57._), custom_call_target="tpu_custom_call" | custom-call | flops 1200000000 | bytes 1200000 | tf_op jit(solution)/shard_map/pallas_call | solution.py:553
  14.8 0.2 collective-permute-done.3.col_odd
  14.9 0.0 collective-permute-done.2.col_even
  14.9 0.0 copy-done.7
  14.9 0.0 copy-done.9
  14.9 0.7 %shard_map.145 = (f32[176,128]{1,0:T(8,128)S(1)}, f32[176,128]{1,0:T(8,128)S(1)}) custom-call(f32[16,128,128]{2,1,0:T(8,128)S(1)} %copy-done.3, f32[16,128,128]{2,1,0:T(8,128)S(1)} %copy-done.4, s32[16,128,128]{2,1,0:T(8,128)S(1)} %copy-done, s32[16,128,128]{2,1,0:T(8,128)S(1)} %copy-done.1, f32[16,128,128]{2,1,0:T(8,128)S(1)} %copy-done.2, ...), custom_call_target="tpu_custom_call" | custom-call | flops 800000000 | bytes 800000 | tf_op jit(solution)/shard_map/pallas_call | solution.py:553
  15.7 0.4 collective-permute-start.5
  16.1 2.8 %collective-permute-start.4 = (f32[128,128]{1,0:T(8,128)S(1)}, f32[128,128]{1,0:T(8,128)S(1)}, u32[]{:S(2)}, u32[]{:S(2)}) collective-permute-start(f32[128,128]{1,0:T(8,128)S(1)} %slice.58), channel_id=1, source_target_pairs={{0,4},{1,5},{2,6},{3,7},{4,0},{5,1},{6,2},{7,3},{8,12},{9,13},{10,... | collective-permute-start | bytes 196616 | tf_op jit(solution)/shard_map/ppermute | solution.py:583
  18.9 3.4 %shard_map.144 = (f32[16,136,128]{2,1,0:T(8,128)S(1)}, f32[136,256]{1,0:T(8,128)S(1)}, f32[136,256]{1,0:T(8,128)S(1)}, f32[16,128,128]{2,1,0:T(8,128)S(1)}) custom-call(f32[16,128,128]{2,1,0:T(8,128)S(1)} %copy-done.3, f32[16,128,128]{2,1,0:T(8,128)S(1)} %copy-done.4, s32[16,128,128]{2,1,0:T(8,128)S(1)} %copy-done, s32[16,128,128]{2,1,0:T(8,128)S(1)} %copy-done.1, ...), custom_call_target="tpu_custom_call" | custom-call | flops 4499999744 | bytes 4500000 | tf_op jit(solution)/shard_map/pallas_call | solution.py:553
  22.3 0.0 collective-permute-done.5.row_odd
  22.3 0.0 collective-permute-done.4.row_even
  22.3 0.4 shard_map.146
  22.7 1.3 %collective-permute-start.7 = (f32[128,128]{1,0:T(8,128)S(1)}, f32[128,128]{1,0:T(8,128)S(1)}, u32[]{:S(2)}, u32[]{:S(2)}) collective-permute-start(f32[128,128]{1,0:T(8,128)S(1)} %slice.61), channel_id=1, source_target_pairs={{0,4},{4,0},{8,12},{12,8},{16,20},{20,16},{24,28},{28,24},{1,2},{5... | collective-permute-start | bytes 196616 | tf_op jit(solution)/shard_map/ppermute | solution.py:583
  24.0 0.0 collective-permute-start.6
  24.0 1.2 %shard_map.147 = (f32[16,128,128]{2,1,0:T(8,128)S(1)}, f32[16,8,128]{2,1,0:T(8,128)S(1)}, f32[136,128]{1,0:T(8,128)S(1)}, f32[136,128]{1,0:T(8,128)S(1)}) custom-call(f32[16,136,128]{2,1,0:T(8,128)S(1)} %get-tuple-element.69.across, f32[128,128]{1,0:T(8,128)S(1)} %collective-permute-done.4.row_even, f32[128,128]{1,0:T(8,128)S(1)} %collective-permute-done.5.row_odd, ...), custom_call_target="tpu_custom_call" | custom-call | flops 1800000000 | bytes 1800000 | tf_op jit(solution)/shard_map/pallas_call | solution.py:553
  25.2 1.8 %collective-permute-done.7.col_odd = f32[128,128]{1,0:T(8,128)S(1)} collective-permute-done((f32[128,128]{1,0:T(8,128)S(1)}, f32[128,128]{1,0:T(8,128)S(1)}, u32[]{:S(2)}, u32[]{:S(2)}) %collective-permute-start.7) | collective-permute-done | bytes 65568 | tf_op jit(solution)/shard_map/ppermute | solution.py:583
  27.0 0.0 collective-permute-done.6.col_even
  27.0 0.7 %shard_map.149 = (f32[176,128]{1,0:T(8,128)S(1)}, f32[176,128]{1,0:T(8,128)S(1)}) custom-call(f32[16,128,128]{2,1,0:T(8,128)S(1)} %copy-done.3, f32[16,128,128]{2,1,0:T(8,128)S(1)} %copy-done.4, s32[16,128,128]{2,1,0:T(8,128)S(1)} %copy-done, s32[16,128,128]{2,1,0:T(8,128)S(1)} %copy-done.1, f32[16,128,128]{2,1,0:T(8,128)S(1)} %copy-done.2, ...), custom_call_target="tpu_custom_call" | custom-call | flops 800000000 | bytes 800000 | tf_op jit(solution)/shard_map/pallas_call | solution.py:553
  27.8 1.3 %collective-permute-start.8 = (f32[176,128]{1,0:T(8,128)S(1)}, f32[176,128]{1,0:T(8,128)S(1)}, u32[]{:S(2)}, u32[]{:S(2)}) collective-permute-start(f32[176,128]{1,0:T(8,128)S(1)} %get-tuple-element.85), channel_id=1, source_target_pairs={{0,4},{1,5},{2,6},{3,7},{4,0},{5,1},{6,2},{7,3},{8,12},{9,13},{10,... | collective-permute-start | bytes 270344 | tf_op jit(solution)/shard_map/ppermute | solution.py:583
  29.1 0.0 collective-permute-start.9
  29.1 3.4 %shard_map.148 = (f32[16,136,128]{2,1,0:T(8,128)S(1)}, f32[136,256]{1,0:T(8,128)S(1)}, f32[136,256]{1,0:T(8,128)S(1)}, f32[16,128,128]{2,1,0:T(8,128)S(1)}) custom-call(f32[16,128,128]{2,1,0:T(8,128)S(1)} %copy-done.3, f32[16,128,128]{2,1,0:T(8,128)S(1)} %copy-done.4, s32[16,128,128]{2,1,0:T(8,128)S(1)} %copy-done, s32[16,128,128]{2,1,0:T(8,128)S(1)} %copy-done.1, ...), custom_call_target="tpu_custom_call" | custom-call | flops 4499999744 | bytes 4500000 | tf_op jit(solution)/shard_map/pallas_call | solution.py:553
  32.5 0.0 collective-permute-done.8
  32.5 0.0 collective-permute-done.9
  32.5 0.4 shard_map.150
  32.9 3.1 %collective-permute-start.11 = (f32[176,128]{1,0:T(8,128)S(1)}, f32[176,128]{1,0:T(8,128)S(1)}, u32[]{:S(2)}, u32[]{:S(2)}) collective-permute-start(f32[176,128]{1,0:T(8,128)S(1)} %slice.68), channel_id=1, source_target_pairs={{0,4},{4,0},{8,12},{12,8},{16,20},{20,16},{24,28},{28,24},{1,2},{5... | collective-permute-start | bytes 270344 | tf_op jit(solution)/shard_map/ppermute | solution.py:583
  36.1 0.0 collective-permute-start.10
  36.1 1.2 %shard_map.151 = (f32[16,128,128]{2,1,0:T(8,128)S(1)}, f32[16,8,128]{2,1,0:T(8,128)S(1)}, f32[136,128]{1,0:T(8,128)S(1)}, f32[136,128]{1,0:T(8,128)S(1)}) custom-call(f32[16,136,128]{2,1,0:T(8,128)S(1)} %get-tuple-element.83.across, f32[128,128]{1,0:T(8,128)S(1)} %slice.72.row_even, f32[128,128]{1,0:T(8,128)S(1)} %slice.73.row_odd, ...), custom_call_target="tpu_custom_call" | custom-call | flops 1800000000 | bytes 1800000 | tf_op jit(solution)/shard_map/pallas_call | solution.py:553
  37.3 1.3 %collective-permute-done.11 = f32[176,128]{1,0:T(8,128)S(1)} collective-permute-done((f32[176,128]{1,0:T(8,128)S(1)}, f32[176,128]{1,0:T(8,128)S(1)}, u32[]{:S(2)}, u32[]{:S(2)}) %collective-permute-start.11) | collective-permute-done | bytes 90144 | tf_op jit(solution)/shard_map/ppermute | solution.py:583
  38.6 0.0 collective-permute-done.10
  38.6 3.1 %shard_map.152 = (f32[16,128,128]{2,1,0:T(8,128)}, f32[16,128,128]{2,1,0:T(8,128)}, f32[2,16,128,128]{3,2,1,0:T(8,128)}) custom-call(f32[16,128,128]{2,1,0:T(8,128)S(1)} %copy-done.3, f32[16,128,128]{2,1,0:T(8,128)S(1)} %copy-done.4, f32[16,128,128]{2,1,0:T(8,128)S(1)} %get-tuple-element.82._.plastic, f32[16,128,128]{2,1,0:T(8,128)S(1)} %get-tuple-element.90.inner, ...), custom_call_target="tpu_custom_call" | custom-call | flops 3000000000 | bytes 3000000 | tf_op jit(solution)/shard_map/pallas_call | solution.py:553
  (18 shorter events, 0.1 us)
Async XLA Ops:
  0.6 6.6 %copy-start.5 = (f32[128,256]{1,0:T(8,128)S(1)}, f32[128,256]{1,0:T(8,128)}, u32[]{:S(2)}) copy-start(f32[128,256]{1,0:T(8,128)} %constant.19.clone.high_ref) | copy-start | bytes 393220
  0.6 6.6 %copy-start.6 = (f32[128,256]{1,0:T(8,128)S(1)}, f32[128,256]{1,0:T(8,128)}, u32[]{:S(2)}) copy-start(f32[128,256]{1,0:T(8,128)} %constant.18.clone.low_ref) | copy-start | bytes 393220
  0.7 6.6 %copy-start.8 = (f32[128,128]{1,0:T(8,128)S(1)}, f32[128,128]{1,0:T(8,128)}, u32[]{:S(2)}) copy-start(f32[128,128]{1,0:T(8,128)} %constant.20.clone.next_ref) | copy-start | bytes 196612
  0.7 6.5 %copy-start.10 = (f32[136,128]{1,0:T(8,128)S(1)}, f32[136,128]{1,0:T(8,128)}, u32[]{:S(2)}) copy-start(f32[136,128]{1,0:T(8,128)} %constant.16.clone.band_ref) | copy-start | bytes 208900
  0.7 6.5 %copy-start.4 = (f32[16,128,128]{2,1,0:T(8,128)S(1)}, f32[16,128,128]{2,1,0:T(8,128)}, u32[]{:S(2)}) copy-start(f32[16,128,128]{2,1,0:T(8,128)} %strain.13) | copy-start | bytes 3145732
  0.7 6.5 %copy-start.3 = (f32[16,128,128]{2,1,0:T(8,128)S(1)}, f32[16,128,128]{2,1,0:T(8,128)}, u32[]{:S(2)}) copy-start(f32[16,128,128]{2,1,0:T(8,128)} %stress.13) | copy-start | bytes 3145732
  0.7 6.5 %copy-start.1 = (s32[16,128,128]{2,1,0:T(8,128)S(1)}, s32[16,128,128]{2,1,0:T(8,128)}, u32[]{:S(2)}) copy-start(s32[16,128,128]{2,1,0:T(8,128)} %count.9) | copy-start | bytes 3145732
  0.7 6.5 %copy-start = (s32[16,128,128]{2,1,0:T(8,128)S(1)}, s32[16,128,128]{2,1,0:T(8,128)}, u32[]{:S(2)}) copy-start(s32[16,128,128]{2,1,0:T(8,128)} %yields.9) | copy-start | bytes 3145732
  2.6 7.5 %collective-permute-start.1 = (f32[128,128]{1,0:T(8,128)S(1)}, f32[128,128]{1,0:T(8,128)S(1)}, u32[]{:S(2)}, u32[]{:S(2)}) collective-permute-start(f32[128,128]{1,0:T(8,128)S(1)} %slice.55), channel_id=1, source_target_pairs={{0,1},{1,0},{2,3},{3,2},{4,8},{5,9},{6,10},{7,11},{8,4},{9,5},{10,... | collective-permute-start | bytes 196616 | tf_op jit(solution)/shard_map/ppermute | solution.py:583
  3.2 7.0 %collective-permute-start = (f32[128,128]{1,0:T(8,128)S(1)}, f32[128,128]{1,0:T(8,128)S(1)}, u32[]{:S(2)}, u32[]{:S(2)}) collective-permute-start(f32[128,128]{1,0:T(8,128)S(1)} %slice.54), channel_id=1, source_target_pairs={{0,4},{1,5},{2,6},{3,7},{4,0},{5,1},{6,2},{7,3},{8,12},{9,13},{10,... | collective-permute-start | bytes 196616 | tf_op jit(solution)/shard_map/ppermute | solution.py:583
  10.2 2.1 %copy-start.2 = (f32[16,128,128]{2,1,0:T(8,128)S(1)}, f32[16,128,128]{2,1,0:T(8,128)}, u32[]{:S(2)}) copy-start(f32[16,128,128]{2,1,0:T(8,128)} %threshold.11) | copy-start | bytes 3145732
  10.2 2.1 %copy-start.11 = (f32[128,128]{1,0:T(8,128)S(1)}, f32[128,128]{1,0:T(8,128)}, u32[]{:S(2)}) copy-start(f32[128,128]{1,0:T(8,128)} %constant.17.clone.band_ref) | copy-start | bytes 196612
  10.6 4.3 %collective-permute-start.3 = (f32[128,128]{1,0:T(8,128)S(1)}, f32[128,128]{1,0:T(8,128)S(1)}, u32[]{:S(2)}, u32[]{:S(2)}) collective-permute-start(f32[128,128]{1,0:T(8,128)S(1)} %slice.57), channel_id=1, source_target_pairs={{0,4},{4,0},{8,12},{12,8},{16,20},{20,16},{24,28},{28,24},{1,2},{5... | collective-permute-start | bytes 196616 | tf_op jit(solution)/shard_map/ppermute | solution.py:583
  12.2 2.7 %collective-permute-start.2 = (f32[128,128]{1,0:T(8,128)S(1)}, f32[128,128]{1,0:T(8,128)S(1)}, u32[]{:S(2)}, u32[]{:S(2)}) collective-permute-start(f32[128,128]{1,0:T(8,128)S(1)} %slice.56), channel_id=1, source_target_pairs={{0,1},{4,5},{8,9},{12,13},{16,17},{20,21},{24,25},{28,29},{1,0},{5... | collective-permute-start | bytes 196616 | tf_op jit(solution)/shard_map/ppermute | solution.py:583
  13.5 1.4 %copy-start.7 = (f32[144,256]{1,0:T(8,128)S(1)}, f32[144,256]{1,0:T(8,128)}, u32[]{:S(2)}) copy-start(f32[144,256]{1,0:T(8,128)} %constant.15.clone.above) | copy-start | bytes 442372
  13.5 1.4 %copy-start.9 = (f32[128,128]{1,0:T(8,128)S(1)}, f32[128,128]{1,0:T(8,128)}, u32[]{:S(2)}) copy-start(f32[128,128]{1,0:T(8,128)} %constant.14.clone.below) | copy-start | bytes 196612
  15.7 6.6 %collective-permute-start.5 = (f32[128,128]{1,0:T(8,128)S(1)}, f32[128,128]{1,0:T(8,128)S(1)}, u32[]{:S(2)}, u32[]{:S(2)}) collective-permute-start(f32[128,128]{1,0:T(8,128)S(1)} %slice.59), channel_id=1, source_target_pairs={{0,1},{1,0},{2,3},{3,2},{4,8},{5,9},{6,10},{7,11},{8,4},{9,5},{10,... | collective-permute-start | bytes 196616 | tf_op jit(solution)/shard_map/ppermute | solution.py:583
  16.1 6.2 %collective-permute-start.4 = (f32[128,128]{1,0:T(8,128)S(1)}, f32[128,128]{1,0:T(8,128)S(1)}, u32[]{:S(2)}, u32[]{:S(2)}) collective-permute-start(f32[128,128]{1,0:T(8,128)S(1)} %slice.58), channel_id=1, source_target_pairs={{0,4},{1,5},{2,6},{3,7},{4,0},{5,1},{6,2},{7,3},{8,12},{9,13},{10,... | collective-permute-start | bytes 196616 | tf_op jit(solution)/shard_map/ppermute | solution.py:583
  22.7 4.3 %collective-permute-start.7 = (f32[128,128]{1,0:T(8,128)S(1)}, f32[128,128]{1,0:T(8,128)S(1)}, u32[]{:S(2)}, u32[]{:S(2)}) collective-permute-start(f32[128,128]{1,0:T(8,128)S(1)} %slice.61), channel_id=1, source_target_pairs={{0,4},{4,0},{8,12},{12,8},{16,20},{20,16},{24,28},{28,24},{1,2},{5... | collective-permute-start | bytes 196616 | tf_op jit(solution)/shard_map/ppermute | solution.py:583
  24.0 3.0 %collective-permute-start.6 = (f32[128,128]{1,0:T(8,128)S(1)}, f32[128,128]{1,0:T(8,128)S(1)}, u32[]{:S(2)}, u32[]{:S(2)}) collective-permute-start(f32[128,128]{1,0:T(8,128)S(1)} %slice.60), channel_id=1, source_target_pairs={{0,1},{4,5},{8,9},{12,13},{16,17},{20,21},{24,25},{28,29},{1,0},{5... | collective-permute-start | bytes 196616 | tf_op jit(solution)/shard_map/ppermute | solution.py:583
  27.8 4.7 %collective-permute-start.8 = (f32[176,128]{1,0:T(8,128)S(1)}, f32[176,128]{1,0:T(8,128)S(1)}, u32[]{:S(2)}, u32[]{:S(2)}) collective-permute-start(f32[176,128]{1,0:T(8,128)S(1)} %get-tuple-element.85), channel_id=1, source_target_pairs={{0,4},{1,5},{2,6},{3,7},{4,0},{5,1},{6,2},{7,3},{8,12},{9,13},{10,... | collective-permute-start | bytes 270344 | tf_op jit(solution)/shard_map/ppermute | solution.py:583
  29.1 3.4 %collective-permute-start.9 = (f32[176,128]{1,0:T(8,128)S(1)}, f32[176,128]{1,0:T(8,128)S(1)}, u32[]{:S(2)}, u32[]{:S(2)}) collective-permute-start(f32[176,128]{1,0:T(8,128)S(1)} %get-tuple-element.86), channel_id=1, source_target_pairs={{0,1},{1,0},{2,3},{3,2},{4,8},{5,9},{6,10},{7,11},{8,4},{9,5},{10,... | collective-permute-start | bytes 270344 | tf_op jit(solution)/shard_map/ppermute | solution.py:583
  32.9 5.6 %collective-permute-start.11 = (f32[176,128]{1,0:T(8,128)S(1)}, f32[176,128]{1,0:T(8,128)S(1)}, u32[]{:S(2)}, u32[]{:S(2)}) collective-permute-start(f32[176,128]{1,0:T(8,128)S(1)} %slice.68), channel_id=1, source_target_pairs={{0,4},{4,0},{8,12},{12,8},{16,20},{20,16},{24,28},{28,24},{1,2},{5... | collective-permute-start | bytes 270344 | tf_op jit(solution)/shard_map/ppermute | solution.py:583
  36.1 2.5 %collective-permute-start.10 = (f32[176,128]{1,0:T(8,128)S(1)}, f32[176,128]{1,0:T(8,128)S(1)}, u32[]{:S(2)}, u32[]{:S(2)}) collective-permute-start(f32[176,128]{1,0:T(8,128)S(1)} %slice.66), channel_id=1, source_target_pairs={{0,1},{4,5},{8,9},{12,13},{16,17},{20,21},{24,25},{28,29},{1,0},{5... | collective-permute-start | bytes 270344 | tf_op jit(solution)/shard_map/ppermute | solution.py:583

commit v11 on v10

--- a/solution.py
+++ b/solution.py
@@ -197,42 +197,45 @@
                 norm_high, col_even, col_odd, below, above,
                 even_ref, odd_ref, low_block, high_block, rest):
     layers, rows, cols = stress.shape
-    starts = (0, rows - 2 * REACH, rows - REACH)
-    packed = [
-        edge_ratios(
-            (edge_low, edge_high), (col_even, col_odd), (norm_low, norm_high),
-            pl.ds(first_row, REACH), pl.ds(first_row + REACH, REACH),
+
+    def packed(part, extended):
+        return edge_ratios(
+            (edge_low, edge_high), (col_even, col_odd), (norm_low, norm_high), part, extended
         )
-        for first_row in starts
-    ]
-
-    def layer_step(layer):
-        for index, first_row in enumerate(starts):
+
+    part = pl.ds(rows - 2 * REACH, REACH)
+    low, high = packed(part, pl.ds(rows - REACH, REACH))
+    for layer in range(layers):
+        rest[pl.ds(layer, 1), :] = with_edges(kept[layer, part, :], layer, low, high)[REACH - 1 :]
+    at = (slice(None), rows - REACH - 1, slice(None))
+    single = newton(stress[at], strain[at], yields[at], count[at], rest[pl.ds(0, layers), :], factor[at])
+
+    for first_row, block in ((0, low_block), (rows - REACH, high_block)):
+        low, high = packed(pl.ds(first_row, REACH), pl.ds(first_row + REACH, REACH))
+        for layer in range(layers):
             at = (layer, pl.ds(first_row, REACH), slice(None))
-            ratios = with_edges(kept[at], layer, *packed[index])
+            ratios = with_edges(kept[at], layer, low, high)
             value = newton(stress[at], strain[at], yields[at], count[at], ratios, factor[at])
-            if index == 0:
-                low_block[pl.ds(layer * REACH, REACH), :] = value
-            else:
-                high_block[pl.ds((2 * layer + index - 1) * REACH, REACH), :] = value
-            if index == 2:
+            block[pl.ds(layer * REACH, REACH), :] = value
+            if first_row:
                 left = (stress[at] + strain[at]) - value
                 rest[pl.ds(layer, 1), :] = left[REACH - 1 :]
                 rest[pl.ds(layers + layer, 1), :] = threshold[at][REACH - 1 :]
 
-    for layer in range(layers):
-        layer_step(layer)
     low = left_product(left_constant(below[...]), low_block[...])
     high = left_product(left_constant(above[...]), high_block[...])
-    extra = jnp.zeros((even_ref.shape[0] - low.shape[0], cols), jnp.float32)
+    strip = layers * REACH
+    spare = jnp.zeros((REACH, cols), jnp.float32)
+    extra = jnp.zeros((even_ref.shape[0] - strip, cols), jnp.float32)
     send(
-        "gx", jnp.concatenate([low, extra], axis=0), jnp.concatenate([high, rest[...]], axis=0),
+        "gx", jnp.concatenate([low, extra], axis=0),
+        jnp.concatenate([high[:strip], high[strip:] + tap(REACH) * single, rest[...], spare], axis=0),
         even_ref, odd_ref,
     )
 
 
 def first_main_kernel(stress, strain, yields, count, band_ref, low_ref, high_ref, next_ref,
-                      across, low_cols, high_cols, plastic, *packs):
+                      across, low_cols, high_cols, plastic, factor, *packs):
     layers, rows, cols = stress.shape
     step_rows = 4 * REACH
 
@@ -241,9 +244,11 @@
             part = pl.ds(pl.multiple_of(index * step_rows + near * REACH, REACH), REACH)
             for layer in range(layers):
                 at = (layer, part, slice(None))
+                lead = first_factor(strain[at])
+                factor[at] = lead
                 plastic[at] = newton(
                     stress[at], strain[at], yields[at], count[at],
-                    jnp.ones((REACH, cols), jnp.float32), first_factor(strain[at]),
+                    jnp.ones((REACH, cols), jnp.float32), lead,
                 )
         return carry
 
@@ -317,7 +322,7 @@
     return high[:, cols:] + behind
 
 
-def prepare_kernel(stress, strain, threshold, _, factor, fixed):
+def prepare_kernel(stress, strain, threshold, _, fixed):
     layers, rows, cols = stress.shape
     lanes = lane_ids((REACH, cols))
     fixed[...] = jnp.zeros_like(fixed)
@@ -329,7 +334,6 @@
             extended = pl.ds(pl.multiple_of(first + REACH, REACH), REACH)
             for layer in range(layers):
                 at = (layer, part, slice(None))
-                factor[at] = first_factor(strain[at])
                 for lane, value in ((layer, threshold[at]), (layers + layer, stress[at] + strain[at])):
                     moved = pltpu.roll(value, lane + 1, 1)
                     pltpu.store(fixed.at[extended, :], moved, mask=lanes == lane)
@@ -599,9 +603,7 @@
     up, down = band(REACH, REACH, REACH), band(REACH, REACH, -REACH)
     same = np.eye(layers)
     below = np.kron(same, up)
-    near = np.concatenate([np.zeros((REACH, REACH)), down], axis=1)
-    line = band(1, 2 * REACH, 1 - 2 * REACH)
-    above = np.concatenate([np.kron(same, near), np.kron(same, line)], axis=0)
+    above = np.concatenate([np.kron(same, down), np.kron(same, band(1, REACH, 1 - REACH))], axis=0)
     rows_band = np.concatenate([np.zeros((REACH - 1, rows)), band(1, rows, 1), band(rows, rows)])
     slots = cols // REACH
     low, high, ahead = np.zeros((cols, 2 * cols)), np.zeros((cols, 2 * cols)), np.zeros((cols, cols))
@@ -629,7 +631,8 @@
     below, above, rows_band, cols_band, *columns = constants
 
     whole, wide, top = (layers, rows, cols), (layers, total, cols), (layers, REACH, cols)
-    sent_rows = (strip + 3 * layers, cols)
+    last_rows = strip + 3 * layers
+    sent_rows = (last_rows + REACH, cols)
     sent_cols = (total + rows // 4 + 2 * REACH, cols)
     last_cols = total + rows // 4 + REACH
     spare = (3 * layers, cols)
@@ -650,12 +653,12 @@
         if outer_no:
             row_even, row_odd = call(
                 edge_kernel, [sent_rows] * 2,
-                [(strip, cols), (2 * strip, cols), (2 * layers, cols)], 800,
+                [(strip, cols), (strip, cols), (2 * layers, cols)], 800,
                 (*inputs, threshold, factor, kept, kept_before, edge_low, edge_high, *norms,
                  col_even, col_odd, below, above),
             )
-        if not last:
-            row_even, row_odd = row_even[:strip], row_odd[:strip]
+        used = last_rows if last else strip
+        row_even, row_odd = row_even[:used], row_odd[:used]
         row_even, row_odd = exchange("gx", "gy", row_even, row_odd)
         if last:
             rest_even, rest_odd = row_even[strip:], row_odd[strip:]
@@ -668,17 +671,15 @@
                  fixed, rows_band, *columns),
             )
         else:
-            across, low_cols, high_cols, plastic = call(
-                first_main_kernel, outs, [packed] * 4, 4500, (*inputs, rows_band, *columns),
+            across, low_cols, high_cols, plastic, factor = call(
+                first_main_kernel, outs + [whole], [packed] * 4, 4500, (*inputs, rows_band, *columns),
             )
         col_even, col_odd, own_cols = call(
             corner_kernel, [sent_cols, sent_cols, packed], [], 400,
             (row_even, row_odd, rest_even, rest_odd, low_cols, high_cols, norm_last, plastic, *columns),
         )
         if not outer_no:
-            factor, fixed = call(
-                prepare_kernel, [whole, packed], [], 1200, (stress, strain, threshold, col_odd),
-            )
+            (fixed,) = call(prepare_kernel, [packed], [], 800, (stress, strain, threshold, col_odd))
         used = last_cols if last else rows
         col_even, col_odd = col_even[:used], col_odd[:used]
         col_even, col_odd = exchange("gy", "gx", col_even, col_odd)

time: 41.9 us -> 42.4 us (1.012)
  waiting for transfers between devices: 3.24 us -> 4.09 us
    ppermute x12, waiting for transfers between devices: 3.24 us -> 4.09 us  [exchange(): results.append(lax.ppermute(value, names, pairs))]
  transfers between devices with their start and end apart: 12 -> 12, of which waited for: 3 -> 3; matrix products, arithmetic and copies ran while one was open for 0% -> 0% of each run, Pallas kernels for 35% -> 34%
where the time goes in v11:
time: 42.4 us; the launch traced here: 42.3 us
  Pallas kernels  21.8 us (51%)
  starting transfers between devices  15.2 us (36%)
  waiting for transfers between devices  4.09 us (10%)
  between operations  1.04 us (2%)
    pallas_call x14, Pallas kernels, call(): pl.pallas_call(kernel, out_shape=shapes, in_specs=[pl.BlockSpec(memory_sp...  21.8 us
    ppermute x12, starting transfers between devices, exchange(): results.append(lax.ppermute(value, names, pairs))  15.2 us
    ppermute x12, waiting for transfers between devices, exchange(): results.append(lax.ppermute(value, names, pairs))  4.09 us
  transfers between devices with their start and end apart: 12, of which 3 were waited for; matrix products, arithmetic and copies ran while one was open for 0% of the time, Pallas kernels for 34%

profile of v11, /device:TPU:0, one launch (start us, length us, event | category | flops | bytes accessed | tf_op | source)
XLA Modules:
  0.0 42.3 jit_solution(12741657278768063973)
XLA Ops:
  0.6 0.0 copy-start.5
  0.6 0.0 copy-start.6
  0.7 0.0 copy-start.7
  0.7 0.0 copy-start.10
  0.7 0.0 copy-start.2
  0.7 0.0 copy-start.1
  0.7 0.0 copy-start.4
  0.7 0.0 copy-start.3
  0.7 1.9 %shard_map.140 = (f32[136,128]{1,0:T(8,128)S(1)}, f32[136,128]{1,0:T(8,128)S(1)}, f32[136,128]{1,0:T(8,128)S(1)}, f32[136,128]{1,0:T(8,128)S(1)}, f32[136,128]{1...) custom-call(f32[16,128,128]{2,1,0:T(8,128)} %stress.13, ...), custom_call_target="tpu_custom_call" | custom-call | flops 1500000000 | bytes 1500000 | tf_op jit(solution)/shard_map/pallas_call | solution.py:557
  2.6 0.5 %collective-permute-start.1 = (f32[128,128]{1,0:T(8,128)S(1)}, f32[128,128]{1,0:T(8,128)S(1)}, u32[]{:S(2)}, u32[]{:S(2)}) collective-permute-start(f32[128,128]{1,0:T(8,128)S(1)} %slice.61), channel_id=1, source_target_pairs={{0,1},{1,0},{2,3},{3,2},{4,8},{5,9},{6,10},{7,11},{8,4},{9,5},{10,... | collective-permute-start | bytes 196616 | tf_op jit(solution)/shard_map/ppermute | solution.py:587
  3.2 4.0 %collective-permute-start = (f32[128,128]{1,0:T(8,128)S(1)}, f32[128,128]{1,0:T(8,128)S(1)}, u32[]{:S(2)}, u32[]{:S(2)}) collective-permute-start(f32[128,128]{1,0:T(8,128)S(1)} %slice.60), channel_id=1, source_target_pairs={{0,4},{1,5},{2,6},{3,7},{4,0},{5,1},{6,2},{7,3},{8,12},{9,13},{10,... | collective-permute-start | bytes 196616 | tf_op jit(solution)/shard_map/ppermute | solution.py:587
  7.2 0.0 copy-done.5
  7.2 0.0 copy-done.6
  7.2 0.0 copy-done.7
  7.2 0.0 copy-done.10
  7.2 0.0 copy-done.2
  7.2 0.0 copy-done.1
  7.2 0.0 copy-done.4
  7.2 0.0 copy-done.3
  7.3 2.9 %shard_map.139 = (f32[16,136,128]{2,1,0:T(8,128)S(1)}, f32[136,256]{1,0:T(8,128)S(1)}, f32[136,256]{1,0:T(8,128)S(1)}, f32[16,128,128]{2,1,0:T(8,128)S(1)}, f32[16,128,128]{2,1,0:T(8,128)S(1)}) custom-call(f32[16,128,128]{2,1,0:T(8,128)S(1)} %copy-done.1, f32[16,128,128]{2,1,0:T(8,128)S(1)} %copy-done.2, s32[16,128,128]{2,1,0:T(8,128)S(1)} %copy-done.3, ...), custom_call_target="tpu_custom_call" | custom-call | flops 4499999744 | bytes 4500000 | tf_op jit(solution)/shard_map/pallas_call | solution.py:557
  10.2 0.0 copy-start
  10.2 0.0 copy-start.11
  10.2 0.0 collective-permute-done.1.row_odd
  10.2 0.0 collective-permute-done.row_even
  10.2 0.4 shard_map.141
  10.6 1.6 %collective-permute-start.3 = (f32[128,128]{1,0:T(8,128)S(1)}, f32[128,128]{1,0:T(8,128)S(1)}, u32[]{:S(2)}, u32[]{:S(2)}) collective-permute-start(f32[128,128]{1,0:T(8,128)S(1)} %slice.63), channel_id=1, source_target_pairs={{0,4},{4,0},{8,12},{12,8},{16,20},{20,16},{24,28},{28,24},{1,2},{5... | collective-permute-start | bytes 196616 | tf_op jit(solution)/shard_map/ppermute | solution.py:587
  12.2 0.1 collective-permute-start.2
  12.3 0.0 copy-done
  12.3 0.0 copy-done.11
  12.3 1.2 %shard_map.142 = (f32[16,128,128]{2,1,0:T(8,128)S(1)}, f32[16,8,128]{2,1,0:T(8,128)S(1)}, f32[136,128]{1,0:T(8,128)S(1)}, f32[136,128]{1,0:T(8,128)S(1)}) custom-call(f32[16,136,128]{2,1,0:T(8,128)S(1)} %get-tuple-element.50.across, f32[128,128]{1,0:T(8,128)S(1)} %collective-permute-done.row_even, f32[128,128]{1,0:T(8,128)S(1)} %collective-permute-done.1.row_odd, ...), custom_call_target="tpu_custom_call" | custom-call | flops 1800000000 | bytes 1800000 | tf_op jit(solution)/shard_map/pallas_call | solution.py:557
  13.5 0.0 copy-start.8
  13.5 0.0 copy-start.9
  13.6 1.1 %shard_map.143.fixed = f32[136,128]{1,0:T(8,128)S(1)} custom-call(f32[16,128,128]{2,1,0:T(8,128)S(1)} %copy-done.1, f32[16,128,128]{2,1,0:T(8,128)S(1)} %copy-done.2, f32[16,128,128]{2,1,0:T(8,128)S(1)} %copy-done, f32[184,128]{1,0:T(8,128)S(1)} %get-tuple-element.66._), custom_call_target="tpu_custom_call" | custom-call | flops 800000000 | bytes 800000 | tf_op jit(solution)/shard_map/pallas_call | solution.py:557
  14.7 0.3 collective-permute-done.3.col_odd
  14.9 0.0 collective-permute-done.2.col_even
  14.9 0.0 copy-done.8
  14.9 0.0 copy-done.9
  14.9 0.6 %shard_map.145 = (f32[184,128]{1,0:T(8,128)S(1)}, f32[184,128]{1,0:T(8,128)S(1)}) custom-call(f32[16,128,128]{2,1,0:T(8,128)S(1)} %copy-done.1, f32[16,128,128]{2,1,0:T(8,128)S(1)} %copy-done.2, s32[16,128,128]{2,1,0:T(8,128)S(1)} %copy-done.3, s32[16,128,128]{2,1,0:T(8,128)S(1)} %copy-done.4, f32[16,128,128]{2,1,0:T(8,128)S(1)} %copy-done, ...), custom_call_target="tpu_custom_call" | custom-call | flops 800000000 | bytes 800000 | tf_op jit(solution)/shard_map/pallas_call | solution.py:557
  15.6 0.3 collective-permute-start.5
  15.9 2.9 %collective-permute-start.4 = (f32[128,128]{1,0:T(8,128)S(1)}, f32[128,128]{1,0:T(8,128)S(1)}, u32[]{:S(2)}, u32[]{:S(2)}) collective-permute-start(f32[128,128]{1,0:T(8,128)S(1)} %slice.64), channel_id=1, source_target_pairs={{0,4},{1,5},{2,6},{3,7},{4,0},{5,1},{6,2},{7,3},{8,12},{9,13},{10,... | collective-permute-start | bytes 196616 | tf_op jit(solution)/shard_map/ppermute | solution.py:587
  18.8 3.4 %shard_map.144 = (f32[16,136,128]{2,1,0:T(8,128)S(1)}, f32[136,256]{1,0:T(8,128)S(1)}, f32[136,256]{1,0:T(8,128)S(1)}, f32[16,128,128]{2,1,0:T(8,128)S(1)}) custom-call(f32[16,128,128]{2,1,0:T(8,128)S(1)} %copy-done.1, f32[16,128,128]{2,1,0:T(8,128)S(1)} %copy-done.2, s32[16,128,128]{2,1,0:T(8,128)S(1)} %copy-done.3, s32[16,128,128]{2,1,0:T(8,128)S(1)} %copy-done.4, ...), custom_call_target="tpu_custom_call" | custom-call | flops 4499999744 | bytes 4500000 | tf_op jit(solution)/shard_map/pallas_call | solution.py:557
  22.2 0.0 collective-permute-done.5.row_odd
  22.2 0.0 collective-permute-done.4.row_even
  22.2 0.4 shard_map.146
  22.6 1.2 %collective-permute-start.7 = (f32[128,128]{1,0:T(8,128)S(1)}, f32[128,128]{1,0:T(8,128)S(1)}, u32[]{:S(2)}, u32[]{:S(2)}) collective-permute-start(f32[128,128]{1,0:T(8,128)S(1)} %slice.67), channel_id=1, source_target_pairs={{0,4},{4,0},{8,12},{12,8},{16,20},{20,16},{24,28},{28,24},{1,2},{5... | collective-permute-start | bytes 196616 | tf_op jit(solution)/shard_map/ppermute | solution.py:587
  23.8 0.0 collective-permute-start.6
  23.8 1.2 %shard_map.147 = (f32[16,128,128]{2,1,0:T(8,128)S(1)}, f32[16,8,128]{2,1,0:T(8,128)S(1)}, f32[136,128]{1,0:T(8,128)S(1)}, f32[136,128]{1,0:T(8,128)S(1)}) custom-call(f32[16,136,128]{2,1,0:T(8,128)S(1)} %get-tuple-element.67.across, f32[128,128]{1,0:T(8,128)S(1)} %collective-permute-done.4.row_even, f32[128,128]{1,0:T(8,128)S(1)} %collective-permute-done.5.row_odd, ...), custom_call_target="tpu_custom_call" | custom-call | flops 1800000000 | bytes 1800000 | tf_op jit(solution)/shard_map/pallas_call | solution.py:557
  25.0 1.9 %collective-permute-done.7.col_odd = f32[128,128]{1,0:T(8,128)S(1)} collective-permute-done((f32[128,128]{1,0:T(8,128)S(1)}, f32[128,128]{1,0:T(8,128)S(1)}, u32[]{:S(2)}, u32[]{:S(2)}) %collective-permute-start.7) | collective-permute-done | bytes 65568 | tf_op jit(solution)/shard_map/ppermute | solution.py:587
  26.9 0.0 collective-permute-done.6.col_even
  26.9 0.6 %shard_map.149 = (f32[184,128]{1,0:T(8,128)S(1)}, f32[184,128]{1,0:T(8,128)S(1)}) custom-call(f32[16,128,128]{2,1,0:T(8,128)S(1)} %copy-done.1, f32[16,128,128]{2,1,0:T(8,128)S(1)} %copy-done.2, s32[16,128,128]{2,1,0:T(8,128)S(1)} %copy-done.3, s32[16,128,128]{2,1,0:T(8,128)S(1)} %copy-done.4, f32[16,128,128]{2,1,0:T(8,128)S(1)} %copy-done, ...), custom_call_target="tpu_custom_call" | custom-call | flops 800000000 | bytes 800000 | tf_op jit(solution)/shard_map/pallas_call | solution.py:557
  27.5 0.1 collective-permute-start.9
  27.6 3.0 %collective-permute-start.8 = (f32[176,128]{1,0:T(8,128)S(1)}, f32[176,128]{1,0:T(8,128)S(1)}, u32[]{:S(2)}, u32[]{:S(2)}) collective-permute-start(f32[176,128]{1,0:T(8,128)S(1)} %slice.68), channel_id=1, source_target_pairs={{0,4},{1,5},{2,6},{3,7},{4,0},{5,1},{6,2},{7,3},{8,12},{9,13},{10,... | collective-permute-start | bytes 270344 | tf_op jit(solution)/shard_map/ppermute | solution.py:587
  30.6 3.4 %shard_map.148 = (f32[16,136,128]{2,1,0:T(8,128)S(1)}, f32[136,256]{1,0:T(8,128)S(1)}, f32[136,256]{1,0:T(8,128)S(1)}, f32[16,128,128]{2,1,0:T(8,128)S(1)}) custom-call(f32[16,128,128]{2,1,0:T(8,128)S(1)} %copy-done.1, f32[16,128,128]{2,1,0:T(8,128)S(1)} %copy-done.2, s32[16,128,128]{2,1,0:T(8,128)S(1)} %copy-done.3, s32[16,128,128]{2,1,0:T(8,128)S(1)} %copy-done.4, ...), custom_call_target="tpu_custom_call" | custom-call | flops 4499999744 | bytes 4500000 | tf_op jit(solution)/shard_map/pallas_call | solution.py:557
  34.0 0.0 collective-permute-done.9
  34.0 0.0 collective-permute-done.8
  34.1 0.4 shard_map.150
  34.5 1.5 %collective-permute-start.11 = (f32[176,128]{1,0:T(8,128)S(1)}, f32[176,128]{1,0:T(8,128)S(1)}, u32[]{:S(2)}, u32[]{:S(2)}) collective-permute-start(f32[176,128]{1,0:T(8,128)S(1)} %slice.76), channel_id=1, source_target_pairs={{0,4},{4,0},{8,12},{12,8},{16,20},{20,16},{24,28},{28,24},{1,2},{5... | collective-permute-start | bytes 270344 | tf_op jit(solution)/shard_map/ppermute | solution.py:587
  36.0 0.0 collective-permute-start.10
  36.0 1.2 %shard_map.151 = (f32[16,128,128]{2,1,0:T(8,128)S(1)}, f32[16,8,128]{2,1,0:T(8,128)S(1)}, f32[136,128]{1,0:T(8,128)S(1)}, f32[136,128]{1,0:T(8,128)S(1)}) custom-call(f32[16,136,128]{2,1,0:T(8,128)S(1)} %get-tuple-element.81.across, f32[128,128]{1,0:T(8,128)S(1)} %slice.80.row_even, f32[128,128]{1,0:T(8,128)S(1)} %slice.81.row_odd, ...), custom_call_target="tpu_custom_call" | custom-call | flops 1800000000 | bytes 1800000 | tf_op jit(solution)/shard_map/pallas_call | solution.py:557
  37.2 1.9 %collective-permute-done.11 = f32[176,128]{1,0:T(8,128)S(1)} collective-permute-done((f32[176,128]{1,0:T(8,128)S(1)}, f32[176,128]{1,0:T(8,128)S(1)}, u32[]{:S(2)}, u32[]{:S(2)}) %collective-permute-start.11) | collective-permute-done | bytes 90144 | tf_op jit(solution)/shard_map/ppermute | solution.py:587
  39.1 0.0 collective-permute-done.10
  39.1 3.1 %shard_map.152 = (f32[16,128,128]{2,1,0:T(8,128)}, f32[16,128,128]{2,1,0:T(8,128)}, f32[2,16,128,128]{3,2,1,0:T(8,128)}) custom-call(f32[16,128,128]{2,1,0:T(8,128)S(1)} %copy-done.1, f32[16,128,128]{2,1,0:T(8,128)S(1)} %copy-done.2, f32[16,128,128]{2,1,0:T(8,128)S(1)} %get-tuple-element.80._.plastic, f32[16,128,128]{2,1,0:T(8,128)S(1)} %get-tuple-element.88.inner, ...), custom_call_target="tpu_custom_call" | custom-call | flops 3000000000 | bytes 3000000 | tf_op jit(solution)/shard_map/pallas_call | solution.py:557
  (20 shorter events, 0.1 us)
Async XLA Ops:
  0.6 6.6 %copy-start.5 = (f32[128,256]{1,0:T(8,128)S(1)}, f32[128,256]{1,0:T(8,128)}, u32[]{:S(2)}) copy-start(f32[128,256]{1,0:T(8,128)} %constant.19.clone.high_ref) | copy-start | bytes 393220
  0.6 6.6 %copy-start.6 = (f32[128,256]{1,0:T(8,128)S(1)}, f32[128,256]{1,0:T(8,128)}, u32[]{:S(2)}) copy-start(f32[128,256]{1,0:T(8,128)} %constant.18.clone.low_ref) | copy-start | bytes 393220
  0.7 6.6 %copy-start.7 = (f32[128,128]{1,0:T(8,128)S(1)}, f32[128,128]{1,0:T(8,128)}, u32[]{:S(2)}) copy-start(f32[128,128]{1,0:T(8,128)} %constant.20.clone.next_ref) | copy-start | bytes 196612
  0.7 6.5 %copy-start.10 = (f32[136,128]{1,0:T(8,128)S(1)}, f32[136,128]{1,0:T(8,128)}, u32[]{:S(2)}) copy-start(f32[136,128]{1,0:T(8,128)} %constant.16.clone.band_ref) | copy-start | bytes 208900
  0.7 6.5 %copy-start.2 = (f32[16,128,128]{2,1,0:T(8,128)S(1)}, f32[16,128,128]{2,1,0:T(8,128)}, u32[]{:S(2)}) copy-start(f32[16,128,128]{2,1,0:T(8,128)} %strain.13) | copy-start | bytes 3145732
  0.7 6.5 %copy-start.1 = (f32[16,128,128]{2,1,0:T(8,128)S(1)}, f32[16,128,128]{2,1,0:T(8,128)}, u32[]{:S(2)}) copy-start(f32[16,128,128]{2,1,0:T(8,128)} %stress.13) | copy-start | bytes 3145732
  0.7 6.5 %copy-start.4 = (s32[16,128,128]{2,1,0:T(8,128)S(1)}, s32[16,128,128]{2,1,0:T(8,128)}, u32[]{:S(2)}) copy-start(s32[16,128,128]{2,1,0:T(8,128)} %count.9) | copy-start | bytes 3145732
  0.7 6.5 %copy-start.3 = (s32[16,128,128]{2,1,0:T(8,128)S(1)}, s32[16,128,128]{2,1,0:T(8,128)}, u32[]{:S(2)}) copy-start(s32[16,128,128]{2,1,0:T(8,128)} %yields.9) | copy-start | bytes 3145732
  2.6 7.5 %collective-permute-start.1 = (f32[128,128]{1,0:T(8,128)S(1)}, f32[128,128]{1,0:T(8,128)S(1)}, u32[]{:S(2)}, u32[]{:S(2)}) collective-permute-start(f32[128,128]{1,0:T(8,128)S(1)} %slice.61), channel_id=1, source_target_pairs={{0,1},{1,0},{2,3},{3,2},{4,8},{5,9},{6,10},{7,11},{8,4},{9,5},{10,... | collective-permute-start | bytes 196616 | tf_op jit(solution)/shard_map/ppermute | solution.py:587
  3.2 7.0 %collective-permute-start = (f32[128,128]{1,0:T(8,128)S(1)}, f32[128,128]{1,0:T(8,128)S(1)}, u32[]{:S(2)}, u32[]{:S(2)}) collective-permute-start(f32[128,128]{1,0:T(8,128)S(1)} %slice.60), channel_id=1, source_target_pairs={{0,4},{1,5},{2,6},{3,7},{4,0},{5,1},{6,2},{7,3},{8,12},{9,13},{10,... | collective-permute-start | bytes 196616 | tf_op jit(solution)/shard_map/ppermute | solution.py:587
  10.2 2.1 %copy-start = (f32[16,128,128]{2,1,0:T(8,128)S(1)}, f32[16,128,128]{2,1,0:T(8,128)}, u32[]{:S(2)}) copy-start(f32[16,128,128]{2,1,0:T(8,128)} %threshold.11) | copy-start | bytes 3145732
  10.2 2.1 %copy-start.11 = (f32[128,128]{1,0:T(8,128)S(1)}, f32[128,128]{1,0:T(8,128)}, u32[]{:S(2)}) copy-start(f32[128,128]{1,0:T(8,128)} %constant.17.clone.band_ref) | copy-start | bytes 196612
  10.6 4.3 %collective-permute-start.3 = (f32[128,128]{1,0:T(8,128)S(1)}, f32[128,128]{1,0:T(8,128)S(1)}, u32[]{:S(2)}, u32[]{:S(2)}) collective-permute-start(f32[128,128]{1,0:T(8,128)S(1)} %slice.63), channel_id=1, source_target_pairs={{0,4},{4,0},{8,12},{12,8},{16,20},{20,16},{24,28},{28,24},{1,2},{5... | collective-permute-start | bytes 196616 | tf_op jit(solution)/shard_map/ppermute | solution.py:587
  12.2 2.7 %collective-permute-start.2 = (f32[128,128]{1,0:T(8,128)S(1)}, f32[128,128]{1,0:T(8,128)S(1)}, u32[]{:S(2)}, u32[]{:S(2)}) collective-permute-start(f32[128,128]{1,0:T(8,128)S(1)} %slice.62), channel_id=1, source_target_pairs={{0,1},{4,5},{8,9},{12,13},{16,17},{20,21},{24,25},{28,29},{1,0},{5... | collective-permute-start | bytes 196616 | tf_op jit(solution)/shard_map/ppermute | solution.py:587
  13.5 1.4 %copy-start.8 = (f32[144,128]{1,0:T(8,128)S(1)}, f32[144,128]{1,0:T(8,128)}, u32[]{:S(2)}) copy-start(f32[144,128]{1,0:T(8,128)} %constant.15.clone.above) | copy-start | bytes 221188
  13.5 1.4 %copy-start.9 = (f32[128,128]{1,0:T(8,128)S(1)}, f32[128,128]{1,0:T(8,128)}, u32[]{:S(2)}) copy-start(f32[128,128]{1,0:T(8,128)} %constant.14.clone.below) | copy-start | bytes 196612
  15.6 6.6 %collective-permute-start.5 = (f32[128,128]{1,0:T(8,128)S(1)}, f32[128,128]{1,0:T(8,128)S(1)}, u32[]{:S(2)}, u32[]{:S(2)}) collective-permute-start(f32[128,128]{1,0:T(8,128)S(1)} %slice.65), channel_id=1, source_target_pairs={{0,1},{1,0},{2,3},{3,2},{4,8},{5,9},{6,10},{7,11},{8,4},{9,5},{10,... | collective-permute-start | bytes 196616 | tf_op jit(solution)/shard_map/ppermute | solution.py:587
  15.9 6.3 %collective-permute-start.4 = (f32[128,128]{1,0:T(8,128)S(1)}, f32[128,128]{1,0:T(8,128)S(1)}, u32[]{:S(2)}, u32[]{:S(2)}) collective-permute-start(f32[128,128]{1,0:T(8,128)S(1)} %slice.64), channel_id=1, source_target_pairs={{0,4},{1,5},{2,6},{3,7},{4,0},{5,1},{6,2},{7,3},{8,12},{9,13},{10,... | collective-permute-start | bytes 196616 | tf_op jit(solution)/shard_map/ppermute | solution.py:587
  22.6 4.3 %collective-permute-start.7 = (f32[128,128]{1,0:T(8,128)S(1)}, f32[128,128]{1,0:T(8,128)S(1)}, u32[]{:S(2)}, u32[]{:S(2)}) collective-permute-start(f32[128,128]{1,0:T(8,128)S(1)} %slice.67), channel_id=1, source_target_pairs={{0,4},{4,0},{8,12},{12,8},{16,20},{20,16},{24,28},{28,24},{1,2},{5... | collective-permute-start | bytes 196616 | tf_op jit(solution)/shard_map/ppermute | solution.py:587
  23.8 3.1 %collective-permute-start.6 = (f32[128,128]{1,0:T(8,128)S(1)}, f32[128,128]{1,0:T(8,128)S(1)}, u32[]{:S(2)}, u32[]{:S(2)}) collective-permute-start(f32[128,128]{1,0:T(8,128)S(1)} %slice.66), channel_id=1, source_target_pairs={{0,1},{4,5},{8,9},{12,13},{16,17},{20,21},{24,25},{28,29},{1,0},{5... | collective-permute-start | bytes 196616 | tf_op jit(solution)/shard_map/ppermute | solution.py:587
  27.5 6.5 %collective-permute-start.9 = (f32[176,128]{1,0:T(8,128)S(1)}, f32[176,128]{1,0:T(8,128)S(1)}, u32[]{:S(2)}, u32[]{:S(2)}) collective-permute-start(f32[176,128]{1,0:T(8,128)S(1)} %slice.70), channel_id=1, source_target_pairs={{0,1},{1,0},{2,3},{3,2},{4,8},{5,9},{6,10},{7,11},{8,4},{9,5},{10,... | collective-permute-start | bytes 270344 | tf_op jit(solution)/shard_map/ppermute | solution.py:587
  27.6 6.4 %collective-permute-start.8 = (f32[176,128]{1,0:T(8,128)S(1)}, f32[176,128]{1,0:T(8,128)S(1)}, u32[]{:S(2)}, u32[]{:S(2)}) collective-permute-start(f32[176,128]{1,0:T(8,128)S(1)} %slice.68), channel_id=1, source_target_pairs={{0,4},{1,5},{2,6},{3,7},{4,0},{5,1},{6,2},{7,3},{8,12},{9,13},{10,... | collective-permute-start | bytes 270344 | tf_op jit(solution)/shard_map/ppermute | solution.py:587
  34.5 4.6 %collective-permute-start.11 = (f32[176,128]{1,0:T(8,128)S(1)}, f32[176,128]{1,0:T(8,128)S(1)}, u32[]{:S(2)}, u32[]{:S(2)}) collective-permute-start(f32[176,128]{1,0:T(8,128)S(1)} %slice.76), channel_id=1, source_target_pairs={{0,4},{4,0},{8,12},{12,8},{16,20},{20,16},{24,28},{28,24},{1,2},{5... | collective-permute-start | bytes 270344 | tf_op jit(solution)/shard_map/ppermute | solution.py:587
  36.0 3.1 %collective-permute-start.10 = (f32[176,128]{1,0:T(8,128)S(1)}, f32[176,128]{1,0:T(8,128)S(1)}, u32[]{:S(2)}, u32[]{:S(2)}) collective-permute-start(f32[176,128]{1,0:T(8,128)S(1)} %slice.74), channel_id=1, source_target_pairs={{0,1},{4,5},{8,9},{12,13},{16,17},{20,21},{24,25},{28,29},{1,0},{5... | collective-permute-start | bytes 270344 | tf_op jit(solution)/shard_map/ppermute | solution.py:587

commit v12 on v11

--- a/solution.py
+++ b/solution.py
@@ -225,11 +225,10 @@
     low = left_product(left_constant(below[...]), low_block[...])
     high = left_product(left_constant(above[...]), high_block[...])
     strip = layers * REACH
-    spare = jnp.zeros((REACH, cols), jnp.float32)
     extra = jnp.zeros((even_ref.shape[0] - strip, cols), jnp.float32)
     send(
         "gx", jnp.concatenate([low, extra], axis=0),
-        jnp.concatenate([high[:strip], high[strip:] + tap(REACH) * single, rest[...], spare], axis=0),
+        jnp.concatenate([high[:strip], high[strip:] + tap(REACH) * single, rest[...]], axis=0),
         even_ref, odd_ref,
     )
 
@@ -631,8 +630,7 @@
     below, above, rows_band, cols_band, *columns = constants
 
     whole, wide, top = (layers, rows, cols), (layers, total, cols), (layers, REACH, cols)
-    last_rows = strip + 3 * layers
-    sent_rows = (last_rows + REACH, cols)
+    sent_rows = (strip + 3 * layers, cols)
     sent_cols = (total + rows // 4 + 2 * REACH, cols)
     last_cols = total + rows // 4 + REACH
     spare = (3 * layers, cols)
@@ -657,8 +655,8 @@
                 (*inputs, threshold, factor, kept, kept_before, edge_low, edge_high, *norms,
                  col_even, col_odd, below, above),
             )
-        used = last_rows if last else strip
-        row_even, row_odd = row_even[:used], row_odd[:used]
+        if not last:
+            row_even, row_odd = row_even[:strip], row_odd[:strip]
         row_even, row_odd = exchange("gx", "gy", row_even, row_odd)
         if last:
             rest_even, rest_odd = row_even[strip:], row_odd[strip:]

time: 42.4 us -> 41.5 us (0.979)
  waiting for transfers between devices: 4.09 us -> 3.49 us
    ppermute x12, waiting for transfers between devices: 4.09 us -> 3.49 us  [exchange(): results.append(lax.ppermute(value, names, pairs))]
  transfers between devices with their start and end apart: 12 -> 12, of which waited for: 3 -> 3; matrix products, arithmetic and copies ran while one was open for 0% -> 0% of each run, Pallas kernels for 34% -> 35%
where the time goes in v12:
time: 41.5 us; the launch traced here: 41.4 us
  Pallas kernels  21.8 us (53%)
  starting transfers between devices  14.9 us (36%)
  waiting for transfers between devices  3.49 us (8%)
  between operations  1.01 us (2%)
    pallas_call x14, Pallas kernels, call(): pl.pallas_call(kernel, out_shape=shapes, in_specs=[pl.BlockSpec(memory_sp...  21.8 us
    ppermute x12, starting transfers between devices, exchange(): results.append(lax.ppermute(value, names, pairs))  14.9 us
    ppermute x12, waiting for transfers between devices, exchange(): results.append(lax.ppermute(value, names, pairs))  3.49 us
  transfers between devices with their start and end apart: 12, of which 3 were waited for; matrix products, arithmetic and copies ran while one was open for 0% of the time, Pallas kernels for 35%

profile of v12, /device:TPU:0, one launch (start us, length us, event | category | flops | bytes accessed | tf_op | source)
XLA Modules:
  0.0 41.4 jit_solution(11384186361939449149)
XLA Ops:
  0.6 0.0 copy-start.5
  0.6 0.0 copy-start.6
  0.7 0.0 copy-start.7
  0.7 0.0 copy-start.10
  0.7 0.0 copy-start.2
  0.7 0.0 copy-start.1
  0.7 0.0 copy-start.4
  0.7 0.0 copy-start.3
  0.7 1.9 %shard_map.140 = (f32[136,128]{1,0:T(8,128)S(1)}, f32[136,128]{1,0:T(8,128)S(1)}, f32[136,128]{1,0:T(8,128)S(1)}, f32[136,128]{1,0:T(8,128)S(1)}, f32[136,128]{1...) custom-call(f32[16,128,128]{2,1,0:T(8,128)} %stress.13, ...), custom_call_target="tpu_custom_call" | custom-call | flops 1500000000 | bytes 1500000 | tf_op jit(solution)/shard_map/pallas_call | solution.py:556
  2.6 0.5 %collective-permute-start.1 = (f32[128,128]{1,0:T(8,128)S(1)}, f32[128,128]{1,0:T(8,128)S(1)}, u32[]{:S(2)}, u32[]{:S(2)}) collective-permute-start(f32[128,128]{1,0:T(8,128)S(1)} %slice.55), channel_id=1, source_target_pairs={{0,1},{1,0},{2,3},{3,2},{4,8},{5,9},{6,10},{7,11},{8,4},{9,5},{10,... | collective-permute-start | bytes 196616 | tf_op jit(solution)/shard_map/ppermute | solution.py:586
  3.2 4.0 %collective-permute-start = (f32[128,128]{1,0:T(8,128)S(1)}, f32[128,128]{1,0:T(8,128)S(1)}, u32[]{:S(2)}, u32[]{:S(2)}) collective-permute-start(f32[128,128]{1,0:T(8,128)S(1)} %slice.54), channel_id=1, source_target_pairs={{0,4},{1,5},{2,6},{3,7},{4,0},{5,1},{6,2},{7,3},{8,12},{9,13},{10,... | collective-permute-start | bytes 196616 | tf_op jit(solution)/shard_map/ppermute | solution.py:586
  7.2 0.0 copy-done.5
  7.2 0.0 copy-done.6
  7.2 0.0 copy-done.7
  7.2 0.0 copy-done.10
  7.2 0.0 copy-done.2
  7.2 0.0 copy-done.1
  7.2 0.0 copy-done.4
  7.2 0.0 copy-done.3
  7.3 2.9 %shard_map.139 = (f32[16,136,128]{2,1,0:T(8,128)S(1)}, f32[136,256]{1,0:T(8,128)S(1)}, f32[136,256]{1,0:T(8,128)S(1)}, f32[16,128,128]{2,1,0:T(8,128)S(1)}, f32[16,128,128]{2,1,0:T(8,128)S(1)}) custom-call(f32[16,128,128]{2,1,0:T(8,128)S(1)} %copy-done.1, f32[16,128,128]{2,1,0:T(8,128)S(1)} %copy-done.2, s32[16,128,128]{2,1,0:T(8,128)S(1)} %copy-done.3, ...), custom_call_target="tpu_custom_call" | custom-call | flops 4499999744 | bytes 4500000 | tf_op jit(solution)/shard_map/pallas_call | solution.py:556
  10.2 0.0 copy-start
  10.2 0.0 copy-start.11
  10.2 0.0 collective-permute-done.1.row_odd
  10.2 0.0 collective-permute-done.row_even
  10.2 0.4 shard_map.141
  10.6 1.6 %collective-permute-start.3 = (f32[128,128]{1,0:T(8,128)S(1)}, f32[128,128]{1,0:T(8,128)S(1)}, u32[]{:S(2)}, u32[]{:S(2)}) collective-permute-start(f32[128,128]{1,0:T(8,128)S(1)} %slice.57), channel_id=1, source_target_pairs={{0,4},{4,0},{8,12},{12,8},{16,20},{20,16},{24,28},{28,24},{1,2},{5... | collective-permute-start | bytes 196616 | tf_op jit(solution)/shard_map/ppermute | solution.py:586
  12.2 0.1 collective-permute-start.2
  12.3 0.0 copy-done
  12.3 0.0 copy-done.11
  12.3 1.2 %shard_map.142 = (f32[16,128,128]{2,1,0:T(8,128)S(1)}, f32[16,8,128]{2,1,0:T(8,128)S(1)}, f32[136,128]{1,0:T(8,128)S(1)}, f32[136,128]{1,0:T(8,128)S(1)}) custom-call(f32[16,136,128]{2,1,0:T(8,128)S(1)} %get-tuple-element.50.across, f32[128,128]{1,0:T(8,128)S(1)} %collective-permute-done.row_even, f32[128,128]{1,0:T(8,128)S(1)} %collective-permute-done.1.row_odd, ...), custom_call_target="tpu_custom_call" | custom-call | flops 1800000000 | bytes 1800000 | tf_op jit(solution)/shard_map/pallas_call | solution.py:556
  13.5 0.0 copy-start.8
  13.5 0.0 copy-start.9
  13.6 1.1 %shard_map.143.fixed = f32[136,128]{1,0:T(8,128)S(1)} custom-call(f32[16,128,128]{2,1,0:T(8,128)S(1)} %copy-done.1, f32[16,128,128]{2,1,0:T(8,128)S(1)} %copy-done.2, f32[16,128,128]{2,1,0:T(8,128)S(1)} %copy-done, f32[184,128]{1,0:T(8,128)S(1)} %get-tuple-element.66._), custom_call_target="tpu_custom_call" | custom-call | flops 800000000 | bytes 800000 | tf_op jit(solution)/shard_map/pallas_call | solution.py:556
  14.7 0.3 collective-permute-done.3.col_odd
  14.9 0.0 collective-permute-done.2.col_even
  14.9 0.0 copy-done.8
  14.9 0.0 copy-done.9
  14.9 0.6 %shard_map.145 = (f32[176,128]{1,0:T(8,128)S(1)}, f32[176,128]{1,0:T(8,128)S(1)}) custom-call(f32[16,128,128]{2,1,0:T(8,128)S(1)} %copy-done.1, f32[16,128,128]{2,1,0:T(8,128)S(1)} %copy-done.2, s32[16,128,128]{2,1,0:T(8,128)S(1)} %copy-done.3, s32[16,128,128]{2,1,0:T(8,128)S(1)} %copy-done.4, f32[16,128,128]{2,1,0:T(8,128)S(1)} %copy-done, ...), custom_call_target="tpu_custom_call" | custom-call | flops 800000000 | bytes 800000 | tf_op jit(solution)/shard_map/pallas_call | solution.py:556
  15.6 0.3 collective-permute-start.5
  15.8 2.9 %collective-permute-start.4 = (f32[128,128]{1,0:T(8,128)S(1)}, f32[128,128]{1,0:T(8,128)S(1)}, u32[]{:S(2)}, u32[]{:S(2)}) collective-permute-start(f32[128,128]{1,0:T(8,128)S(1)} %slice.58), channel_id=1, source_target_pairs={{0,4},{1,5},{2,6},{3,7},{4,0},{5,1},{6,2},{7,3},{8,12},{9,13},{10,... | collective-permute-start | bytes 196616 | tf_op jit(solution)/shard_map/ppermute | solution.py:586
  18.8 3.4 %shard_map.144 = (f32[16,136,128]{2,1,0:T(8,128)S(1)}, f32[136,256]{1,0:T(8,128)S(1)}, f32[136,256]{1,0:T(8,128)S(1)}, f32[16,128,128]{2,1,0:T(8,128)S(1)}) custom-call(f32[16,128,128]{2,1,0:T(8,128)S(1)} %copy-done.1, f32[16,128,128]{2,1,0:T(8,128)S(1)} %copy-done.2, s32[16,128,128]{2,1,0:T(8,128)S(1)} %copy-done.3, s32[16,128,128]{2,1,0:T(8,128)S(1)} %copy-done.4, ...), custom_call_target="tpu_custom_call" | custom-call | flops 4499999744 | bytes 4500000 | tf_op jit(solution)/shard_map/pallas_call | solution.py:556
  22.1 0.0 collective-permute-done.5.row_odd
  22.2 0.0 collective-permute-done.4.row_even
  22.2 0.4 shard_map.146
  22.6 1.2 %collective-permute-start.7 = (f32[128,128]{1,0:T(8,128)S(1)}, f32[128,128]{1,0:T(8,128)S(1)}, u32[]{:S(2)}, u32[]{:S(2)}) collective-permute-start(f32[128,128]{1,0:T(8,128)S(1)} %slice.61), channel_id=1, source_target_pairs={{0,4},{4,0},{8,12},{12,8},{16,20},{20,16},{24,28},{28,24},{1,2},{5... | collective-permute-start | bytes 196616 | tf_op jit(solution)/shard_map/ppermute | solution.py:586
  23.8 0.0 collective-permute-start.6
  23.8 1.2 %shard_map.147 = (f32[16,128,128]{2,1,0:T(8,128)S(1)}, f32[16,8,128]{2,1,0:T(8,128)S(1)}, f32[136,128]{1,0:T(8,128)S(1)}, f32[136,128]{1,0:T(8,128)S(1)}) custom-call(f32[16,136,128]{2,1,0:T(8,128)S(1)} %get-tuple-element.67.across, f32[128,128]{1,0:T(8,128)S(1)} %collective-permute-done.4.row_even, f32[128,128]{1,0:T(8,128)S(1)} %collective-permute-done.5.row_odd, ...), custom_call_target="tpu_custom_call" | custom-call | flops 1800000000 | bytes 1800000 | tf_op jit(solution)/shard_map/pallas_call | solution.py:556
  25.0 1.9 %collective-permute-done.7.col_odd = f32[128,128]{1,0:T(8,128)S(1)} collective-permute-done((f32[128,128]{1,0:T(8,128)S(1)}, f32[128,128]{1,0:T(8,128)S(1)}, u32[]{:S(2)}, u32[]{:S(2)}) %collective-permute-start.7) | collective-permute-done | bytes 65568 | tf_op jit(solution)/shard_map/ppermute | solution.py:586
  26.9 0.0 collective-permute-done.6.col_even
  26.9 0.6 %shard_map.149 = (f32[176,128]{1,0:T(8,128)S(1)}, f32[176,128]{1,0:T(8,128)S(1)}) custom-call(f32[16,128,128]{2,1,0:T(8,128)S(1)} %copy-done.1, f32[16,128,128]{2,1,0:T(8,128)S(1)} %copy-done.2, s32[16,128,128]{2,1,0:T(8,128)S(1)} %copy-done.3, s32[16,128,128]{2,1,0:T(8,128)S(1)} %copy-done.4, f32[16,128,128]{2,1,0:T(8,128)S(1)} %copy-done, ...), custom_call_target="tpu_custom_call" | custom-call | flops 800000000 | bytes 800000 | tf_op jit(solution)/shard_map/pallas_call | solution.py:556
  27.5 1.2 %collective-permute-start.8 = (f32[176,128]{1,0:T(8,128)S(1)}, f32[176,128]{1,0:T(8,128)S(1)}, u32[]{:S(2)}, u32[]{:S(2)}) collective-permute-start(f32[176,128]{1,0:T(8,128)S(1)} %get-tuple-element.83), channel_id=1, source_target_pairs={{0,4},{1,5},{2,6},{3,7},{4,0},{5,1},{6,2},{7,3},{8,12},{9,13},{10,... | collective-permute-start | bytes 270344 | tf_op jit(solution)/shard_map/ppermute | solution.py:586
  28.7 0.0 collective-permute-start.9
  28.7 3.4 %shard_map.148 = (f32[16,136,128]{2,1,0:T(8,128)S(1)}, f32[136,256]{1,0:T(8,128)S(1)}, f32[136,256]{1,0:T(8,128)S(1)}, f32[16,128,128]{2,1,0:T(8,128)S(1)}) custom-call(f32[16,128,128]{2,1,0:T(8,128)S(1)} %copy-done.1, f32[16,128,128]{2,1,0:T(8,128)S(1)} %copy-done.2, s32[16,128,128]{2,1,0:T(8,128)S(1)} %copy-done.3, s32[16,128,128]{2,1,0:T(8,128)S(1)} %copy-done.4, ...), custom_call_target="tpu_custom_call" | custom-call | flops 4499999744 | bytes 4500000 | tf_op jit(solution)/shard_map/pallas_call | solution.py:556
  32.1 0.0 collective-permute-done.8
  32.1 0.0 collective-permute-done.9
  32.1 0.4 shard_map.150
  32.6 3.1 %collective-permute-start.11 = (f32[176,128]{1,0:T(8,128)S(1)}, f32[176,128]{1,0:T(8,128)S(1)}, u32[]{:S(2)}, u32[]{:S(2)}) collective-permute-start(f32[176,128]{1,0:T(8,128)S(1)} %slice.68), channel_id=1, source_target_pairs={{0,4},{4,0},{8,12},{12,8},{16,20},{20,16},{24,28},{28,24},{1,2},{5... | collective-permute-start | bytes 270344 | tf_op jit(solution)/shard_map/ppermute | solution.py:586
  35.7 0.0 collective-permute-start.10
  35.7 1.2 %shard_map.151 = (f32[16,128,128]{2,1,0:T(8,128)S(1)}, f32[16,8,128]{2,1,0:T(8,128)S(1)}, f32[136,128]{1,0:T(8,128)S(1)}, f32[136,128]{1,0:T(8,128)S(1)}) custom-call(f32[16,136,128]{2,1,0:T(8,128)S(1)} %get-tuple-element.81.across, f32[128,128]{1,0:T(8,128)S(1)} %slice.72.row_even, f32[128,128]{1,0:T(8,128)S(1)} %slice.73.row_odd, ...), custom_call_target="tpu_custom_call" | custom-call | flops 1800000000 | bytes 1800000 | tf_op jit(solution)/shard_map/pallas_call | solution.py:556
  36.9 1.3 %collective-permute-done.11 = f32[176,128]{1,0:T(8,128)S(1)} collective-permute-done((f32[176,128]{1,0:T(8,128)S(1)}, f32[176,128]{1,0:T(8,128)S(1)}, u32[]{:S(2)}, u32[]{:S(2)}) %collective-permute-start.11) | collective-permute-done | bytes 90144 | tf_op jit(solution)/shard_map/ppermute | solution.py:586
  38.2 0.0 collective-permute-done.10
  38.2 3.2 %shard_map.152 = (f32[16,128,128]{2,1,0:T(8,128)}, f32[16,128,128]{2,1,0:T(8,128)}, f32[2,16,128,128]{3,2,1,0:T(8,128)}) custom-call(f32[16,128,128]{2,1,0:T(8,128)S(1)} %copy-done.1, f32[16,128,128]{2,1,0:T(8,128)S(1)} %copy-done.2, f32[16,128,128]{2,1,0:T(8,128)S(1)} %get-tuple-element.80._.plastic, f32[16,128,128]{2,1,0:T(8,128)S(1)} %get-tuple-element.88.inner, ...), custom_call_target="tpu_custom_call" | custom-call | flops 3000000000 | bytes 3000000 | tf_op jit(solution)/shard_map/pallas_call | solution.py:556
  (18 shorter events, 0.1 us)
Async XLA Ops:
  0.6 6.6 %copy-start.5 = (f32[128,256]{1,0:T(8,128)S(1)}, f32[128,256]{1,0:T(8,128)}, u32[]{:S(2)}) copy-start(f32[128,256]{1,0:T(8,128)} %constant.19.clone.high_ref) | copy-start | bytes 393220
  0.6 6.6 %copy-start.6 = (f32[128,256]{1,0:T(8,128)S(1)}, f32[128,256]{1,0:T(8,128)}, u32[]{:S(2)}) copy-start(f32[128,256]{1,0:T(8,128)} %constant.18.clone.low_ref) | copy-start | bytes 393220
  0.7 6.6 %copy-start.7 = (f32[128,128]{1,0:T(8,128)S(1)}, f32[128,128]{1,0:T(8,128)}, u32[]{:S(2)}) copy-start(f32[128,128]{1,0:T(8,128)} %constant.20.clone.next_ref) | copy-start | bytes 196612
  0.7 6.5 %copy-start.10 = (f32[136,128]{1,0:T(8,128)S(1)}, f32[136,128]{1,0:T(8,128)}, u32[]{:S(2)}) copy-start(f32[136,128]{1,0:T(8,128)} %constant.16.clone.band_ref) | copy-start | bytes 208900
  0.7 6.5 %copy-start.2 = (f32[16,128,128]{2,1,0:T(8,128)S(1)}, f32[16,128,128]{2,1,0:T(8,128)}, u32[]{:S(2)}) copy-start(f32[16,128,128]{2,1,0:T(8,128)} %strain.13) | copy-start | bytes 3145732
  0.7 6.5 %copy-start.1 = (f32[16,128,128]{2,1,0:T(8,128)S(1)}, f32[16,128,128]{2,1,0:T(8,128)}, u32[]{:S(2)}) copy-start(f32[16,128,128]{2,1,0:T(8,128)} %stress.13) | copy-start | bytes 3145732
  0.7 6.5 %copy-start.4 = (s32[16,128,128]{2,1,0:T(8,128)S(1)}, s32[16,128,128]{2,1,0:T(8,128)}, u32[]{:S(2)}) copy-start(s32[16,128,128]{2,1,0:T(8,128)} %count.9) | copy-start | bytes 3145732
  0.7 6.5 %copy-start.3 = (s32[16,128,128]{2,1,0:T(8,128)S(1)}, s32[16,128,128]{2,1,0:T(8,128)}, u32[]{:S(2)}) copy-start(s32[16,128,128]{2,1,0:T(8,128)} %yields.9) | copy-start | bytes 3145732
  2.6 7.5 %collective-permute-start.1 = (f32[128,128]{1,0:T(8,128)S(1)}, f32[128,128]{1,0:T(8,128)S(1)}, u32[]{:S(2)}, u32[]{:S(2)}) collective-permute-start(f32[128,128]{1,0:T(8,128)S(1)} %slice.55), channel_id=1, source_target_pairs={{0,1},{1,0},{2,3},{3,2},{4,8},{5,9},{6,10},{7,11},{8,4},{9,5},{10,... | collective-permute-start | bytes 196616 | tf_op jit(solution)/shard_map/ppermute | solution.py:586
  3.2 7.0 %collective-permute-start = (f32[128,128]{1,0:T(8,128)S(1)}, f32[128,128]{1,0:T(8,128)S(1)}, u32[]{:S(2)}, u32[]{:S(2)}) collective-permute-start(f32[128,128]{1,0:T(8,128)S(1)} %slice.54), channel_id=1, source_target_pairs={{0,4},{1,5},{2,6},{3,7},{4,0},{5,1},{6,2},{7,3},{8,12},{9,13},{10,... | collective-permute-start | bytes 196616 | tf_op jit(solution)/shard_map/ppermute | solution.py:586
  10.2 2.1 %copy-start = (f32[16,128,128]{2,1,0:T(8,128)S(1)}, f32[16,128,128]{2,1,0:T(8,128)}, u32[]{:S(2)}) copy-start(f32[16,128,128]{2,1,0:T(8,128)} %threshold.11) | copy-start | bytes 3145732
  10.2 2.1 %copy-start.11 = (f32[128,128]{1,0:T(8,128)S(1)}, f32[128,128]{1,0:T(8,128)}, u32[]{:S(2)}) copy-start(f32[128,128]{1,0:T(8,128)} %constant.17.clone.band_ref) | copy-start | bytes 196612
  10.6 4.3 %collective-permute-start.3 = (f32[128,128]{1,0:T(8,128)S(1)}, f32[128,128]{1,0:T(8,128)S(1)}, u32[]{:S(2)}, u32[]{:S(2)}) collective-permute-start(f32[128,128]{1,0:T(8,128)S(1)} %slice.57), channel_id=1, source_target_pairs={{0,4},{4,0},{8,12},{12,8},{16,20},{20,16},{24,28},{28,24},{1,2},{5... | collective-permute-start | bytes 196616 | tf_op jit(solution)/shard_map/ppermute | solution.py:586
  12.2 2.7 %collective-permute-start.2 = (f32[128,128]{1,0:T(8,128)S(1)}, f32[128,128]{1,0:T(8,128)S(1)}, u32[]{:S(2)}, u32[]{:S(2)}) collective-permute-start(f32[128,128]{1,0:T(8,128)S(1)} %slice.56), channel_id=1, source_target_pairs={{0,1},{4,5},{8,9},{12,13},{16,17},{20,21},{24,25},{28,29},{1,0},{5... | collective-permute-start | bytes 196616 | tf_op jit(solution)/shard_map/ppermute | solution.py:586
  13.5 1.4 %copy-start.8 = (f32[144,128]{1,0:T(8,128)S(1)}, f32[144,128]{1,0:T(8,128)}, u32[]{:S(2)}) copy-start(f32[144,128]{1,0:T(8,128)} %constant.15.clone.above) | copy-start | bytes 221188
  13.5 1.4 %copy-start.9 = (f32[128,128]{1,0:T(8,128)S(1)}, f32[128,128]{1,0:T(8,128)}, u32[]{:S(2)}) copy-start(f32[128,128]{1,0:T(8,128)} %constant.14.clone.below) | copy-start | bytes 196612
  15.6 6.6 %collective-permute-start.5 = (f32[128,128]{1,0:T(8,128)S(1)}, f32[128,128]{1,0:T(8,128)S(1)}, u32[]{:S(2)}, u32[]{:S(2)}) collective-permute-start(f32[128,128]{1,0:T(8,128)S(1)} %slice.59), channel_id=1, source_target_pairs={{0,1},{1,0},{2,3},{3,2},{4,8},{5,9},{6,10},{7,11},{8,4},{9,5},{10,... | collective-permute-start | bytes 196616 | tf_op jit(solution)/shard_map/ppermute | solution.py:586
  15.8 6.3 %collective-permute-start.4 = (f32[128,128]{1,0:T(8,128)S(1)}, f32[128,128]{1,0:T(8,128)S(1)}, u32[]{:S(2)}, u32[]{:S(2)}) collective-permute-start(f32[128,128]{1,0:T(8,128)S(1)} %slice.58), channel_id=1, source_target_pairs={{0,4},{1,5},{2,6},{3,7},{4,0},{5,1},{6,2},{7,3},{8,12},{9,13},{10,... | collective-permute-start | bytes 196616 | tf_op jit(solution)/shard_map/ppermute | solution.py:586
  22.6 4.3 %collective-permute-start.7 = (f32[128,128]{1,0:T(8,128)S(1)}, f32[128,128]{1,0:T(8,128)S(1)}, u32[]{:S(2)}, u32[]{:S(2)}) collective-permute-start(f32[128,128]{1,0:T(8,128)S(1)} %slice.61), channel_id=1, source_target_pairs={{0,4},{4,0},{8,12},{12,8},{16,20},{20,16},{24,28},{28,24},{1,2},{5... | collective-permute-start | bytes 196616 | tf_op jit(solution)/shard_map/ppermute | solution.py:586
  23.8 3.1 %collective-permute-start.6 = (f32[128,128]{1,0:T(8,128)S(1)}, f32[128,128]{1,0:T(8,128)S(1)}, u32[]{:S(2)}, u32[]{:S(2)}) collective-permute-start(f32[128,128]{1,0:T(8,128)S(1)} %slice.60), channel_id=1, source_target_pairs={{0,1},{4,5},{8,9},{12,13},{16,17},{20,21},{24,25},{28,29},{1,0},{5... | collective-permute-start | bytes 196616 | tf_op jit(solution)/shard_map/ppermute | solution.py:586
  27.5 4.6 %collective-permute-start.8 = (f32[176,128]{1,0:T(8,128)S(1)}, f32[176,128]{1,0:T(8,128)S(1)}, u32[]{:S(2)}, u32[]{:S(2)}) collective-permute-start(f32[176,128]{1,0:T(8,128)S(1)} %get-tuple-element.83), channel_id=1, source_target_pairs={{0,4},{1,5},{2,6},{3,7},{4,0},{5,1},{6,2},{7,3},{8,12},{9,13},{10,... | collective-permute-start | bytes 270344 | tf_op jit(solution)/shard_map/ppermute | solution.py:586
  28.7 3.4 %collective-permute-start.9 = (f32[176,128]{1,0:T(8,128)S(1)}, f32[176,128]{1,0:T(8,128)S(1)}, u32[]{:S(2)}, u32[]{:S(2)}) collective-permute-start(f32[176,128]{1,0:T(8,128)S(1)} %get-tuple-element.84), channel_id=1, source_target_pairs={{0,1},{1,0},{2,3},{3,2},{4,8},{5,9},{6,10},{7,11},{8,4},{9,5},{10,... | collective-permute-start | bytes 270344 | tf_op jit(solution)/shard_map/ppermute | solution.py:586
  32.6 5.6 %collective-permute-start.11 = (f32[176,128]{1,0:T(8,128)S(1)}, f32[176,128]{1,0:T(8,128)S(1)}, u32[]{:S(2)}, u32[]{:S(2)}) collective-permute-start(f32[176,128]{1,0:T(8,128)S(1)} %slice.68), channel_id=1, source_target_pairs={{0,4},{4,0},{8,12},{12,8},{16,20},{20,16},{24,28},{28,24},{1,2},{5... | collective-permute-start | bytes 270344 | tf_op jit(solution)/shard_map/ppermute | solution.py:586
  35.7 2.5 %collective-permute-start.10 = (f32[176,128]{1,0:T(8,128)S(1)}, f32[176,128]{1,0:T(8,128)S(1)}, u32[]{:S(2)}, u32[]{:S(2)}) collective-permute-start(f32[176,128]{1,0:T(8,128)S(1)} %slice.66), channel_id=1, source_target_pairs={{0,1},{4,5},{8,9},{12,13},{16,17},{20,21},{24,25},{28,29},{1,0},{5... | collective-permute-start | bytes 270344 | tf_op jit(solution)/shard_map/ppermute | solution.py:586

commit v13 on v12

--- a/solution.py
+++ b/solution.py
@@ -413,8 +413,10 @@
 
 
 def column_kernel(depth, across, row_even, row_odd, rest_even, rest_odd, threshold, norm, band_ref, _,
-                  kept, kept_before, edge_low, edge_high, deep):
+                  plastic, kept, kept_before, edge_low, edge_high, plastic_out, deep, copy_sem):
     layers, total, cols = across.shape
+    whole = pltpu.make_async_copy(plastic, plastic_out, copy_sem)
+    whole.start()
 
     def depth_sums(part, values):
         for layer, value in enumerate(depth_smooth(values, depth)):
@@ -453,15 +455,13 @@
         moved = pltpu.roll(moved, layer * REACH, 1) if layer else moved
         pltpu.store(edge_low, moved, mask=slots == layer)
         pltpu.store(edge_high, moved, mask=slots == (layer - 1) % (cols // REACH))
+    whole.wait()
 
 
 def final_kernel(stress, strain, plastic, inner, inner_before, edge_low, edge_high, norm_low, norm_high,
                  col_even, col_odd, last_even, last_odd, rest_even, rest_odd, norm_before, own_cols,
-                 plastic_out, damage_out, force_out, columns, lows, highs, damage_s, force_s, sums, diffs,
-                 copy_sem, sems):
+                 damage_out, force_out, columns, lows, highs, damage_s, force_s, sums, diffs, sems):
     layers, rows, cols = stress.shape
-    whole = pltpu.make_async_copy(plastic, plastic_out, copy_sem)
-    whole.start()
     from_low, _ = sides("gy", last_even[...], last_odd[...])
     folded = from_low[REACH : REACH + rows // 4]
     pieces = [from_low[REACH + rows // 4 :], folded]
@@ -546,18 +546,18 @@
         return carry
 
     lax.fori_loop(0, layers, drain, 0)
-    whole.wait()
-
-
-def call(kernel, outs, scratch, nanoseconds, operands, spaces=None, outs_space=pltpu.VMEM, limit=VMEM_BYTES):
+
+
+def call(kernel, outs, scratch, nanoseconds, operands, spaces=None, outs_space=None, limit=VMEM_BYTES):
     spaces = spaces or [pltpu.VMEM] * len(operands)
+    outs_space = outs_space or [pltpu.VMEM] * len(outs)
     shapes = [out if isinstance(out, jax.ShapeDtypeStruct) else jax.ShapeDtypeStruct(out, jnp.float32)
               for out in outs]
     return pl.pallas_call(
         kernel,
         out_shape=shapes,
         in_specs=[pl.BlockSpec(memory_space=space) for space in spaces],
-        out_specs=[pl.BlockSpec(memory_space=outs_space)] * len(outs),
+        out_specs=[pl.BlockSpec(memory_space=space) for space in outs_space],
         scratch_shapes=[pltpu.VMEM(s, jnp.float32) if isinstance(s, tuple) else s for s in scratch],
         compiler_params=pltpu.CompilerParams(vmem_limit_bytes=limit),
         cost_estimate=pl.CostEstimate(
@@ -684,19 +684,22 @@
         if last:
             last_even, last_odd = col_even[rows:], col_odd[rows:]
             col_even, col_odd = col_even[:rows], col_odd[:rows]
-        kept, kept_before, edge_low, edge_high = call(
-            functools.partial(column_kernel, depth), [whole, top, packed, packed], [wide], 1800,
-            (across, row_even, row_odd, rest_even, rest_odd, threshold, norm, cols_band, own_cols),
+        kept, kept_before, edge_low, edge_high, plastic_out = call(
+            functools.partial(column_kernel, depth), [whole, top, packed, packed, whole],
+            [wide, pltpu.SemaphoreType.DMA(())], 1800,
+            (across, row_even, row_odd, rest_even, rest_odd, threshold, norm, cols_band, own_cols,
+             plastic),
+            outs_space=[pltpu.VMEM] * 4 + [pltpu.HBM],
         )
-    return tuple(call(
-        final_kernel, [whole, whole, (2, *whole)],
-        [packed] * 3 + [whole, (2, *whole), wide, wide,
-         pltpu.SemaphoreType.DMA(()), pltpu.SemaphoreType.DMA((3, layers))],
+    damage, force = call(
+        final_kernel, [whole, (2, *whole)],
+        [packed] * 3 + [whole, (2, *whole), wide, wide, pltpu.SemaphoreType.DMA((3, layers))],
         3000,
         (stress, strain, plastic, kept, kept_before, edge_low, edge_high, *norms, col_even, col_odd,
          last_even, last_odd, rest_even, rest_odd, norm_before, own_cols),
-        outs_space=pltpu.HBM,
-    ))
+        outs_space=[pltpu.HBM] * 2,
+    )
+    return plastic_out, damage, force
 
 
 def solution(mesh):

time: 41.5 us -> 41.5 us (level)
  no operation moved by 1% of the time
where the time goes in v13:
time: 41.5 us; the launch traced here: 41.4 us
  Pallas kernels  21.8 us (53%)
  starting transfers between devices  15 us (36%)
  waiting for transfers between devices  3.4 us (8%)
  between operations  1.02 us (2%)
    pallas_call x14, Pallas kernels, call(): pl.pallas_call(kernel, out_shape=shapes, in_specs=[pl.BlockSpec(memory_sp...  21.8 us
    ppermute x12, starting transfers between devices, exchange(): results.append(lax.ppermute(value, names, pairs))  15 us
    ppermute x12, waiting for transfers between devices, exchange(): results.append(lax.ppermute(value, names, pairs))  3.4 us
  transfers between devices with their start and end apart: 12, of which 3 were waited for; matrix products, arithmetic and copies ran while one was open for 0% of the time, Pallas kernels for 35%

profile of v13, /device:TPU:0, one launch (start us, length us, event | category | flops | bytes accessed | tf_op | source)
XLA Modules:
  0.0 41.4 jit_solution(3304235937157305850)
XLA Ops:
  0.6 0.0 copy-start.5
  0.6 0.0 copy-start.6
  0.7 0.0 copy-start.7
  0.7 0.0 copy-start.10
  0.7 0.0 copy-start.2
  0.7 0.0 copy-start.1
  0.7 0.0 copy-start.4
  0.7 0.0 copy-start.3
  0.7 1.9 %shard_map.140 = (f32[136,128]{1,0:T(8,128)S(1)}, f32[136,128]{1,0:T(8,128)S(1)}, f32[136,128]{1,0:T(8,128)S(1)}, f32[136,128]{1,0:T(8,128)S(1)}, f32[136,128]{1...) custom-call(f32[16,128,128]{2,1,0:T(8,128)} %stress.13, ...), custom_call_target="tpu_custom_call" | custom-call | flops 1500000000 | bytes 1500000 | tf_op jit(solution)/shard_map/pallas_call | solution.py:556
  2.6 0.5 %collective-permute-start.1 = (f32[128,128]{1,0:T(8,128)S(1)}, f32[128,128]{1,0:T(8,128)S(1)}, u32[]{:S(2)}, u32[]{:S(2)}) collective-permute-start(f32[128,128]{1,0:T(8,128)S(1)} %slice.55), channel_id=1, source_target_pairs={{0,1},{1,0},{2,3},{3,2},{4,8},{5,9},{6,10},{7,11},{8,4},{9,5},{10,... | collective-permute-start | bytes 196616 | tf_op jit(solution)/shard_map/ppermute | solution.py:586
  3.2 4.0 %collective-permute-start = (f32[128,128]{1,0:T(8,128)S(1)}, f32[128,128]{1,0:T(8,128)S(1)}, u32[]{:S(2)}, u32[]{:S(2)}) collective-permute-start(f32[128,128]{1,0:T(8,128)S(1)} %slice.54), channel_id=1, source_target_pairs={{0,4},{1,5},{2,6},{3,7},{4,0},{5,1},{6,2},{7,3},{8,12},{9,13},{10,... | collective-permute-start | bytes 196616 | tf_op jit(solution)/shard_map/ppermute | solution.py:586
  7.2 0.0 copy-done.5
  7.2 0.0 copy-done.6
  7.2 0.0 copy-done.7
  7.2 0.0 copy-done.10
  7.2 0.0 copy-done.2
  7.2 0.0 copy-done.1
  7.2 0.0 copy-done.4
  7.2 0.0 copy-done.3
  7.3 2.9 %shard_map.139 = (f32[16,136,128]{2,1,0:T(8,128)S(1)}, f32[136,256]{1,0:T(8,128)S(1)}, f32[136,256]{1,0:T(8,128)S(1)}, f32[16,128,128]{2,1,0:T(8,128)S(1)}, f32[16,128,128]{2,1,0:T(8,128)S(1)}) custom-call(f32[16,128,128]{2,1,0:T(8,128)S(1)} %copy-done.1, f32[16,128,128]{2,1,0:T(8,128)S(1)} %copy-done.2, s32[16,128,128]{2,1,0:T(8,128)S(1)} %copy-done.3, ...), custom_call_target="tpu_custom_call" | custom-call | flops 4499999744 | bytes 4500000 | tf_op jit(solution)/shard_map/pallas_call | solution.py:556
  10.2 0.0 copy-start
  10.2 0.0 copy-start.11
  10.2 0.0 collective-permute-done.1.row_odd
  10.2 0.0 collective-permute-done.row_even
  10.2 0.4 shard_map.141
  10.6 1.6 %collective-permute-start.3 = (f32[128,128]{1,0:T(8,128)S(1)}, f32[128,128]{1,0:T(8,128)S(1)}, u32[]{:S(2)}, u32[]{:S(2)}) collective-permute-start(f32[128,128]{1,0:T(8,128)S(1)} %slice.57), channel_id=1, source_target_pairs={{0,4},{4,0},{8,12},{12,8},{16,20},{20,16},{24,28},{28,24},{1,2},{5... | collective-permute-start | bytes 196616 | tf_op jit(solution)/shard_map/ppermute | solution.py:586
  12.2 0.1 collective-permute-start.2
  12.3 0.0 copy-done
  12.3 0.0 copy-done.11
  12.3 1.2 %shard_map.142 = (f32[16,128,128]{2,1,0:T(8,128)S(1)}, f32[16,8,128]{2,1,0:T(8,128)S(1)}, f32[136,128]{1,0:T(8,128)S(1)}, f32[136,128]{1,0:T(8,128)S(1)}, f32[16,128,128]{2,1,0:T(8,128)}) custom-call(f32[16,136,128]{2,1,0:T(8,128)S(1)} %get-tuple-element.53.across, f32[128,128]{1,0:T(8,128)S(1)} %collective-permute-done.row_even, ...), custom_call_target="tpu_custom_call" | custom-call | flops 1800000000 | bytes 1800000 | tf_op jit(solution)/shard_map/pallas_call | solution.py:556
  13.6 0.0 copy-start.8
  13.6 0.0 copy-start.9
  13.6 1.1 %shard_map.143.fixed = f32[136,128]{1,0:T(8,128)S(1)} custom-call(f32[16,128,128]{2,1,0:T(8,128)S(1)} %copy-done.1, f32[16,128,128]{2,1,0:T(8,128)S(1)} %copy-done.2, f32[16,128,128]{2,1,0:T(8,128)S(1)} %copy-done, f32[184,128]{1,0:T(8,128)S(1)} %get-tuple-element.69._), custom_call_target="tpu_custom_call" | custom-call | flops 800000000 | bytes 800000 | tf_op jit(solution)/shard_map/pallas_call | solution.py:556
  14.7 0.3 collective-permute-done.3.col_odd
  14.9 0.0 collective-permute-done.2.col_even
  14.9 0.0 copy-done.8
  14.9 0.0 copy-done.9
  14.9 0.6 %shard_map.145 = (f32[176,128]{1,0:T(8,128)S(1)}, f32[176,128]{1,0:T(8,128)S(1)}) custom-call(f32[16,128,128]{2,1,0:T(8,128)S(1)} %copy-done.1, f32[16,128,128]{2,1,0:T(8,128)S(1)} %copy-done.2, s32[16,128,128]{2,1,0:T(8,128)S(1)} %copy-done.3, s32[16,128,128]{2,1,0:T(8,128)S(1)} %copy-done.4, f32[16,128,128]{2,1,0:T(8,128)S(1)} %copy-done, ...), custom_call_target="tpu_custom_call" | custom-call | flops 800000000 | bytes 800000 | tf_op jit(solution)/shard_map/pallas_call | solution.py:556
  15.6 0.3 collective-permute-start.5
  15.9 2.9 %collective-permute-start.4 = (f32[128,128]{1,0:T(8,128)S(1)}, f32[128,128]{1,0:T(8,128)S(1)}, u32[]{:S(2)}, u32[]{:S(2)}) collective-permute-start(f32[128,128]{1,0:T(8,128)S(1)} %slice.58), channel_id=1, source_target_pairs={{0,4},{1,5},{2,6},{3,7},{4,0},{5,1},{6,2},{7,3},{8,12},{9,13},{10,... | collective-permute-start | bytes 196616 | tf_op jit(solution)/shard_map/ppermute | solution.py:586
  18.8 3.4 %shard_map.144 = (f32[16,136,128]{2,1,0:T(8,128)S(1)}, f32[136,256]{1,0:T(8,128)S(1)}, f32[136,256]{1,0:T(8,128)S(1)}, f32[16,128,128]{2,1,0:T(8,128)S(1)}) custom-call(f32[16,128,128]{2,1,0:T(8,128)S(1)} %copy-done.1, f32[16,128,128]{2,1,0:T(8,128)S(1)} %copy-done.2, s32[16,128,128]{2,1,0:T(8,128)S(1)} %copy-done.3, s32[16,128,128]{2,1,0:T(8,128)S(1)} %copy-done.4, ...), custom_call_target="tpu_custom_call" | custom-call | flops 4499999744 | bytes 4500000 | tf_op jit(solution)/shard_map/pallas_call | solution.py:556
  22.1 0.0 collective-permute-done.5.row_odd
  22.2 0.0 collective-permute-done.4.row_even
  22.2 0.4 shard_map.146
  22.6 1.2 %collective-permute-start.7 = (f32[128,128]{1,0:T(8,128)S(1)}, f32[128,128]{1,0:T(8,128)S(1)}, u32[]{:S(2)}, u32[]{:S(2)}) collective-permute-start(f32[128,128]{1,0:T(8,128)S(1)} %slice.61), channel_id=1, source_target_pairs={{0,4},{4,0},{8,12},{12,8},{16,20},{20,16},{24,28},{28,24},{1,2},{5... | collective-permute-start | bytes 196616 | tf_op jit(solution)/shard_map/ppermute | solution.py:586
  23.8 0.0 collective-permute-start.6
  23.8 1.2 %shard_map.147 = (f32[16,128,128]{2,1,0:T(8,128)S(1)}, f32[16,8,128]{2,1,0:T(8,128)S(1)}, f32[136,128]{1,0:T(8,128)S(1)}, f32[136,128]{1,0:T(8,128)S(1)}, f32[16,128,128]{2,1,0:T(8,128)}) custom-call(f32[16,136,128]{2,1,0:T(8,128)S(1)} %get-tuple-element.70.across, f32[128,128]{1,0:T(8,128)S(1)} %collective-permute-done.4.row_even, ...), custom_call_target="tpu_custom_call" | custom-call | flops 1800000000 | bytes 1800000 | tf_op jit(solution)/shard_map/pallas_call | solution.py:556
  25.0 1.9 %collective-permute-done.7.col_odd = f32[128,128]{1,0:T(8,128)S(1)} collective-permute-done((f32[128,128]{1,0:T(8,128)S(1)}, f32[128,128]{1,0:T(8,128)S(1)}, u32[]{:S(2)}, u32[]{:S(2)}) %collective-permute-start.7) | collective-permute-done | bytes 65568 | tf_op jit(solution)/shard_map/ppermute | solution.py:586
  26.9 0.0 collective-permute-done.6.col_even
  26.9 0.6 %shard_map.149 = (f32[176,128]{1,0:T(8,128)S(1)}, f32[176,128]{1,0:T(8,128)S(1)}) custom-call(f32[16,128,128]{2,1,0:T(8,128)S(1)} %copy-done.1, f32[16,128,128]{2,1,0:T(8,128)S(1)} %copy-done.2, s32[16,128,128]{2,1,0:T(8,128)S(1)} %copy-done.3, s32[16,128,128]{2,1,0:T(8,128)S(1)} %copy-done.4, f32[16,128,128]{2,1,0:T(8,128)S(1)} %copy-done, ...), custom_call_target="tpu_custom_call" | custom-call | flops 800000000 | bytes 800000 | tf_op jit(solution)/shard_map/pallas_call | solution.py:556
  27.5 1.2 %collective-permute-start.8 = (f32[176,128]{1,0:T(8,128)S(1)}, f32[176,128]{1,0:T(8,128)S(1)}, u32[]{:S(2)}, u32[]{:S(2)}) collective-permute-start(f32[176,128]{1,0:T(8,128)S(1)} %get-tuple-element.85), channel_id=1, source_target_pairs={{0,4},{1,5},{2,6},{3,7},{4,0},{5,1},{6,2},{7,3},{8,12},{9,13},{10,... | collective-permute-start | bytes 270344 | tf_op jit(solution)/shard_map/ppermute | solution.py:586
  28.7 0.0 collective-permute-start.9
  28.7 3.4 %shard_map.148 = (f32[16,136,128]{2,1,0:T(8,128)S(1)}, f32[136,256]{1,0:T(8,128)S(1)}, f32[136,256]{1,0:T(8,128)S(1)}, f32[16,128,128]{2,1,0:T(8,128)S(1)}) custom-call(f32[16,128,128]{2,1,0:T(8,128)S(1)} %copy-done.1, f32[16,128,128]{2,1,0:T(8,128)S(1)} %copy-done.2, s32[16,128,128]{2,1,0:T(8,128)S(1)} %copy-done.3, s32[16,128,128]{2,1,0:T(8,128)S(1)} %copy-done.4, ...), custom_call_target="tpu_custom_call" | custom-call | flops 4499999744 | bytes 4500000 | tf_op jit(solution)/shard_map/pallas_call | solution.py:556
  32.1 0.0 collective-permute-done.8
  32.1 0.0 collective-permute-done.9
  32.2 0.4 shard_map.150
  32.6 3.1 %collective-permute-start.11 = (f32[176,128]{1,0:T(8,128)S(1)}, f32[176,128]{1,0:T(8,128)S(1)}, u32[]{:S(2)}, u32[]{:S(2)}) collective-permute-start(f32[176,128]{1,0:T(8,128)S(1)} %slice.68), channel_id=1, source_target_pairs={{0,4},{4,0},{8,12},{12,8},{16,20},{20,16},{24,28},{28,24},{1,2},{5... | collective-permute-start | bytes 270344 | tf_op jit(solution)/shard_map/ppermute | solution.py:586
  35.7 0.0 collective-permute-start.10
  35.7 1.2 %shard_map.151 = (f32[16,128,128]{2,1,0:T(8,128)S(1)}, f32[16,8,128]{2,1,0:T(8,128)S(1)}, f32[136,128]{1,0:T(8,128)S(1)}, f32[136,128]{1,0:T(8,128)S(1)}, f32[16,128,128]{2,1,0:T(8,128)}) custom-call(f32[16,136,128]{2,1,0:T(8,128)S(1)} %get-tuple-element.83.across, f32[128,128]{1,0:T(8,128)S(1)} %slice.72.row_even, f32[128,128]{1,0:T(8,128)S(1)} %slice.73.row_odd, ...), custom_call_target="tpu_custom_call" | custom-call | flops 1800000000 | bytes 1800000 | tf_op jit(solution)/shard_map/pallas_call | solution.py:556
  36.9 1.3 %collective-permute-done.11 = f32[176,128]{1,0:T(8,128)S(1)} collective-permute-done((f32[176,128]{1,0:T(8,128)S(1)}, f32[176,128]{1,0:T(8,128)S(1)}, u32[]{:S(2)}, u32[]{:S(2)}) %collective-permute-start.11) | collective-permute-done | bytes 90144 | tf_op jit(solution)/shard_map/ppermute | solution.py:586
  38.2 0.0 collective-permute-done.10
  38.2 3.1 %shard_map.152 = (f32[16,128,128]{2,1,0:T(8,128)}, f32[2,16,128,128]{3,2,1,0:T(8,128)}) custom-call(f32[16,128,128]{2,1,0:T(8,128)S(1)} %copy-done.1, f32[16,128,128]{2,1,0:T(8,128)S(1)} %copy-done.2, f32[16,128,128]{2,1,0:T(8,128)S(1)} %get-tuple-element.89._.plastic, f32[16,128,128]{2,1,0:T(8,128)S(1)} %get-tuple-element.92.inner, ...), custom_call_target="tpu_custom_call" | custom-call | flops 3000000000 | bytes 3000000 | tf_op jit(solution)/shard_map/pallas_call | solution.py:556
  (18 shorter events, 0.1 us)
Async XLA Ops:
  0.6 6.6 %copy-start.5 = (f32[128,256]{1,0:T(8,128)S(1)}, f32[128,256]{1,0:T(8,128)}, u32[]{:S(2)}) copy-start(f32[128,256]{1,0:T(8,128)} %constant.19.clone.high_ref) | copy-start | bytes 393220
  0.6 6.6 %copy-start.6 = (f32[128,256]{1,0:T(8,128)S(1)}, f32[128,256]{1,0:T(8,128)}, u32[]{:S(2)}) copy-start(f32[128,256]{1,0:T(8,128)} %constant.18.clone.low_ref) | copy-start | bytes 393220
  0.7 6.6 %copy-start.7 = (f32[128,128]{1,0:T(8,128)S(1)}, f32[128,128]{1,0:T(8,128)}, u32[]{:S(2)}) copy-start(f32[128,128]{1,0:T(8,128)} %constant.20.clone.next_ref) | copy-start | bytes 196612
  0.7 6.5 %copy-start.10 = (f32[136,128]{1,0:T(8,128)S(1)}, f32[136,128]{1,0:T(8,128)}, u32[]{:S(2)}) copy-start(f32[136,128]{1,0:T(8,128)} %constant.16.clone.band_ref) | copy-start | bytes 208900
  0.7 6.5 %copy-start.2 = (f32[16,128,128]{2,1,0:T(8,128)S(1)}, f32[16,128,128]{2,1,0:T(8,128)}, u32[]{:S(2)}) copy-start(f32[16,128,128]{2,1,0:T(8,128)} %strain.13) | copy-start | bytes 3145732
  0.7 6.5 %copy-start.1 = (f32[16,128,128]{2,1,0:T(8,128)S(1)}, f32[16,128,128]{2,1,0:T(8,128)}, u32[]{:S(2)}) copy-start(f32[16,128,128]{2,1,0:T(8,128)} %stress.13) | copy-start | bytes 3145732
  0.7 6.5 %copy-start.4 = (s32[16,128,128]{2,1,0:T(8,128)S(1)}, s32[16,128,128]{2,1,0:T(8,128)}, u32[]{:S(2)}) copy-start(s32[16,128,128]{2,1,0:T(8,128)} %count.9) | copy-start | bytes 3145732
  0.7 6.5 %copy-start.3 = (s32[16,128,128]{2,1,0:T(8,128)S(1)}, s32[16,128,128]{2,1,0:T(8,128)}, u32[]{:S(2)}) copy-start(s32[16,128,128]{2,1,0:T(8,128)} %yields.9) | copy-start | bytes 3145732
  2.6 7.5 %collective-permute-start.1 = (f32[128,128]{1,0:T(8,128)S(1)}, f32[128,128]{1,0:T(8,128)S(1)}, u32[]{:S(2)}, u32[]{:S(2)}) collective-permute-start(f32[128,128]{1,0:T(8,128)S(1)} %slice.55), channel_id=1, source_target_pairs={{0,1},{1,0},{2,3},{3,2},{4,8},{5,9},{6,10},{7,11},{8,4},{9,5},{10,... | collective-permute-start | bytes 196616 | tf_op jit(solution)/shard_map/ppermute | solution.py:586
  3.2 7.0 %collective-permute-start = (f32[128,128]{1,0:T(8,128)S(1)}, f32[128,128]{1,0:T(8,128)S(1)}, u32[]{:S(2)}, u32[]{:S(2)}) collective-permute-start(f32[128,128]{1,0:T(8,128)S(1)} %slice.54), channel_id=1, source_target_pairs={{0,4},{1,5},{2,6},{3,7},{4,0},{5,1},{6,2},{7,3},{8,12},{9,13},{10,... | collective-permute-start | bytes 196616 | tf_op jit(solution)/shard_map/ppermute | solution.py:586
  10.2 2.1 %copy-start = (f32[16,128,128]{2,1,0:T(8,128)S(1)}, f32[16,128,128]{2,1,0:T(8,128)}, u32[]{:S(2)}) copy-start(f32[16,128,128]{2,1,0:T(8,128)} %threshold.11) | copy-start | bytes 3145732
  10.2 2.1 %copy-start.11 = (f32[128,128]{1,0:T(8,128)S(1)}, f32[128,128]{1,0:T(8,128)}, u32[]{:S(2)}) copy-start(f32[128,128]{1,0:T(8,128)} %constant.17.clone.band_ref) | copy-start | bytes 196612
  10.6 4.3 %collective-permute-start.3 = (f32[128,128]{1,0:T(8,128)S(1)}, f32[128,128]{1,0:T(8,128)S(1)}, u32[]{:S(2)}, u32[]{:S(2)}) collective-permute-start(f32[128,128]{1,0:T(8,128)S(1)} %slice.57), channel_id=1, source_target_pairs={{0,4},{4,0},{8,12},{12,8},{16,20},{20,16},{24,28},{28,24},{1,2},{5... | collective-permute-start | bytes 196616 | tf_op jit(solution)/shard_map/ppermute | solution.py:586
  12.2 2.7 %collective-permute-start.2 = (f32[128,128]{1,0:T(8,128)S(1)}, f32[128,128]{1,0:T(8,128)S(1)}, u32[]{:S(2)}, u32[]{:S(2)}) collective-permute-start(f32[128,128]{1,0:T(8,128)S(1)} %slice.56), channel_id=1, source_target_pairs={{0,1},{4,5},{8,9},{12,13},{16,17},{20,21},{24,25},{28,29},{1,0},{5... | collective-permute-start | bytes 196616 | tf_op jit(solution)/shard_map/ppermute | solution.py:586
  13.6 1.4 %copy-start.8 = (f32[144,128]{1,0:T(8,128)S(1)}, f32[144,128]{1,0:T(8,128)}, u32[]{:S(2)}) copy-start(f32[144,128]{1,0:T(8,128)} %constant.15.clone.above) | copy-start | bytes 221188
  13.6 1.4 %copy-start.9 = (f32[128,128]{1,0:T(8,128)S(1)}, f32[128,128]{1,0:T(8,128)}, u32[]{:S(2)}) copy-start(f32[128,128]{1,0:T(8,128)} %constant.14.clone.below) | copy-start | bytes 196612
  15.6 6.6 %collective-permute-start.5 = (f32[128,128]{1,0:T(8,128)S(1)}, f32[128,128]{1,0:T(8,128)S(1)}, u32[]{:S(2)}, u32[]{:S(2)}) collective-permute-start(f32[128,128]{1,0:T(8,128)S(1)} %slice.59), channel_id=1, source_target_pairs={{0,1},{1,0},{2,3},{3,2},{4,8},{5,9},{6,10},{7,11},{8,4},{9,5},{10,... | collective-permute-start | bytes 196616 | tf_op jit(solution)/shard_map/ppermute | solution.py:586
  15.9 6.3 %collective-permute-start.4 = (f32[128,128]{1,0:T(8,128)S(1)}, f32[128,128]{1,0:T(8,128)S(1)}, u32[]{:S(2)}, u32[]{:S(2)}) collective-permute-start(f32[128,128]{1,0:T(8,128)S(1)} %slice.58), channel_id=1, source_target_pairs={{0,4},{1,5},{2,6},{3,7},{4,0},{5,1},{6,2},{7,3},{8,12},{9,13},{10,... | collective-permute-start | bytes 196616 | tf_op jit(solution)/shard_map/ppermute | solution.py:586
  22.6 4.3 %collective-permute-start.7 = (f32[128,128]{1,0:T(8,128)S(1)}, f32[128,128]{1,0:T(8,128)S(1)}, u32[]{:S(2)}, u32[]{:S(2)}) collective-permute-start(f32[128,128]{1,0:T(8,128)S(1)} %slice.61), channel_id=1, source_target_pairs={{0,4},{4,0},{8,12},{12,8},{16,20},{20,16},{24,28},{28,24},{1,2},{5... | collective-permute-start | bytes 196616 | tf_op jit(solution)/shard_map/ppermute | solution.py:586
  23.8 3.1 %collective-permute-start.6 = (f32[128,128]{1,0:T(8,128)S(1)}, f32[128,128]{1,0:T(8,128)S(1)}, u32[]{:S(2)}, u32[]{:S(2)}) collective-permute-start(f32[128,128]{1,0:T(8,128)S(1)} %slice.60), channel_id=1, source_target_pairs={{0,1},{4,5},{8,9},{12,13},{16,17},{20,21},{24,25},{28,29},{1,0},{5... | collective-permute-start | bytes 196616 | tf_op jit(solution)/shard_map/ppermute | solution.py:586
  27.5 4.6 %collective-permute-start.8 = (f32[176,128]{1,0:T(8,128)S(1)}, f32[176,128]{1,0:T(8,128)S(1)}, u32[]{:S(2)}, u32[]{:S(2)}) collective-permute-start(f32[176,128]{1,0:T(8,128)S(1)} %get-tuple-element.85), channel_id=1, source_target_pairs={{0,4},{1,5},{2,6},{3,7},{4,0},{5,1},{6,2},{7,3},{8,12},{9,13},{10,... | collective-permute-start | bytes 270344 | tf_op jit(solution)/shard_map/ppermute | solution.py:586
  28.7 3.4 %collective-permute-start.9 = (f32[176,128]{1,0:T(8,128)S(1)}, f32[176,128]{1,0:T(8,128)S(1)}, u32[]{:S(2)}, u32[]{:S(2)}) collective-permute-start(f32[176,128]{1,0:T(8,128)S(1)} %get-tuple-element.86), channel_id=1, source_target_pairs={{0,1},{1,0},{2,3},{3,2},{4,8},{5,9},{6,10},{7,11},{8,4},{9,5},{10,... | collective-permute-start | bytes 270344 | tf_op jit(solution)/shard_map/ppermute | solution.py:586
  32.6 5.6 %collective-permute-start.11 = (f32[176,128]{1,0:T(8,128)S(1)}, f32[176,128]{1,0:T(8,128)S(1)}, u32[]{:S(2)}, u32[]{:S(2)}) collective-permute-start(f32[176,128]{1,0:T(8,128)S(1)} %slice.68), channel_id=1, source_target_pairs={{0,4},{4,0},{8,12},{12,8},{16,20},{20,16},{24,28},{28,24},{1,2},{5... | collective-permute-start | bytes 270344 | tf_op jit(solution)/shard_map/ppermute | solution.py:586
  35.7 2.5 %collective-permute-start.10 = (f32[176,128]{1,0:T(8,128)S(1)}, f32[176,128]{1,0:T(8,128)S(1)}, u32[]{:S(2)}, u32[]{:S(2)}) collective-permute-start(f32[176,128]{1,0:T(8,128)S(1)} %slice.66), channel_id=1, source_target_pairs={{0,1},{4,5},{8,9},{12,13},{16,17},{20,21},{24,25},{28,29},{1,0},{5... | collective-permute-start | bytes 270344 | tf_op jit(solution)/shard_map/ppermute | solution.py:586

commit v14 on v12

--- a/solution.py
+++ b/solution.py
@@ -457,7 +457,7 @@
 
 def final_kernel(stress, strain, plastic, inner, inner_before, edge_low, edge_high, norm_low, norm_high,
                  col_even, col_odd, last_even, last_odd, rest_even, rest_odd, norm_before, own_cols,
-                 plastic_out, damage_out, force_out, columns, lows, highs, damage_s, force_s, sums, diffs,
+                 plastic_out, damage_out, force_out, columns, lows, highs, damage_s, force_s, half, sums, diffs,
                  copy_sem, sems):
     layers, rows, cols = stress.shape
     whole = pltpu.make_async_copy(plastic, plastic_out, copy_sem)
@@ -491,29 +491,35 @@
 
     lanes = lane_ids((REACH, cols))
 
-    def stresses(pair):
+    def layers_of(pair):
         for near in range(2):
-            layer = 2 * pair + near
             for block in range(rows // REACH + 1):
-                extended = pl.ds(block * REACH, REACH)
-                at = (layer, pl.ds((block - 1) * REACH if block else 0, REACH), slice(None))
-                if block:
-                    rest = (stress[at] + strain[at]) - plastic[at]
-                else:
-                    line = pl.ds(layers + layer, 1)
-                    rest, _ = sides("gx", rest_even[line, :], rest_odd[line, :])
-                kept = inner[at] if block else inner_before[layer]
-                kept = with_edges(kept, layer, lows[extended, :], highs[extended, :])
-                value = (0.5 * kept) * rest
-                left = jnp.where(
-                    lanes == 0,
-                    pltpu.roll(columns[extended, :], (cols - layer) % cols, 1),
-                    pltpu.roll(value, 1, 1),
-                )
-                sums[layer, extended, :] = left + value
-                diffs[layer, extended, :] = left - value
-                if block:
-                    damage_s[at] = 1.0 - kept
+                yield 2 * pair + near, block, pl.ds(block * REACH, REACH)
+
+    def damages(pair):
+        for layer, block, extended in layers_of(pair):
+            at = (layer, pl.ds((block - 1) * REACH if block else 0, REACH), slice(None))
+            if block:
+                rest = (stress[at] + strain[at]) - plastic[at]
+            else:
+                line = pl.ds(layers + layer, 1)
+                rest, _ = sides("gx", rest_even[line, :], rest_odd[line, :])
+            kept = inner[at] if block else inner_before[layer]
+            kept = with_edges(kept, layer, lows[extended, :], highs[extended, :])
+            half[layer, extended, :] = (0.5 * kept) * rest
+            if block:
+                damage_s[at] = 1.0 - kept
+
+    def neighbours(pair):
+        for layer, block, extended in layers_of(pair):
+            value = half[layer, extended, :]
+            left = jnp.where(
+                lanes == 0,
+                pltpu.roll(columns[extended, :], (cols - layer) % cols, 1),
+                pltpu.roll(value, 1, 1),
+            )
+            sums[layer, extended, :] = left + value
+            diffs[layer, extended, :] = left - value
 
     def forces(pair):
         for near in range(2):
@@ -530,15 +536,22 @@
                 copy.start()
 
     def step(pair, carry):
-        forces(pair - 1)
-        stresses(pair)
-        start(pair - 1)
+        forces(pair - 2)
+        neighbours(pair - 1)
+        damages(pair)
+        start(pair - 2)
         return carry
 
-    stresses(0)
-    lax.fori_loop(1, layers // 2, step, 0)
-    forces(layers // 2 - 1)
-    start(layers // 2 - 1)
+    pairs = layers // 2
+    damages(0)
+    neighbours(0)
+    damages(1)
+    lax.fori_loop(2, pairs, step, 0)
+    forces(pairs - 2)
+    neighbours(pairs - 1)
+    start(pairs - 2)
+    forces(pairs - 1)
+    start(pairs - 1)
 
     def drain(layer, carry):
         for copy in copies(layer):
@@ -690,7 +703,7 @@
         )
     return tuple(call(
         final_kernel, [whole, whole, (2, *whole)],
-        [packed] * 3 + [whole, (2, *whole), wide, wide,
+        [packed] * 3 + [whole, (2, *whole), wide, wide, wide,
          pltpu.SemaphoreType.DMA(()), pltpu.SemaphoreType.DMA((3, layers))],
         3000,
         (stress, strain, plastic, kept, kept_before, edge_low, edge_high, *norms, col_even, col_odd,

time: 41.5 us -> 41.2 us (level)
  no operation moved by 1% of the time
where the time goes in v14:
time: 41.2 us; the launch traced here: 41.1 us
  Pallas kernels  21.5 us (52%)
  starting transfers between devices  14.9 us (36%)
  waiting for transfers between devices  3.49 us (8%)
  between operations  1.01 us (2%)
    pallas_call x14, Pallas kernels, call(): pl.pallas_call(kernel, out_shape=shapes, in_specs=[pl.BlockSpec(memory_sp...  21.5 us
    ppermute x12, starting transfers between devices, exchange(): results.append(lax.ppermute(value, names, pairs))  14.9 us
    ppermute x12, waiting for transfers between devices, exchange(): results.append(lax.ppermute(value, names, pairs))  3.49 us
  transfers between devices with their start and end apart: 12, of which 3 were waited for; matrix products, arithmetic and copies ran while one was open for 0% of the time, Pallas kernels for 35%

profile of v14, /device:TPU:0, one launch (start us, length us, event | category | flops | bytes accessed | tf_op | source)
XLA Modules:
  0.0 41.1 jit_solution(1730398981596652316)
XLA Ops:
  0.6 0.0 copy-start.5
  0.6 0.0 copy-start.6
  0.7 0.0 copy-start.7
  0.7 0.0 copy-start.10
  0.7 0.0 copy-start.2
  0.7 0.0 copy-start.1
  0.7 0.0 copy-start.4
  0.7 0.0 copy-start.3
  0.7 1.9 %shard_map.140 = (f32[136,128]{1,0:T(8,128)S(1)}, f32[136,128]{1,0:T(8,128)S(1)}, f32[136,128]{1,0:T(8,128)S(1)}, f32[136,128]{1,0:T(8,128)S(1)}, f32[136,128]{1...) custom-call(f32[16,128,128]{2,1,0:T(8,128)} %stress.13, ...), custom_call_target="tpu_custom_call" | custom-call | flops 1500000000 | bytes 1500000 | tf_op jit(solution)/shard_map/pallas_call | solution.py:569
  2.6 0.5 %collective-permute-start.1 = (f32[128,128]{1,0:T(8,128)S(1)}, f32[128,128]{1,0:T(8,128)S(1)}, u32[]{:S(2)}, u32[]{:S(2)}) collective-permute-start(f32[128,128]{1,0:T(8,128)S(1)} %slice.55), channel_id=1, source_target_pairs={{0,1},{1,0},{2,3},{3,2},{4,8},{5,9},{6,10},{7,11},{8,4},{9,5},{10,... | collective-permute-start | bytes 196616 | tf_op jit(solution)/shard_map/ppermute | solution.py:599
  3.2 4.0 %collective-permute-start = (f32[128,128]{1,0:T(8,128)S(1)}, f32[128,128]{1,0:T(8,128)S(1)}, u32[]{:S(2)}, u32[]{:S(2)}) collective-permute-start(f32[128,128]{1,0:T(8,128)S(1)} %slice.54), channel_id=1, source_target_pairs={{0,4},{1,5},{2,6},{3,7},{4,0},{5,1},{6,2},{7,3},{8,12},{9,13},{10,... | collective-permute-start | bytes 196616 | tf_op jit(solution)/shard_map/ppermute | solution.py:599
  7.2 0.0 copy-done.5
  7.2 0.0 copy-done.6
  7.2 0.0 copy-done.7
  7.2 0.0 copy-done.10
  7.2 0.0 copy-done.2
  7.2 0.0 copy-done.1
  7.2 0.0 copy-done.4
  7.2 0.0 copy-done.3
  7.3 2.9 %shard_map.139 = (f32[16,136,128]{2,1,0:T(8,128)S(1)}, f32[136,256]{1,0:T(8,128)S(1)}, f32[136,256]{1,0:T(8,128)S(1)}, f32[16,128,128]{2,1,0:T(8,128)S(1)}, f32[16,128,128]{2,1,0:T(8,128)S(1)}) custom-call(f32[16,128,128]{2,1,0:T(8,128)S(1)} %copy-done.1, f32[16,128,128]{2,1,0:T(8,128)S(1)} %copy-done.2, s32[16,128,128]{2,1,0:T(8,128)S(1)} %copy-done.3, ...), custom_call_target="tpu_custom_call" | custom-call | flops 4499999744 | bytes 4500000 | tf_op jit(solution)/shard_map/pallas_call | solution.py:569
  10.2 0.0 copy-start
  10.2 0.0 copy-start.11
  10.2 0.0 collective-permute-done.1.row_odd
  10.2 0.0 collective-permute-done.row_even
  10.2 0.4 shard_map.141
  10.6 1.6 %collective-permute-start.3 = (f32[128,128]{1,0:T(8,128)S(1)}, f32[128,128]{1,0:T(8,128)S(1)}, u32[]{:S(2)}, u32[]{:S(2)}) collective-permute-start(f32[128,128]{1,0:T(8,128)S(1)} %slice.57), channel_id=1, source_target_pairs={{0,4},{4,0},{8,12},{12,8},{16,20},{20,16},{24,28},{28,24},{1,2},{5... | collective-permute-start | bytes 196616 | tf_op jit(solution)/shard_map/ppermute | solution.py:599
  12.2 0.1 collective-permute-start.2
  12.3 0.0 copy-done
  12.3 0.0 copy-done.11
  12.3 1.2 %shard_map.142 = (f32[16,128,128]{2,1,0:T(8,128)S(1)}, f32[16,8,128]{2,1,0:T(8,128)S(1)}, f32[136,128]{1,0:T(8,128)S(1)}, f32[136,128]{1,0:T(8,128)S(1)}) custom-call(f32[16,136,128]{2,1,0:T(8,128)S(1)} %get-tuple-element.50.across, f32[128,128]{1,0:T(8,128)S(1)} %collective-permute-done.row_even, f32[128,128]{1,0:T(8,128)S(1)} %collective-permute-done.1.row_odd, ...), custom_call_target="tpu_custom_call" | custom-call | flops 1800000000 | bytes 1800000 | tf_op jit(solution)/shard_map/pallas_call | solution.py:569
  13.5 0.0 copy-start.8
  13.5 0.0 copy-start.9
  13.6 1.1 %shard_map.143.fixed = f32[136,128]{1,0:T(8,128)S(1)} custom-call(f32[16,128,128]{2,1,0:T(8,128)S(1)} %copy-done.1, f32[16,128,128]{2,1,0:T(8,128)S(1)} %copy-done.2, f32[16,128,128]{2,1,0:T(8,128)S(1)} %copy-done, f32[184,128]{1,0:T(8,128)S(1)} %get-tuple-element.66._), custom_call_target="tpu_custom_call" | custom-call | flops 800000000 | bytes 800000 | tf_op jit(solution)/shard_map/pallas_call | solution.py:569
  14.7 0.3 collective-permute-done.3.col_odd
  14.9 0.0 collective-permute-done.2.col_even
  14.9 0.0 copy-done.8
  14.9 0.0 copy-done.9
  14.9 0.6 %shard_map.145 = (f32[176,128]{1,0:T(8,128)S(1)}, f32[176,128]{1,0:T(8,128)S(1)}) custom-call(f32[16,128,128]{2,1,0:T(8,128)S(1)} %copy-done.1, f32[16,128,128]{2,1,0:T(8,128)S(1)} %copy-done.2, s32[16,128,128]{2,1,0:T(8,128)S(1)} %copy-done.3, s32[16,128,128]{2,1,0:T(8,128)S(1)} %copy-done.4, f32[16,128,128]{2,1,0:T(8,128)S(1)} %copy-done, ...), custom_call_target="tpu_custom_call" | custom-call | flops 800000000 | bytes 800000 | tf_op jit(solution)/shard_map/pallas_call | solution.py:569
  15.6 0.3 collective-permute-start.5
  15.8 2.9 %collective-permute-start.4 = (f32[128,128]{1,0:T(8,128)S(1)}, f32[128,128]{1,0:T(8,128)S(1)}, u32[]{:S(2)}, u32[]{:S(2)}) collective-permute-start(f32[128,128]{1,0:T(8,128)S(1)} %slice.58), channel_id=1, source_target_pairs={{0,4},{1,5},{2,6},{3,7},{4,0},{5,1},{6,2},{7,3},{8,12},{9,13},{10,... | collective-permute-start | bytes 196616 | tf_op jit(solution)/shard_map/ppermute | solution.py:599
  18.8 3.4 %shard_map.144 = (f32[16,136,128]{2,1,0:T(8,128)S(1)}, f32[136,256]{1,0:T(8,128)S(1)}, f32[136,256]{1,0:T(8,128)S(1)}, f32[16,128,128]{2,1,0:T(8,128)S(1)}) custom-call(f32[16,128,128]{2,1,0:T(8,128)S(1)} %copy-done.1, f32[16,128,128]{2,1,0:T(8,128)S(1)} %copy-done.2, s32[16,128,128]{2,1,0:T(8,128)S(1)} %copy-done.3, s32[16,128,128]{2,1,0:T(8,128)S(1)} %copy-done.4, ...), custom_call_target="tpu_custom_call" | custom-call | flops 4499999744 | bytes 4500000 | tf_op jit(solution)/shard_map/pallas_call | solution.py:569
  22.1 0.0 collective-permute-done.5.row_odd
  22.2 0.0 collective-permute-done.4.row_even
  22.2 0.4 shard_map.146
  22.6 1.2 %collective-permute-start.7 = (f32[128,128]{1,0:T(8,128)S(1)}, f32[128,128]{1,0:T(8,128)S(1)}, u32[]{:S(2)}, u32[]{:S(2)}) collective-permute-start(f32[128,128]{1,0:T(8,128)S(1)} %slice.61), channel_id=1, source_target_pairs={{0,4},{4,0},{8,12},{12,8},{16,20},{20,16},{24,28},{28,24},{1,2},{5... | collective-permute-start | bytes 196616 | tf_op jit(solution)/shard_map/ppermute | solution.py:599
  23.8 0.0 collective-permute-start.6
  23.8 1.2 %shard_map.147 = (f32[16,128,128]{2,1,0:T(8,128)S(1)}, f32[16,8,128]{2,1,0:T(8,128)S(1)}, f32[136,128]{1,0:T(8,128)S(1)}, f32[136,128]{1,0:T(8,128)S(1)}) custom-call(f32[16,136,128]{2,1,0:T(8,128)S(1)} %get-tuple-element.67.across, f32[128,128]{1,0:T(8,128)S(1)} %collective-permute-done.4.row_even, f32[128,128]{1,0:T(8,128)S(1)} %collective-permute-done.5.row_odd, ...), custom_call_target="tpu_custom_call" | custom-call | flops 1800000000 | bytes 1800000 | tf_op jit(solution)/shard_map/pallas_call | solution.py:569
  25.0 1.9 %collective-permute-done.7.col_odd = f32[128,128]{1,0:T(8,128)S(1)} collective-permute-done((f32[128,128]{1,0:T(8,128)S(1)}, f32[128,128]{1,0:T(8,128)S(1)}, u32[]{:S(2)}, u32[]{:S(2)}) %collective-permute-start.7) | collective-permute-done | bytes 65568 | tf_op jit(solution)/shard_map/ppermute | solution.py:599
  26.9 0.0 collective-permute-done.6.col_even
  26.9 0.6 %shard_map.149 = (f32[176,128]{1,0:T(8,128)S(1)}, f32[176,128]{1,0:T(8,128)S(1)}) custom-call(f32[16,128,128]{2,1,0:T(8,128)S(1)} %copy-done.1, f32[16,128,128]{2,1,0:T(8,128)S(1)} %copy-done.2, s32[16,128,128]{2,1,0:T(8,128)S(1)} %copy-done.3, s32[16,128,128]{2,1,0:T(8,128)S(1)} %copy-done.4, f32[16,128,128]{2,1,0:T(8,128)S(1)} %copy-done, ...), custom_call_target="tpu_custom_call" | custom-call | flops 800000000 | bytes 800000 | tf_op jit(solution)/shard_map/pallas_call | solution.py:569
  27.5 1.2 %collective-permute-start.8 = (f32[176,128]{1,0:T(8,128)S(1)}, f32[176,128]{1,0:T(8,128)S(1)}, u32[]{:S(2)}, u32[]{:S(2)}) collective-permute-start(f32[176,128]{1,0:T(8,128)S(1)} %get-tuple-element.83), channel_id=1, source_target_pairs={{0,4},{1,5},{2,6},{3,7},{4,0},{5,1},{6,2},{7,3},{8,12},{9,13},{10,... | collective-permute-start | bytes 270344 | tf_op jit(solution)/shard_map/ppermute | solution.py:599
  28.7 0.0 collective-permute-start.9
  28.7 3.4 %shard_map.148 = (f32[16,136,128]{2,1,0:T(8,128)S(1)}, f32[136,256]{1,0:T(8,128)S(1)}, f32[136,256]{1,0:T(8,128)S(1)}, f32[16,128,128]{2,1,0:T(8,128)S(1)}) custom-call(f32[16,128,128]{2,1,0:T(8,128)S(1)} %copy-done.1, f32[16,128,128]{2,1,0:T(8,128)S(1)} %copy-done.2, s32[16,128,128]{2,1,0:T(8,128)S(1)} %copy-done.3, s32[16,128,128]{2,1,0:T(8,128)S(1)} %copy-done.4, ...), custom_call_target="tpu_custom_call" | custom-call | flops 4499999744 | bytes 4500000 | tf_op jit(solution)/shard_map/pallas_call | solution.py:569
  32.1 0.0 collective-permute-done.8
  32.1 0.0 collective-permute-done.9
  32.1 0.4 shard_map.150
  32.6 3.1 %collective-permute-start.11 = (f32[176,128]{1,0:T(8,128)S(1)}, f32[176,128]{1,0:T(8,128)S(1)}, u32[]{:S(2)}, u32[]{:S(2)}) collective-permute-start(f32[176,128]{1,0:T(8,128)S(1)} %slice.68), channel_id=1, source_target_pairs={{0,4},{4,0},{8,12},{12,8},{16,20},{20,16},{24,28},{28,24},{1,2},{5... | collective-permute-start | bytes 270344 | tf_op jit(solution)/shard_map/ppermute | solution.py:599
  35.7 0.0 collective-permute-start.10
  35.7 1.2 %shard_map.151 = (f32[16,128,128]{2,1,0:T(8,128)S(1)}, f32[16,8,128]{2,1,0:T(8,128)S(1)}, f32[136,128]{1,0:T(8,128)S(1)}, f32[136,128]{1,0:T(8,128)S(1)}) custom-call(f32[16,136,128]{2,1,0:T(8,128)S(1)} %get-tuple-element.81.across, f32[128,128]{1,0:T(8,128)S(1)} %slice.72.row_even, f32[128,128]{1,0:T(8,128)S(1)} %slice.73.row_odd, ...), custom_call_target="tpu_custom_call" | custom-call | flops 1800000000 | bytes 1800000 | tf_op jit(solution)/shard_map/pallas_call | solution.py:569
  36.9 1.3 %collective-permute-done.11 = f32[176,128]{1,0:T(8,128)S(1)} collective-permute-done((f32[176,128]{1,0:T(8,128)S(1)}, f32[176,128]{1,0:T(8,128)S(1)}, u32[]{:S(2)}, u32[]{:S(2)}) %collective-permute-start.11) | collective-permute-done | bytes 90144 | tf_op jit(solution)/shard_map/ppermute | solution.py:599
  38.2 0.0 collective-permute-done.10
  38.2 2.9 %shard_map.152 = (f32[16,128,128]{2,1,0:T(8,128)}, f32[16,128,128]{2,1,0:T(8,128)}, f32[2,16,128,128]{3,2,1,0:T(8,128)}) custom-call(f32[16,128,128]{2,1,0:T(8,128)S(1)} %copy-done.1, f32[16,128,128]{2,1,0:T(8,128)S(1)} %copy-done.2, f32[16,128,128]{2,1,0:T(8,128)S(1)} %get-tuple-element.80._.plastic, f32[16,128,128]{2,1,0:T(8,128)S(1)} %get-tuple-element.88.inner, ...), custom_call_target="tpu_custom_call" | custom-call | flops 3000000000 | bytes 3000000 | tf_op jit(solution)/shard_map/pallas_call | solution.py:569
  (18 shorter events, 0.1 us)
Async XLA Ops:
  0.6 6.6 %copy-start.5 = (f32[128,256]{1,0:T(8,128)S(1)}, f32[128,256]{1,0:T(8,128)}, u32[]{:S(2)}) copy-start(f32[128,256]{1,0:T(8,128)} %constant.19.clone.high_ref) | copy-start | bytes 393220
  0.6 6.6 %copy-start.6 = (f32[128,256]{1,0:T(8,128)S(1)}, f32[128,256]{1,0:T(8,128)}, u32[]{:S(2)}) copy-start(f32[128,256]{1,0:T(8,128)} %constant.18.clone.low_ref) | copy-start | bytes 393220
  0.7 6.6 %copy-start.7 = (f32[128,128]{1,0:T(8,128)S(1)}, f32[128,128]{1,0:T(8,128)}, u32[]{:S(2)}) copy-start(f32[128,128]{1,0:T(8,128)} %constant.20.clone.next_ref) | copy-start | bytes 196612
  0.7 6.5 %copy-start.10 = (f32[136,128]{1,0:T(8,128)S(1)}, f32[136,128]{1,0:T(8,128)}, u32[]{:S(2)}) copy-start(f32[136,128]{1,0:T(8,128)} %constant.16.clone.band_ref) | copy-start | bytes 208900
  0.7 6.5 %copy-start.2 = (f32[16,128,128]{2,1,0:T(8,128)S(1)}, f32[16,128,128]{2,1,0:T(8,128)}, u32[]{:S(2)}) copy-start(f32[16,128,128]{2,1,0:T(8,128)} %strain.13) | copy-start | bytes 3145732
  0.7 6.5 %copy-start.1 = (f32[16,128,128]{2,1,0:T(8,128)S(1)}, f32[16,128,128]{2,1,0:T(8,128)}, u32[]{:S(2)}) copy-start(f32[16,128,128]{2,1,0:T(8,128)} %stress.13) | copy-start | bytes 3145732
  0.7 6.5 %copy-start.4 = (s32[16,128,128]{2,1,0:T(8,128)S(1)}, s32[16,128,128]{2,1,0:T(8,128)}, u32[]{:S(2)}) copy-start(s32[16,128,128]{2,1,0:T(8,128)} %count.9) | copy-start | bytes 3145732
  0.7 6.5 %copy-start.3 = (s32[16,128,128]{2,1,0:T(8,128)S(1)}, s32[16,128,128]{2,1,0:T(8,128)}, u32[]{:S(2)}) copy-start(s32[16,128,128]{2,1,0:T(8,128)} %yields.9) | copy-start | bytes 3145732
  2.6 7.5 %collective-permute-start.1 = (f32[128,128]{1,0:T(8,128)S(1)}, f32[128,128]{1,0:T(8,128)S(1)}, u32[]{:S(2)}, u32[]{:S(2)}) collective-permute-start(f32[128,128]{1,0:T(8,128)S(1)} %slice.55), channel_id=1, source_target_pairs={{0,1},{1,0},{2,3},{3,2},{4,8},{5,9},{6,10},{7,11},{8,4},{9,5},{10,... | collective-permute-start | bytes 196616 | tf_op jit(solution)/shard_map/ppermute | solution.py:599
  3.2 7.0 %collective-permute-start = (f32[128,128]{1,0:T(8,128)S(1)}, f32[128,128]{1,0:T(8,128)S(1)}, u32[]{:S(2)}, u32[]{:S(2)}) collective-permute-start(f32[128,128]{1,0:T(8,128)S(1)} %slice.54), channel_id=1, source_target_pairs={{0,4},{1,5},{2,6},{3,7},{4,0},{5,1},{6,2},{7,3},{8,12},{9,13},{10,... | collective-permute-start | bytes 196616 | tf_op jit(solution)/shard_map/ppermute | solution.py:599
  10.2 2.1 %copy-start = (f32[16,128,128]{2,1,0:T(8,128)S(1)}, f32[16,128,128]{2,1,0:T(8,128)}, u32[]{:S(2)}) copy-start(f32[16,128,128]{2,1,0:T(8,128)} %threshold.11) | copy-start | bytes 3145732
  10.2 2.1 %copy-start.11 = (f32[128,128]{1,0:T(8,128)S(1)}, f32[128,128]{1,0:T(8,128)}, u32[]{:S(2)}) copy-start(f32[128,128]{1,0:T(8,128)} %constant.17.clone.band_ref) | copy-start | bytes 196612
  10.6 4.3 %collective-permute-start.3 = (f32[128,128]{1,0:T(8,128)S(1)}, f32[128,128]{1,0:T(8,128)S(1)}, u32[]{:S(2)}, u32[]{:S(2)}) collective-permute-start(f32[128,128]{1,0:T(8,128)S(1)} %slice.57), channel_id=1, source_target_pairs={{0,4},{4,0},{8,12},{12,8},{16,20},{20,16},{24,28},{28,24},{1,2},{5... | collective-permute-start | bytes 196616 | tf_op jit(solution)/shard_map/ppermute | solution.py:599
  12.2 2.7 %collective-permute-start.2 = (f32[128,128]{1,0:T(8,128)S(1)}, f32[128,128]{1,0:T(8,128)S(1)}, u32[]{:S(2)}, u32[]{:S(2)}) collective-permute-start(f32[128,128]{1,0:T(8,128)S(1)} %slice.56), channel_id=1, source_target_pairs={{0,1},{4,5},{8,9},{12,13},{16,17},{20,21},{24,25},{28,29},{1,0},{5... | collective-permute-start | bytes 196616 | tf_op jit(solution)/shard_map/ppermute | solution.py:599
  13.5 1.4 %copy-start.8 = (f32[144,128]{1,0:T(8,128)S(1)}, f32[144,128]{1,0:T(8,128)}, u32[]{:S(2)}) copy-start(f32[144,128]{1,0:T(8,128)} %constant.15.clone.above) | copy-start | bytes 221188
  13.5 1.4 %copy-start.9 = (f32[128,128]{1,0:T(8,128)S(1)}, f32[128,128]{1,0:T(8,128)}, u32[]{:S(2)}) copy-start(f32[128,128]{1,0:T(8,128)} %constant.14.clone.below) | copy-start | bytes 196612
  15.6 6.6 %collective-permute-start.5 = (f32[128,128]{1,0:T(8,128)S(1)}, f32[128,128]{1,0:T(8,128)S(1)}, u32[]{:S(2)}, u32[]{:S(2)}) collective-permute-start(f32[128,128]{1,0:T(8,128)S(1)} %slice.59), channel_id=1, source_target_pairs={{0,1},{1,0},{2,3},{3,2},{4,8},{5,9},{6,10},{7,11},{8,4},{9,5},{10,... | collective-permute-start | bytes 196616 | tf_op jit(solution)/shard_map/ppermute | solution.py:599
  15.8 6.3 %collective-permute-start.4 = (f32[128,128]{1,0:T(8,128)S(1)}, f32[128,128]{1,0:T(8,128)S(1)}, u32[]{:S(2)}, u32[]{:S(2)}) collective-permute-start(f32[128,128]{1,0:T(8,128)S(1)} %slice.58), channel_id=1, source_target_pairs={{0,4},{1,5},{2,6},{3,7},{4,0},{5,1},{6,2},{7,3},{8,12},{9,13},{10,... | collective-permute-start | bytes 196616 | tf_op jit(solution)/shard_map/ppermute | solution.py:599
  22.6 4.3 %collective-permute-start.7 = (f32[128,128]{1,0:T(8,128)S(1)}, f32[128,128]{1,0:T(8,128)S(1)}, u32[]{:S(2)}, u32[]{:S(2)}) collective-permute-start(f32[128,128]{1,0:T(8,128)S(1)} %slice.61), channel_id=1, source_target_pairs={{0,4},{4,0},{8,12},{12,8},{16,20},{20,16},{24,28},{28,24},{1,2},{5... | collective-permute-start | bytes 196616 | tf_op jit(solution)/shard_map/ppermute | solution.py:599
  23.8 3.1 %collective-permute-start.6 = (f32[128,128]{1,0:T(8,128)S(1)}, f32[128,128]{1,0:T(8,128)S(1)}, u32[]{:S(2)}, u32[]{:S(2)}) collective-permute-start(f32[128,128]{1,0:T(8,128)S(1)} %slice.60), channel_id=1, source_target_pairs={{0,1},{4,5},{8,9},{12,13},{16,17},{20,21},{24,25},{28,29},{1,0},{5... | collective-permute-start | bytes 196616 | tf_op jit(solution)/shard_map/ppermute | solution.py:599
  27.5 4.6 %collective-permute-start.8 = (f32[176,128]{1,0:T(8,128)S(1)}, f32[176,128]{1,0:T(8,128)S(1)}, u32[]{:S(2)}, u32[]{:S(2)}) collective-permute-start(f32[176,128]{1,0:T(8,128)S(1)} %get-tuple-element.83), channel_id=1, source_target_pairs={{0,4},{1,5},{2,6},{3,7},{4,0},{5,1},{6,2},{7,3},{8,12},{9,13},{10,... | collective-permute-start | bytes 270344 | tf_op jit(solution)/shard_map/ppermute | solution.py:599
  28.7 3.4 %collective-permute-start.9 = (f32[176,128]{1,0:T(8,128)S(1)}, f32[176,128]{1,0:T(8,128)S(1)}, u32[]{:S(2)}, u32[]{:S(2)}) collective-permute-start(f32[176,128]{1,0:T(8,128)S(1)} %get-tuple-element.84), channel_id=1, source_target_pairs={{0,1},{1,0},{2,3},{3,2},{4,8},{5,9},{6,10},{7,11},{8,4},{9,5},{10,... | collective-permute-start | bytes 270344 | tf_op jit(solution)/shard_map/ppermute | solution.py:599
  32.6 5.6 %collective-permute-start.11 = (f32[176,128]{1,0:T(8,128)S(1)}, f32[176,128]{1,0:T(8,128)S(1)}, u32[]{:S(2)}, u32[]{:S(2)}) collective-permute-start(f32[176,128]{1,0:T(8,128)S(1)} %slice.68), channel_id=1, source_target_pairs={{0,4},{4,0},{8,12},{12,8},{16,20},{20,16},{24,28},{28,24},{1,2},{5... | collective-permute-start | bytes 270344 | tf_op jit(solution)/shard_map/ppermute | solution.py:599
  35.7 2.5 %collective-permute-start.10 = (f32[176,128]{1,0:T(8,128)S(1)}, f32[176,128]{1,0:T(8,128)S(1)}, u32[]{:S(2)}, u32[]{:S(2)}) collective-permute-start(f32[176,128]{1,0:T(8,128)S(1)} %slice.66), channel_id=1, source_target_pairs={{0,1},{4,5},{8,9},{12,13},{16,17},{20,21},{24,25},{28,29},{1,0},{5... | collective-permute-start | bytes 270344 | tf_op jit(solution)/shard_map/ppermute | solution.py:599

commit v15 on v14

--- a/solution.py
+++ b/solution.py
@@ -188,8 +188,7 @@
                 stress[at], strain[at], yields[at], count[at], jnp.ones((REACH, cols), jnp.float32),
                 first_factor(strain[at]),
             )
-        product = left_product(left_constant(matrix), block[...])
-        sent.append(jnp.concatenate([product, product[:REACH]], axis=0))
+        sent.append(left_product(left_constant(matrix), block[...]))
     send("gx", *sent, even_ref, odd_ref)
 
 
@@ -653,7 +652,7 @@
     threshold = damage_threshold
     edge = [pltpu.VMEM((layers, 2 * REACH, cols), value.dtype) for value in inputs]
     row_even, row_odd, norm, norm_low, norm_high, norm_last, norm_before, rest = call(
-        first_edge_kernel, [(strip + REACH, cols)] * 2 + [packed] * 5 + [spare],
+        first_edge_kernel, [(strip, cols)] * 2 + [packed] * 5 + [spare],
         edge + [(strip, cols), pltpu.SemaphoreType.DMA((2, 4))], 1500,
         inputs, [pltpu.HBM] * 4, limit=EDGE_VMEM_BYTES,
     )

time: 41.2 us -> 41.6 us (level)
  transfers between devices with their start and end apart: 12 -> 12, of which waited for: 3 -> 4; matrix products, arithmetic and copies ran while one was open for 0% -> 0% of each run, Pallas kernels for 35% -> 35%
where the time goes in v15:
time: 41.6 us; the launch traced here: 41.4 us
  Pallas kernels  21.4 us (51%)
  starting transfers between devices  15.1 us (36%)
  waiting for transfers between devices  3.67 us (9%)
  between operations  1.02 us (2%)
    pallas_call x14, Pallas kernels, call(): pl.pallas_call(kernel, out_shape=shapes, in_specs=[pl.BlockSpec(memory_sp...  21.4 us
    ppermute x12, starting transfers between devices, exchange(): results.append(lax.ppermute(value, names, pairs))  15.1 us
    ppermute x12, waiting for transfers between devices, exchange(): results.append(lax.ppermute(value, names, pairs))  3.67 us
  transfers between devices with their start and end apart: 12, of which 4 were waited for; matrix products, arithmetic and copies ran while one was open for 0% of the time, Pallas kernels for 35%

profile of v15, /device:TPU:0, one launch (start us, length us, event | category | flops | bytes accessed | tf_op | source)
XLA Modules:
  0.0 41.4 jit_solution(3921156594992416822)
XLA Ops:
  0.6 0.0 copy-start.5
  0.6 0.0 copy-start.6
  0.7 0.0 copy-start.7
  0.7 0.0 copy-start.10
  0.7 0.0 copy-start.2
  0.7 0.0 copy-start.1
  0.7 0.0 copy-start.4
  0.7 0.0 copy-start.3
  0.7 1.9 %shard_map.140 = (f32[128,128]{1,0:T(8,128)S(1)}, f32[128,128]{1,0:T(8,128)S(1)}, f32[136,128]{1,0:T(8,128)S(1)}, f32[136,128]{1,0:T(8,128)S(1)}, f32[136,128]{1...) custom-call(f32[16,128,128]{2,1,0:T(8,128)} %stress.13, ...), custom_call_target="tpu_custom_call" | custom-call | flops 1500000000 | bytes 1500000 | tf_op jit(solution)/shard_map/pallas_call | solution.py:568
  2.6 3.0 %collective-permute-start = (f32[128,128]{1,0:T(8,128)S(1)}, f32[128,128]{1,0:T(8,128)S(1)}, u32[]{:S(2)}, u32[]{:S(2)}) collective-permute-start(f32[128,128]{1,0:T(8,128)S(1)} %get-tuple-element.51), channel_id=1, source_target_pairs={{0,4},{1,5},{2,6},{3,7},{4,0},{5,1},{6,2},{7,3},{8,12},{9,13},{10,... | collective-permute-start | bytes 196616 | tf_op jit(solution)/shard_map/ppermute | solution.py:598
  5.6 0.0 collective-permute-start.1
  5.6 0.0 copy-done.5
  5.6 0.0 copy-done.6
  5.6 0.0 copy-done.7
  5.6 0.0 copy-done.10
  5.7 0.0 copy-done.2
  5.7 0.0 copy-done.1
  5.7 0.0 copy-done.4
  5.7 0.0 copy-done.3
  5.7 2.9 %shard_map.139 = (f32[16,136,128]{2,1,0:T(8,128)S(1)}, f32[136,256]{1,0:T(8,128)S(1)}, f32[136,256]{1,0:T(8,128)S(1)}, f32[16,128,128]{2,1,0:T(8,128)S(1)}, f32[16,128,128]{2,1,0:T(8,128)S(1)}) custom-call(f32[16,128,128]{2,1,0:T(8,128)S(1)} %copy-done.1, f32[16,128,128]{2,1,0:T(8,128)S(1)} %copy-done.2, s32[16,128,128]{2,1,0:T(8,128)S(1)} %copy-done.3, ...), custom_call_target="tpu_custom_call" | custom-call | flops 4499999744 | bytes 4500000 | tf_op jit(solution)/shard_map/pallas_call | solution.py:568
  8.6 0.0 copy-start
  8.6 0.0 copy-start.11
  8.6 0.1 collective-permute-done.row_even
  8.7 0.0 collective-permute-done.1.row_odd
  8.7 0.4 shard_map.141
  9.1 3.0 %collective-permute-start.3 = (f32[128,128]{1,0:T(8,128)S(1)}, f32[128,128]{1,0:T(8,128)S(1)}, u32[]{:S(2)}, u32[]{:S(2)}) collective-permute-start(f32[128,128]{1,0:T(8,128)S(1)} %slice.49), channel_id=1, source_target_pairs={{0,4},{4,0},{8,12},{12,8},{16,20},{20,16},{24,28},{28,24},{1,2},{5... | collective-permute-start | bytes 196616 | tf_op jit(solution)/shard_map/ppermute | solution.py:598
  12.1 0.0 collective-permute-start.2
  12.1 0.0 copy-done
  12.2 0.0 copy-done.11
  12.2 1.2 %shard_map.142 = (f32[16,128,128]{2,1,0:T(8,128)S(1)}, f32[16,8,128]{2,1,0:T(8,128)S(1)}, f32[136,128]{1,0:T(8,128)S(1)}, f32[136,128]{1,0:T(8,128)S(1)}) custom-call(f32[16,136,128]{2,1,0:T(8,128)S(1)} %get-tuple-element.50.across, f32[128,128]{1,0:T(8,128)S(1)} %collective-permute-done.row_even, f32[128,128]{1,0:T(8,128)S(1)} %collective-permute-done.1.row_odd, ...), custom_call_target="tpu_custom_call" | custom-call | flops 1800000000 | bytes 1800000 | tf_op jit(solution)/shard_map/pallas_call | solution.py:568
  13.4 0.0 copy-start.8
  13.4 0.0 copy-start.9
  13.4 1.1 %shard_map.143.fixed = f32[136,128]{1,0:T(8,128)S(1)} custom-call(f32[16,128,128]{2,1,0:T(8,128)S(1)} %copy-done.1, f32[16,128,128]{2,1,0:T(8,128)S(1)} %copy-done.2, f32[16,128,128]{2,1,0:T(8,128)S(1)} %copy-done, f32[184,128]{1,0:T(8,128)S(1)} %get-tuple-element.66._), custom_call_target="tpu_custom_call" | custom-call | flops 800000000 | bytes 800000 | tf_op jit(solution)/shard_map/pallas_call | solution.py:568
  14.5 0.0 collective-permute-done.3.col_odd
  14.5 0.0 collective-permute-done.2.col_even
  14.5 0.0 copy-done.8
  14.6 0.0 copy-done.9
  14.6 0.6 %shard_map.145 = (f32[176,128]{1,0:T(8,128)S(1)}, f32[176,128]{1,0:T(8,128)S(1)}) custom-call(f32[16,128,128]{2,1,0:T(8,128)S(1)} %copy-done.1, f32[16,128,128]{2,1,0:T(8,128)S(1)} %copy-done.2, s32[16,128,128]{2,1,0:T(8,128)S(1)} %copy-done.3, s32[16,128,128]{2,1,0:T(8,128)S(1)} %copy-done.4, f32[16,128,128]{2,1,0:T(8,128)S(1)} %copy-done, ...), custom_call_target="tpu_custom_call" | custom-call | flops 800000000 | bytes 800000 | tf_op jit(solution)/shard_map/pallas_call | solution.py:568
  15.2 0.6 %collective-permute-start.5 = (f32[128,128]{1,0:T(8,128)S(1)}, f32[128,128]{1,0:T(8,128)S(1)}, u32[]{:S(2)}, u32[]{:S(2)}) collective-permute-start(f32[128,128]{1,0:T(8,128)S(1)} %slice.51), channel_id=1, source_target_pairs={{0,1},{1,0},{2,3},{3,2},{4,8},{5,9},{6,10},{7,11},{8,4},{9,5},{10,... | collective-permute-start | bytes 196616 | tf_op jit(solution)/shard_map/ppermute | solution.py:598
  15.7 3.5 %collective-permute-start.4 = (f32[128,128]{1,0:T(8,128)S(1)}, f32[128,128]{1,0:T(8,128)S(1)}, u32[]{:S(2)}, u32[]{:S(2)}) collective-permute-start(f32[128,128]{1,0:T(8,128)S(1)} %slice.50), channel_id=1, source_target_pairs={{0,4},{1,5},{2,6},{3,7},{4,0},{5,1},{6,2},{7,3},{8,12},{9,13},{10,... | collective-permute-start | bytes 196616 | tf_op jit(solution)/shard_map/ppermute | solution.py:598
  19.3 3.3 %shard_map.144 = (f32[16,136,128]{2,1,0:T(8,128)S(1)}, f32[136,256]{1,0:T(8,128)S(1)}, f32[136,256]{1,0:T(8,128)S(1)}, f32[16,128,128]{2,1,0:T(8,128)S(1)}) custom-call(f32[16,128,128]{2,1,0:T(8,128)S(1)} %copy-done.1, f32[16,128,128]{2,1,0:T(8,128)S(1)} %copy-done.2, s32[16,128,128]{2,1,0:T(8,128)S(1)} %copy-done.3, s32[16,128,128]{2,1,0:T(8,128)S(1)} %copy-done.4, ...), custom_call_target="tpu_custom_call" | custom-call | flops 4499999744 | bytes 4500000 | tf_op jit(solution)/shard_map/pallas_call | solution.py:568
  22.6 0.0 collective-permute-done.5.row_odd
  22.6 0.0 collective-permute-done.4.row_even
  22.6 0.4 shard_map.146
  23.0 1.0 %collective-permute-start.7 = (f32[128,128]{1,0:T(8,128)S(1)}, f32[128,128]{1,0:T(8,128)S(1)}, u32[]{:S(2)}, u32[]{:S(2)}) collective-permute-start(f32[128,128]{1,0:T(8,128)S(1)} %slice.53), channel_id=1, source_target_pairs={{0,4},{4,0},{8,12},{12,8},{16,20},{20,16},{24,28},{28,24},{1,2},{5... | collective-permute-start | bytes 196616 | tf_op jit(solution)/shard_map/ppermute | solution.py:598
  24.0 0.2 collective-permute-start.6
  24.2 1.2 %shard_map.147 = (f32[16,128,128]{2,1,0:T(8,128)S(1)}, f32[16,8,128]{2,1,0:T(8,128)S(1)}, f32[136,128]{1,0:T(8,128)S(1)}, f32[136,128]{1,0:T(8,128)S(1)}) custom-call(f32[16,136,128]{2,1,0:T(8,128)S(1)} %get-tuple-element.67.across, f32[128,128]{1,0:T(8,128)S(1)} %collective-permute-done.4.row_even, f32[128,128]{1,0:T(8,128)S(1)} %collective-permute-done.5.row_odd, ...), custom_call_target="tpu_custom_call" | custom-call | flops 1800000000 | bytes 1800000 | tf_op jit(solution)/shard_map/pallas_call | solution.py:568
  25.4 2.0 %collective-permute-done.7.col_odd = f32[128,128]{1,0:T(8,128)S(1)} collective-permute-done((f32[128,128]{1,0:T(8,128)S(1)}, f32[128,128]{1,0:T(8,128)S(1)}, u32[]{:S(2)}, u32[]{:S(2)}) %collective-permute-start.7) | collective-permute-done | bytes 65568 | tf_op jit(solution)/shard_map/ppermute | solution.py:598
  27.4 0.0 collective-permute-done.6.col_even
  27.4 0.6 %shard_map.149 = (f32[176,128]{1,0:T(8,128)S(1)}, f32[176,128]{1,0:T(8,128)S(1)}) custom-call(f32[16,128,128]{2,1,0:T(8,128)S(1)} %copy-done.1, f32[16,128,128]{2,1,0:T(8,128)S(1)} %copy-done.2, s32[16,128,128]{2,1,0:T(8,128)S(1)} %copy-done.3, s32[16,128,128]{2,1,0:T(8,128)S(1)} %copy-done.4, f32[16,128,128]{2,1,0:T(8,128)S(1)} %copy-done, ...), custom_call_target="tpu_custom_call" | custom-call | flops 800000000 | bytes 800000 | tf_op jit(solution)/shard_map/pallas_call | solution.py:568
  28.0 1.0 %collective-permute-start.8 = (f32[176,128]{1,0:T(8,128)S(1)}, f32[176,128]{1,0:T(8,128)S(1)}, u32[]{:S(2)}, u32[]{:S(2)}) collective-permute-start(f32[176,128]{1,0:T(8,128)S(1)} %get-tuple-element.83), channel_id=1, source_target_pairs={{0,4},{1,5},{2,6},{3,7},{4,0},{5,1},{6,2},{7,3},{8,12},{9,13},{10,... | collective-permute-start | bytes 270344 | tf_op jit(solution)/shard_map/ppermute | solution.py:598
  28.9 0.0 collective-permute-start.9
  28.9 3.3 %shard_map.148 = (f32[16,136,128]{2,1,0:T(8,128)S(1)}, f32[136,256]{1,0:T(8,128)S(1)}, f32[136,256]{1,0:T(8,128)S(1)}, f32[16,128,128]{2,1,0:T(8,128)S(1)}) custom-call(f32[16,128,128]{2,1,0:T(8,128)S(1)} %copy-done.1, f32[16,128,128]{2,1,0:T(8,128)S(1)} %copy-done.2, s32[16,128,128]{2,1,0:T(8,128)S(1)} %copy-done.3, s32[16,128,128]{2,1,0:T(8,128)S(1)} %copy-done.4, ...), custom_call_target="tpu_custom_call" | custom-call | flops 4499999744 | bytes 4500000 | tf_op jit(solution)/shard_map/pallas_call | solution.py:568
  32.3 0.3 collective-permute-done.8
  32.6 0.0 collective-permute-done.9
  32.6 0.4 shard_map.150
  33.0 3.0 %collective-permute-start.11 = (f32[176,128]{1,0:T(8,128)S(1)}, f32[176,128]{1,0:T(8,128)S(1)}, u32[]{:S(2)}, u32[]{:S(2)}) collective-permute-start(f32[176,128]{1,0:T(8,128)S(1)} %slice.60), channel_id=1, source_target_pairs={{0,4},{4,0},{8,12},{12,8},{16,20},{20,16},{24,28},{28,24},{1,2},{5... | collective-permute-start | bytes 270344 | tf_op jit(solution)/shard_map/ppermute | solution.py:598
  36.0 0.0 collective-permute-start.10
  36.0 1.2 %shard_map.151 = (f32[16,128,128]{2,1,0:T(8,128)S(1)}, f32[16,8,128]{2,1,0:T(8,128)S(1)}, f32[136,128]{1,0:T(8,128)S(1)}, f32[136,128]{1,0:T(8,128)S(1)}) custom-call(f32[16,136,128]{2,1,0:T(8,128)S(1)} %get-tuple-element.81.across, f32[128,128]{1,0:T(8,128)S(1)} %slice.64.row_even, f32[128,128]{1,0:T(8,128)S(1)} %slice.65.row_odd, ...), custom_call_target="tpu_custom_call" | custom-call | flops 1800000000 | bytes 1800000 | tf_op jit(solution)/shard_map/pallas_call | solution.py:568
  37.2 1.3 %collective-permute-done.11 = f32[176,128]{1,0:T(8,128)S(1)} collective-permute-done((f32[176,128]{1,0:T(8,128)S(1)}, f32[176,128]{1,0:T(8,128)S(1)}, u32[]{:S(2)}, u32[]{:S(2)}) %collective-permute-start.11) | collective-permute-done | bytes 90144 | tf_op jit(solution)/shard_map/ppermute | solution.py:598
  38.5 0.0 collective-permute-done.10
  38.5 2.9 %shard_map.152 = (f32[16,128,128]{2,1,0:T(8,128)}, f32[16,128,128]{2,1,0:T(8,128)}, f32[2,16,128,128]{3,2,1,0:T(8,128)}) custom-call(f32[16,128,128]{2,1,0:T(8,128)S(1)} %copy-done.1, f32[16,128,128]{2,1,0:T(8,128)S(1)} %copy-done.2, f32[16,128,128]{2,1,0:T(8,128)S(1)} %get-tuple-element.80._.plastic, f32[16,128,128]{2,1,0:T(8,128)S(1)} %get-tuple-element.88.inner, ...), custom_call_target="tpu_custom_call" | custom-call | flops 3000000000 | bytes 3000000 | tf_op jit(solution)/shard_map/pallas_call | solution.py:568
  (16 shorter events, 0.1 us)
Async XLA Ops:
  0.6 5.0 %copy-start.5 = (f32[128,256]{1,0:T(8,128)S(1)}, f32[128,256]{1,0:T(8,128)}, u32[]{:S(2)}) copy-start(f32[128,256]{1,0:T(8,128)} %constant.19.clone.high_ref) | copy-start | bytes 393220
  0.6 5.0 %copy-start.6 = (f32[128,256]{1,0:T(8,128)S(1)}, f32[128,256]{1,0:T(8,128)}, u32[]{:S(2)}) copy-start(f32[128,256]{1,0:T(8,128)} %constant.18.clone.low_ref) | copy-start | bytes 393220
  0.7 5.0 %copy-start.7 = (f32[128,128]{1,0:T(8,128)S(1)}, f32[128,128]{1,0:T(8,128)}, u32[]{:S(2)}) copy-start(f32[128,128]{1,0:T(8,128)} %constant.20.clone.next_ref) | copy-start | bytes 196612
  0.7 5.0 %copy-start.10 = (f32[136,128]{1,0:T(8,128)S(1)}, f32[136,128]{1,0:T(8,128)}, u32[]{:S(2)}) copy-start(f32[136,128]{1,0:T(8,128)} %constant.16.clone.band_ref) | copy-start | bytes 208900
  0.7 5.0 %copy-start.2 = (f32[16,128,128]{2,1,0:T(8,128)S(1)}, f32[16,128,128]{2,1,0:T(8,128)}, u32[]{:S(2)}) copy-start(f32[16,128,128]{2,1,0:T(8,128)} %strain.13) | copy-start | bytes 3145732
  0.7 5.0 %copy-start.1 = (f32[16,128,128]{2,1,0:T(8,128)S(1)}, f32[16,128,128]{2,1,0:T(8,128)}, u32[]{:S(2)}) copy-start(f32[16,128,128]{2,1,0:T(8,128)} %stress.13) | copy-start | bytes 3145732
  0.7 5.0 %copy-start.4 = (s32[16,128,128]{2,1,0:T(8,128)S(1)}, s32[16,128,128]{2,1,0:T(8,128)}, u32[]{:S(2)}) copy-start(s32[16,128,128]{2,1,0:T(8,128)} %count.9) | copy-start | bytes 3145732
  0.7 5.0 %copy-start.3 = (s32[16,128,128]{2,1,0:T(8,128)S(1)}, s32[16,128,128]{2,1,0:T(8,128)}, u32[]{:S(2)}) copy-start(s32[16,128,128]{2,1,0:T(8,128)} %yields.9) | copy-start | bytes 3145732
  2.6 6.1 %collective-permute-start = (f32[128,128]{1,0:T(8,128)S(1)}, f32[128,128]{1,0:T(8,128)S(1)}, u32[]{:S(2)}, u32[]{:S(2)}) collective-permute-start(f32[128,128]{1,0:T(8,128)S(1)} %get-tuple-element.51), channel_id=1, source_target_pairs={{0,4},{1,5},{2,6},{3,7},{4,0},{5,1},{6,2},{7,3},{8,12},{9,13},{10,... | collective-permute-start | bytes 196616 | tf_op jit(solution)/shard_map/ppermute | solution.py:598
  5.6 3.1 %collective-permute-start.1 = (f32[128,128]{1,0:T(8,128)S(1)}, f32[128,128]{1,0:T(8,128)S(1)}, u32[]{:S(2)}, u32[]{:S(2)}) collective-permute-start(f32[128,128]{1,0:T(8,128)S(1)} %get-tuple-element.52), channel_id=1, source_target_pairs={{0,1},{1,0},{2,3},{3,2},{4,8},{5,9},{6,10},{7,11},{8,4},{9,5},{10,... | collective-permute-start | bytes 196616 | tf_op jit(solution)/shard_map/ppermute | solution.py:598
  8.6 3.5 %copy-start = (f32[16,128,128]{2,1,0:T(8,128)S(1)}, f32[16,128,128]{2,1,0:T(8,128)}, u32[]{:S(2)}) copy-start(f32[16,128,128]{2,1,0:T(8,128)} %threshold.11) | copy-start | bytes 3145732
  8.6 3.5 %copy-start.11 = (f32[128,128]{1,0:T(8,128)S(1)}, f32[128,128]{1,0:T(8,128)}, u32[]{:S(2)}) copy-start(f32[128,128]{1,0:T(8,128)} %constant.17.clone.band_ref) | copy-start | bytes 196612
  9.1 5.4 %collective-permute-start.3 = (f32[128,128]{1,0:T(8,128)S(1)}, f32[128,128]{1,0:T(8,128)S(1)}, u32[]{:S(2)}, u32[]{:S(2)}) collective-permute-start(f32[128,128]{1,0:T(8,128)S(1)} %slice.49), channel_id=1, source_target_pairs={{0,4},{4,0},{8,12},{12,8},{16,20},{20,16},{24,28},{28,24},{1,2},{5... | collective-permute-start | bytes 196616 | tf_op jit(solution)/shard_map/ppermute | solution.py:598
  12.1 2.4 %collective-permute-start.2 = (f32[128,128]{1,0:T(8,128)S(1)}, f32[128,128]{1,0:T(8,128)S(1)}, u32[]{:S(2)}, u32[]{:S(2)}) collective-permute-start(f32[128,128]{1,0:T(8,128)S(1)} %slice.48), channel_id=1, source_target_pairs={{0,1},{4,5},{8,9},{12,13},{16,17},{20,21},{24,25},{28,29},{1,0},{5... | collective-permute-start | bytes 196616 | tf_op jit(solution)/shard_map/ppermute | solution.py:598
  13.4 1.2 %copy-start.8 = (f32[144,128]{1,0:T(8,128)S(1)}, f32[144,128]{1,0:T(8,128)}, u32[]{:S(2)}) copy-start(f32[144,128]{1,0:T(8,128)} %constant.15.clone.above) | copy-start | bytes 221188
  13.4 1.1 %copy-start.9 = (f32[128,128]{1,0:T(8,128)S(1)}, f32[128,128]{1,0:T(8,128)}, u32[]{:S(2)}) copy-start(f32[128,128]{1,0:T(8,128)} %constant.14.clone.below) | copy-start | bytes 196612
  15.2 7.4 %collective-permute-start.5 = (f32[128,128]{1,0:T(8,128)S(1)}, f32[128,128]{1,0:T(8,128)S(1)}, u32[]{:S(2)}, u32[]{:S(2)}) collective-permute-start(f32[128,128]{1,0:T(8,128)S(1)} %slice.51), channel_id=1, source_target_pairs={{0,1},{1,0},{2,3},{3,2},{4,8},{5,9},{6,10},{7,11},{8,4},{9,5},{10,... | collective-permute-start | bytes 196616 | tf_op jit(solution)/shard_map/ppermute | solution.py:598
  15.7 6.9 %collective-permute-start.4 = (f32[128,128]{1,0:T(8,128)S(1)}, f32[128,128]{1,0:T(8,128)S(1)}, u32[]{:S(2)}, u32[]{:S(2)}) collective-permute-start(f32[128,128]{1,0:T(8,128)S(1)} %slice.50), channel_id=1, source_target_pairs={{0,4},{1,5},{2,6},{3,7},{4,0},{5,1},{6,2},{7,3},{8,12},{9,13},{10,... | collective-permute-start | bytes 196616 | tf_op jit(solution)/shard_map/ppermute | solution.py:598
  23.0 4.3 %collective-permute-start.7 = (f32[128,128]{1,0:T(8,128)S(1)}, f32[128,128]{1,0:T(8,128)S(1)}, u32[]{:S(2)}, u32[]{:S(2)}) collective-permute-start(f32[128,128]{1,0:T(8,128)S(1)} %slice.53), channel_id=1, source_target_pairs={{0,4},{4,0},{8,12},{12,8},{16,20},{20,16},{24,28},{28,24},{1,2},{5... | collective-permute-start | bytes 196616 | tf_op jit(solution)/shard_map/ppermute | solution.py:598
  24.0 3.4 %collective-permute-start.6 = (f32[128,128]{1,0:T(8,128)S(1)}, f32[128,128]{1,0:T(8,128)S(1)}, u32[]{:S(2)}, u32[]{:S(2)}) collective-permute-start(f32[128,128]{1,0:T(8,128)S(1)} %slice.52), channel_id=1, source_target_pairs={{0,1},{4,5},{8,9},{12,13},{16,17},{20,21},{24,25},{28,29},{1,0},{5... | collective-permute-start | bytes 196616 | tf_op jit(solution)/shard_map/ppermute | solution.py:598
  28.0 4.6 %collective-permute-start.8 = (f32[176,128]{1,0:T(8,128)S(1)}, f32[176,128]{1,0:T(8,128)S(1)}, u32[]{:S(2)}, u32[]{:S(2)}) collective-permute-start(f32[176,128]{1,0:T(8,128)S(1)} %get-tuple-element.83), channel_id=1, source_target_pairs={{0,4},{1,5},{2,6},{3,7},{4,0},{5,1},{6,2},{7,3},{8,12},{9,13},{10,... | collective-permute-start | bytes 270344 | tf_op jit(solution)/shard_map/ppermute | solution.py:598
  28.9 3.7 %collective-permute-start.9 = (f32[176,128]{1,0:T(8,128)S(1)}, f32[176,128]{1,0:T(8,128)S(1)}, u32[]{:S(2)}, u32[]{:S(2)}) collective-permute-start(f32[176,128]{1,0:T(8,128)S(1)} %get-tuple-element.84), channel_id=1, source_target_pairs={{0,1},{1,0},{2,3},{3,2},{4,8},{5,9},{6,10},{7,11},{8,4},{9,5},{10,... | collective-permute-start | bytes 270344 | tf_op jit(solution)/shard_map/ppermute | solution.py:598
  33.0 5.5 %collective-permute-start.11 = (f32[176,128]{1,0:T(8,128)S(1)}, f32[176,128]{1,0:T(8,128)S(1)}, u32[]{:S(2)}, u32[]{:S(2)}) collective-permute-start(f32[176,128]{1,0:T(8,128)S(1)} %slice.60), channel_id=1, source_target_pairs={{0,4},{4,0},{8,12},{12,8},{16,20},{20,16},{24,28},{28,24},{1,2},{5... | collective-permute-start | bytes 270344 | tf_op jit(solution)/shard_map/ppermute | solution.py:598
  36.0 2.5 %collective-permute-start.10 = (f32[176,128]{1,0:T(8,128)S(1)}, f32[176,128]{1,0:T(8,128)S(1)}, u32[]{:S(2)}, u32[]{:S(2)}) collective-permute-start(f32[176,128]{1,0:T(8,128)S(1)} %slice.58), channel_id=1, source_target_pairs={{0,1},{4,5},{8,9},{12,13},{16,17},{20,21},{24,25},{28,29},{1,0},{5... | collective-permute-start | bytes 270344 | tf_op jit(solution)/shard_map/ppermute | solution.py:598

commit v16 on v14

--- a/solution.py
+++ b/solution.py
@@ -413,8 +413,10 @@
 
 
 def column_kernel(depth, across, row_even, row_odd, rest_even, rest_odd, threshold, norm, band_ref, _,
-                  kept, kept_before, edge_low, edge_high, deep):
+                  plastic, kept, kept_before, edge_low, edge_high, plastic_out, deep, copy_sem):
     layers, total, cols = across.shape
+    whole = pltpu.make_async_copy(plastic, plastic_out, copy_sem)
+    whole.start()
 
     def depth_sums(part, values):
         for layer, value in enumerate(depth_smooth(values, depth)):
@@ -453,15 +455,14 @@
         moved = pltpu.roll(moved, layer * REACH, 1) if layer else moved
         pltpu.store(edge_low, moved, mask=slots == layer)
         pltpu.store(edge_high, moved, mask=slots == (layer - 1) % (cols // REACH))
+    whole.wait()
 
 
 def final_kernel(stress, strain, plastic, inner, inner_before, edge_low, edge_high, norm_low, norm_high,
                  col_even, col_odd, last_even, last_odd, rest_even, rest_odd, norm_before, own_cols,
-                 plastic_out, damage_out, force_out, columns, lows, highs, damage_s, force_s, half, sums, diffs,
-                 copy_sem, sems):
+                 damage_out, force_out, columns, lows, highs, damage_s, force_s, half, sums, diffs,
+                 sems):
     layers, rows, cols = stress.shape
-    whole = pltpu.make_async_copy(plastic, plastic_out, copy_sem)
-    whole.start()
     from_low, _ = sides("gy", last_even[...], last_odd[...])
     folded = from_low[REACH : REACH + rows // 4]
     pieces = [from_low[REACH + rows // 4 :], folded]
@@ -559,18 +560,18 @@
         return carry
 
     lax.fori_loop(0, layers, drain, 0)
-    whole.wait()
-
-
-def call(kernel, outs, scratch, nanoseconds, operands, spaces=None, outs_space=pltpu.VMEM, limit=VMEM_BYTES):
+
+
+def call(kernel, outs, scratch, nanoseconds, operands, spaces=None, outs_space=None, limit=VMEM_BYTES):
     spaces = spaces or [pltpu.VMEM] * len(operands)
+    outs_space = outs_space or [pltpu.VMEM] * len(outs)
     shapes = [out if isinstance(out, jax.ShapeDtypeStruct) else jax.ShapeDtypeStruct(out, jnp.float32)
               for out in outs]
     return pl.pallas_call(
         kernel,
         out_shape=shapes,
         in_specs=[pl.BlockSpec(memory_space=space) for space in spaces],
-        out_specs=[pl.BlockSpec(memory_space=outs_space)] * len(outs),
+        out_specs=[pl.BlockSpec(memory_space=space) for space in outs_space],
         scratch_shapes=[pltpu.VMEM(s, jnp.float32) if isinstance(s, tuple) else s for s in scratch],
         compiler_params=pltpu.CompilerParams(vmem_limit_bytes=limit),
         cost_estimate=pl.CostEstimate(
@@ -697,19 +698,23 @@
         if last:
             last_even, last_odd = col_even[rows:], col_odd[rows:]
             col_even, col_odd = col_even[:rows], col_odd[:rows]
-        kept, kept_before, edge_low, edge_high = call(
-            functools.partial(column_kernel, depth), [whole, top, packed, packed], [wide], 1800,
-            (across, row_even, row_odd, rest_even, rest_odd, threshold, norm, cols_band, own_cols),
+        kept, kept_before, edge_low, edge_high, plastic_out = call(
+            functools.partial(column_kernel, depth), [whole, top, packed, packed, whole],
+            [wide, pltpu.SemaphoreType.DMA(())], 1800,
+            (across, row_even, row_odd, rest_even, rest_odd, threshold, norm, cols_band, own_cols,
+             plastic),
+            outs_space=[pltpu.VMEM] * 4 + [pltpu.HBM],
         )
-    return tuple(call(
-        final_kernel, [whole, whole, (2, *whole)],
+    damage, force = call(
+        final_kernel, [whole, (2, *whole)],
         [packed] * 3 + [whole, (2, *whole), wide, wide, wide,
-         pltpu.SemaphoreType.DMA(()), pltpu.SemaphoreType.DMA((3, layers))],
+         pltpu.SemaphoreType.DMA((3, layers))],
         3000,
         (stress, strain, plastic, kept, kept_before, edge_low, edge_high, *norms, col_even, col_odd,
          last_even, last_odd, rest_even, rest_odd, norm_before, own_cols),
-        outs_space=pltpu.HBM,
-    ))
+        outs_space=[pltpu.HBM] * 2,
+    )
+    return plastic_out, damage, force
 
 
 def solution(mesh):

time: 41.2 us -> 41.2 us (level)
  no operation moved by 1% of the time
where the time goes in v16:
time: 41.2 us; the launch traced here: 41.1 us
  Pallas kernels  21.5 us (52%)
  starting transfers between devices  15 us (36%)
  waiting for transfers between devices  3.4 us (8%)
  between operations  1.02 us (2%)
    pallas_call x14, Pallas kernels, call(): pl.pallas_call(kernel, out_shape=shapes, in_specs=[pl.BlockSpec(memory_sp...  21.5 us
    ppermute x12, starting transfers between devices, exchange(): results.append(lax.ppermute(value, names, pairs))  15 us
    ppermute x12, waiting for transfers between devices, exchange(): results.append(lax.ppermute(value, names, pairs))  3.4 us
  transfers between devices with their start and end apart: 12, of which 3 were waited for; matrix products, arithmetic and copies ran while one was open for 0% of the time, Pallas kernels for 35%

profile of v16, /device:TPU:0, one launch (start us, length us, event | category | flops | bytes accessed | tf_op | source)
XLA Modules:
  0.0 41.1 jit_solution(16004630146236547112)
XLA Ops:
  0.6 0.0 copy-start.5
  0.6 0.0 copy-start.6
  0.7 0.0 copy-start.7
  0.7 0.0 copy-start.10
  0.7 0.0 copy-start.2
  0.7 0.0 copy-start.1
  0.7 0.0 copy-start.4
  0.7 0.0 copy-start.3
  0.7 1.9 %shard_map.140 = (f32[136,128]{1,0:T(8,128)S(1)}, f32[136,128]{1,0:T(8,128)S(1)}, f32[136,128]{1,0:T(8,128)S(1)}, f32[136,128]{1,0:T(8,128)S(1)}, f32[136,128]{1...) custom-call(f32[16,128,128]{2,1,0:T(8,128)} %stress.13, ...), custom_call_target="tpu_custom_call" | custom-call | flops 1500000000 | bytes 1500000 | tf_op jit(solution)/shard_map/pallas_call | solution.py:570
  2.6 0.5 %collective-permute-start.1 = (f32[128,128]{1,0:T(8,128)S(1)}, f32[128,128]{1,0:T(8,128)S(1)}, u32[]{:S(2)}, u32[]{:S(2)}) collective-permute-start(f32[128,128]{1,0:T(8,128)S(1)} %slice.55), channel_id=1, source_target_pairs={{0,1},{1,0},{2,3},{3,2},{4,8},{5,9},{6,10},{7,11},{8,4},{9,5},{10,... | collective-permute-start | bytes 196616 | tf_op jit(solution)/shard_map/ppermute | solution.py:600
  3.2 4.0 %collective-permute-start = (f32[128,128]{1,0:T(8,128)S(1)}, f32[128,128]{1,0:T(8,128)S(1)}, u32[]{:S(2)}, u32[]{:S(2)}) collective-permute-start(f32[128,128]{1,0:T(8,128)S(1)} %slice.54), channel_id=1, source_target_pairs={{0,4},{1,5},{2,6},{3,7},{4,0},{5,1},{6,2},{7,3},{8,12},{9,13},{10,... | collective-permute-start | bytes 196616 | tf_op jit(solution)/shard_map/ppermute | solution.py:600
  7.2 0.0 copy-done.5
  7.2 0.0 copy-done.6
  7.2 0.0 copy-done.7
  7.2 0.0 copy-done.10
  7.2 0.0 copy-done.2
  7.2 0.0 copy-done.1
  7.2 0.0 copy-done.4
  7.2 0.0 copy-done.3
  7.3 2.9 %shard_map.139 = (f32[16,136,128]{2,1,0:T(8,128)S(1)}, f32[136,256]{1,0:T(8,128)S(1)}, f32[136,256]{1,0:T(8,128)S(1)}, f32[16,128,128]{2,1,0:T(8,128)S(1)}, f32[16,128,128]{2,1,0:T(8,128)S(1)}) custom-call(f32[16,128,128]{2,1,0:T(8,128)S(1)} %copy-done.1, f32[16,128,128]{2,1,0:T(8,128)S(1)} %copy-done.2, s32[16,128,128]{2,1,0:T(8,128)S(1)} %copy-done.3, ...), custom_call_target="tpu_custom_call" | custom-call | flops 4499999744 | bytes 4500000 | tf_op jit(solution)/shard_map/pallas_call | solution.py:570
  10.2 0.0 copy-start
  10.2 0.0 copy-start.11
  10.2 0.0 collective-permute-done.1.row_odd
  10.2 0.0 collective-permute-done.row_even
  10.2 0.4 shard_map.141
  10.6 1.6 %collective-permute-start.3 = (f32[128,128]{1,0:T(8,128)S(1)}, f32[128,128]{1,0:T(8,128)S(1)}, u32[]{:S(2)}, u32[]{:S(2)}) collective-permute-start(f32[128,128]{1,0:T(8,128)S(1)} %slice.57), channel_id=1, source_target_pairs={{0,4},{4,0},{8,12},{12,8},{16,20},{20,16},{24,28},{28,24},{1,2},{5... | collective-permute-start | bytes 196616 | tf_op jit(solution)/shard_map/ppermute | solution.py:600
  12.2 0.1 collective-permute-start.2
  12.3 0.0 copy-done
  12.3 0.0 copy-done.11
  12.3 1.2 %shard_map.142 = (f32[16,128,128]{2,1,0:T(8,128)S(1)}, f32[16,8,128]{2,1,0:T(8,128)S(1)}, f32[136,128]{1,0:T(8,128)S(1)}, f32[136,128]{1,0:T(8,128)S(1)}, f32[16,128,128]{2,1,0:T(8,128)}) custom-call(f32[16,136,128]{2,1,0:T(8,128)S(1)} %get-tuple-element.53.across, f32[128,128]{1,0:T(8,128)S(1)} %collective-permute-done.row_even, ...), custom_call_target="tpu_custom_call" | custom-call | flops 1800000000 | bytes 1800000 | tf_op jit(solution)/shard_map/pallas_call | solution.py:570
  13.6 0.0 copy-start.8
  13.6 0.0 copy-start.9
  13.6 1.1 %shard_map.143.fixed = f32[136,128]{1,0:T(8,128)S(1)} custom-call(f32[16,128,128]{2,1,0:T(8,128)S(1)} %copy-done.1, f32[16,128,128]{2,1,0:T(8,128)S(1)} %copy-done.2, f32[16,128,128]{2,1,0:T(8,128)S(1)} %copy-done, f32[184,128]{1,0:T(8,128)S(1)} %get-tuple-element.69._), custom_call_target="tpu_custom_call" | custom-call | flops 800000000 | bytes 800000 | tf_op jit(solution)/shard_map/pallas_call | solution.py:570
  14.7 0.3 collective-permute-done.3.col_odd
  14.9 0.0 collective-permute-done.2.col_even
  14.9 0.0 copy-done.8
  14.9 0.0 copy-done.9
  14.9 0.6 %shard_map.145 = (f32[176,128]{1,0:T(8,128)S(1)}, f32[176,128]{1,0:T(8,128)S(1)}) custom-call(f32[16,128,128]{2,1,0:T(8,128)S(1)} %copy-done.1, f32[16,128,128]{2,1,0:T(8,128)S(1)} %copy-done.2, s32[16,128,128]{2,1,0:T(8,128)S(1)} %copy-done.3, s32[16,128,128]{2,1,0:T(8,128)S(1)} %copy-done.4, f32[16,128,128]{2,1,0:T(8,128)S(1)} %copy-done, ...), custom_call_target="tpu_custom_call" | custom-call | flops 800000000 | bytes 800000 | tf_op jit(solution)/shard_map/pallas_call | solution.py:570
  15.6 0.3 collective-permute-start.5
  15.9 2.9 %collective-permute-start.4 = (f32[128,128]{1,0:T(8,128)S(1)}, f32[128,128]{1,0:T(8,128)S(1)}, u32[]{:S(2)}, u32[]{:S(2)}) collective-permute-start(f32[128,128]{1,0:T(8,128)S(1)} %slice.58), channel_id=1, source_target_pairs={{0,4},{1,5},{2,6},{3,7},{4,0},{5,1},{6,2},{7,3},{8,12},{9,13},{10,... | collective-permute-start | bytes 196616 | tf_op jit(solution)/shard_map/ppermute | solution.py:600
  18.8 3.4 %shard_map.144 = (f32[16,136,128]{2,1,0:T(8,128)S(1)}, f32[136,256]{1,0:T(8,128)S(1)}, f32[136,256]{1,0:T(8,128)S(1)}, f32[16,128,128]{2,1,0:T(8,128)S(1)}) custom-call(f32[16,128,128]{2,1,0:T(8,128)S(1)} %copy-done.1, f32[16,128,128]{2,1,0:T(8,128)S(1)} %copy-done.2, s32[16,128,128]{2,1,0:T(8,128)S(1)} %copy-done.3, s32[16,128,128]{2,1,0:T(8,128)S(1)} %copy-done.4, ...), custom_call_target="tpu_custom_call" | custom-call | flops 4499999744 | bytes 4500000 | tf_op jit(solution)/shard_map/pallas_call | solution.py:570
  22.1 0.0 collective-permute-done.5.row_odd
  22.2 0.0 collective-permute-done.4.row_even
  22.2 0.4 shard_map.146
  22.6 1.2 %collective-permute-start.7 = (f32[128,128]{1,0:T(8,128)S(1)}, f32[128,128]{1,0:T(8,128)S(1)}, u32[]{:S(2)}, u32[]{:S(2)}) collective-permute-start(f32[128,128]{1,0:T(8,128)S(1)} %slice.61), channel_id=1, source_target_pairs={{0,4},{4,0},{8,12},{12,8},{16,20},{20,16},{24,28},{28,24},{1,2},{5... | collective-permute-start | bytes 196616 | tf_op jit(solution)/shard_map/ppermute | solution.py:600
  23.8 0.0 collective-permute-start.6
  23.8 1.2 %shard_map.147 = (f32[16,128,128]{2,1,0:T(8,128)S(1)}, f32[16,8,128]{2,1,0:T(8,128)S(1)}, f32[136,128]{1,0:T(8,128)S(1)}, f32[136,128]{1,0:T(8,128)S(1)}, f32[16,128,128]{2,1,0:T(8,128)}) custom-call(f32[16,136,128]{2,1,0:T(8,128)S(1)} %get-tuple-element.70.across, f32[128,128]{1,0:T(8,128)S(1)} %collective-permute-done.4.row_even, ...), custom_call_target="tpu_custom_call" | custom-call | flops 1800000000 | bytes 1800000 | tf_op jit(solution)/shard_map/pallas_call | solution.py:570
  25.0 1.9 %collective-permute-done.7.col_odd = f32[128,128]{1,0:T(8,128)S(1)} collective-permute-done((f32[128,128]{1,0:T(8,128)S(1)}, f32[128,128]{1,0:T(8,128)S(1)}, u32[]{:S(2)}, u32[]{:S(2)}) %collective-permute-start.7) | collective-permute-done | bytes 65568 | tf_op jit(solution)/shard_map/ppermute | solution.py:600
  26.9 0.0 collective-permute-done.6.col_even
  26.9 0.6 %shard_map.149 = (f32[176,128]{1,0:T(8,128)S(1)}, f32[176,128]{1,0:T(8,128)S(1)}) custom-call(f32[16,128,128]{2,1,0:T(8,128)S(1)} %copy-done.1, f32[16,128,128]{2,1,0:T(8,128)S(1)} %copy-done.2, s32[16,128,128]{2,1,0:T(8,128)S(1)} %copy-done.3, s32[16,128,128]{2,1,0:T(8,128)S(1)} %copy-done.4, f32[16,128,128]{2,1,0:T(8,128)S(1)} %copy-done, ...), custom_call_target="tpu_custom_call" | custom-call | flops 800000000 | bytes 800000 | tf_op jit(solution)/shard_map/pallas_call | solution.py:570
  27.5 1.2 %collective-permute-start.8 = (f32[176,128]{1,0:T(8,128)S(1)}, f32[176,128]{1,0:T(8,128)S(1)}, u32[]{:S(2)}, u32[]{:S(2)}) collective-permute-start(f32[176,128]{1,0:T(8,128)S(1)} %get-tuple-element.85), channel_id=1, source_target_pairs={{0,4},{1,5},{2,6},{3,7},{4,0},{5,1},{6,2},{7,3},{8,12},{9,13},{10,... | collective-permute-start | bytes 270344 | tf_op jit(solution)/shard_map/ppermute | solution.py:600
  28.7 0.0 collective-permute-start.9
  28.7 3.4 %shard_map.148 = (f32[16,136,128]{2,1,0:T(8,128)S(1)}, f32[136,256]{1,0:T(8,128)S(1)}, f32[136,256]{1,0:T(8,128)S(1)}, f32[16,128,128]{2,1,0:T(8,128)S(1)}) custom-call(f32[16,128,128]{2,1,0:T(8,128)S(1)} %copy-done.1, f32[16,128,128]{2,1,0:T(8,128)S(1)} %copy-done.2, s32[16,128,128]{2,1,0:T(8,128)S(1)} %copy-done.3, s32[16,128,128]{2,1,0:T(8,128)S(1)} %copy-done.4, ...), custom_call_target="tpu_custom_call" | custom-call | flops 4499999744 | bytes 4500000 | tf_op jit(solution)/shard_map/pallas_call | solution.py:570
  32.1 0.0 collective-permute-done.8
  32.1 0.0 collective-permute-done.9
  32.2 0.4 shard_map.150
  32.6 3.1 %collective-permute-start.11 = (f32[176,128]{1,0:T(8,128)S(1)}, f32[176,128]{1,0:T(8,128)S(1)}, u32[]{:S(2)}, u32[]{:S(2)}) collective-permute-start(f32[176,128]{1,0:T(8,128)S(1)} %slice.68), channel_id=1, source_target_pairs={{0,4},{4,0},{8,12},{12,8},{16,20},{20,16},{24,28},{28,24},{1,2},{5... | collective-permute-start | bytes 270344 | tf_op jit(solution)/shard_map/ppermute | solution.py:600
  35.7 0.0 collective-permute-start.10
  35.7 1.2 %shard_map.151 = (f32[16,128,128]{2,1,0:T(8,128)S(1)}, f32[16,8,128]{2,1,0:T(8,128)S(1)}, f32[136,128]{1,0:T(8,128)S(1)}, f32[136,128]{1,0:T(8,128)S(1)}, f32[16,128,128]{2,1,0:T(8,128)}) custom-call(f32[16,136,128]{2,1,0:T(8,128)S(1)} %get-tuple-element.83.across, f32[128,128]{1,0:T(8,128)S(1)} %slice.72.row_even, f32[128,128]{1,0:T(8,128)S(1)} %slice.73.row_odd, ...), custom_call_target="tpu_custom_call" | custom-call | flops 1800000000 | bytes 1800000 | tf_op jit(solution)/shard_map/pallas_call | solution.py:570
  36.9 1.3 %collective-permute-done.11 = f32[176,128]{1,0:T(8,128)S(1)} collective-permute-done((f32[176,128]{1,0:T(8,128)S(1)}, f32[176,128]{1,0:T(8,128)S(1)}, u32[]{:S(2)}, u32[]{:S(2)}) %collective-permute-start.11) | collective-permute-done | bytes 90144 | tf_op jit(solution)/shard_map/ppermute | solution.py:600
  38.2 0.0 collective-permute-done.10
  38.2 2.8 %shard_map.152 = (f32[16,128,128]{2,1,0:T(8,128)}, f32[2,16,128,128]{3,2,1,0:T(8,128)}) custom-call(f32[16,128,128]{2,1,0:T(8,128)S(1)} %copy-done.1, f32[16,128,128]{2,1,0:T(8,128)S(1)} %copy-done.2, f32[16,128,128]{2,1,0:T(8,128)S(1)} %get-tuple-element.89._.plastic, f32[16,128,128]{2,1,0:T(8,128)S(1)} %get-tuple-element.92.inner, ...), custom_call_target="tpu_custom_call" | custom-call | flops 3000000000 | bytes 3000000 | tf_op jit(solution)/shard_map/pallas_call | solution.py:570
  (18 shorter events, 0.1 us)
Async XLA Ops:
  0.6 6.6 %copy-start.5 = (f32[128,256]{1,0:T(8,128)S(1)}, f32[128,256]{1,0:T(8,128)}, u32[]{:S(2)}) copy-start(f32[128,256]{1,0:T(8,128)} %constant.19.clone.high_ref) | copy-start | bytes 393220
  0.6 6.6 %copy-start.6 = (f32[128,256]{1,0:T(8,128)S(1)}, f32[128,256]{1,0:T(8,128)}, u32[]{:S(2)}) copy-start(f32[128,256]{1,0:T(8,128)} %constant.18.clone.low_ref) | copy-start | bytes 393220
  0.7 6.6 %copy-start.7 = (f32[128,128]{1,0:T(8,128)S(1)}, f32[128,128]{1,0:T(8,128)}, u32[]{:S(2)}) copy-start(f32[128,128]{1,0:T(8,128)} %constant.20.clone.next_ref) | copy-start | bytes 196612
  0.7 6.5 %copy-start.10 = (f32[136,128]{1,0:T(8,128)S(1)}, f32[136,128]{1,0:T(8,128)}, u32[]{:S(2)}) copy-start(f32[136,128]{1,0:T(8,128)} %constant.16.clone.band_ref) | copy-start | bytes 208900
  0.7 6.5 %copy-start.2 = (f32[16,128,128]{2,1,0:T(8,128)S(1)}, f32[16,128,128]{2,1,0:T(8,128)}, u32[]{:S(2)}) copy-start(f32[16,128,128]{2,1,0:T(8,128)} %strain.13) | copy-start | bytes 3145732
  0.7 6.5 %copy-start.1 = (f32[16,128,128]{2,1,0:T(8,128)S(1)}, f32[16,128,128]{2,1,0:T(8,128)}, u32[]{:S(2)}) copy-start(f32[16,128,128]{2,1,0:T(8,128)} %stress.13) | copy-start | bytes 3145732
  0.7 6.5 %copy-start.4 = (s32[16,128,128]{2,1,0:T(8,128)S(1)}, s32[16,128,128]{2,1,0:T(8,128)}, u32[]{:S(2)}) copy-start(s32[16,128,128]{2,1,0:T(8,128)} %count.9) | copy-start | bytes 3145732
  0.7 6.5 %copy-start.3 = (s32[16,128,128]{2,1,0:T(8,128)S(1)}, s32[16,128,128]{2,1,0:T(8,128)}, u32[]{:S(2)}) copy-start(s32[16,128,128]{2,1,0:T(8,128)} %yields.9) | copy-start | bytes 3145732
  2.6 7.5 %collective-permute-start.1 = (f32[128,128]{1,0:T(8,128)S(1)}, f32[128,128]{1,0:T(8,128)S(1)}, u32[]{:S(2)}, u32[]{:S(2)}) collective-permute-start(f32[128,128]{1,0:T(8,128)S(1)} %slice.55), channel_id=1, source_target_pairs={{0,1},{1,0},{2,3},{3,2},{4,8},{5,9},{6,10},{7,11},{8,4},{9,5},{10,... | collective-permute-start | bytes 196616 | tf_op jit(solution)/shard_map/ppermute | solution.py:600
  3.2 7.0 %collective-permute-start = (f32[128,128]{1,0:T(8,128)S(1)}, f32[128,128]{1,0:T(8,128)S(1)}, u32[]{:S(2)}, u32[]{:S(2)}) collective-permute-start(f32[128,128]{1,0:T(8,128)S(1)} %slice.54), channel_id=1, source_target_pairs={{0,4},{1,5},{2,6},{3,7},{4,0},{5,1},{6,2},{7,3},{8,12},{9,13},{10,... | collective-permute-start | bytes 196616 | tf_op jit(solution)/shard_map/ppermute | solution.py:600
  10.2 2.1 %copy-start = (f32[16,128,128]{2,1,0:T(8,128)S(1)}, f32[16,128,128]{2,1,0:T(8,128)}, u32[]{:S(2)}) copy-start(f32[16,128,128]{2,1,0:T(8,128)} %threshold.11) | copy-start | bytes 3145732
  10.2 2.1 %copy-start.11 = (f32[128,128]{1,0:T(8,128)S(1)}, f32[128,128]{1,0:T(8,128)}, u32[]{:S(2)}) copy-start(f32[128,128]{1,0:T(8,128)} %constant.17.clone.band_ref) | copy-start | bytes 196612
  10.6 4.3 %collective-permute-start.3 = (f32[128,128]{1,0:T(8,128)S(1)}, f32[128,128]{1,0:T(8,128)S(1)}, u32[]{:S(2)}, u32[]{:S(2)}) collective-permute-start(f32[128,128]{1,0:T(8,128)S(1)} %slice.57), channel_id=1, source_target_pairs={{0,4},{4,0},{8,12},{12,8},{16,20},{20,16},{24,28},{28,24},{1,2},{5... | collective-permute-start | bytes 196616 | tf_op jit(solution)/shard_map/ppermute | solution.py:600
  12.2 2.7 %collective-permute-start.2 = (f32[128,128]{1,0:T(8,128)S(1)}, f32[128,128]{1,0:T(8,128)S(1)}, u32[]{:S(2)}, u32[]{:S(2)}) collective-permute-start(f32[128,128]{1,0:T(8,128)S(1)} %slice.56), channel_id=1, source_target_pairs={{0,1},{4,5},{8,9},{12,13},{16,17},{20,21},{24,25},{28,29},{1,0},{5... | collective-permute-start | bytes 196616 | tf_op jit(solution)/shard_map/ppermute | solution.py:600
  13.6 1.4 %copy-start.8 = (f32[144,128]{1,0:T(8,128)S(1)}, f32[144,128]{1,0:T(8,128)}, u32[]{:S(2)}) copy-start(f32[144,128]{1,0:T(8,128)} %constant.15.clone.above) | copy-start | bytes 221188
  13.6 1.4 %copy-start.9 = (f32[128,128]{1,0:T(8,128)S(1)}, f32[128,128]{1,0:T(8,128)}, u32[]{:S(2)}) copy-start(f32[128,128]{1,0:T(8,128)} %constant.14.clone.below) | copy-start | bytes 196612
  15.6 6.6 %collective-permute-start.5 = (f32[128,128]{1,0:T(8,128)S(1)}, f32[128,128]{1,0:T(8,128)S(1)}, u32[]{:S(2)}, u32[]{:S(2)}) collective-permute-start(f32[128,128]{1,0:T(8,128)S(1)} %slice.59), channel_id=1, source_target_pairs={{0,1},{1,0},{2,3},{3,2},{4,8},{5,9},{6,10},{7,11},{8,4},{9,5},{10,... | collective-permute-start | bytes 196616 | tf_op jit(solution)/shard_map/ppermute | solution.py:600
  15.9 6.3 %collective-permute-start.4 = (f32[128,128]{1,0:T(8,128)S(1)}, f32[128,128]{1,0:T(8,128)S(1)}, u32[]{:S(2)}, u32[]{:S(2)}) collective-permute-start(f32[128,128]{1,0:T(8,128)S(1)} %slice.58), channel_id=1, source_target_pairs={{0,4},{1,5},{2,6},{3,7},{4,0},{5,1},{6,2},{7,3},{8,12},{9,13},{10,... | collective-permute-start | bytes 196616 | tf_op jit(solution)/shard_map/ppermute | solution.py:600
  22.6 4.3 %collective-permute-start.7 = (f32[128,128]{1,0:T(8,128)S(1)}, f32[128,128]{1,0:T(8,128)S(1)}, u32[]{:S(2)}, u32[]{:S(2)}) collective-permute-start(f32[128,128]{1,0:T(8,128)S(1)} %slice.61), channel_id=1, source_target_pairs={{0,4},{4,0},{8,12},{12,8},{16,20},{20,16},{24,28},{28,24},{1,2},{5... | collective-permute-start | bytes 196616 | tf_op jit(solution)/shard_map/ppermute | solution.py:600
  23.8 3.1 %collective-permute-start.6 = (f32[128,128]{1,0:T(8,128)S(1)}, f32[128,128]{1,0:T(8,128)S(1)}, u32[]{:S(2)}, u32[]{:S(2)}) collective-permute-start(f32[128,128]{1,0:T(8,128)S(1)} %slice.60), channel_id=1, source_target_pairs={{0,1},{4,5},{8,9},{12,13},{16,17},{20,21},{24,25},{28,29},{1,0},{5... | collective-permute-start | bytes 196616 | tf_op jit(solution)/shard_map/ppermute | solution.py:600
  27.5 4.6 %collective-permute-start.8 = (f32[176,128]{1,0:T(8,128)S(1)}, f32[176,128]{1,0:T(8,128)S(1)}, u32[]{:S(2)}, u32[]{:S(2)}) collective-permute-start(f32[176,128]{1,0:T(8,128)S(1)} %get-tuple-element.85), channel_id=1, source_target_pairs={{0,4},{1,5},{2,6},{3,7},{4,0},{5,1},{6,2},{7,3},{8,12},{9,13},{10,... | collective-permute-start | bytes 270344 | tf_op jit(solution)/shard_map/ppermute | solution.py:600
  28.7 3.4 %collective-permute-start.9 = (f32[176,128]{1,0:T(8,128)S(1)}, f32[176,128]{1,0:T(8,128)S(1)}, u32[]{:S(2)}, u32[]{:S(2)}) collective-permute-start(f32[176,128]{1,0:T(8,128)S(1)} %get-tuple-element.86), channel_id=1, source_target_pairs={{0,1},{1,0},{2,3},{3,2},{4,8},{5,9},{6,10},{7,11},{8,4},{9,5},{10,... | collective-permute-start | bytes 270344 | tf_op jit(solution)/shard_map/ppermute | solution.py:600
  32.6 5.6 %collective-permute-start.11 = (f32[176,128]{1,0:T(8,128)S(1)}, f32[176,128]{1,0:T(8,128)S(1)}, u32[]{:S(2)}, u32[]{:S(2)}) collective-permute-start(f32[176,128]{1,0:T(8,128)S(1)} %slice.68), channel_id=1, source_target_pairs={{0,4},{4,0},{8,12},{12,8},{16,20},{20,16},{24,28},{28,24},{1,2},{5... | collective-permute-start | bytes 270344 | tf_op jit(solution)/shard_map/ppermute | solution.py:600
  35.7 2.5 %collective-permute-start.10 = (f32[176,128]{1,0:T(8,128)S(1)}, f32[176,128]{1,0:T(8,128)S(1)}, u32[]{:S(2)}, u32[]{:S(2)}) collective-permute-start(f32[176,128]{1,0:T(8,128)S(1)} %slice.66), channel_id=1, source_target_pairs={{0,1},{4,5},{8,9},{12,13},{16,17},{20,21},{24,25},{28,29},{1,0},{5... | collective-permute-start | bytes 270344 | tf_op jit(solution)/shard_map/ppermute | solution.py:600
